TPU v7x, 32 devices: a whole 2x2x4 slice. The times are simulated.
32 devices in a mesh: wall: 8 (over y, x, core), span: 4 (over z).
Axes of the slice: x: 2, y: 2, z: 4, core: 2. Of those that a mesh axis runs over, the one named last changes fastest.
Arguments:
- field: float32 [4, 3, 2, 256, 6144], P(None, None, None, 'wall', 'span'), may hold values from -6 to 6
- mean_flow: float32 [2, 256], P(None, 'wall'), may hold values from 0.2 to 1.5
- d2_coef: float32 [15, 256], P(None, 'wall'), may hold values from -2 to 2
- wall_coef: float32 [2, 8], replicated, may hold values from -0.4375 to 0.4375
- kx_index: int32 [4], replicated, may hold values from 1 to 7
- patch_of: int32 [6144], P('span'), may hold values from 0 to 63
Outputs:
- new_field: float32 [4, 3, 2, 256, 6144], P(None, None, None, 'wall', 'span')
- wall_grad: float32 [2, 4, 2, 64], replicated
All inputs are finite; a program needn't handle non-finite values.
Results may differ from a plain program's by a relative error of at most 0.000073.
Values sent between devices are 32-bit elements; how exact they have to be, the bound alone decides.
No kernel may reach another device: no remote copies, remote signals or barrier semaphores. Data moves between devices by JAX's collectives and lax.ppermute only.
A program may use at most 192 MiB of HBM per device.

v0:
```python
import math

import jax
import jax.numpy as jnp
from jax import lax
from jax.sharding import PartitionSpec as P

HALO = 7
STEN = 15
PATCH = 64


TAU = 0.25
VIS = 0.5


def with_halo(block, sides, width):
    for axis, dim in sides:
        count = lax.axis_size(axis)
        forward = [(i, i + 1) for i in range(count - 1)]
        backward = [(target, source) for source, target in forward]
        low = lax.ppermute(
            lax.slice_in_dim(block, block.shape[dim] - width, None, axis=dim), axis, forward
        )
        high = lax.ppermute(lax.slice_in_dim(block, 0, width, axis=dim), axis, backward)
        block = jnp.concatenate([low, block, high], axis=dim)
    return block


def spanwise_operator(line_data):
    item_count, part_count, row_count, length = line_data.shape
    inner_size = 128
    outer_size = length // inner_size
    highest = lax.Precision.HIGHEST
    real_part = line_data[:, 0].reshape(item_count, row_count, outer_size, inner_size)
    imag_part = line_data[:, 1].reshape(item_count, row_count, outer_size, inner_size)
    outer = jnp.arange(outer_size, dtype=jnp.int32)
    inner = jnp.arange(inner_size, dtype=jnp.int32)
    angle_one = (
        -2.0
        * math.pi
        / outer_size
        * (outer[:, None] * outer[None, :] % outer_size).astype(jnp.float32)
    )
    angle_two = (
        -2.0
        * math.pi
        / inner_size
        * (inner[:, None] * inner[None, :] % inner_size).astype(jnp.float32)
    )
    angle_twist = (
        -2.0 * math.pi / length * (outer[:, None] * inner[None, :] % length).astype(jnp.float32)
    )
    cos_one, sin_one = (jnp.cos(angle_one), jnp.sin(angle_one))
    cos_two, sin_two = (jnp.cos(angle_two), jnp.sin(angle_two))
    cos_twist, sin_twist = (jnp.cos(angle_twist), jnp.sin(angle_twist))

    def first_section(table, values):
        return jnp.einsum("kn,irnm->irkm", table, values, precision=highest)

    def second_section(values, table):
        return jnp.einsum("irkn,nm->irkm", values, table, precision=highest)

    def second_back(values, table):
        return jnp.einsum("irkm,nm->irkn", values, table, precision=highest)

    def first_back(table, values):
        return jnp.einsum("kn,irkm->irnm", table, values, precision=highest)

    section_real = first_section(cos_one, real_part) - first_section(sin_one, imag_part)
    section_imag = first_section(cos_one, imag_part) + first_section(sin_one, real_part)
    twist_real = section_real * cos_twist - section_imag * sin_twist
    twist_imag = section_real * sin_twist + section_imag * cos_twist
    modes_real = second_section(twist_real, cos_two) - second_section(twist_imag, sin_two)
    modes_imag = second_section(twist_real, sin_two) + second_section(twist_imag, cos_two)
    wave_index = outer[:, None] + outer_size * inner[None, :]
    signed = jnp.where(wave_index > length // 2, wave_index - length, wave_index)
    cutoff = length // 3
    wave_ratio = signed.astype(jnp.float32) / cutoff
    multiplier = jnp.where(
        jnp.abs(signed) < cutoff, -VIS * wave_ratio * wave_ratio, 0.0 * wave_ratio
    )
    modes_real = modes_real * multiplier
    modes_imag = modes_imag * multiplier
    back_real = second_back(modes_real, cos_two) + second_back(modes_imag, sin_two)
    back_imag = second_back(modes_imag, cos_two) - second_back(modes_real, sin_two)
    untwist_real = back_real * cos_twist + back_imag * sin_twist
    untwist_imag = back_imag * cos_twist - back_real * sin_twist
    result_real = (first_back(cos_one, untwist_real) + first_back(sin_one, untwist_imag)) / length
    result_imag = (first_back(cos_one, untwist_imag) - first_back(sin_one, untwist_real)) / length
    result_real = result_real.reshape(item_count, row_count, length)
    result_imag = result_imag.reshape(item_count, row_count, length)
    return jnp.stack([result_real, result_imag], axis=1)


def on_device(field, mean_flow, d2_coef, wall_coef, kx_index, patch_of):
    mode_count, comp_count, part_count, row_count, col_count = field.shape
    padded = with_halo(field, (("wall", 3),), HALO)
    diffusion = jnp.zeros_like(field)
    for offset in range(STEN):
        diffusion = (
            diffusion + d2_coef[offset][:, None] * padded[:, :, :, offset : offset + row_count, :]
        )
    flattened = field.reshape(mode_count * comp_count, part_count, row_count, col_count)
    spectral_lines = spanwise_operator(
        lax.all_to_all(flattened, "span", split_axis=2, concat_axis=3, tiled=True)
    )
    spanwise = lax.all_to_all(spectral_lines, "span", split_axis=3, concat_axis=2, tiled=True)
    spanwise = spanwise.reshape(field.shape)
    wave_number = kx_index.astype(jnp.float32) * 0.25
    velocity = mean_flow[0]
    shear_rate = mean_flow[1]
    advect_rate = wave_number[:, None, None, None] * velocity[None, None, :, None]
    advect_real = -advect_rate * field[:, :, 1]
    advect_imag = advect_rate * field[:, :, 0]
    advection = jnp.stack([advect_real, advect_imag], axis=2)
    coupling = shear_rate[None, None, :, None] * field[:, 0]
    advection = advection.at[:, 1].add(-coupling)
    new_field = field + TAU * advection + diffusion + spanwise
    lower_wall = jnp.zeros_like(new_field[:, 0, :, 0, :])
    upper_wall = jnp.zeros_like(new_field[:, 0, :, 0, :])
    for offset in range(HALO + 1):
        lower_wall = lower_wall + wall_coef[0, offset] * new_field[:, 0, :, offset, :]
        upper_wall = (
            upper_wall + wall_coef[1, offset] * new_field[:, 0, :, row_count - 1 - offset, :]
        )
    wall_index = lax.axis_index("wall")
    wall_count = lax.axis_size("wall")
    lower_wall = jnp.where(wall_index == 0, lower_wall, 0.0 * lower_wall)
    upper_wall = jnp.where(wall_index == wall_count - 1, upper_wall, 0.0 * upper_wall)
    shear_rows = jnp.stack([lower_wall, upper_wall])
    onehot = (patch_of[:, None] == jnp.arange(PATCH, dtype=jnp.int32)[None, :]).astype(jnp.float32)
    partial_grad = jnp.einsum("wmcz,zp->wmcp", shear_rows, onehot, precision=lax.Precision.HIGHEST)
    wall_grad = lax.psum(partial_grad, ("wall", "span"))
    return (new_field, wall_grad)


def solution(mesh):
    return jax.shard_map(
        on_device,
        mesh=mesh,
        in_specs=(
            P(None, None, None, "wall", "span"),
            P(None, "wall"),
            P(None, "wall"),
            P(),
            P(),
            P("span"),
        ),
        out_specs=(P(None, None, None, "wall", "span"), P()),
        check_vma=False,
    )
```

profile of v0, /device:TPU:10, one launch (start us, length us, event | category | flops | bytes accessed | tf_op | source)
XLA Modules:
  0.0 637.4 jit_solution(16478057708921564509)
XLA Ops:
  0.6 8.2 %copy.115 = f32[4,3,2,32,1536]{4,2,1,0,3:T(2,128)} copy(f32[4,3,2,32,1536]{4,3,2,1,0:T(8,128)} %param.8) | data formatting | bytes 9437184 | tf_op args[0]
  8.8 5.6 all-to-all-start
  14.4 0.1 fusion.115
  14.5 101.0 %all-to-all-done = f32[12,2,32,1536]{3,1,0,2:T(2,128)} async-done(((f32[12,2,32,1536]{3,1,0,2:T(2,128)}), f32[12,2,32,1536]{3,1,0,2:T(2,128)}, u32[]{:S(2)}, u32[]{:S(2)}) %all-to-all-start) | async-done | bytes 4718624 | tf_op jit(solution)/shard_map/all_to_all | solution.py:106
  115.5 5.1 copy.116
  120.6 0.5 slice_bitcast_fusion.1
  121.1 2.4 fusion.18
  123.4 2.3 fusion.16
  125.8 2.4 fusion.40
  128.2 2.9 fusion.43
  131.1 2.4 fusion.24
  133.5 2.3 fusion.26
  135.8 2.4 add_multiply_fusion
  138.2 2.3 fusion.62
  140.6 2.6 subtract_multiply_fusion
  143.2 2.3 fusion.65
  145.5 2.4 convolution_subtract_fusion
  147.9 2.3 convolution_add_fusion
  150.2 0.0 copy-start
  150.2 2.7 fusion.50
  152.9 4.3 fusion.51
  157.3 0.0 copy-done
  157.3 4.3 multiply_bitcast_fusion.1
  161.6 12.0 %copy.141 = f32[12,8,48,128]{0,1,3,2:T(8,128)} copy(f32[12,8,48,128]{3,2,1,0:T(8,128)} %multiply_bitcast_fusion.1) | data formatting | bytes 4718592 | tf_op jit(solution)/shard_map/stack;reshape | solution.py:93
  173.5 6.6 %multiply_bitcast_fusion = f32[12,8,48,128]{3,2,1,0:T(8,128)} fusion(f32[12,8,128,48]{2,3,1,0:T(8,128)} %fusion.51, f32[12,8,48,128]{3,2,1,0:T(8,128)S(1)} %convolution_subtract_fusion, f32[12,8,48,128]{3,2,1,0:T(8,128)} %copy-done, f32[48,128]{1,0:T(8,128)S(1)} %get-tuple-element.69, f32[48,128]{1,0:T(8,128)S(1)} %get-tuple-element.70), kind=kOutput, calls=%fused_computation.54 | convolution fusion | flops 342708480 | bytes 9486336 | tf_op jit(solution)/shard_map/kn,irkm->irnm/dot_general | solution.py:68
  180.1 12.0 %copy.142 = f32[12,8,48,128]{0,1,3,2:T(8,128)} copy(f32[12,8,48,128]{3,2,1,0:T(8,128)} %multiply_bitcast_fusion) | data formatting | bytes 4718592 | tf_op jit(solution)/shard_map/stack;reshape | solution.py:93
  192.0 33.8 %fusion.215 = f32[6144,2,8,12]{3,2,1,0:T(8,128)} fusion(f32[12,1,8,6144]{0,2,1,3:T(8,128)} %bitcast.174, f32[12,1,8,6144]{0,2,1,3:T(8,128)} %bitcast.173), kind=kLoop, calls=%fused_computation.268 | loop fusion | flops 1179648 | bytes 9437184
  225.8 77.0 %reshape.465 = f32[4,1,294912]{2,1,0:T(1,128)} reshape(f32[6144,2,8,12]{3,2,1,0:T(8,128)} %fusion.215) | data formatting | bytes 9437184
  302.8 8.3 %all-to-all-start.1 = ((f32[4,1,294912]{2,1,0:T(1,128)}), f32[4,1,294912]{2,1,0:T(1,128)}, u32[]{:S(2)}, u32[]{:S(2)}) async-start(f32[4,1,294912]{2,1,0:T(1,128)} %reshape.465), calls=%async_computation.1 | async-start | bytes 9437184 | tf_op jit(solution)/shard_map/all_to_all | solution.py:108
  311.1 5.4 copy.109
  316.5 2.2 copy-done.1
  318.7 0.1 fusion.213
  318.8 1.9 collective-permute-start
  320.8 3.6 collective-permute-start.1
  324.4 0.0 copy-done.7
  324.4 0.0 copy-done.5
  324.5 0.1 fusion.155
  324.6 3.3 slice_multiply_fusion.15
  327.9 0.7 fusion.214
  328.6 1.1 pad_maximum_fusion.1
  329.7 0.0 slice-start
  329.7 0.0 slice-start.1
  329.7 2.3 fusion.48
  332.0 2.1 copy-done.2
  334.1 0.8 collective-permute-done
  334.9 2.4 constant_dynamic-update-slice_fusion.1
  337.3 0.0 slice-done
  337.3 7.3 %constant_dynamic-update-slice_fusion = (f32[4,3,2,39,1536]{4,0,2,3,1:T(4,128)}, f32[4,3,2,39,1536]{4,0,2,3,1:T(4,128)}) fusion(f32[4,3,2,39,1536]{4,0,2,3,1:T(4,128)} %constant_dynamic-update-slice_fusion.1, f32[4,3,2,32,1536]{4,3,2,1,0:T(8,128)S(1)} %bitcast.176), kind=kLoop, calls=%fused_computation.184 | loop fusion | bytes 14155776 | tf_op jit(solution)/shard_map/concatenate | solution.py:26
  344.5 0.3 collective-permute-done.1
  344.8 1.2 constant_dynamic-update-slice_fusion.2
  346.0 65.7 %all-to-all-done.1 = f32[4,1,294912]{2,1,0:T(1,128)} async-done(((f32[4,1,294912]{2,1,0:T(1,128)}), f32[4,1,294912]{2,1,0:T(1,128)}, u32[]{:S(2)}, u32[]{:S(2)}) %all-to-all-start.1) | async-done | bytes 4718624 | tf_op jit(solution)/shard_map/all_to_all | solution.py:108
  411.7 0.5 broadcast.394
  412.2 17.3 %reduce.2 = f32[4,294912]{1,0:T(4,128)} reduce(f32[4,1,294912]{2,1,0:T(1,128)} %all-to-all-done.1, f32[]{:T(128)} %broadcast.394), dimensions={1}, to_apply=%all_to_all.28.reduce_sub_computation | reduce | bytes 9437188 | tf_op jit(solution)/shard_map/all_to_all | solution.py:108
  429.5 78.0 %reshape.466 = f32[6144,2,8,12]{3,2,1,0:T(8,128)} reshape(f32[4,294912]{1,0:T(4,128)} %reduce.2) | data formatting | bytes 9437184
  507.5 31.1 %copy.143 = f32[12,2,8,4,1536]{4,3,2,1,0:T(4,128)} copy(f32[12,2,8,4,1536]{0,2,1,4,3:T(8,128)} %bitcast.172) | data formatting | bytes 9437184 | tf_op jit(solution)/shard_map/all_to_all | solution.py:108
  538.6 6.4 %copy.124 = f32[12,2,4,8,1536]{4,3,2,1,0:T(8,128)} copy(f32[12,2,4,8,1536]{4,2,3,1,0:T(4,128)} %bitcast.182) | data formatting | bytes 9437184 | tf_op jit(solution)/shard_map/all_to_all | solution.py:108
  545.0 33.0 %fusion.2 = f32[4,3,2,32,1536]{4,0,2,3,1:T(4,128)S(1)} fusion(f32[4,3,2,39,1536]{4,0,2,3,1:T(4,128)} %constant_dynamic-update-slice_fusion.2, f32[4,3,2,39,1536]{4,0,2,3,1:T(4,128)} %get-tuple-element.30, f32[4,3,2,32,1536]{4,3,2,1,0:T(8,128)} %bitcast.179, f32[4,3,2,32,1536]{4,0,2,3,1:T(4,128)} %copy-done.2, f32[32]{0:T(128)S(1)} %get-tuple-element.47, ...), kind=kLoop, calls=%fused_computation.7 | loop fusion | flops 38928384 | bytes 84936576 | tf_op jit(solution)/shard_map/add | solution.py:119
  578.0 0.0 copy-start.6
  578.0 4.9 copy.126
  582.9 5.1 multiply_select_fusion
  588.1 5.0 multiply_select_fusion.1
  593.1 0.3 fusion.53
  593.4 42.9 %psum.7 = f32[2,4,2,64]{3,1,2,0:T(4,128)S(1)} all-reduce(f32[2,4,2,64]{3,1,2,0:T(4,128)S(1)} %fusion.53), channel_id=1, replica_groups=mesh['wall'=8,'span'=4] {'wall','span'}, use_global_device_ids=true, to_apply=%region_0.1 | all-reduce | flops 1024 | bytes 8192 | tf_op jit(solution)/shard_map/psum | solution.py:134
  636.3 0.6 copy.127
  (21 shorter events, 0.1 us)
Async XLA Ops:
  8.8 106.8 %all-to-all-start = ((f32[12,2,32,1536]{3,1,0,2:T(2,128)}), f32[12,2,32,1536]{3,1,0,2:T(2,128)}, u32[]{:S(2)}, u32[]{:S(2)}) async-start(f32[12,2,32,1536]{3,1,0,2:T(2,128)} %bitcast.180), calls=%async_computation | async-start | bytes 9437184 | tf_op jit(solution)/shard_map/all_to_all | solution.py:106
  150.2 7.1 %copy-start = (f32[12,8,48,128]{3,2,1,0:T(8,128)}, f32[12,8,48,128]{3,2,1,0:T(8,128)S(1)}, u32[]{:S(2)}) copy-start(f32[12,8,48,128]{3,2,1,0:T(8,128)S(1)} %convolution_add_fusion) | copy-start | bytes 7077892
  302.8 108.9 %all-to-all-start.1 = ((f32[4,1,294912]{2,1,0:T(1,128)}), f32[4,1,294912]{2,1,0:T(1,128)}, u32[]{:S(2)}, u32[]{:S(2)}) async-start(f32[4,1,294912]{2,1,0:T(1,128)} %reshape.465), calls=%async_computation.1 | async-start | bytes 9437184 | tf_op jit(solution)/shard_map/all_to_all | solution.py:108
  316.5 2.2 copy-start.1
  318.7 5.7 copy-start.7
  318.7 5.8 copy-start.5
  318.7 5.8 copy-start.4
  318.8 16.0 %collective-permute-start = (f32[4,3,2,7,1536]{4,0,2,3,1:T(4,128)S(1)}, f32[4,3,2,7,1536]{4,0,2,3,1:T(4,128)}, u32[]{:S(2)}, u32[]{:S(2)}) collective-permute-start(f32[4,3,2,7,1536]{4,0,2,3,1:T(4,128)S(1)} %get-tuple-element.32), channel_id=1, source_target_pairs={{0,4},{4,8},{8,12},{12,16},{16,20},{20,24},{24,28},{1,5},{5,9},{9,... | collective-permute-start | bytes 3096584 | tf_op jit(solution)/shard_map/ppermute | solution.py:22
  320.8 24.1 %collective-permute-start.1 = (f32[4,3,2,7,1536]{4,0,2,3,1:T(4,128)S(1)}, f32[4,3,2,7,1536]{4,0,2,3,1:T(4,128)S(1)}, u32[]{:S(2)}, u32[]{:S(2)}) collective-permute-start(f32[4,3,2,7,1536]{4,0,2,3,1:T(4,128)S(1)} %get-tuple-element.33), channel_id=1, source_target_pairs={{4,0},{8,4},{12,8},{16,12},{20,16},{24,20},{28,24},{5,1},{9,5},{13... | collective-permute-start | bytes 3096584 | tf_op jit(solution)/shard_map/ppermute | solution.py:25
  324.6 3.3 copy-start.3
  329.7 7.6 %slice-start = ((s8[4718592]{0:T(1024)(128)(4,1)}), s8[4194304]{0:T(1024)(128)(4,1)S(1)}, s32[]{:S(2)}) async-start(s8[4718592]{0:T(1024)(128)(4,1)} %bitcast.175), calls=%async_computation.2 | async-start | bytes 8388608
  329.7 7.5 %slice-start.1 = ((s8[4718592]{0:T(1024)(128)(4,1)}), s8[524288]{0:T(1024)(128)(4,1)S(1)}, s32[]{:S(2)}) async-start(s8[4718592]{0:T(1024)(128)(4,1)} %bitcast.175), calls=%async_computation.3 | async-start | bytes 1048576
  332.0 2.1 copy-start.2
  538.6 6.4 %slice-start.2 = ((s8[4718592]{0:T(1024)(128)(4,1)}), s8[4194304]{0:T(1024)(128)(4,1)S(1)}, s32[]{:S(2)}) async-start(s8[4718592]{0:T(1024)(128)(4,1)} %bitcast.177), calls=%async_computation.4 | async-start | bytes 8388608
  538.6 6.4 %slice-start.3 = ((s8[4718592]{0:T(1024)(128)(4,1)}), s8[524288]{0:T(1024)(128)(4,1)S(1)}, s32[]{:S(2)}) async-start(s8[4718592]{0:T(1024)(128)(4,1)} %bitcast.177), calls=%async_computation.5 | async-start | bytes 1048576
  578.0 15.0 %copy-start.6 = (s32[1536]{0:T(1024)S(1)}, s32[1536]{0:T(1024)}, u32[]{:S(2)}) copy-start(s32[1536]{0:T(1024)} %param.13) | copy-start | bytes 18436
where the time goes:
time: 642 us; the launch traced here: 637 us
  local copies, waits for them, and re-layouts  257 us (40%)
  waiting for transfers between devices  168 us (26%)
  other arithmetic  101 us (16%)
  matrix products  47.3 us (7%)
  blocking collectives  42.9 us (7%)
  starting transfers between devices  19.4 us (3%)
    unnamed x32, local copies, waits for them, and re-layouts  181 us
    all_to_all x1, waiting for transfers between devices, on_device(): lax.all_to_all(flattened, 'span', split_axis=2, concat_axis=3, tiled=True)  101 us
    all_to_all x1, waiting for transfers between devices, on_device(): lax.all_to_all(spectral_lines, 'span', split_axis=3, concat_axis=2, tiled...  65.7 us
    psum x1, blocking collectives, on_device(): wall_grad = lax.psum(partial_grad, ('wall', 'span'))  42.9 us
    all_to_all x3, local copies, waits for them, and re-layouts, on_device(): lax.all_to_all(spectral_lines, 'span', split_axis=3, concat_axis=2, tiled...  38 us
    unnamed x3, other arithmetic  33.8 us
    add x1, other arithmetic, on_device(): new_field = field + TAU * advection + diffusion + spanwise  33 us
    another operation x2, local copies, waits for them, and re-layouts, spanwise_operator(): return jnp.stack([result_real, result_imag], axis=1)  23.9 us
  transfers between devices with their start and end apart: 4, of which 4 were waited for; matrix products, arithmetic and copies ran while one was open for 4% of the time, Pallas kernels for 0%

commit v1 on v0

v1 whole, which is shorter than its diff:
```python
import functools
import math

import jax
import jax.numpy as jnp
import numpy as np
from jax import lax
from jax.experimental import pallas as pl
from jax.experimental.pallas import tpu as pltpu
from jax.sharding import PartitionSpec as P

HALO = 7
STEN = 15
PATCH = 64
TAU = 0.25
VIS = 0.5

LANES = 128
OUTER = 48
PAD = 8
TILES = OUTER // 2

QUARTER = (0, 4, 2, 1, 5, 9)
KEPT = tuple(4 * q for q in QUARTER) + tuple(2 + 8 * t for t in range(6)) + tuple(4 * q + 1 for q in range(12))


@functools.cache
def spectral_tables(length):
    signed = np.arange(length)
    signed = np.where(signed > length // 2, signed - length, signed)
    cutoff = length // 3
    ratio = signed.astype(np.float64) / cutoff
    multiplier = np.where(np.abs(signed) < cutoff, -VIS * ratio * ratio, 0.0)
    shift = np.arange(LANES)[None, :] - np.arange(LANES)[:, None]
    inner = np.arange(LANES)

    def complex_table(k1):
        wave = k1 + OUTER * inner
        spots = np.arange(-LANES + 1, LANES)
        phase = np.exp(2j * np.pi * ((wave[:, None] * spots[None, :]) % length) / length)
        return ((multiplier[wave][:, None] * phase).sum(axis=0) / LANES)[shift + LANES - 1]

    tables = np.zeros((TILES, 2 * LANES, 2 * LANES))
    tables[0, :LANES, :LANES] = complex_table(0).real / OUTER
    tables[0, LANES:, LANES:] = complex_table(OUTER // 2).real / OUTER
    for tile, k1 in enumerate(KEPT[1:], 1):
        table = complex_table(k1) * 2.0 / OUTER
        tables[tile, :LANES, :LANES] = table.real
        tables[tile, :LANES, LANES:] = table.imag
        tables[tile, LANES:, :LANES] = -table.imag
        tables[tile, LANES:, LANES:] = table.real
    high = tables.astype(jnp.bfloat16)
    low = (tables - high.astype(np.float64)).astype(jnp.bfloat16)
    return np.stack([high, low], axis=1)


def turn(value, numerator, denominator):
    re, im = value
    numerator %= denominator
    if numerator == 0:
        return value
    if 2 * numerator == denominator:
        return (-re, -im)
    if 4 * numerator == denominator:
        return (-im, re)
    if 4 * numerator == 3 * denominator:
        return (im, -re)
    cos = math.cos(2 * math.pi * numerator / denominator)
    sin = math.sin(2 * math.pi * numerator / denominator)
    return (re * cos - im * sin, re * sin + im * cos)


def add(a, b):
    return (a[0] + b[0], a[1] + b[1])


def sub(a, b):
    return (a[0] - b[0], a[1] - b[1])


ROOT = math.sqrt(3.0) / 2.0


def dft3(x, sign):
    total = add(x[1], x[2])
    other = sub(x[1], x[2])
    middle = (x[0][0] - 0.5 * total[0], x[0][1] - 0.5 * total[1])
    side = (-sign * ROOT * other[1], sign * ROOT * other[0])
    return [add(x[0], total), add(middle, side), sub(middle, side)]


def dft6(x, sign):
    even = dft3([add(x[b], x[b + 3]) for b in range(3)], sign)
    odd = dft3([turn(sub(x[b], x[b + 3]), sign * b, 6) for b in range(3)], sign)
    return [even[0], odd[0], even[1], odd[1], even[2], odd[2]]


def dft12(x, sign):
    out = [None] * 12
    parts = [[], [], [], []]
    for b in range(3):
        a0, a1, a2, a3 = x[b], x[b + 3], x[b + 6], x[b + 9]
        s0, s1, d0, d1 = add(a0, a2), add(a1, a3), sub(a0, a2), turn(sub(a1, a3), sign, 4)
        for r, value in enumerate((add(s0, s1), add(d0, d1), sub(s0, s1), sub(d0, d1))):
            parts[r].append(turn(value, sign * b * r, 12))
    for r in range(4):
        for q, value in enumerate(dft3(parts[r], sign)):
            out[4 * q + r] = value
    return out


def real_forward(x):
    whole, halved, turned = [], [], []
    for b in range(12):
        s0, s1 = x[b] + x[b + 24], x[b + 12] + x[b + 36]
        whole.append(s0 + s1)
        halved.append(s0 - s1)
        turned.append(turn((x[b] - x[b + 24], x[b + 36] - x[b + 12]), -b, 48))
    w, h, t = [], [], []
    for b in range(3):
        s0, s1 = whole[b] + whole[b + 6], whole[b + 3] + whole[b + 9]
        w.append(s0 + s1)
        h.append(s0 - s1)
        t.append(turn((whole[b] - whole[b + 6], whole[b + 9] - whole[b + 3]), -b, 12))
    total, other = w[1] + w[2], w[1] - w[2]
    four = (w[0] - 0.5 * total, -ROOT * other)
    two = (h[0] + 0.5 * (h[1] - h[2]), -ROOT * (h[1] + h[2]))
    tiles = [(w[0] + total, h[0] - h[1] + h[2]), four, two] + dft3(t, -1)
    tiles += dft6([turn((halved[b], -halved[b + 6]), -b, 24) for b in range(6)], -1)
    return tiles + dft12(turned, -1)


def real_backward(tiles):
    (zero, half), four, two = tiles[:3]
    w0 = zero + four[0]
    rest, side = zero - 0.5 * four[0], ROOT * four[1]
    w = [w0, rest - side, rest + side]
    h_side = 0.5 * two[0] - ROOT * two[1]
    h = [two[0] + half, h_side - half, -0.5 * two[0] - ROOT * two[1] + half]
    t = [turn(value, b, 12) for b, value in enumerate(dft3(tiles[3:6], 1))]
    whole = [None] * 12
    for b in range(3):
        s, d = w[b] + h[b], w[b] - h[b]
        whole[b], whole[b + 6] = s + t[b][0], s - t[b][0]
        whole[b + 3], whole[b + 9] = d - t[b][1], d + t[b][1]
    halved = [None] * 12
    for b, value in enumerate(dft6(tiles[6:12], 1)):
        halved[b], halved[b + 6] = turn(value, b, 24)
        halved[b + 6] = -halved[b + 6]
    x = [None] * 48
    for b, value in enumerate(dft12(tiles[12:], 1)):
        re, im = turn(value, b, 48)
        s, d = whole[b] + halved[b], whole[b] - halved[b]
        x[b], x[b + 24] = s + re, s - re
        x[b + 12], x[b + 36] = d - im, d + im
    return x


def spectral_kernel(table_ref, line_ref, out_ref, wave_ref):
    source_count, line_count, row_count, width = line_ref.shape
    pieces = width // LANES
    groups = row_count // PAD

    def place(n1):
        return n1 // pieces, pl.ds(n1 % pieces * LANES, LANES)

    def forward(step, _):
        line, rows = step // groups, pl.ds(pl.multiple_of(step % groups * PAD, PAD), PAD)
        values = []
        for n1 in range(OUTER):
            source, lanes = place(n1)
            values.append(line_ref[source, line, rows, lanes])
        spot = pl.ds(pl.multiple_of(step * PAD, PAD), PAD)
        for tile, (re, im) in enumerate(real_forward(values)):
            wave_ref[tile, spot, :LANES] = re
            wave_ref[tile, spot, LANES:] = im
        return 0

    lax.fori_loop(0, line_count * groups, forward, 0)

    def middle(tile, _):
        value = wave_ref[tile]
        high = value.astype(jnp.bfloat16)
        low = (value - high.astype(jnp.float32)).astype(jnp.bfloat16)
        table_high, table_low = table_ref[tile, 0], table_ref[tile, 1]
        wave_ref[tile] = (
            jnp.dot(high, table_low, preferred_element_type=jnp.float32)
            + jnp.dot(low, table_high, preferred_element_type=jnp.float32)
            + jnp.dot(high, table_high, preferred_element_type=jnp.float32)
        )
        return 0

    lax.fori_loop(0, TILES, middle, 0)

    def backward(step, _):
        line, rows = step // groups, pl.ds(pl.multiple_of(step % groups * PAD, PAD), PAD)
        spot = pl.ds(pl.multiple_of(step * PAD, PAD), PAD)
        tiles = [(wave_ref[tile, spot, :LANES], wave_ref[tile, spot, LANES:]) for tile in range(TILES)]
        for n1, value in enumerate(real_backward(tiles)):
            source, lanes = place(n1)
            out_ref[source, line, rows, lanes] = value
        return 0

    lax.fori_loop(0, line_count * groups, backward, 0)


def spanwise_operator(lines, tables):
    source_count, line_count, row_count, width = lines.shape
    rows = line_count * row_count
    flops = 3 * 2 * TILES * rows * (2 * LANES) ** 2
    return pl.pallas_call(
        spectral_kernel,
        out_shape=jax.ShapeDtypeStruct(lines.shape, jnp.float32),
        in_specs=[pl.BlockSpec(memory_space=pltpu.VMEM)] * 2,
        out_specs=pl.BlockSpec(memory_space=pltpu.VMEM),
        scratch_shapes=[pltpu.VMEM((TILES, rows, 2 * LANES), jnp.float32)],
        compiler_params=pltpu.CompilerParams(vmem_limit_bytes=40 << 20),
        cost_estimate=pl.CostEstimate(flops=flops, bytes_accessed=8 * lines.size + 2 * tables.size, transcendentals=0),
        name="spanwise",
    )(tables, lines)


def local_kernel(rate_ref, coef_ref, flow_ref, field_ref, low_ref, high_ref, out_ref, pad_ref):
    _, comp_count, part_count, row_count, width = field_ref.shape
    pad_ref[:, :, :PAD] = low_ref[0]
    pad_ref[:, :, PAD : PAD + row_count] = field_ref[0]
    pad_ref[:, :, PAD + row_count :] = high_ref[0]
    rate = rate_ref[pl.program_id(0)]

    def column(step, _):
        lanes = pl.ds(pl.multiple_of(step * LANES, LANES), LANES)
        for top in range(0, row_count, PAD):
            rows = pl.ds(top, PAD)
            advect = rate * flow_ref[0, rows, :]
            shear = TAU * flow_ref[1, rows, :]
            centre = [[field_ref[0, c, p, rows, lanes] for p in range(2)] for c in range(comp_count)]
            for c in range(comp_count):
                for p in range(2):
                    total = centre[c][p]
                    total = total - advect * centre[c][1] if p == 0 else total + advect * centre[c][0]
                    if c == 1:
                        total = total - shear * centre[0][p]
                    for offset in range(STEN):
                        near = pad_ref[c, p, pl.ds(top + offset + PAD - HALO, PAD), lanes]
                        total = total + coef_ref[offset, rows, :] * near
                    out_ref[0, c, p, rows, lanes] = total
        return 0

    lax.fori_loop(0, width // LANES, column, 0)


def local_terms(field, low, high, rate, coef, flow):
    mode_count, comp_count, part_count, row_count, width = field.shape
    block = (1, comp_count, part_count, row_count, width)
    edge = (1, comp_count, part_count, PAD, width)

    def by_mode(m):
        return (m, 0, 0, 0, 0)

    return pl.pallas_call(
        local_kernel,
        grid=(mode_count,),
        out_shape=jax.ShapeDtypeStruct(field.shape, jnp.float32),
        in_specs=[
            pl.BlockSpec(memory_space=pltpu.SMEM),
            pl.BlockSpec(coef.shape, lambda m: (0, 0, 0)),
            pl.BlockSpec(flow.shape, lambda m: (0, 0, 0)),
            pl.BlockSpec(block, by_mode),
            pl.BlockSpec(edge, by_mode),
            pl.BlockSpec(edge, by_mode),
        ],
        out_specs=pl.BlockSpec(block, by_mode),
        scratch_shapes=[pltpu.VMEM((comp_count, part_count, row_count + 2 * PAD, width), jnp.float32)],
        compiler_params=pltpu.CompilerParams(vmem_limit_bytes=24 << 20),
        cost_estimate=pl.CostEstimate(flops=40 * field.size, bytes_accessed=10 * field.size, transcendentals=0),
        name="local_terms",
    )(rate, coef, flow, field, low, high)


def wall_sum_kernel(weight_ref, base_ref, term_ref, out_ref, shear_ref):
    row_count = base_ref.shape[3]
    for p in range(2):
        new = base_ref[0, 0, p] + term_ref[0, 0, p]
        out_ref[0, 0, p] = new
        low, high = new[:PAD], new[row_count - PAD :]
        shear_ref[0, p] = jnp.sum(low * weight_ref[0][:, :1], axis=0)
        shear_ref[0, 2 + p] = jnp.sum(high * weight_ref[1][:, :1], axis=0)


def sum_kernel(base_ref, term_ref, out_ref):
    out_ref[...] = base_ref[...] + term_ref[...]


def add_first(base, term, weight):
    mode_count, _, part_count, row_count, width = base.shape
    block = pl.BlockSpec((1, 1, part_count, row_count, width), lambda m: (m, 0, 0, 0, 0))
    return pl.pallas_call(
        wall_sum_kernel,
        grid=(mode_count,),
        out_shape=(
            jax.ShapeDtypeStruct(base.shape, jnp.float32),
            jax.ShapeDtypeStruct((mode_count, 4, width), jnp.float32),
        ),
        in_specs=[pl.BlockSpec(weight.shape, lambda m: (0, 0, 0)), block, block],
        out_specs=(block, pl.BlockSpec((1, 4, width), lambda m: (m, 0, 0))),
        input_output_aliases={1: 0},
        cost_estimate=pl.CostEstimate(flops=term.size, bytes_accessed=12 * term.size, transcendentals=0),
        name="add_first",
    )(weight, base, term)


def add_rest(base, term, first):
    mode_count, comp_count, part_count, row_count, width = term.shape
    shape = (1, 1, part_count, row_count, width)
    block = pl.BlockSpec(shape, lambda m, c: (m, c + first, 0, 0, 0))
    return pl.pallas_call(
        sum_kernel,
        grid=(mode_count, comp_count),
        out_shape=jax.ShapeDtypeStruct(base.shape, jnp.float32),
        in_specs=[block, pl.BlockSpec(shape, lambda m, c: (m, c, 0, 0, 0))],
        out_specs=block,
        input_output_aliases={0: 0},
        cost_estimate=pl.CostEstimate(flops=term.size, bytes_accessed=12 * term.size, transcendentals=0),
        name="add_rest",
    )(base, term)


def on_device(field, mean_flow, d2_coef, wall_coef, kx_index, patch_of):
    mode_count, comp_count, part_count, row_count, width = field.shape
    span = lax.axis_size("span")
    wall_count = lax.axis_size("wall")
    wall_index = lax.axis_index("wall")
    mode_split = math.gcd(span, mode_count)
    row_split = span // mode_split
    tables = jnp.asarray(spectral_tables(width * span))

    def to_lines(chunk):
        lines = chunk.reshape(mode_split, -1, row_split, row_count // row_split, width)
        lines = lines.transpose(0, 2, 1, 3, 4).reshape(span, -1, row_count // row_split, width)
        return lax.all_to_all(lines, "span", split_axis=0, concat_axis=0)

    def from_lines(lines, comps):
        blocks = lax.all_to_all(lines, "span", split_axis=0, concat_axis=0)
        blocks = blocks.reshape(mode_split, row_split, -1, row_count // row_split, width)
        return blocks.transpose(0, 2, 1, 3, 4).reshape(mode_count, comps, part_count, row_count, width)

    parts = [(0, 1), (1, comp_count)]
    lines = [to_lines(field[:, first:last]) for first, last in parts]

    forward = [(i, i + 1) for i in range(wall_count - 1)]
    backward = [(i + 1, i) for i in range(wall_count - 1)]
    low = lax.ppermute(field[:, :, :, row_count - PAD :], "wall", forward)
    high = lax.ppermute(field[:, :, :, :PAD], "wall", backward)
    rate = kx_index.astype(jnp.float32) * (0.25 * TAU)
    coef = jnp.broadcast_to(d2_coef[:, :, None], (STEN, row_count, LANES))
    flow = jnp.broadcast_to(mean_flow[:, :, None], (2, row_count, LANES))
    base = local_terms(field, low, high, rate, coef, flow)

    terms = [
        from_lines(spanwise_operator(value, tables), last - first) for value, (first, last) in zip(lines, parts)
    ]
    lower = jnp.where(wall_index == 0, wall_coef[0], 0.0)
    upper = jnp.where(wall_index == wall_count - 1, wall_coef[1, ::-1], 0.0)
    weight = jnp.broadcast_to(jnp.stack([lower, upper])[:, :, None], (2, PAD, LANES))
    base, shear = add_first(base, terms[0], weight)
    onehot = (patch_of[:, None] == jnp.arange(PATCH, dtype=jnp.int32)[None, :]).astype(jnp.float32)
    grad = jnp.einsum("mwz,zq->mwq", shear, onehot, precision=lax.Precision.HIGHEST)
    grad = grad.reshape(mode_count, 2, part_count, PATCH).transpose(1, 0, 2, 3)
    wall_grad = lax.psum(grad, ("wall", "span"))
    new_field = add_rest(base, terms[1], 1)
    return (new_field, wall_grad)


def solution(mesh):
    return jax.shard_map(
        on_device,
        mesh=mesh,
        in_specs=(
            P(None, None, None, "wall", "span"),
            P(None, "wall"),
            P(None, "wall"),
            P(),
            P(),
            P("span"),
        ),
        out_specs=(P(None, None, None, "wall", "span"), P()),
        check_vma=False,
    )
```

time: 642 us -> 271 us (0.42)
  local copies, waits for them, and re-layouts: 257 us -> 23.2 us
  other arithmetic: 101 us -> 1.95 us
  matrix products: 47.3 us -> 1.19 us
  waiting for transfers between devices: 168 us -> 125 us
  Pallas kernels: 0 us -> 40.9 us
  starting transfers between devices: 19.4 us -> 32.2 us
    unnamed x32 -> x18, local copies, waits for them, and re-layouts: 181 us -> 11.7 us
    all_to_all x2 -> x4, waiting for transfers between devices: 167 us -> 107 us  [the longest x2 85.4 us: to_lines(): return lax.all_to_all(lines, 'span', split_axis=0, concat_axis=0)]
    dot_general x17 -> x1, matrix products: 47.3 us -> 1.19 us  [on_device(): jnp.einsum('mwz,zq->mwq', shear, onehot, precision=lax.Precision.HIGHEST)]
    all_to_all x4 -> x0, local copies, waits for them, and re-layouts: 43.1 us -> none  [the longest x3 38 us: on_device(): lax.all_to_all(spectral_lines, 'span', split_axis=3, concat_axis=2, tiled...]
    pallas_call x0 -> x5, Pallas kernels: none -> 40.9 us  [the longest x2 15.3 us: spanwise_operator(): pl.pallas_call(spectral_kernel, out_shape=jax.ShapeDtypeStruct(lines.shap...]
    unnamed x3 -> x0, other arithmetic: 33.8 us -> none
    add x1 -> x0, other arithmetic: 33 us -> none  [on_device(): new_field = field + TAU * advection + diffusion + spanwise]
    another operation x2 -> x1, local copies, waits for them, and re-layouts: 23.9 us -> 2.71 us  [to_lines(): lines.transpose(0, 2, 1, 3, 4)]
  transfers between devices with their start and end apart: 4 -> 6, of which waited for: 4 -> 4; matrix products, arithmetic and copies ran while one was open for 4% -> 4% of each run, Pallas kernels for 0% -> 13%
where the time goes in v1:
time: 271 us; the launch traced here: 270 us
  waiting for transfers between devices  125 us (46%)
  blocking collectives  44.7 us (16%)
  Pallas kernels  40.9 us (15%)
  starting transfers between devices  32.2 us (12%)
  local copies, waits for them, and re-layouts  23.2 us (9%)
    all_to_all x2, waiting for transfers between devices, to_lines(): return lax.all_to_all(lines, 'span', split_axis=0, concat_axis=0)  85.4 us
    psum x1, blocking collectives, on_device(): wall_grad = lax.psum(grad, ('wall', 'span'))  44.7 us
    all_to_all x2, waiting for transfers between devices, from_lines(): blocks = lax.all_to_all(lines, 'span', split_axis=0, concat_axis=0)  21.1 us
    ppermute x1, waiting for transfers between devices, on_device(): high = lax.ppermute(field[:, :, :, :PAD], 'wall', backward)  18.3 us
    all_to_all x2, starting transfers between devices, from_lines(): blocks = lax.all_to_all(lines, 'span', split_axis=0, concat_axis=0)  15.6 us
    pallas_call x2, Pallas kernels, spanwise_operator(): pl.pallas_call(spectral_kernel, out_shape=jax.ShapeDtypeStruct(lines.shap...  15.3 us
    pallas_call x1, Pallas kernels, local_terms(): pl.pallas_call(local_kernel, grid=(mode_count,), out_shape=jax.ShapeDtype...  15 us
    all_to_all x2, starting transfers between devices, to_lines(): return lax.all_to_all(lines, 'span', split_axis=0, concat_axis=0)  12.3 us
  transfers between devices with their start and end apart: 6, of which 4 were waited for; matrix products, arithmetic and copies ran while one was open for 4% of the time, Pallas kernels for 13%

profile of v1, /device:TPU:10, one launch (start us, length us, event | category | flops | bytes accessed | tf_op | source)
XLA Modules:
  0.0 269.6 jit_solution(16871001058065028392)
XLA Ops:
  0.6 2.7 %slice_bitcast_fusion = f32[4,2,32,1536]{3,2,1,0:T(8,128)} fusion(f32[4,3,2,32,1536]{4,3,2,1,0:T(8,128)} %field_ref.1), kind=kLoop, calls=%fused_computation | loop fusion | bytes 3145728 | tf_op jit(solution)/shard_map/reshape;transpose;reshape | solution.py:339
  3.3 5.3 %all-to-all-start = ((f32[4,2,32,1536]{3,2,1,0:T(8,128)}), f32[4,2,32,1536]{3,2,1,0:T(8,128)S(1)}, u32[]{:S(2)}, u32[]{:S(2)}) async-start(f32[4,2,32,1536]{3,2,1,0:T(8,128)} %slice_bitcast_fusion), calls=%async_computation | async-start | bytes 3145728 | tf_op jit(solution)/shard_map/all_to_all | solution.py:340
  8.7 3.8 %slice.23 = f32[4,2,2,32,1536]{4,3,2,1,0:T(8,128)} slice(f32[4,3,2,32,1536]{4,3,2,1,0:T(8,128)} %field_ref.1), slice={[0:4], [1:3], [0:2], [0:32], [0:1536]} | slice | bytes 6291456 | tf_op jit(solution)/shard_map/slice | solution.py:348
  12.5 29.9 %all-to-all-done.line_ref = f32[4,2,32,1536]{3,2,1,0:T(8,128)S(1)} async-done(((f32[4,2,32,1536]{3,2,1,0:T(8,128)}), f32[4,2,32,1536]{3,2,1,0:T(8,128)S(1)}, u32[]{:S(2)}, u32[]{:S(2)}) %all-to-all-start) | async-done | bytes 1572896 | tf_op jit(solution)/shard_map/all_to_all | solution.py:340
  42.3 0.0 copy-start.3
  42.3 1.2 copy-done.3
  43.5 6.9 %all-to-all-start.2 = ((f32[4,4,32,1536]{3,2,1,0:T(8,128)}), f32[4,4,32,1536]{3,2,1,0:T(8,128)S(1)}, u32[]{:S(2)}, u32[]{:S(2)}) async-start(f32[4,4,32,1536]{3,2,1,0:T(8,128)} %bitcast.15), calls=%async_computation.2 | async-start | bytes 6291456 | tf_op jit(solution)/shard_map/all_to_all | solution.py:340
  50.5 0.0 copy-start.1
  50.5 2.8 %copy-done.1 = bf16[24,2,256,256]{3,2,1,0:T(8,128)(2,1)S(1)} copy-done((bf16[24,2,256,256]{3,2,1,0:T(8,128)(2,1)S(1)}, bf16[24,2,256,256]{3,2,1,0:T(8,128)(2,1)}, u32[]{:S(2)}) %copy-start.1) | copy-done | bytes 6291480
  53.3 0.0 copy-start.4
  53.3 1.4 copy-done.4
  54.7 6.0 %spanwise.2 = f32[4,2,32,1536]{3,2,1,0:T(8,128)S(1)} custom-call(bf16[24,2,256,256]{3,2,1,0:T(8,128)(2,1)S(1)} %copy-done.1, f32[4,2,32,1536]{3,2,1,0:T(8,128)S(1)} %copy-done.4), custom_call_target="tpu_custom_call" | custom-call | flops 603979776 | bytes 9437184 | tf_op jit(solution)/shard_map/spanwise/pallas_call | solution.py:211
  60.7 0.0 copy-start.5
  60.7 1.1 copy-done.5
  61.8 55.5 %all-to-all-done.2.line_ref = f32[4,4,32,1536]{3,2,1,0:T(8,128)S(1)} async-done(((f32[4,4,32,1536]{3,2,1,0:T(8,128)}), f32[4,4,32,1536]{3,2,1,0:T(8,128)S(1)}, u32[]{:S(2)}, u32[]{:S(2)}) %all-to-all-start.2) | async-done | bytes 3145760 | tf_op jit(solution)/shard_map/all_to_all | solution.py:340
  117.4 7.6 %all-to-all-start.1 = ((f32[4,2,32,1536]{3,2,1,0:T(8,128)}), f32[4,2,32,1536]{3,2,1,0:T(8,128)}, u32[]{:S(2)}, u32[]{:S(2)}) async-start(f32[4,2,32,1536]{3,2,1,0:T(8,128)} %copy-done.5), calls=%async_computation.1 | async-start | bytes 3145728 | tf_op jit(solution)/shard_map/all_to_all | solution.py:343
  125.0 0.0 copy-start.2
  125.0 2.8 %copy-done.2 = bf16[24,2,256,256]{3,2,1,0:T(8,128)(2,1)S(1)} copy-done((bf16[24,2,256,256]{3,2,1,0:T(8,128)(2,1)S(1)}, bf16[24,2,256,256]{3,2,1,0:T(8,128)(2,1)}, u32[]{:S(2)}) %copy-start.2) | copy-done | bytes 6291480
  127.7 9.3 %spanwise.3 = f32[4,4,32,1536]{3,2,1,0:T(8,128)} custom-call(bf16[24,2,256,256]{3,2,1,0:T(8,128)(2,1)S(1)} %copy-done.2, f32[4,4,32,1536]{3,2,1,0:T(8,128)S(1)} %all-to-all-done.2.line_ref), custom_call_target="tpu_custom_call" | custom-call | flops 1207959552 | bytes 12582912 | tf_op jit(solution)/shard_map/spanwise/pallas_call | solution.py:211
  137.0 21.1 %all-to-all-done.1 = f32[4,2,32,1536]{3,2,1,0:T(8,128)} async-done(((f32[4,2,32,1536]{3,2,1,0:T(8,128)}), f32[4,2,32,1536]{3,2,1,0:T(8,128)}, u32[]{:S(2)}, u32[]{:S(2)}) %all-to-all-start.1) | async-done | bytes 1572896 | tf_op jit(solution)/shard_map/all_to_all | solution.py:343
  158.1 8.0 %all-to-all-start.3 = ((f32[4,4,32,1536]{3,2,1,0:T(8,128)}), f32[4,4,32,1536]{3,2,1,0:T(8,128)}, u32[]{:S(2)}, u32[]{:S(2)}) async-start(f32[4,4,32,1536]{3,2,1,0:T(8,128)} %spanwise.3), calls=%async_computation.3 | async-start | bytes 6291456 | tf_op jit(solution)/shard_map/all_to_all | solution.py:343
  166.1 0.0 copy-start.7
  166.1 0.0 copy-start.6
  166.1 2.9 %fusion.4 = (f32[4,3,2,8,1536]{4,3,2,1,0:T(8,128)}, f32[4,3,2,8,1536]{4,3,2,1,0:T(8,128)S(1)}) fusion(f32[4,3,2,32,1536]{4,3,2,1,0:T(8,128)} %field_ref.1), kind=kLoop, calls=%fused_computation.10 | loop fusion | bytes 4718592 | tf_op jit(solution)/shard_map/slice | solution.py:353
  169.0 1.9 collective-permute-start.1
  171.0 2.4 collective-permute-start
  173.4 1.3 broadcast_select_fusion.1
  174.6 1.3 rev.3
  175.9 0.7 convert_multiply_fusion.rate_ref
  176.6 18.3 %collective-permute-done.1.high_ref = f32[4,3,2,8,1536]{4,3,2,1,0:T(8,128)S(1)} collective-permute-done((f32[4,3,2,8,1536]{4,3,2,1,0:T(8,128)}, f32[4,3,2,8,1536]{4,3,2,1,0:T(8,128)S(1)}, u32[]{:S(2)}, u32[]{:S(2)}) %collective-permute-start.1) | collective-permute-done | bytes 1179680 | tf_op jit(solution)/shard_map/ppermute | solution.py:353
  194.9 0.0 collective-permute-done.low_ref
  194.9 0.0 copy-done.7
  194.9 0.1 broadcast_in_dim.14.flow_ref
  195.0 0.0 copy-done.6
  195.0 0.1 broadcast_in_dim.13.coef_ref
  195.1 0.0 copy-start
  195.1 2.3 copy-done
  197.5 15.0 %local_terms.1.base_ref = f32[4,3,2,32,1536]{4,3,2,1,0:T(8,128)} custom-call(f32[4]{0:T(128)S(1)} %convert_multiply_fusion.rate_ref, f32[15,32,128]{2,1,0:T(8,128)S(1)} %broadcast_in_dim.13.coef_ref, f32[2,32,128]{2,1,0:T(8,128)S(1)} %broadcast_in_dim.14.flow_ref, f32[4,3,2,32,1536]{4,3,2,1,0:T(8,128)S(1)} %copy-done, ...), custom_call_target="tpu_custom_call" | custom-call | flops 47185920 | bytes 11796480 | tf_op jit(solution)/shard_map/local_terms/pallas_call | solution.py:260
  212.4 0.7 broadcast_in_dim.12.weight_ref
  213.1 0.0 copy-start.8
  213.1 3.9 %add_first.1 = (f32[4,3,2,32,1536]{4,3,2,1,0:T(8,128)}, f32[4,4,1536]{2,1,0:T(4,128)}) custom-call(f32[2,8,128]{2,1,0:T(8,128)} %broadcast_in_dim.12.weight_ref, f32[4,3,2,32,1536]{4,3,2,1,0:T(8,128)} %local_terms.1.base_ref, f32[4,1,2,32,1536]{4,3,2,1,0:T(8,128)} %bitcast.1.term_ref), custom_call_target="tpu_custom_call", output_to_operand_aliasing={{0}: (1, {})} | custom-call | flops 393216 | bytes 4718592 | tf_op jit(solution)/shard_map/add_first/pallas_call | solution.py:297
  217.0 0.0 copy-done.8
  217.0 1.2 fusion.1
  218.2 44.7 %psum.7 = f32[2,4,2,64]{3,2,1,0:T(2,128)} all-reduce(f32[2,4,2,64]{3,2,1,0:T(2,128)S(1)} %bitcast.16), channel_id=1, replica_groups=mesh['wall'=8,'span'=4] {'wall','span'}, use_global_device_ids=true, to_apply=%region_0.1 | all-reduce | flops 1024 | bytes 8192 | tf_op jit(solution)/shard_map/psum | solution.py:369
  262.9 0.0 all-to-all-done.3
  262.9 6.7 %add_rest.1 = f32[4,3,2,32,1536]{4,3,2,1,0:T(8,128)} custom-call(f32[4,3,2,32,1536]{4,3,2,1,0:T(8,128)} %get-tuple-element.4.base_ref, f32[4,2,2,32,1536]{4,3,2,1,0:T(8,128)} %bitcast.3.term_ref), custom_call_target="tpu_custom_call", output_to_operand_aliasing={{}: (0, {})} | custom-call | flops 786432 | bytes 9437184 | tf_op jit(solution)/shard_map/add_rest/pallas_call | solution.py:316
  (3 shorter events, 0.0 us)
Async XLA Ops:
  3.3 39.0 %all-to-all-start = ((f32[4,2,32,1536]{3,2,1,0:T(8,128)}), f32[4,2,32,1536]{3,2,1,0:T(8,128)S(1)}, u32[]{:S(2)}, u32[]{:S(2)}) async-start(f32[4,2,32,1536]{3,2,1,0:T(8,128)} %slice_bitcast_fusion), calls=%async_computation | async-start | bytes 3145728 | tf_op jit(solution)/shard_map/all_to_all | solution.py:340
  42.3 1.2 copy-start.3
  43.5 73.8 %all-to-all-start.2 = ((f32[4,4,32,1536]{3,2,1,0:T(8,128)}), f32[4,4,32,1536]{3,2,1,0:T(8,128)S(1)}, u32[]{:S(2)}, u32[]{:S(2)}) async-start(f32[4,4,32,1536]{3,2,1,0:T(8,128)} %bitcast.15), calls=%async_computation.2 | async-start | bytes 6291456 | tf_op jit(solution)/shard_map/all_to_all | solution.py:340
  50.5 2.8 %copy-start.1 = (bf16[24,2,256,256]{3,2,1,0:T(8,128)(2,1)S(1)}, bf16[24,2,256,256]{3,2,1,0:T(8,128)(2,1)}, u32[]{:S(2)}) copy-start(bf16[24,2,256,256]{3,2,1,0:T(8,128)(2,1)} %constant.16.clone.table_ref) | copy-start | bytes 18874372
  53.3 1.4 copy-start.4
  60.7 1.2 copy-start.5
  117.4 40.8 %all-to-all-start.1 = ((f32[4,2,32,1536]{3,2,1,0:T(8,128)}), f32[4,2,32,1536]{3,2,1,0:T(8,128)}, u32[]{:S(2)}, u32[]{:S(2)}) async-start(f32[4,2,32,1536]{3,2,1,0:T(8,128)} %copy-done.5), calls=%async_computation.1 | async-start | bytes 3145728 | tf_op jit(solution)/shard_map/all_to_all | solution.py:343
  125.0 2.8 %copy-start.2 = (bf16[24,2,256,256]{3,2,1,0:T(8,128)(2,1)S(1)}, bf16[24,2,256,256]{3,2,1,0:T(8,128)(2,1)}, u32[]{:S(2)}) copy-start(bf16[24,2,256,256]{3,2,1,0:T(8,128)(2,1)} %constant.16.clone.table_ref) | copy-start | bytes 18874372
  158.1 104.8 %all-to-all-start.3 = ((f32[4,4,32,1536]{3,2,1,0:T(8,128)}), f32[4,4,32,1536]{3,2,1,0:T(8,128)}, u32[]{:S(2)}, u32[]{:S(2)}) async-start(f32[4,4,32,1536]{3,2,1,0:T(8,128)} %spanwise.3), calls=%async_computation.3 | async-start | bytes 6291456 | tf_op jit(solution)/shard_map/all_to_all | solution.py:343
  166.1 28.8 %copy-start.7 = (f32[2,32]{1,0:T(2,128)S(1)}, f32[2,32]{1,0:T(2,128)}, u32[]{:S(2)}) copy-start(f32[2,32]{1,0:T(2,128)} %param.8) | copy-start | bytes 772
  166.1 28.9 %copy-start.6 = (f32[15,32]{1,0:T(8,128)S(1)}, f32[15,32]{1,0:T(8,128)}, u32[]{:S(2)}) copy-start(f32[15,32]{1,0:T(8,128)} %param.9) | copy-start | bytes 5764
  169.0 25.9 %collective-permute-start.1 = (f32[4,3,2,8,1536]{4,3,2,1,0:T(8,128)}, f32[4,3,2,8,1536]{4,3,2,1,0:T(8,128)S(1)}, u32[]{:S(2)}, u32[]{:S(2)}) collective-permute-start(f32[4,3,2,8,1536]{4,3,2,1,0:T(8,128)} %get-tuple-element.6), channel_id=1, source_target_pairs={{4,0},{8,4},{12,8},{16,12},{20,16},{24,20},{28,24},{5,1},{9,5},{13... | collective-permute-start | bytes 3538952 | tf_op jit(solution)/shard_map/ppermute | solution.py:353
  171.0 24.0 %collective-permute-start = (f32[4,3,2,8,1536]{4,3,2,1,0:T(8,128)S(1)}, f32[4,3,2,8,1536]{4,3,2,1,0:T(8,128)S(1)}, u32[]{:S(2)}, u32[]{:S(2)}) collective-permute-start(f32[4,3,2,8,1536]{4,3,2,1,0:T(8,128)S(1)} %get-tuple-element.7), channel_id=1, source_target_pairs={{0,4},{4,8},{8,12},{12,16},{16,20},{20,24},{24,28},{1,5},{5,9},{9,... | collective-permute-start | bytes 3538952 | tf_op jit(solution)/shard_map/ppermute | solution.py:352
  195.1 2.3 copy-start
  213.1 3.9 %copy-start.8 = (s32[1536]{0:T(1024)S(1)}, s32[1536]{0:T(1024)}, u32[]{:S(2)}) copy-start(s32[1536]{0:T(1024)} %param.12) | copy-start | bytes 18436

commit v2 on v1

--- a/solution.py
+++ b/solution.py
@@ -156,10 +156,25 @@
     return x
 
 
-def spectral_kernel(table_ref, line_ref, out_ref, wave_ref):
-    source_count, line_count, row_count, width = line_ref.shape
+def spectral_kernel(sheared, me_ref, table_ref, weight_ref, field_ref, *refs):
+    line_ref, wave_ref, sems = refs[-3:]
+    count, part_count, row_count, width = line_ref.shape
+    received, sent = refs[: count - 1], refs[count - 1 : 2 * count - 1]
     pieces = width // LANES
     groups = row_count // PAD
+    me, mode, top, comp = me_ref[0], me_ref[1], me_ref[2], me_ref[3]
+
+    copies = []
+    for x in range(count):
+        if x == 0:
+            source = field_ref.at[mode, comp, :, pl.ds(pl.multiple_of(top, PAD), row_count)]
+        else:
+            source = received[x - 1]
+        copies.append(pltpu.make_async_copy(source, line_ref.at[me ^ x], sems.at[x]))
+    for copy in copies:
+        copy.start()
+    for copy in copies:
+        copy.wait()
 
     def place(n1):
         return n1 // pieces, pl.ds(n1 % pieces * LANES, LANES)
@@ -176,7 +191,7 @@
             wave_ref[tile, spot, LANES:] = im
         return 0
 
-    lax.fori_loop(0, line_count * groups, forward, 0)
+    lax.fori_loop(0, part_count * groups, forward, 0)
 
     def middle(tile, _):
         value = wave_ref[tile]
@@ -198,29 +213,50 @@
         tiles = [(wave_ref[tile, spot, :LANES], wave_ref[tile, spot, LANES:]) for tile in range(TILES)]
         for n1, value in enumerate(real_backward(tiles)):
             source, lanes = place(n1)
-            out_ref[source, line, rows, lanes] = value
+            line_ref[source, line, rows, lanes] = value
         return 0
 
-    lax.fori_loop(0, line_count * groups, backward, 0)
-
-
-def spanwise_operator(lines, tables):
-    source_count, line_count, row_count, width = lines.shape
-    rows = line_count * row_count
+    lax.fori_loop(0, part_count * groups, backward, 0)
+    copies = [pltpu.make_async_copy(line_ref.at[me ^ x], sent[x], sems.at[x]) for x in range(count)]
+    for copy in copies:
+        copy.start()
+    if sheared:
+        shear_ref = refs[2 * count - 1]
+        for source in range(count):
+            for p in range(part_count):
+                lower, upper = line_ref[source, p, :PAD], line_ref[source, p, row_count - PAD :]
+                shear_ref[source, p] = jnp.sum(lower * weight_ref[0][:, :1], axis=0)
+                shear_ref[source, part_count + p] = jnp.sum(upper * weight_ref[1][:, :1], axis=0)
+    for copy in copies:
+        copy.wait()
+
+
+def spanwise_operator(field, received, spots, weight, tables, sheared):
+    count = len(received) + 1
+    part_count, row_count, width = received[0].shape
+    rows = part_count * row_count
     flops = 3 * 2 * TILES * rows * (2 * LANES) ** 2
+    anywhere = pl.BlockSpec(memory_space=pl.ANY)
+    vector = pl.BlockSpec(memory_space=pltpu.VMEM)
+    sent = jax.ShapeDtypeStruct((part_count, row_count, width), jnp.float32)
+    shear = jax.ShapeDtypeStruct((count, 2 * part_count, width), jnp.float32)
     return pl.pallas_call(
-        spectral_kernel,
-        out_shape=jax.ShapeDtypeStruct(lines.shape, jnp.float32),
-        in_specs=[pl.BlockSpec(memory_space=pltpu.VMEM)] * 2,
-        out_specs=pl.BlockSpec(memory_space=pltpu.VMEM),
-        scratch_shapes=[pltpu.VMEM((TILES, rows, 2 * LANES), jnp.float32)],
-        compiler_params=pltpu.CompilerParams(vmem_limit_bytes=40 << 20),
-        cost_estimate=pl.CostEstimate(flops=flops, bytes_accessed=8 * lines.size + 2 * tables.size, transcendentals=0),
+        functools.partial(spectral_kernel, sheared),
+        out_shape=[sent] * count + [shear] * sheared,
+        in_specs=[pl.BlockSpec(memory_space=pltpu.SMEM), vector, vector] + [anywhere] * count,
+        out_specs=[anywhere] * count + [vector] * sheared,
+        scratch_shapes=[
+            pltpu.VMEM((count, part_count, row_count, width), jnp.float32),
+            pltpu.VMEM((TILES, rows, 2 * LANES), jnp.float32),
+            pltpu.SemaphoreType.DMA((count,)),
+        ],
+        compiler_params=pltpu.CompilerParams(vmem_limit_bytes=32 << 20),
+        cost_estimate=pl.CostEstimate(flops=flops, bytes_accessed=8 * count * rows * width, transcendentals=0),
         name="spanwise",
-    )(tables, lines)
-
-
-def local_kernel(rate_ref, coef_ref, flow_ref, field_ref, low_ref, high_ref, out_ref, pad_ref):
+    )(spots, tables, weight, field, *received)
+
+
+def local_kernel(rate_ref, coef_ref, flow_ref, weight_ref, field_ref, low_ref, high_ref, out_ref, shear_ref, pad_ref):
     _, comp_count, part_count, row_count, width = field_ref.shape
     pad_ref[:, :, :PAD] = low_ref[0]
     pad_ref[:, :, PAD : PAD + row_count] = field_ref[0]
@@ -247,9 +283,13 @@
         return 0
 
     lax.fori_loop(0, width // LANES, column, 0)
-
-
-def local_terms(field, low, high, rate, coef, flow):
+    for p in range(part_count):
+        lower, upper = out_ref[0, 0, p, :PAD], out_ref[0, 0, p, row_count - PAD :]
+        shear_ref[0, p] = jnp.sum(lower * weight_ref[0][:, :1], axis=0)
+        shear_ref[0, part_count + p] = jnp.sum(upper * weight_ref[1][:, :1], axis=0)
+
+
+def local_terms(field, low, high, rate, coef, flow, weight):
     mode_count, comp_count, part_count, row_count, width = field.shape
     block = (1, comp_count, part_count, row_count, width)
     edge = (1, comp_count, part_count, PAD, width)
@@ -260,92 +300,88 @@
     return pl.pallas_call(
         local_kernel,
         grid=(mode_count,),
-        out_shape=jax.ShapeDtypeStruct(field.shape, jnp.float32),
+        out_shape=(
+            jax.ShapeDtypeStruct(field.shape, jnp.float32),
+            jax.ShapeDtypeStruct((mode_count, 2 * part_count, width), jnp.float32),
+        ),
         in_specs=[
             pl.BlockSpec(memory_space=pltpu.SMEM),
             pl.BlockSpec(coef.shape, lambda m: (0, 0, 0)),
             pl.BlockSpec(flow.shape, lambda m: (0, 0, 0)),
+            pl.BlockSpec(weight.shape, lambda m: (0, 0, 0)),
             pl.BlockSpec(block, by_mode),
             pl.BlockSpec(edge, by_mode),
             pl.BlockSpec(edge, by_mode),
         ],
-        out_specs=pl.BlockSpec(block, by_mode),
+        out_specs=(pl.BlockSpec(block, by_mode), pl.BlockSpec((1, 2 * part_count, width), lambda m: (m, 0, 0))),
         scratch_shapes=[pltpu.VMEM((comp_count, part_count, row_count + 2 * PAD, width), jnp.float32)],
         compiler_params=pltpu.CompilerParams(vmem_limit_bytes=24 << 20),
         cost_estimate=pl.CostEstimate(flops=40 * field.size, bytes_accessed=10 * field.size, transcendentals=0),
         name="local_terms",
-    )(rate, coef, flow, field, low, high)
-
-
-def wall_sum_kernel(weight_ref, base_ref, term_ref, out_ref, shear_ref):
-    row_count = base_ref.shape[3]
-    for p in range(2):
-        new = base_ref[0, 0, p] + term_ref[0, 0, p]
-        out_ref[0, 0, p] = new
-        low, high = new[:PAD], new[row_count - PAD :]
-        shear_ref[0, p] = jnp.sum(low * weight_ref[0][:, :1], axis=0)
-        shear_ref[0, 2 + p] = jnp.sum(high * weight_ref[1][:, :1], axis=0)
-
-
-def sum_kernel(base_ref, term_ref, out_ref):
-    out_ref[...] = base_ref[...] + term_ref[...]
-
-
-def add_first(base, term, weight):
-    mode_count, _, part_count, row_count, width = base.shape
-    block = pl.BlockSpec((1, 1, part_count, row_count, width), lambda m: (m, 0, 0, 0, 0))
+    )(rate, coef, flow, weight, field, low, high)
+
+
+def add_kernel(row_split, me_ref, base_ref, *refs):
+    buffer_ref, sems = refs[-2:]
+    count, part_count, row_count, _ = buffer_ref.shape
+    terms, out_ref = refs[:count], refs[count]
+    me, comp = me_ref[0], me_ref[3]
+
+    def spot(ref, x):
+        other = me ^ x
+        top = pl.multiple_of(other % row_split * row_count, PAD)
+        return ref.at[other // row_split, comp, :, pl.ds(top, row_count)]
+
+    loads = [pltpu.make_async_copy(spot(base_ref, x), buffer_ref.at[x], sems.at[x]) for x in range(count)]
+    stores = [pltpu.make_async_copy(buffer_ref.at[x], spot(out_ref, x), sems.at[x]) for x in range(count)]
+    for load in loads:
+        load.start()
+    for x in range(count):
+        loads[x].wait()
+        buffer_ref[x] = buffer_ref[x] + terms[x][...]
+        stores[x].start()
+    for store in stores:
+        store.wait()
+
+
+def add_term(base, terms, spots, row_split):
+    count = len(terms)
+    size = count * terms[0].size
     return pl.pallas_call(
-        wall_sum_kernel,
-        grid=(mode_count,),
-        out_shape=(
-            jax.ShapeDtypeStruct(base.shape, jnp.float32),
-            jax.ShapeDtypeStruct((mode_count, 4, width), jnp.float32),
-        ),
-        in_specs=[pl.BlockSpec(weight.shape, lambda m: (0, 0, 0)), block, block],
-        out_specs=(block, pl.BlockSpec((1, 4, width), lambda m: (m, 0, 0))),
+        functools.partial(add_kernel, row_split),
+        out_shape=jax.ShapeDtypeStruct(base.shape, jnp.float32),
+        in_specs=[pl.BlockSpec(memory_space=pltpu.SMEM), pl.BlockSpec(memory_space=pl.ANY)]
+        + [pl.BlockSpec(memory_space=pltpu.VMEM)] * count,
+        out_specs=pl.BlockSpec(memory_space=pl.ANY),
+        scratch_shapes=[pltpu.VMEM((count,) + terms[0].shape, jnp.float32), pltpu.SemaphoreType.DMA((count,))],
         input_output_aliases={1: 0},
-        cost_estimate=pl.CostEstimate(flops=term.size, bytes_accessed=12 * term.size, transcendentals=0),
-        name="add_first",
-    )(weight, base, term)
-
-
-def add_rest(base, term, first):
-    mode_count, comp_count, part_count, row_count, width = term.shape
-    shape = (1, 1, part_count, row_count, width)
-    block = pl.BlockSpec(shape, lambda m, c: (m, c + first, 0, 0, 0))
-    return pl.pallas_call(
-        sum_kernel,
-        grid=(mode_count, comp_count),
-        out_shape=jax.ShapeDtypeStruct(base.shape, jnp.float32),
-        in_specs=[block, pl.BlockSpec(shape, lambda m, c: (m, c, 0, 0, 0))],
-        out_specs=block,
-        input_output_aliases={0: 0},
-        cost_estimate=pl.CostEstimate(flops=term.size, bytes_accessed=12 * term.size, transcendentals=0),
-        name="add_rest",
-    )(base, term)
+        compiler_params=pltpu.CompilerParams(vmem_limit_bytes=16 << 20),
+        cost_estimate=pl.CostEstimate(flops=size, bytes_accessed=12 * size, transcendentals=0),
+        name="add_term",
+    )(spots, base, *terms)
 
 
 def on_device(field, mean_flow, d2_coef, wall_coef, kx_index, patch_of):
     mode_count, comp_count, part_count, row_count, width = field.shape
     span = lax.axis_size("span")
+    me = lax.axis_index("span")
     wall_count = lax.axis_size("wall")
     wall_index = lax.axis_index("wall")
     mode_split = math.gcd(span, mode_count)
     row_split = span // mode_split
+    line_rows = row_count // row_split
     tables = jnp.asarray(spectral_tables(width * span))
-
-    def to_lines(chunk):
-        lines = chunk.reshape(mode_split, -1, row_split, row_count // row_split, width)
-        lines = lines.transpose(0, 2, 1, 3, 4).reshape(span, -1, row_count // row_split, width)
-        return lax.all_to_all(lines, "span", split_axis=0, concat_axis=0)
-
-    def from_lines(lines, comps):
-        blocks = lax.all_to_all(lines, "span", split_axis=0, concat_axis=0)
-        blocks = blocks.reshape(mode_split, row_split, -1, row_count // row_split, width)
-        return blocks.transpose(0, 2, 1, 3, 4).reshape(mode_count, comps, part_count, row_count, width)
-
-    parts = [(0, 1), (1, comp_count)]
-    lines = [to_lines(field[:, first:last]) for first, last in parts]
+    pairs = [[(i, i ^ x) for i in range(span)] for x in range(span)]
+
+    def block_of(x, comp):
+        other = me ^ x
+        start = (other // row_split, comp, 0, other % row_split * line_rows, 0)
+        return lax.dynamic_slice(field, start, (1, 1, part_count, line_rows, width))[0, 0]
+
+    lines = [
+        [lax.ppermute(block_of(x, comp), "span", pairs[x]) for x in range(span - 1, 0, -1)][::-1]
+        for comp in range(comp_count)
+    ]
 
     forward = [(i, i + 1) for i in range(wall_count - 1)]
     backward = [(i + 1, i) for i in range(wall_count - 1)]
@@ -354,21 +390,33 @@
     rate = kx_index.astype(jnp.float32) * (0.25 * TAU)
     coef = jnp.broadcast_to(d2_coef[:, :, None], (STEN, row_count, LANES))
     flow = jnp.broadcast_to(mean_flow[:, :, None], (2, row_count, LANES))
-    base = local_terms(field, low, high, rate, coef, flow)
-
-    terms = [
-        from_lines(spanwise_operator(value, tables), last - first) for value, (first, last) in zip(lines, parts)
-    ]
     lower = jnp.where(wall_index == 0, wall_coef[0], 0.0)
     upper = jnp.where(wall_index == wall_count - 1, wall_coef[1, ::-1], 0.0)
-    weight = jnp.broadcast_to(jnp.stack([lower, upper])[:, :, None], (2, PAD, LANES))
-    base, shear = add_first(base, terms[0], weight)
-    onehot = (patch_of[:, None] == jnp.arange(PATCH, dtype=jnp.int32)[None, :]).astype(jnp.float32)
+    ends = jnp.stack([me % row_split == 0, me % row_split == row_split - 1])
+    walls = jnp.stack([lower, upper])
+    weight = jnp.broadcast_to(walls[:, :, None], (2, PAD, LANES))
+    line_weight = jnp.where(ends[:, None, None], weight, 0.0)
+    base, shear = local_terms(field, low, high, rate, coef, flow, weight)
+
+    patches = lax.all_gather(patch_of, "span", tiled=True)
+    names = jnp.arange(PATCH, dtype=jnp.int32)
+    onehot = (patch_of[:, None] == names[None, :]).astype(jnp.float32)
+    onehot_all = (patches.reshape(span, width)[:, :, None] == names).astype(jnp.float32)
     grad = jnp.einsum("mwz,zq->mwq", shear, onehot, precision=lax.Precision.HIGHEST)
-    grad = grad.reshape(mode_count, 2, part_count, PATCH).transpose(1, 0, 2, 3)
-    wall_grad = lax.psum(grad, ("wall", "span"))
-    new_field = add_rest(base, terms[1], 1)
-    return (new_field, wall_grad)
+
+    result = base
+    for comp in range(comp_count):
+        spots = jnp.stack([me, me // row_split, me % row_split * line_rows, comp]).astype(jnp.int32)
+        sent = spanwise_operator(field, lines[comp], spots, line_weight, tables, comp == 0)
+        if comp == 0:
+            line_grad = jnp.einsum("szq,swz->wq", onehot_all, sent[span], precision=lax.Precision.HIGHEST)
+            mine = jnp.arange(mode_count) == me // row_split
+            grad = grad + jnp.where(mine[:, None, None], line_grad, 0.0)
+            grad = grad.reshape(mode_count, 2, part_count, PATCH).transpose(1, 0, 2, 3)
+            wall_grad = lax.psum(grad, ("wall", "span"))
+        terms = [sent[0]] + [lax.ppermute(sent[x], "span", pairs[x]) for x in range(1, span)]
+        result = add_term(result, terms, spots, row_split)
+    return (result, wall_grad)
 
 
 def solution(mesh):

time: 271 us -> 284 us (1.048)
  blocking collectives: 44.7 us -> 97.1 us
  waiting for transfers between devices: 125 us -> 77.6 us
  starting transfers between devices: 32.2 us -> 47.3 us
  local copies, waits for them, and re-layouts: 23.2 us -> 10.6 us
  Pallas kernels: 40.9 us -> 48.2 us
    all_to_all x4 -> x0, waiting for transfers between devices: 107 us -> none  [the longest x2 85.4 us: to_lines(): return lax.all_to_all(lines, 'span', split_axis=0, concat_axis=0)]
    ppermute x0 -> x18, waiting for transfers between devices: none -> 77.6 us  [the longest x9 69.3 us: on_device(): lax.ppermute(block_of(x, comp), 'span', pairs[x])]
    all_gather x0 -> x1, blocking collectives: none -> 55 us  [on_device(): patches = lax.all_gather(patch_of, 'span', tiled=True)]
    ppermute x0 -> x18, starting transfers between devices: none -> 43.5 us  [the longest x9 27 us: on_device(): lax.ppermute(sent[x], 'span', pairs[x])]
    all_to_all x4 -> x0, starting transfers between devices: 27.9 us -> none  [the longest x2 15.6 us: from_lines(): blocks = lax.all_to_all(lines, 'span', split_axis=0, concat_axis=0)]
    ppermute x1, waiting for transfers between devices: 18.3 us -> 0.01 us  [on_device(): high = lax.ppermute(field[:, :, :, :PAD], 'wall', backward)]
    pallas_call x5 -> x7, Pallas kernels: 40.9 us -> 48.2 us  [the longest x3 24.6 us: spanwise_operator(): pl.pallas_call(functools.partial(spectral_kernel, sheared), out_shape=[se...]
    unnamed x18, local copies, waits for them, and re-layouts: 11.7 us -> 5.16 us
  transfers between devices with their start and end apart: 6 -> 20, of which waited for: 4 -> 7; matrix products, arithmetic and copies ran while one was open for 4% -> 1% of each run, Pallas kernels for 13% -> 16%
where the time goes in v2:
time: 284 us; the launch traced here: 283 us
  blocking collectives  97.1 us (34%)
  waiting for transfers between devices  77.6 us (27%)
  Pallas kernels  48.2 us (17%)
  starting transfers between devices  47.3 us (17%)
  local copies, waits for them, and re-layouts  10.6 us (4%)
    ppermute x9, waiting for transfers between devices, on_device(): lax.ppermute(block_of(x, comp), 'span', pairs[x])  69.3 us
    all_gather x1, blocking collectives, on_device(): patches = lax.all_gather(patch_of, 'span', tiled=True)  55 us
    psum x1, blocking collectives, on_device(): wall_grad = lax.psum(grad, ('wall', 'span'))  42 us
    ppermute x9, starting transfers between devices, on_device(): lax.ppermute(sent[x], 'span', pairs[x])  27 us
    pallas_call x3, Pallas kernels, spanwise_operator(): pl.pallas_call(functools.partial(spectral_kernel, sheared), out_shape=[se...  24.6 us
    ppermute x9, starting transfers between devices, on_device(): lax.ppermute(block_of(x, comp), 'span', pairs[x])  16.5 us
    pallas_call x1, Pallas kernels, local_terms(): pl.pallas_call(local_kernel, grid=(mode_count,), out_shape=(jax.ShapeDtyp...  15.4 us
    ppermute x9, waiting for transfers between devices, on_device(): lax.ppermute(sent[x], 'span', pairs[x])  8.26 us
  transfers between devices with their start and end apart: 20, of which 7 were waited for; matrix products, arithmetic and copies ran while one was open for 1% of the time, Pallas kernels for 16%

profile of v2, /device:TPU:10, one launch (start us, length us, event | category | flops | bytes accessed | tf_op | source)
XLA Modules:
  0.0 283.0 jit_solution(3530470109100262940)
XLA Ops:
  0.7 0.0 copy-start
  0.7 0.0 copy-start.6
  0.7 3.4 %dynamic-slice_bitcast_fusion = (f32[2,32,1536]{2,1,0:T(8,128)S(1)}, f32[2,32,1536]{2,1,0:T(8,128)S(1)}, f32[2,32,1536]{2,1,0:T(8,128)S(1)}, f32[2,32,1536]{2,1,...) fusion(f32[4,3,2,32,1536]{4,3,2,1,0:T(8,128)} %field_ref.7, ...), kind=kLoop, calls=%fused_computation.6 | loop fusion | bytes 7077900 | tf_op jit(solution)/shard_map/squeeze | solution.py:379
  4.1 0.4 collective-permute-start.2
  4.6 2.6 collective-permute-start.3
  7.2 0.5 collective-permute-start.4
  7.6 1.6 collective-permute-start.10
  9.2 3.4 %collective-permute-start.8 = (f32[2,32,1536]{2,1,0:T(8,128)}, f32[2,32,1536]{2,1,0:T(8,128)S(1)}, u32[]{:S(2)}, u32[]{:S(2)}) collective-permute-start(f32[2,32,1536]{2,1,0:T(8,128)} %get-tuple-element.39), channel_id=1, source_target_pairs={{0,1},{1,0},{2,3},{3,2},{4,5},{5,4},{6,7},{7,6},{8,9},{9,8},{10,11... | collective-permute-start | bytes 1179656 | tf_op jit(solution)/shard_map/ppermute | solution.py:382
  12.6 1.6 fusion.6
  14.2 7.5 %collective-permute-done.2.refs_0_ = f32[2,32,1536]{2,1,0:T(8,128)S(1)} collective-permute-done((f32[2,32,1536]{2,1,0:T(8,128)S(1)}, f32[2,32,1536]{2,1,0:T(8,128)S(1)}, u32[]{:S(2)}, u32[]{:S(2)}) %collective-permute-start.2) | collective-permute-done | bytes 393248 | tf_op jit(solution)/shard_map/ppermute | solution.py:382
  21.6 5.0 %collective-permute-start.9 = (f32[2,32,1536]{2,1,0:T(8,128)}, f32[2,32,1536]{2,1,0:T(8,128)S(1)}, u32[]{:S(2)}, u32[]{:S(2)}) collective-permute-start(f32[2,32,1536]{2,1,0:T(8,128)} %get-tuple-element.38), channel_id=1, source_target_pairs={{0,2},{1,3},{2,0},{3,1},{4,6},{5,7},{6,4},{7,5},{8,10},{9,11},{10,... | collective-permute-start | bytes 1179656 | tf_op jit(solution)/shard_map/ppermute | solution.py:382
  26.6 0.1 rev.3
  26.7 15.6 %collective-permute-done.3.refs_1_ = f32[2,32,1536]{2,1,0:T(8,128)S(1)} collective-permute-done((f32[2,32,1536]{2,1,0:T(8,128)}, f32[2,32,1536]{2,1,0:T(8,128)S(1)}, u32[]{:S(2)}, u32[]{:S(2)}) %collective-permute-start.3) | collective-permute-done | bytes 393248 | tf_op jit(solution)/shard_map/ppermute | solution.py:382
  42.4 1.9 collective-permute-start
  44.3 15.7 %collective-permute-done.4.refs_2_ = f32[2,32,1536]{2,1,0:T(8,128)S(1)} collective-permute-done((f32[2,32,1536]{2,1,0:T(8,128)}, f32[2,32,1536]{2,1,0:T(8,128)S(1)}, u32[]{:S(2)}, u32[]{:S(2)}) %collective-permute-start.4) | collective-permute-done | bytes 393248 | tf_op jit(solution)/shard_map/ppermute | solution.py:382
  60.0 1.9 collective-permute-start.1
  61.9 6.5 %collective-permute-done.10.refs_2_ = f32[2,32,1536]{2,1,0:T(8,128)S(1)} collective-permute-done((f32[2,32,1536]{2,1,0:T(8,128)}, f32[2,32,1536]{2,1,0:T(8,128)S(1)}, u32[]{:S(2)}, u32[]{:S(2)}) %collective-permute-start.10) | collective-permute-done | bytes 393248 | tf_op jit(solution)/shard_map/ppermute | solution.py:382
  68.4 0.0 collective-permute-start.14
  68.4 0.0 collective-permute-done.8.refs_0_
  68.4 3.0 %collective-permute-start.15 = (f32[2,32,1536]{2,1,0:T(8,128)S(1)}, f32[2,32,1536]{2,1,0:T(8,128)S(1)}, u32[]{:S(2)}, u32[]{:S(2)}) collective-permute-start(f32[2,32,1536]{2,1,0:T(8,128)S(1)} %get-tuple-element.35), channel_id=1, source_target_pairs={{0,2},{1,3},{2,0},{3,1},{4,6},{5,7},{6,4},{7,5},{8,10},{9,11},{10,... | collective-permute-start | bytes 1179656 | tf_op jit(solution)/shard_map/ppermute | solution.py:382
  71.5 8.2 %collective-permute-done.9.refs_1_ = f32[2,32,1536]{2,1,0:T(8,128)S(1)} collective-permute-done((f32[2,32,1536]{2,1,0:T(8,128)}, f32[2,32,1536]{2,1,0:T(8,128)S(1)}, u32[]{:S(2)}, u32[]{:S(2)}) %collective-permute-start.9) | collective-permute-done | bytes 393248 | tf_op jit(solution)/shard_map/ppermute | solution.py:382
  79.7 0.0 collective-permute-start.16
  79.7 0.1 pad_add_fusion.3
  79.8 0.1 broadcast_in_dim.55.weight_ref
  79.8 2.3 copy-done.1
  82.2 2.8 copy-done.2
  85.0 8.4 %spanwise.3 = (f32[2,32,1536]{2,1,0:T(8,128)S(1)}, f32[2,32,1536]{2,1,0:T(8,128)S(1)}, f32[2,32,1536]{2,1,0:T(8,128)S(1)}, f32[2,32,1536]{2,1,0:T(8,128)S(1)}, f32[4,4,1536]{2,1,0:T(4,128)S(1)}) custom-call(s32[4]{0:T(128)S(1)} %get-tuple-element.32.me_ref, bf16[24,2,256,256]{3,2,1,0:T(8,128)(2,1)S(1)} %copy-done.2, ...), custom_call_target="tpu_custom_call" | custom-call | flops 603979776 | bytes 3145728 | tf_op jit(solution)/shard_map/spanwise/pallas_call | solution.py:243
  93.4 0.0 collective-permute-done.14.refs_0_
  93.4 13.9 %collective-permute-start.5 = (f32[2,32,1536]{2,1,0:T(8,128)S(1)}, f32[2,32,1536]{2,1,0:T(8,128)S(1)}, u32[]{:S(2)}, u32[]{:S(2)}) collective-permute-start(f32[2,32,1536]{2,1,0:T(8,128)S(1)} %get-tuple-element.19), channel_id=1, source_target_pairs={{0,1},{1,0},{2,3},{3,2},{4,5},{5,4},{6,7},{7,6},{8,9},{9,8},{10,11... | collective-permute-start | bytes 1179656 | tf_op jit(solution)/shard_map/ppermute | solution.py:417
  107.2 0.0 collective-permute-done.15.refs_1_
  107.2 4.5 %collective-permute-start.6 = (f32[2,32,1536]{2,1,0:T(8,128)S(1)}, f32[2,32,1536]{2,1,0:T(8,128)S(1)}, u32[]{:S(2)}, u32[]{:S(2)}) collective-permute-start(f32[2,32,1536]{2,1,0:T(8,128)S(1)} %get-tuple-element.20), channel_id=1, source_target_pairs={{0,2},{1,3},{2,0},{3,1},{4,6},{5,7},{6,4},{7,5},{8,10},{9,11},{10,... | collective-permute-start | bytes 1179656 | tf_op jit(solution)/shard_map/ppermute | solution.py:417
  111.7 15.8 %collective-permute-done.16.refs_2_ = f32[2,32,1536]{2,1,0:T(8,128)S(1)} collective-permute-done((f32[2,32,1536]{2,1,0:T(8,128)S(1)}, f32[2,32,1536]{2,1,0:T(8,128)S(1)}, u32[]{:S(2)}, u32[]{:S(2)}) %collective-permute-start.16) | collective-permute-done | bytes 393248 | tf_op jit(solution)/shard_map/ppermute | solution.py:382
  127.5 1.6 collective-permute-start.7
  129.1 0.1 pad_add_fusion.2
  129.2 8.1 %spanwise.4 = (f32[2,32,1536]{2,1,0:T(8,128)S(1)}, f32[2,32,1536]{2,1,0:T(8,128)S(1)}, f32[2,32,1536]{2,1,0:T(8,128)S(1)}, f32[2,32,1536]{2,1,0:T(8,128)S(1)}) custom-call(s32[4]{0:T(128)S(1)} %get-tuple-element.47.me_ref, bf16[24,2,256,256]{3,2,1,0:T(8,128)(2,1)S(1)} %copy-done.2, f32[2,8,128]{2,1,0:T(8,128)S(1)} %broadcast_in_dim.55.weight_ref, ...), custom_call_target="tpu_custom_call" | custom-call | flops 603979776 | bytes 3145728 | tf_op jit(solution)/shard_map/spanwise/pallas_call | solution.py:243
  137.3 0.0 collective-permute-done.5.refs_1_
  137.3 0.1 collective-permute-start.11
  137.4 0.0 collective-permute-done.6.refs_2_
  137.4 1.8 collective-permute-start.12
  139.3 8.2 %collective-permute-done.7.refs_3_ = f32[2,32,1536]{2,1,0:T(8,128)S(1)} collective-permute-done((f32[2,32,1536]{2,1,0:T(8,128)S(1)}, f32[2,32,1536]{2,1,0:T(8,128)S(1)}, u32[]{:S(2)}, u32[]{:S(2)}) %collective-permute-start.7) | collective-permute-done | bytes 393248 | tf_op jit(solution)/shard_map/ppermute | solution.py:417
  147.5 1.6 collective-permute-start.13
  149.1 0.0 copy-start.5
  149.2 8.1 %spanwise.5 = (f32[2,32,1536]{2,1,0:T(8,128)S(1)}, f32[2,32,1536]{2,1,0:T(8,128)S(1)}, f32[2,32,1536]{2,1,0:T(8,128)S(1)}, f32[2,32,1536]{2,1,0:T(8,128)S(1)}) custom-call(s32[4]{0:T(128)S(1)} %get-tuple-element.48.me_ref, bf16[24,2,256,256]{3,2,1,0:T(8,128)(2,1)S(1)} %copy-done.2, f32[2,8,128]{2,1,0:T(8,128)S(1)} %broadcast_in_dim.55.weight_ref, ...), custom_call_target="tpu_custom_call" | custom-call | flops 603979776 | bytes 3145728 | tf_op jit(solution)/shard_map/spanwise/pallas_call | solution.py:243
  157.3 0.0 collective-permute-done.11.refs_1_
  157.3 0.1 collective-permute-start.17
  157.4 0.0 collective-permute-done.low_ref
  157.4 1.8 collective-permute-start.18
  159.2 0.0 collective-permute-done.1.high_ref
  159.2 1.6 collective-permute-start.19
  160.9 55.0 %all-gather = s32[4,1,1536]{2,1,0:T(1,128)S(1)} all-gather(s32[1,1,1536]{2,1,0:T(1,128)S(1)} %reshape.18), channel_id=1, replica_groups=mesh['wall'=8,'span'=4] {'span'}, dimensions={0}, use_global_device_ids=true | all-gather | bytes 30720 | tf_op jit(solution)/shard_map/all_gather | solution.py:401
  215.9 0.8 fusion.1
  216.7 0.1 broadcast_in_dim.30.coef_ref
  216.9 0.1 broadcast_in_dim.31.flow_ref
  216.9 15.4 %local_terms.1 = (f32[4,3,2,32,1536]{4,3,2,1,0:T(8,128)}, f32[4,4,1536]{2,1,0:T(4,128)S(1)}) custom-call(f32[4]{0:T(128)S(1)} %convert_multiply_fusion.rate_ref, f32[15,32,128]{2,1,0:T(8,128)S(1)} %broadcast_in_dim.30.coef_ref, f32[2,32,128]{2,1,0:T(8,128)S(1)} %broadcast_in_dim.31.flow_ref, f32[2,8,128]{2,1,0:T(8,128)S(1)} %broadcast_in_dim.55.weight_ref, ...), custom_call_target="tpu_custom_call" | custom-call | flops 47185920 | bytes 11796480 | tf_op jit(solution)/shard_map/local_terms/pallas_call | solution.py:300
  232.3 2.7 add_term.3.base_ref
  235.1 0.0 collective-permute-done.12.refs_2_
  235.1 0.0 collective-permute-done.13.refs_3_
  235.1 2.8 add_term.4.base_ref
  237.9 0.3 convolution_add_fusion
  238.2 42.0 %psum.7 = f32[2,4,2,64]{3,2,1,0:T(2,128)} all-reduce(f32[2,4,2,64]{3,2,1,0:T(2,128)S(1)} %bitcast.33), channel_id=1, replica_groups=mesh['wall'=8,'span'=4] {'wall','span'}, use_global_device_ids=true, to_apply=%region_0.1 | all-reduce | flops 1024 | bytes 8192 | tf_op jit(solution)/shard_map/psum | solution.py:416
  280.2 0.0 collective-permute-done.17.refs_1_
  280.2 0.0 collective-permute-done.18.refs_2_
  280.2 0.0 collective-permute-done.19.refs_3_
  280.2 2.8 add_term.5
  (19 shorter events, 0.1 us)
Async XLA Ops:
  0.7 11.9 %copy-start = (f32[4,3,2,32,1536]{4,3,2,1,0:T(8,128)S(1)}, f32[4,3,2,32,1536]{4,3,2,1,0:T(8,128)}, u32[]{:S(2)}) copy-start(f32[4,3,2,32,1536]{4,3,2,1,0:T(8,128)} %field_ref.7) | copy-start | bytes 14155780
  0.7 26.0 %copy-start.6 = (f32[2,8]{1,0:T(2,128)S(1)}, f32[2,8]{1,0:T(2,128)}, u32[]{:S(2)}) copy-start(f32[2,8]{1,0:T(2,128)} %param.10) | copy-start | bytes 196
  4.1 17.5 %collective-permute-start.2 = (f32[2,32,1536]{2,1,0:T(8,128)S(1)}, f32[2,32,1536]{2,1,0:T(8,128)S(1)}, u32[]{:S(2)}, u32[]{:S(2)}) collective-permute-start(f32[2,32,1536]{2,1,0:T(8,128)S(1)} %get-tuple-element.42), channel_id=1, source_target_pairs={{0,1},{1,0},{2,3},{3,2},{4,5},{5,4},{6,7},{7,6},{8,9},{9,8},{10,11... | collective-permute-start | bytes 1179656 | tf_op jit(solution)/shard_map/ppermute | solution.py:382
  4.6 37.8 %collective-permute-start.3 = (f32[2,32,1536]{2,1,0:T(8,128)}, f32[2,32,1536]{2,1,0:T(8,128)S(1)}, u32[]{:S(2)}, u32[]{:S(2)}) collective-permute-start(f32[2,32,1536]{2,1,0:T(8,128)} %get-tuple-element.41), channel_id=1, source_target_pairs={{0,2},{1,3},{2,0},{3,1},{4,6},{5,7},{6,4},{7,5},{8,10},{9,11},{10,... | collective-permute-start | bytes 1179656 | tf_op jit(solution)/shard_map/ppermute | solution.py:382
  7.2 52.8 %collective-permute-start.4 = (f32[2,32,1536]{2,1,0:T(8,128)}, f32[2,32,1536]{2,1,0:T(8,128)S(1)}, u32[]{:S(2)}, u32[]{:S(2)}) collective-permute-start(f32[2,32,1536]{2,1,0:T(8,128)} %get-tuple-element.40), channel_id=1, source_target_pairs={{0,3},{1,2},{2,1},{3,0},{4,7},{5,6},{6,5},{7,4},{8,11},{9,10},{10,... | collective-permute-start | bytes 1179656 | tf_op jit(solution)/shard_map/ppermute | solution.py:382
  7.6 60.8 %collective-permute-start.10 = (f32[2,32,1536]{2,1,0:T(8,128)}, f32[2,32,1536]{2,1,0:T(8,128)S(1)}, u32[]{:S(2)}, u32[]{:S(2)}) collective-permute-start(f32[2,32,1536]{2,1,0:T(8,128)} %get-tuple-element.37), channel_id=1, source_target_pairs={{0,3},{1,2},{2,1},{3,0},{4,7},{5,6},{6,5},{7,4},{8,11},{9,10},{10,... | collective-permute-start | bytes 1179656 | tf_op jit(solution)/shard_map/ppermute | solution.py:382
  9.2 59.3 %collective-permute-start.8 = (f32[2,32,1536]{2,1,0:T(8,128)}, f32[2,32,1536]{2,1,0:T(8,128)S(1)}, u32[]{:S(2)}, u32[]{:S(2)}) collective-permute-start(f32[2,32,1536]{2,1,0:T(8,128)} %get-tuple-element.39), channel_id=1, source_target_pairs={{0,1},{1,0},{2,3},{3,2},{4,5},{5,4},{6,7},{7,6},{8,9},{9,8},{10,11... | collective-permute-start | bytes 1179656 | tf_op jit(solution)/shard_map/ppermute | solution.py:382
  21.6 58.0 %collective-permute-start.9 = (f32[2,32,1536]{2,1,0:T(8,128)}, f32[2,32,1536]{2,1,0:T(8,128)S(1)}, u32[]{:S(2)}, u32[]{:S(2)}) collective-permute-start(f32[2,32,1536]{2,1,0:T(8,128)} %get-tuple-element.38), channel_id=1, source_target_pairs={{0,2},{1,3},{2,0},{3,1},{4,6},{5,7},{6,4},{7,5},{8,10},{9,11},{10,... | collective-permute-start | bytes 1179656 | tf_op jit(solution)/shard_map/ppermute | solution.py:382
  42.4 115.0 %collective-permute-start = (f32[4,3,2,8,1536]{4,3,2,1,0:T(8,128)}, f32[4,3,2,8,1536]{4,3,2,1,0:T(8,128)S(1)}, u32[]{:S(2)}, u32[]{:S(2)}) collective-permute-start(f32[4,3,2,8,1536]{4,3,2,1,0:T(8,128)} %get-tuple-element.44), channel_id=1, source_target_pairs={{0,4},{4,8},{8,12},{12,16},{16,20},{20,24},{24,28},{1,5},{5,9},{9,... | collective-permute-start | bytes 3538952 | tf_op jit(solution)/shard_map/ppermute | solution.py:388
  60.0 99.2 %collective-permute-start.1 = (f32[4,3,2,8,1536]{4,3,2,1,0:T(8,128)}, f32[4,3,2,8,1536]{4,3,2,1,0:T(8,128)S(1)}, u32[]{:S(2)}, u32[]{:S(2)}) collective-permute-start(f32[4,3,2,8,1536]{4,3,2,1,0:T(8,128)} %get-tuple-element.43), channel_id=1, source_target_pairs={{4,0},{8,4},{12,8},{16,12},{20,16},{24,20},{28,24},{5,1},{9,5},{13... | collective-permute-start | bytes 3538952 | tf_op jit(solution)/shard_map/ppermute | solution.py:389
  68.4 24.9 %collective-permute-start.14 = (f32[2,32,1536]{2,1,0:T(8,128)S(1)}, f32[2,32,1536]{2,1,0:T(8,128)S(1)}, u32[]{:S(2)}, u32[]{:S(2)}) collective-permute-start(f32[2,32,1536]{2,1,0:T(8,128)S(1)} %get-tuple-element.36), channel_id=1, source_target_pairs={{0,1},{1,0},{2,3},{3,2},{4,5},{5,4},{6,7},{7,6},{8,9},{9,8},{10,11... | collective-permute-start | bytes 1179656 | tf_op jit(solution)/shard_map/ppermute | solution.py:382
  68.4 38.8 %collective-permute-start.15 = (f32[2,32,1536]{2,1,0:T(8,128)S(1)}, f32[2,32,1536]{2,1,0:T(8,128)S(1)}, u32[]{:S(2)}, u32[]{:S(2)}) collective-permute-start(f32[2,32,1536]{2,1,0:T(8,128)S(1)} %get-tuple-element.35), channel_id=1, source_target_pairs={{0,2},{1,3},{2,0},{3,1},{4,6},{5,7},{6,4},{7,5},{8,10},{9,11},{10,... | collective-permute-start | bytes 1179656 | tf_op jit(solution)/shard_map/ppermute | solution.py:382
  79.7 47.8 %collective-permute-start.16 = (f32[2,32,1536]{2,1,0:T(8,128)S(1)}, f32[2,32,1536]{2,1,0:T(8,128)S(1)}, u32[]{:S(2)}, u32[]{:S(2)}) collective-permute-start(f32[2,32,1536]{2,1,0:T(8,128)S(1)} %get-tuple-element.34), channel_id=1, source_target_pairs={{0,3},{1,2},{2,1},{3,0},{4,7},{5,6},{6,5},{7,4},{8,11},{9,10},{10,... | collective-permute-start | bytes 1179656 | tf_op jit(solution)/shard_map/ppermute | solution.py:382
  79.8 2.3 copy-start.1
  82.2 2.8 copy-start.2
  93.4 43.9 %collective-permute-start.5 = (f32[2,32,1536]{2,1,0:T(8,128)S(1)}, f32[2,32,1536]{2,1,0:T(8,128)S(1)}, u32[]{:S(2)}, u32[]{:S(2)}) collective-permute-start(f32[2,32,1536]{2,1,0:T(8,128)S(1)} %get-tuple-element.19), channel_id=1, source_target_pairs={{0,1},{1,0},{2,3},{3,2},{4,5},{5,4},{6,7},{7,6},{8,9},{9,8},{10,11... | collective-permute-start | bytes 1179656 | tf_op jit(solution)/shard_map/ppermute | solution.py:417
  107.2 30.2 %collective-permute-start.6 = (f32[2,32,1536]{2,1,0:T(8,128)S(1)}, f32[2,32,1536]{2,1,0:T(8,128)S(1)}, u32[]{:S(2)}, u32[]{:S(2)}) collective-permute-start(f32[2,32,1536]{2,1,0:T(8,128)S(1)} %get-tuple-element.20), channel_id=1, source_target_pairs={{0,2},{1,3},{2,0},{3,1},{4,6},{5,7},{6,4},{7,5},{8,10},{9,11},{10,... | collective-permute-start | bytes 1179656 | tf_op jit(solution)/shard_map/ppermute | solution.py:417
  127.5 20.0 %collective-permute-start.7 = (f32[2,32,1536]{2,1,0:T(8,128)S(1)}, f32[2,32,1536]{2,1,0:T(8,128)S(1)}, u32[]{:S(2)}, u32[]{:S(2)}) collective-permute-start(f32[2,32,1536]{2,1,0:T(8,128)S(1)} %get-tuple-element.21), channel_id=1, source_target_pairs={{0,3},{1,2},{2,1},{3,0},{4,7},{5,6},{6,5},{7,4},{8,11},{9,10},{10,... | collective-permute-start | bytes 1179656 | tf_op jit(solution)/shard_map/ppermute | solution.py:417
  129.2 19.9 %copy-start.7 = (s32[4]{0:T(128)S(1)}, s32[4]{0:T(128)}, u32[]{:S(2)}) copy-start(s32[4]{0:T(128)} %param.11) | copy-start | bytes 52
  137.3 19.9 %collective-permute-start.11 = (f32[2,32,1536]{2,1,0:T(8,128)S(1)}, f32[2,32,1536]{2,1,0:T(8,128)S(1)}, u32[]{:S(2)}, u32[]{:S(2)}) collective-permute-start(f32[2,32,1536]{2,1,0:T(8,128)S(1)} %get-tuple-element.23), channel_id=1, source_target_pairs={{0,1},{1,0},{2,3},{3,2},{4,5},{5,4},{6,7},{7,6},{8,9},{9,8},{10,11... | collective-permute-start | bytes 1179656 | tf_op jit(solution)/shard_map/ppermute | solution.py:417
  137.4 97.7 %collective-permute-start.12 = (f32[2,32,1536]{2,1,0:T(8,128)S(1)}, f32[2,32,1536]{2,1,0:T(8,128)S(1)}, u32[]{:S(2)}, u32[]{:S(2)}) collective-permute-start(f32[2,32,1536]{2,1,0:T(8,128)S(1)} %get-tuple-element.24), channel_id=1, source_target_pairs={{0,2},{1,3},{2,0},{3,1},{4,6},{5,7},{6,4},{7,5},{8,10},{9,11},{10,... | collective-permute-start | bytes 1179656 | tf_op jit(solution)/shard_map/ppermute | solution.py:417
  147.5 87.6 %collective-permute-start.13 = (f32[2,32,1536]{2,1,0:T(8,128)S(1)}, f32[2,32,1536]{2,1,0:T(8,128)S(1)}, u32[]{:S(2)}, u32[]{:S(2)}) collective-permute-start(f32[2,32,1536]{2,1,0:T(8,128)S(1)} %get-tuple-element.25), channel_id=1, source_target_pairs={{0,3},{1,2},{2,1},{3,0},{4,7},{5,6},{6,5},{7,4},{8,11},{9,10},{10,... | collective-permute-start | bytes 1179656 | tf_op jit(solution)/shard_map/ppermute | solution.py:417
  149.1 11.7 %copy-start.4 = (s32[1536]{0:T(1024)S(1)}, s32[1536]{0:T(1024)}, u32[]{:S(2)}) copy-start(s32[1536]{0:T(1024)} %param.12) | copy-start | bytes 18436
  149.1 67.6 %copy-start.3 = (f32[15,32]{1,0:T(8,128)S(1)}, f32[15,32]{1,0:T(8,128)}, u32[]{:S(2)}) copy-start(f32[15,32]{1,0:T(8,128)} %param.9) | copy-start | bytes 5764
  149.1 67.7 %copy-start.5 = (f32[2,32]{1,0:T(2,128)S(1)}, f32[2,32]{1,0:T(2,128)}, u32[]{:S(2)}) copy-start(f32[2,32]{1,0:T(2,128)} %param.8) | copy-start | bytes 772
  157.3 122.9 %collective-permute-start.17 = (f32[2,32,1536]{2,1,0:T(8,128)S(1)}, f32[2,32,1536]{2,1,0:T(8,128)S(1)}, u32[]{:S(2)}, u32[]{:S(2)}) collective-permute-start(f32[2,32,1536]{2,1,0:T(8,128)S(1)} %get-tuple-element.27), channel_id=1, source_target_pairs={{0,1},{1,0},{2,3},{3,2},{4,5},{5,4},{6,7},{7,6},{8,9},{9,8},{10,11... | collective-permute-start | bytes 1179656 | tf_op jit(solution)/shard_map/ppermute | solution.py:417
  157.4 122.9 %collective-permute-start.18 = (f32[2,32,1536]{2,1,0:T(8,128)S(1)}, f32[2,32,1536]{2,1,0:T(8,128)S(1)}, u32[]{:S(2)}, u32[]{:S(2)}) collective-permute-start(f32[2,32,1536]{2,1,0:T(8,128)S(1)} %get-tuple-element.28), channel_id=1, source_target_pairs={{0,2},{1,3},{2,0},{3,1},{4,6},{5,7},{6,4},{7,5},{8,10},{9,11},{10,... | collective-permute-start | bytes 1179656 | tf_op jit(solution)/shard_map/ppermute | solution.py:417
  159.2 121.0 %collective-permute-start.19 = (f32[2,32,1536]{2,1,0:T(8,128)S(1)}, f32[2,32,1536]{2,1,0:T(8,128)S(1)}, u32[]{:S(2)}, u32[]{:S(2)}) collective-permute-start(f32[2,32,1536]{2,1,0:T(8,128)S(1)} %get-tuple-element.29), channel_id=1, source_target_pairs={{0,3},{1,2},{2,1},{3,0},{4,7},{5,6},{6,5},{7,4},{8,11},{9,10},{10,... | collective-permute-start | bytes 1179656 | tf_op jit(solution)/shard_map/ppermute | solution.py:417

commit v3 on v1

--- a/solution.py
+++ b/solution.py
@@ -156,21 +156,17 @@
     return x
 
 
-def spectral_kernel(table_ref, line_ref, out_ref, wave_ref):
-    source_count, line_count, row_count, width = line_ref.shape
+def filter_lines(line_ref, wave_ref, table_ref):
+    _, line_count, row_count, width = line_ref.shape
     pieces = width // LANES
     groups = row_count // PAD
 
-    def place(n1):
-        return n1 // pieces, pl.ds(n1 % pieces * LANES, LANES)
+    def spots(step):
+        return step // groups, pl.ds(pl.multiple_of(step % groups * PAD, PAD), PAD), pl.ds(pl.multiple_of(step * PAD, PAD), PAD)
 
     def forward(step, _):
-        line, rows = step // groups, pl.ds(pl.multiple_of(step % groups * PAD, PAD), PAD)
-        values = []
-        for n1 in range(OUTER):
-            source, lanes = place(n1)
-            values.append(line_ref[source, line, rows, lanes])
-        spot = pl.ds(pl.multiple_of(step * PAD, PAD), PAD)
+        line, rows, spot = spots(step)
+        values = [line_ref[n1 // pieces, line, rows, pl.ds(n1 % pieces * LANES, LANES)] for n1 in range(OUTER)]
         for tile, (re, im) in enumerate(real_forward(values)):
             wave_ref[tile, spot, :LANES] = re
             wave_ref[tile, spot, LANES:] = im
@@ -193,30 +189,79 @@
     lax.fori_loop(0, TILES, middle, 0)
 
     def backward(step, _):
-        line, rows = step // groups, pl.ds(pl.multiple_of(step % groups * PAD, PAD), PAD)
-        spot = pl.ds(pl.multiple_of(step * PAD, PAD), PAD)
+        line, rows, spot = spots(step)
         tiles = [(wave_ref[tile, spot, :LANES], wave_ref[tile, spot, LANES:]) for tile in range(TILES)]
         for n1, value in enumerate(real_backward(tiles)):
-            source, lanes = place(n1)
-            out_ref[source, line, rows, lanes] = value
+            line_ref[n1 // pieces, line, rows, pl.ds(n1 % pieces * LANES, LANES)] = value
         return 0
 
     lax.fori_loop(0, line_count * groups, backward, 0)
 
 
-def spanwise_operator(lines, tables):
-    source_count, line_count, row_count, width = lines.shape
+def paired_kernel(me_ref, table_ref, field_ref, *refs):
+    line_ref, wave_ref, sems = refs[-3:]
+    count, _, row_count, _ = line_ref.shape
+    received, sent = refs[: count - 1], refs[count - 1 : 2 * count - 1]
+    me, mode, top = me_ref[0], me_ref[1], me_ref[2]
+    own = field_ref.at[mode, 0, :, pl.ds(pl.multiple_of(top, PAD), row_count)]
+    sources = (own,) + received
+    copies = [pltpu.make_async_copy(sources[x], line_ref.at[me ^ x], sems.at[x]) for x in range(count)]
+    for copy in copies:
+        copy.start()
+    for copy in copies:
+        copy.wait()
+    filter_lines(line_ref, wave_ref, table_ref)
+    copies = [pltpu.make_async_copy(line_ref.at[me ^ x], sent[x], sems.at[x]) for x in range(count)]
+    for copy in copies:
+        copy.start()
+    for copy in copies:
+        copy.wait()
+
+
+def filter_cost(count, rows, width):
+    flops = 3 * 2 * TILES * rows * (2 * LANES) ** 2
+    return pl.CostEstimate(flops=flops, bytes_accessed=8 * count * rows * width, transcendentals=0)
+
+
+def filter_paired(field, received, spots, tables):
+    count = len(received) + 1
+    part_count, row_count, width = received[0].shape
+    rows = part_count * row_count
+    anywhere = pl.BlockSpec(memory_space=pl.ANY)
+    return pl.pallas_call(
+        paired_kernel,
+        out_shape=[jax.ShapeDtypeStruct(received[0].shape, jnp.float32)] * count,
+        in_specs=[pl.BlockSpec(memory_space=pltpu.SMEM), pl.BlockSpec(memory_space=pltpu.VMEM)] + [anywhere] * count,
+        out_specs=[anywhere] * count,
+        scratch_shapes=[
+            pltpu.VMEM((count, part_count, row_count, width), jnp.float32),
+            pltpu.VMEM((TILES, rows, 2 * LANES), jnp.float32),
+            pltpu.SemaphoreType.DMA((count,)),
+        ],
+        compiler_params=pltpu.CompilerParams(vmem_limit_bytes=24 << 20),
+        cost_estimate=filter_cost(count, rows, width),
+        name="filter_paired",
+    )(spots, tables, field, *received)
+
+
+def whole_kernel(table_ref, line_ref, out_ref, wave_ref):
+    out_ref[...] = line_ref[...]
+    filter_lines(out_ref, wave_ref, table_ref)
+
+
+def filter_whole(lines, tables):
+    count, line_count, row_count, width = lines.shape
     rows = line_count * row_count
-    flops = 3 * 2 * TILES * rows * (2 * LANES) ** 2
+    vector = pl.BlockSpec(memory_space=pltpu.VMEM)
     return pl.pallas_call(
-        spectral_kernel,
+        whole_kernel,
         out_shape=jax.ShapeDtypeStruct(lines.shape, jnp.float32),
-        in_specs=[pl.BlockSpec(memory_space=pltpu.VMEM)] * 2,
-        out_specs=pl.BlockSpec(memory_space=pltpu.VMEM),
+        in_specs=[vector] * 2,
+        out_specs=vector,
         scratch_shapes=[pltpu.VMEM((TILES, rows, 2 * LANES), jnp.float32)],
-        compiler_params=pltpu.CompilerParams(vmem_limit_bytes=40 << 20),
-        cost_estimate=pl.CostEstimate(flops=flops, bytes_accessed=8 * lines.size + 2 * tables.size, transcendentals=0),
-        name="spanwise",
+        compiler_params=pltpu.CompilerParams(vmem_limit_bytes=24 << 20),
+        cost_estimate=filter_cost(count, rows, width),
+        name="filter_whole",
     )(tables, lines)
 
 
@@ -277,98 +322,150 @@
     )(rate, coef, flow, field, low, high)
 
 
-def wall_sum_kernel(weight_ref, base_ref, term_ref, out_ref, shear_ref):
-    row_count = base_ref.shape[3]
-    for p in range(2):
-        new = base_ref[0, 0, p] + term_ref[0, 0, p]
-        out_ref[0, 0, p] = new
-        low, high = new[:PAD], new[row_count - PAD :]
-        shear_ref[0, p] = jnp.sum(low * weight_ref[0][:, :1], axis=0)
-        shear_ref[0, 2 + p] = jnp.sum(high * weight_ref[1][:, :1], axis=0)
-
-
-def sum_kernel(base_ref, term_ref, out_ref):
-    out_ref[...] = base_ref[...] + term_ref[...]
-
-
-def add_first(base, term, weight):
-    mode_count, _, part_count, row_count, width = base.shape
-    block = pl.BlockSpec((1, 1, part_count, row_count, width), lambda m: (m, 0, 0, 0, 0))
+def add_paired_kernel(row_split, me_ref, weight_ref, base_ref, *refs):
+    buffer_ref, sems = refs[-2:]
+    count, part_count, row_count, _ = buffer_ref.shape
+    terms, out_ref, shear_ref = refs[:count], refs[count], refs[count + 1]
+    me = me_ref[0]
+
+    def spot(ref, x):
+        other = me ^ x
+        top = pl.multiple_of(other % row_split * row_count, PAD)
+        return ref.at[other // row_split, 0, :, pl.ds(top, row_count)]
+
+    loads = [pltpu.make_async_copy(spot(base_ref, x), buffer_ref.at[x], sems.at[x]) for x in range(count)]
+    stores = [pltpu.make_async_copy(buffer_ref.at[x], spot(out_ref, x), sems.at[x]) for x in range(count)]
+    for load in loads:
+        load.start()
+    for x in range(count):
+        loads[x].wait()
+        buffer_ref[x] = buffer_ref[x] + terms[x][...]
+        stores[x].start()
+        for p in range(part_count):
+            lower, upper = buffer_ref[x, p, :PAD], buffer_ref[x, p, row_count - PAD :]
+            shear_ref[me ^ x, p] = jnp.sum(lower * weight_ref[x, 0][:, :1], axis=0)
+            shear_ref[me ^ x, part_count + p] = jnp.sum(upper * weight_ref[x, 1][:, :1], axis=0)
+    for store in stores:
+        store.wait()
+
+
+def add_paired(base, terms, weight, spots, row_split):
+    count = len(terms)
+    part_count, _, width = terms[0].shape
+    size = count * terms[0].size
+    anywhere, vector = pl.BlockSpec(memory_space=pl.ANY), pl.BlockSpec(memory_space=pltpu.VMEM)
     return pl.pallas_call(
-        wall_sum_kernel,
-        grid=(mode_count,),
+        functools.partial(add_paired_kernel, row_split),
         out_shape=(
             jax.ShapeDtypeStruct(base.shape, jnp.float32),
-            jax.ShapeDtypeStruct((mode_count, 4, width), jnp.float32),
+            jax.ShapeDtypeStruct((count, 2 * part_count, width), jnp.float32),
         ),
-        in_specs=[pl.BlockSpec(weight.shape, lambda m: (0, 0, 0)), block, block],
-        out_specs=(block, pl.BlockSpec((1, 4, width), lambda m: (m, 0, 0))),
-        input_output_aliases={1: 0},
+        in_specs=[pl.BlockSpec(memory_space=pltpu.SMEM), vector, anywhere] + [vector] * count,
+        out_specs=(anywhere, vector),
+        scratch_shapes=[pltpu.VMEM((count,) + terms[0].shape, jnp.float32), pltpu.SemaphoreType.DMA((count,))],
+        input_output_aliases={2: 0},
+        compiler_params=pltpu.CompilerParams(vmem_limit_bytes=16 << 20),
+        cost_estimate=pl.CostEstimate(flops=size, bytes_accessed=12 * size, transcendentals=0),
+        name="add_paired",
+    )(spots, weight, base, *terms)
+
+
+def add_whole_kernel(row_split, base_ref, term_ref, out_ref, buffer_ref, sems):
+    count, comps, _, row_count, _ = term_ref.shape
+
+    def spot(ref, source):
+        rows = pl.ds(source % row_split * row_count, row_count)
+        return ref.at[source // row_split, pl.ds(1, comps), :, rows]
+
+    loads = [pltpu.make_async_copy(spot(base_ref, x), buffer_ref.at[x], sems.at[x]) for x in range(count)]
+    stores = [pltpu.make_async_copy(buffer_ref.at[x], spot(out_ref, x), sems.at[x]) for x in range(count)]
+    for load in loads:
+        load.start()
+    for x in range(count):
+        loads[x].wait()
+        buffer_ref[x] = buffer_ref[x] + term_ref[x]
+        stores[x].start()
+    for store in stores:
+        store.wait()
+
+
+def add_whole(base, term, row_split):
+    anywhere, vector = pl.BlockSpec(memory_space=pl.ANY), pl.BlockSpec(memory_space=pltpu.VMEM)
+    return pl.pallas_call(
+        functools.partial(add_whole_kernel, row_split),
+        out_shape=jax.ShapeDtypeStruct(base.shape, jnp.float32),
+        in_specs=[anywhere, vector],
+        out_specs=anywhere,
+        scratch_shapes=[pltpu.VMEM(term.shape, jnp.float32), pltpu.SemaphoreType.DMA((term.shape[0],))],
+        input_output_aliases={0: 0},
+        compiler_params=pltpu.CompilerParams(vmem_limit_bytes=16 << 20),
         cost_estimate=pl.CostEstimate(flops=term.size, bytes_accessed=12 * term.size, transcendentals=0),
-        name="add_first",
-    )(weight, base, term)
-
-
-def add_rest(base, term, first):
-    mode_count, comp_count, part_count, row_count, width = term.shape
-    shape = (1, 1, part_count, row_count, width)
-    block = pl.BlockSpec(shape, lambda m, c: (m, c + first, 0, 0, 0))
-    return pl.pallas_call(
-        sum_kernel,
-        grid=(mode_count, comp_count),
-        out_shape=jax.ShapeDtypeStruct(base.shape, jnp.float32),
-        in_specs=[block, pl.BlockSpec(shape, lambda m, c: (m, c, 0, 0, 0))],
-        out_specs=block,
-        input_output_aliases={0: 0},
-        cost_estimate=pl.CostEstimate(flops=term.size, bytes_accessed=12 * term.size, transcendentals=0),
-        name="add_rest",
+        name="add_whole",
     )(base, term)
+
+
+def after(value, *others):
+    return lax.optimization_barrier((value,) + others)[0]
 
 
 def on_device(field, mean_flow, d2_coef, wall_coef, kx_index, patch_of):
     mode_count, comp_count, part_count, row_count, width = field.shape
     span = lax.axis_size("span")
+    me = lax.axis_index("span")
     wall_count = lax.axis_size("wall")
     wall_index = lax.axis_index("wall")
     mode_split = math.gcd(span, mode_count)
     row_split = span // mode_split
+    line_rows = row_count // row_split
     tables = jnp.asarray(spectral_tables(width * span))
-
-    def to_lines(chunk):
-        lines = chunk.reshape(mode_split, -1, row_split, row_count // row_split, width)
-        lines = lines.transpose(0, 2, 1, 3, 4).reshape(span, -1, row_count // row_split, width)
+    pairs = [[(i, i ^ x) for i in range(span)] for x in range(span)]
+    spots = jnp.stack([me, me // row_split, me % row_split * line_rows]).astype(jnp.int32)
+
+    def block_of(x):
+        other = me ^ x
+        start = (other // row_split, 0, 0, other % row_split * line_rows, 0)
+        return lax.dynamic_slice(field, start, (1, 1, part_count, line_rows, width))[0, 0]
+
+    def exchange(lines):
         return lax.all_to_all(lines, "span", split_axis=0, concat_axis=0)
-
-    def from_lines(lines, comps):
-        blocks = lax.all_to_all(lines, "span", split_axis=0, concat_axis=0)
-        blocks = blocks.reshape(mode_split, row_split, -1, row_count // row_split, width)
-        return blocks.transpose(0, 2, 1, 3, 4).reshape(mode_count, comps, part_count, row_count, width)
-
-    parts = [(0, 1), (1, comp_count)]
-    lines = [to_lines(field[:, first:last]) for first, last in parts]
 
     forward = [(i, i + 1) for i in range(wall_count - 1)]
     backward = [(i + 1, i) for i in range(wall_count - 1)]
+    first = [lax.ppermute(block_of(x), "span", pairs[x]) for x in range(span - 1, 0, -1)][::-1]
+    rest = field[:, 1:].reshape(mode_split, -1, row_split, line_rows, width)
+    rest = exchange(rest.transpose(0, 2, 1, 3, 4).reshape(span, -1, line_rows, width))
     low = lax.ppermute(field[:, :, :, row_count - PAD :], "wall", forward)
     high = lax.ppermute(field[:, :, :, :PAD], "wall", backward)
+
     rate = kx_index.astype(jnp.float32) * (0.25 * TAU)
     coef = jnp.broadcast_to(d2_coef[:, :, None], (STEN, row_count, LANES))
     flow = jnp.broadcast_to(mean_flow[:, :, None], (2, row_count, LANES))
     base = local_terms(field, low, high, rate, coef, flow)
 
-    terms = [
-        from_lines(spanwise_operator(value, tables), last - first) for value, (first, last) in zip(lines, parts)
-    ]
+    first = list(lax.optimization_barrier((tuple(first), base))[0])
+    sent = filter_paired(field, first, spots, tables)
+    terms = [sent[0]] + [lax.ppermute(sent[x], "span", pairs[x]) for x in range(span - 1, 0, -1)][::-1]
+    filtered = filter_whole(after(rest, sent[0]), tables)
+    back = exchange(filtered).reshape(span, comp_count - 1, part_count, line_rows, width)
+
     lower = jnp.where(wall_index == 0, wall_coef[0], 0.0)
     upper = jnp.where(wall_index == wall_count - 1, wall_coef[1, ::-1], 0.0)
-    weight = jnp.broadcast_to(jnp.stack([lower, upper])[:, :, None], (2, PAD, LANES))
-    base, shear = add_first(base, terms[0], weight)
+    group = (me ^ jnp.arange(span)) % row_split
+    weight = jnp.stack(
+        [jnp.where((group == 0)[:, None], lower, 0.0), jnp.where((group == row_split - 1)[:, None], upper, 0.0)], axis=1
+    )
+    weight = jnp.broadcast_to(weight[..., None], (span, 2, PAD, LANES))
     onehot = (patch_of[:, None] == jnp.arange(PATCH, dtype=jnp.int32)[None, :]).astype(jnp.float32)
-    grad = jnp.einsum("mwz,zq->mwq", shear, onehot, precision=lax.Precision.HIGHEST)
-    grad = grad.reshape(mode_count, 2, part_count, PATCH).transpose(1, 0, 2, 3)
-    wall_grad = lax.psum(grad, ("wall", "span"))
-    new_field = add_rest(base, terms[1], 1)
-    return (new_field, wall_grad)
+    terms[0] = after(terms[0], filtered)
+    result, shear = add_paired(base, terms, weight, spots, row_split)
+    grad = jnp.einsum("swz,zq->swq", shear, onehot, precision=lax.Precision.HIGHEST)
+    grad = grad.reshape(mode_count, row_split, 2, part_count, PATCH).sum(axis=1)
+    for axis, count in (("wall", wall_count), ("span", span)):
+        distance = 1
+        while distance < count:
+            grad = grad + lax.ppermute(grad, axis, [(i, i ^ distance) for i in range(count)])
+            distance *= 2
+    return (add_whole(result, back, row_split), grad.transpose(1, 0, 2, 3))
 
 
 def solution(mesh):

time: 271 us -> 272 us (level)
  waiting for transfers between devices: 125 us -> 184 us
  blocking collectives: 44.7 us -> 0 us
  starting transfers between devices: 32.2 us -> 26.3 us
  local copies, waits for them, and re-layouts: 23.2 us -> 18.9 us
    ppermute x0 -> x11, waiting for transfers between devices: none -> 168 us  [the longest x3 98.8 us: on_device(): lax.ppermute(sent[x], 'span', pairs[x])]
    all_to_all x4 -> x2, waiting for transfers between devices: 107 us -> 0.01 us  [exchange(): return lax.all_to_all(lines, 'span', split_axis=0, concat_axis=0)]
    psum x1 -> x0, blocking collectives: 44.7 us -> none  [on_device(): wall_grad = lax.psum(grad, ('wall', 'span'))]
    all_to_all x4 -> x2, starting transfers between devices: 27.9 us -> 12.5 us  [exchange(): return lax.all_to_all(lines, 'span', split_axis=0, concat_axis=0)]
    ppermute x0 -> x11, starting transfers between devices: none -> 9.49 us  [the longest x3 3.89 us: on_device(): lax.ppermute(block_of(x), 'span', pairs[x])]
    unnamed x18 -> x28, local copies, waits for them, and re-layouts: 11.7 us -> 9.97 us
  transfers between devices with their start and end apart: 6 -> 15, of which waited for: 4 -> 11; matrix products, arithmetic and copies ran while one was open for 4% -> 2% of each run, Pallas kernels for 13% -> 10%
where the time goes in v3:
time: 272 us; the launch traced here: 270 us
  waiting for transfers between devices  184 us (68%)
  Pallas kernels  39.2 us (14%)
  starting transfers between devices  26.3 us (10%)
  local copies, waits for them, and re-layouts  18.9 us (7%)
    ppermute x3, waiting for transfers between devices, on_device(): lax.ppermute(sent[x], 'span', pairs[x])  98.8 us
    ppermute x3, waiting for transfers between devices, on_device(): lax.ppermute(block_of(x), 'span', pairs[x])  54.7 us
    ppermute x1, waiting for transfers between devices, on_device(): high = lax.ppermute(field[:, :, :, :PAD], 'wall', backward)  15.7 us
    pallas_call x1, Pallas kernels, local_terms(): pl.pallas_call(local_kernel, grid=(mode_count,), out_shape=jax.ShapeDtype...  15 us
    ppermute x5, waiting for transfers between devices, on_device(): lax.ppermute(grad, axis, [(i, i ^ distance) for i in range(count)])  14.6 us
    all_to_all x2, starting transfers between devices, exchange(): return lax.all_to_all(lines, 'span', split_axis=0, concat_axis=0)  12.5 us
    unnamed x28, local copies, waits for them, and re-layouts  9.97 us
    pallas_call x1, Pallas kernels, filter_whole(): pl.pallas_call(whole_kernel, out_shape=jax.ShapeDtypeStruct(lines.shape,...  9.7 us
  transfers between devices with their start and end apart: 15, of which 11 were waited for; matrix products, arithmetic and copies ran while one was open for 2% of the time, Pallas kernels for 10%

profile of v3, /device:TPU:10, one launch (start us, length us, event | category | flops | bytes accessed | tf_op | source)
XLA Modules:
  0.0 270.2 jit_solution(16469826675950083408)
XLA Ops:
  0.6 3.9 %slice.19 = f32[4,2,2,32,1536]{4,3,2,1,0:T(8,128)} slice(f32[4,3,2,32,1536]{4,3,2,1,0:T(8,128)} %field_ref.3), slice={[0:4], [1:3], [0:2], [0:32], [0:1536]} | slice | bytes 6291456 | tf_op jit(solution)/shard_map/slice | solution.py:435
  4.5 5.3 %all-to-all-start = ((f32[4,4,32,1536]{3,2,1,0:T(8,128)}), f32[4,4,32,1536]{3,2,1,0:T(8,128)}, u32[]{:S(2)}, u32[]{:S(2)}) async-start(f32[4,4,32,1536]{3,2,1,0:T(8,128)} %bitcast.6), calls=%async_computation | async-start | bytes 6291456 | tf_op jit(solution)/shard_map/all_to_all | solution.py:430
  9.8 3.3 %fusion.6 = (f32[4,3,2,8,1536]{4,3,2,1,0:T(8,128)}, f32[4,3,2,8,1536]{4,3,2,1,0:T(8,128)}) fusion(f32[4,3,2,32,1536]{4,3,2,1,0:T(8,128)} %field_ref.3), kind=kLoop, calls=%fused_computation.16 | loop fusion | bytes 4718592 | tf_op jit(solution)/shard_map/slice | solution.py:438
  13.2 1.9 collective-permute-start.1
  15.1 2.4 collective-permute-start
  17.5 1.3 dynamic-slice_bitcast_fusion
  18.8 1.5 collective-permute-start.4
  20.4 1.0 collective-permute-start.3
  21.3 1.4 collective-permute-start.2
  22.7 0.1 pad_add_fusion.me_ref
  22.8 0.0 copy-done.11
  22.8 15.7 %collective-permute-done.1.high_ref = f32[4,3,2,8,1536]{4,3,2,1,0:T(8,128)S(1)} collective-permute-done((f32[4,3,2,8,1536]{4,3,2,1,0:T(8,128)}, f32[4,3,2,8,1536]{4,3,2,1,0:T(8,128)S(1)}, u32[]{:S(2)}, u32[]{:S(2)}) %collective-permute-start.1) | collective-permute-done | bytes 1179680 | tf_op jit(solution)/shard_map/ppermute | solution.py:438
  38.5 0.0 collective-permute-done.low_ref
  38.5 0.0 copy-done.8
  38.5 0.1 broadcast_in_dim.51.flow_ref
  38.6 0.0 copy-done.7
  38.6 0.1 broadcast_in_dim.50.coef_ref
  38.7 0.0 copy-start
  38.7 2.3 copy-done
  41.1 15.0 %local_terms.1.base_ref = f32[4,3,2,32,1536]{4,3,2,1,0:T(8,128)} custom-call(f32[4]{0:T(128)S(1)} %convert_multiply_fusion.rate_ref, f32[15,32,128]{2,1,0:T(8,128)S(1)} %broadcast_in_dim.50.coef_ref, f32[2,32,128]{2,1,0:T(8,128)S(1)} %broadcast_in_dim.51.flow_ref, f32[4,3,2,32,1536]{4,3,2,1,0:T(8,128)S(1)} %copy-done, ...), custom_call_target="tpu_custom_call" | custom-call | flops 47185920 | bytes 11796480 | tf_op jit(solution)/shard_map/local_terms/pallas_call | solution.py:305
  56.1 49.3 %collective-permute-done.4.refs_2_ = f32[2,32,1536]{2,1,0:T(8,128)S(1)} collective-permute-done((f32[2,32,1536]{2,1,0:T(8,128)S(1)}, f32[2,32,1536]{2,1,0:T(8,128)S(1)}, u32[]{:S(2)}, u32[]{:S(2)}) %collective-permute-start.4) | collective-permute-done | bytes 393248 | tf_op jit(solution)/shard_map/ppermute | solution.py:434
  105.4 5.4 %collective-permute-done.3.refs_1_ = f32[2,32,1536]{2,1,0:T(8,128)S(1)} collective-permute-done((f32[2,32,1536]{2,1,0:T(8,128)S(1)}, f32[2,32,1536]{2,1,0:T(8,128)S(1)}, u32[]{:S(2)}, u32[]{:S(2)}) %collective-permute-start.3) | collective-permute-done | bytes 393248 | tf_op jit(solution)/shard_map/ppermute | solution.py:434
  110.8 0.0 collective-permute-done.2.refs_0_
  110.8 0.0 slice-done
  110.8 0.0 slice-done.1
  110.8 2.8 %copy-done.1 = bf16[24,2,256,256]{3,2,1,0:T(8,128)(2,1)S(1)} copy-done((bf16[24,2,256,256]{3,2,1,0:T(8,128)(2,1)S(1)}, bf16[24,2,256,256]{3,2,1,0:T(8,128)(2,1)}, u32[]{:S(2)}) %copy-start.1) | copy-done | bytes 6291480
  113.6 8.1 %filter_paired.1 = (f32[2,32,1536]{2,1,0:T(8,128)S(1)}, f32[2,32,1536]{2,1,0:T(8,128)S(1)}, f32[2,32,1536]{2,1,0:T(8,128)S(1)}, f32[2,32,1536]{2,1,0:T(8,128)S(1)}) custom-call(s32[3]{0:T(128)S(1)} %pad_add_fusion.me_ref, bf16[24,2,256,256]{3,2,1,0:T(8,128)(2,1)S(1)} %copy-done.1, f32[4,3,2,32,1536]{4,3,2,1,0:T(8,128)S(1)} %bitcast.21, ...), custom_call_target="tpu_custom_call" | custom-call | flops 603979776 | bytes 3145728 | tf_op jit(solution)/shard_map/filter_paired/pallas_call | solution.py:231
  121.7 0.0 copy-start.4
  121.7 0.0 copy-start.5
  121.8 0.0 all-to-all-done.line_ref
  121.8 0.0 copy-start.2
  121.8 3.2 %copy-done.2 = bf16[24,2,256,256]{3,2,1,0:T(8,128)(2,1)S(1)} copy-done((bf16[24,2,256,256]{3,2,1,0:T(8,128)(2,1)S(1)}, bf16[24,2,256,256]{3,2,1,0:T(8,128)(2,1)}, u32[]{:S(2)}) %copy-start.2) | copy-done | bytes 6291480
  125.0 9.7 %filter_whole.1 = f32[4,4,32,1536]{3,2,1,0:T(8,128)S(1)} custom-call(bf16[24,2,256,256]{3,2,1,0:T(8,128)(2,1)S(1)} %copy-done.2, f32[4,4,32,1536]{3,2,1,0:T(8,128)} %all-to-all-done.line_ref), custom_call_target="tpu_custom_call" | custom-call | flops 1207959552 | bytes 6291456 | tf_op jit(solution)/shard_map/filter_whole/pallas_call | solution.py:256
  134.7 0.0 copy-done.4
  134.7 0.0 copy-done.5
  134.7 0.0 copy-done.6
  134.7 0.0 copy-start.3
  134.7 1.6 copy-done.3
  136.3 7.2 %all-to-all-start.1 = ((f32[4,4,32,1536]{3,2,1,0:T(8,128)}), f32[4,4,32,1536]{3,2,1,0:T(8,128)S(1)}, u32[]{:S(2)}, u32[]{:S(2)}) async-start(f32[4,4,32,1536]{3,2,1,0:T(8,128)} %copy-done.3), calls=%async_computation.1 | async-start | bytes 6291456 | tf_op jit(solution)/shard_map/all_to_all | solution.py:430
  143.5 0.1 collective-permute-start.5
  143.6 2.8 %collective-permute-start.6 = (f32[2,32,1536]{2,1,0:T(8,128)}, f32[2,32,1536]{2,1,0:T(8,128)}, u32[]{:S(2)}, u32[]{:S(2)}) collective-permute-start(f32[2,32,1536]{2,1,0:T(8,128)} %copy-done.5), channel_id=1, source_target_pairs={{0,2},{1,3},{2,0},{3,1},{4,6},{5,7},{6,4},{7,5},{8,10},{9,11},{10,... | collective-permute-start | bytes 1179656 | tf_op jit(solution)/shard_map/ppermute | solution.py:447
  146.5 0.6 collective-permute-start.7
  147.0 0.0 copy-done.9
  147.0 0.1 rev.3
  147.2 57.3 %collective-permute-done.5.refs_1_ = f32[2,32,1536]{2,1,0:T(8,128)} collective-permute-done((f32[2,32,1536]{2,1,0:T(8,128)}, f32[2,32,1536]{2,1,0:T(8,128)}, u32[]{:S(2)}, u32[]{:S(2)}) %collective-permute-start.5) | collective-permute-done | bytes 393248 | tf_op jit(solution)/shard_map/ppermute | solution.py:447
  204.5 33.2 %collective-permute-done.6.refs_2_ = f32[2,32,1536]{2,1,0:T(8,128)} collective-permute-done((f32[2,32,1536]{2,1,0:T(8,128)}, f32[2,32,1536]{2,1,0:T(8,128)}, u32[]{:S(2)}, u32[]{:S(2)}) %collective-permute-start.6) | collective-permute-done | bytes 393248 | tf_op jit(solution)/shard_map/ppermute | solution.py:447
  237.7 8.3 %collective-permute-done.7.refs_3_ = f32[2,32,1536]{2,1,0:T(8,128)} collective-permute-done((f32[2,32,1536]{2,1,0:T(8,128)}, f32[2,32,1536]{2,1,0:T(8,128)}, u32[]{:S(2)}, u32[]{:S(2)}) %collective-permute-start.7) | collective-permute-done | bytes 393248 | tf_op jit(solution)/shard_map/ppermute | solution.py:447
  246.0 0.1 broadcast_in_dim.49.weight_ref
  246.1 3.5 %add_paired.1 = (f32[4,3,2,32,1536]{4,3,2,1,0:T(8,128)}, f32[4,4,1536]{2,1,0:T(4,128)S(1)}) custom-call(s32[3]{0:T(128)S(1)} %pad_add_fusion.me_ref, f32[4,2,8,128]{3,2,1,0:T(8,128)S(1)} %broadcast_in_dim.49.weight_ref, f32[4,3,2,32,1536]{4,3,2,1,0:T(8,128)} %local_terms.1.base_ref, ...), custom_call_target="tpu_custom_call", output_to_operand_aliasing={{0}: (2, {})} | custom-call | flops 393216 | bytes 4718592 | tf_op jit(solution)/shard_map/add_paired/pallas_call | solution.py:357
  249.5 0.0 copy-done.10
  249.6 0.3 fusion.1
  249.9 0.1 collective-permute-start.8
  250.0 1.2 collective-permute-done.8
  251.1 0.5 collective-permute-start.9
  251.6 3.1 %collective-permute-done.9 = f32[4,2,2,64]{3,2,0,1:T(2,128)S(1)} collective-permute-done((f32[4,2,2,64]{3,2,0,1:T(2,128)S(1)}, f32[4,2,2,64]{3,2,0,1:T(2,128)S(1)}, u32[]{:S(2)}, u32[]{:S(2)}) %collective-permute-start.9) | collective-permute-done | bytes 4128 | tf_op jit(solution)/shard_map/ppermute | solution.py:466
  254.8 1.5 collective-permute-start.10
  256.3 2.1 collective-permute-done.10
  258.4 0.0 collective-permute-start.11
  258.5 3.6 %collective-permute-done.11 = f32[4,2,2,64]{3,2,0,1:T(2,128)S(1)} collective-permute-done((f32[4,2,2,64]{3,2,0,1:T(2,128)S(1)}, f32[4,2,2,64]{3,2,0,1:T(2,128)S(1)}, u32[]{:S(2)}, u32[]{:S(2)}) %collective-permute-start.11) | collective-permute-done | bytes 4128 | tf_op jit(solution)/shard_map/ppermute | solution.py:466
  262.1 0.0 collective-permute-start.12
  262.1 4.5 %collective-permute-done.12 = f32[4,2,2,64]{3,2,0,1:T(2,128)S(1)} collective-permute-done((f32[4,2,2,64]{3,2,0,1:T(2,128)S(1)}, f32[4,2,2,64]{3,2,0,1:T(2,128)S(1)}, u32[]{:S(2)}, u32[]{:S(2)}) %collective-permute-start.12) | collective-permute-done | bytes 4128 | tf_op jit(solution)/shard_map/ppermute | solution.py:466
  266.7 0.6 add_bitcast_fusion
  267.3 0.0 all-to-all-done.1
  267.3 2.9 %add_whole.1 = f32[4,3,2,32,1536]{4,3,2,1,0:T(8,128)} custom-call(f32[4,3,2,32,1536]{4,3,2,1,0:T(8,128)} %get-tuple-element.22.base_ref, f32[4,2,2,32,1536]{4,3,2,1,0:T(8,128)S(1)} %bitcast.22), custom_call_target="tpu_custom_call", output_to_operand_aliasing={{}: (0, {})} | custom-call | flops 786432 | bytes 9437184 | tf_op jit(solution)/shard_map/add_whole/pallas_call | solution.py:394
  (21 shorter events, 0.1 us)
Async XLA Ops:
  4.5 117.3 %all-to-all-start = ((f32[4,4,32,1536]{3,2,1,0:T(8,128)}), f32[4,4,32,1536]{3,2,1,0:T(8,128)}, u32[]{:S(2)}, u32[]{:S(2)}) async-start(f32[4,4,32,1536]{3,2,1,0:T(8,128)} %bitcast.6), calls=%async_computation | async-start | bytes 6291456 | tf_op jit(solution)/shard_map/all_to_all | solution.py:430
  9.8 13.0 %copy-start.11 = (s32[4]{0:T(128)S(1)}, s32[4]{0:T(128)}, u32[]{:S(2)}) copy-start(s32[4]{0:T(128)} %param.11) | copy-start | bytes 52
  9.8 28.7 %copy-start.8 = (f32[2,32]{1,0:T(2,128)S(1)}, f32[2,32]{1,0:T(2,128)}, u32[]{:S(2)}) copy-start(f32[2,32]{1,0:T(2,128)} %param.8) | copy-start | bytes 772
  9.8 28.8 %copy-start.7 = (f32[15,32]{1,0:T(8,128)S(1)}, f32[15,32]{1,0:T(8,128)}, u32[]{:S(2)}) copy-start(f32[15,32]{1,0:T(8,128)} %param.9) | copy-start | bytes 5764
  9.8 101.0 %slice-start = ((s8[4718592]{0:T(1024)(128)(4,1)}), s8[524288]{0:T(1024)(128)(4,1)S(1)}, s32[]{:S(2)}) async-start(s8[4718592]{0:T(1024)(128)(4,1)} %bitcast.20), calls=%async_computation.2 | async-start | bytes 1048576
  13.2 25.4 %collective-permute-start.1 = (f32[4,3,2,8,1536]{4,3,2,1,0:T(8,128)}, f32[4,3,2,8,1536]{4,3,2,1,0:T(8,128)S(1)}, u32[]{:S(2)}, u32[]{:S(2)}) collective-permute-start(f32[4,3,2,8,1536]{4,3,2,1,0:T(8,128)} %get-tuple-element.27), channel_id=1, source_target_pairs={{4,0},{8,4},{12,8},{16,12},{20,16},{24,20},{28,24},{5,1},{9,5},{13... | collective-permute-start | bytes 3538952 | tf_op jit(solution)/shard_map/ppermute | solution.py:438
  15.1 23.4 %collective-permute-start = (f32[4,3,2,8,1536]{4,3,2,1,0:T(8,128)}, f32[4,3,2,8,1536]{4,3,2,1,0:T(8,128)S(1)}, u32[]{:S(2)}, u32[]{:S(2)}) collective-permute-start(f32[4,3,2,8,1536]{4,3,2,1,0:T(8,128)} %get-tuple-element.28), channel_id=1, source_target_pairs={{0,4},{4,8},{8,12},{12,16},{16,20},{20,24},{24,28},{1,5},{5,9},{9,... | collective-permute-start | bytes 3538952 | tf_op jit(solution)/shard_map/ppermute | solution.py:437
  18.8 86.6 %collective-permute-start.4 = (f32[2,32,1536]{2,1,0:T(8,128)S(1)}, f32[2,32,1536]{2,1,0:T(8,128)S(1)}, u32[]{:S(2)}, u32[]{:S(2)}) collective-permute-start(f32[2,32,1536]{2,1,0:T(8,128)S(1)} %get-tuple-element.24), channel_id=1, source_target_pairs={{0,3},{1,2},{2,1},{3,0},{4,7},{5,6},{6,5},{7,4},{8,11},{9,10},{10,... | collective-permute-start | bytes 1179656 | tf_op jit(solution)/shard_map/ppermute | solution.py:434
  20.4 90.5 %collective-permute-start.3 = (f32[2,32,1536]{2,1,0:T(8,128)S(1)}, f32[2,32,1536]{2,1,0:T(8,128)S(1)}, u32[]{:S(2)}, u32[]{:S(2)}) collective-permute-start(f32[2,32,1536]{2,1,0:T(8,128)S(1)} %get-tuple-element.25), channel_id=1, source_target_pairs={{0,2},{1,3},{2,0},{3,1},{4,6},{5,7},{6,4},{7,5},{8,10},{9,11},{10,... | collective-permute-start | bytes 1179656 | tf_op jit(solution)/shard_map/ppermute | solution.py:434
  21.3 89.5 %collective-permute-start.2 = (f32[2,32,1536]{2,1,0:T(8,128)S(1)}, f32[2,32,1536]{2,1,0:T(8,128)S(1)}, u32[]{:S(2)}, u32[]{:S(2)}) collective-permute-start(f32[2,32,1536]{2,1,0:T(8,128)S(1)} %get-tuple-element.26), channel_id=1, source_target_pairs={{0,1},{1,0},{2,3},{3,2},{4,5},{5,4},{6,7},{7,6},{8,9},{9,8},{10,11... | collective-permute-start | bytes 1179656 | tf_op jit(solution)/shard_map/ppermute | solution.py:434
  38.7 2.3 copy-start
  41.1 69.8 %slice-start.1 = ((s8[4718592]{0:T(1024)(128)(4,1)}), s8[4194304]{0:T(1024)(128)(4,1)S(1)}, s32[]{:S(2)}) async-start(s8[4718592]{0:T(1024)(128)(4,1)} %bitcast.20), calls=%async_computation.3 | async-start | bytes 8388608
  110.8 2.8 %copy-start.1 = (bf16[24,2,256,256]{3,2,1,0:T(8,128)(2,1)S(1)}, bf16[24,2,256,256]{3,2,1,0:T(8,128)(2,1)}, u32[]{:S(2)}) copy-start(bf16[24,2,256,256]{3,2,1,0:T(8,128)(2,1)} %constant.98.clone.table_ref) | copy-start | bytes 18874372
  121.7 12.9 %copy-start.4 = (f32[2,32,1536]{2,1,0:T(8,128)}, f32[2,32,1536]{2,1,0:T(8,128)S(1)}, u32[]{:S(2)}) copy-start(f32[2,32,1536]{2,1,0:T(8,128)S(1)} %get-tuple-element.21) | copy-start | bytes 1179652
  121.7 12.9 %copy-start.5 = (f32[2,32,1536]{2,1,0:T(8,128)}, f32[2,32,1536]{2,1,0:T(8,128)S(1)}, u32[]{:S(2)}) copy-start(f32[2,32,1536]{2,1,0:T(8,128)S(1)} %get-tuple-element.20) | copy-start | bytes 1179652
  121.8 12.9 %copy-start.6 = (f32[2,32,1536]{2,1,0:T(8,128)}, f32[2,32,1536]{2,1,0:T(8,128)S(1)}, u32[]{:S(2)}) copy-start(f32[2,32,1536]{2,1,0:T(8,128)S(1)} %get-tuple-element.19) | copy-start | bytes 1179652
  121.8 3.2 %copy-start.2 = (bf16[24,2,256,256]{3,2,1,0:T(8,128)(2,1)S(1)}, bf16[24,2,256,256]{3,2,1,0:T(8,128)(2,1)}, u32[]{:S(2)}) copy-start(bf16[24,2,256,256]{3,2,1,0:T(8,128)(2,1)} %constant.98.clone.table_ref) | copy-start | bytes 18874372
  134.7 1.6 copy-start.3
  136.3 10.7 %copy-start.9 = (f32[2,8]{1,0:T(2,128)S(1)}, f32[2,8]{1,0:T(2,128)}, u32[]{:S(2)}) copy-start(f32[2,8]{1,0:T(2,128)} %param.10) | copy-start | bytes 196
  136.3 130.9 %all-to-all-start.1 = ((f32[4,4,32,1536]{3,2,1,0:T(8,128)}), f32[4,4,32,1536]{3,2,1,0:T(8,128)S(1)}, u32[]{:S(2)}, u32[]{:S(2)}) async-start(f32[4,4,32,1536]{3,2,1,0:T(8,128)} %copy-done.3), calls=%async_computation.1 | async-start | bytes 6291456 | tf_op jit(solution)/shard_map/all_to_all | solution.py:430
  143.5 61.0 %collective-permute-start.5 = (f32[2,32,1536]{2,1,0:T(8,128)}, f32[2,32,1536]{2,1,0:T(8,128)}, u32[]{:S(2)}, u32[]{:S(2)}) collective-permute-start(f32[2,32,1536]{2,1,0:T(8,128)} %copy-done.6), channel_id=1, source_target_pairs={{0,1},{1,0},{2,3},{3,2},{4,5},{5,4},{6,7},{7,6},{8,9},{9,8},{10,11... | collective-permute-start | bytes 1179656 | tf_op jit(solution)/shard_map/ppermute | solution.py:447
  143.6 94.0 %collective-permute-start.6 = (f32[2,32,1536]{2,1,0:T(8,128)}, f32[2,32,1536]{2,1,0:T(8,128)}, u32[]{:S(2)}, u32[]{:S(2)}) collective-permute-start(f32[2,32,1536]{2,1,0:T(8,128)} %copy-done.5), channel_id=1, source_target_pairs={{0,2},{1,3},{2,0},{3,1},{4,6},{5,7},{6,4},{7,5},{8,10},{9,11},{10,... | collective-permute-start | bytes 1179656 | tf_op jit(solution)/shard_map/ppermute | solution.py:447
  146.5 99.5 %collective-permute-start.7 = (f32[2,32,1536]{2,1,0:T(8,128)}, f32[2,32,1536]{2,1,0:T(8,128)}, u32[]{:S(2)}, u32[]{:S(2)}) collective-permute-start(f32[2,32,1536]{2,1,0:T(8,128)} %copy-done.4), channel_id=1, source_target_pairs={{0,3},{1,2},{2,1},{3,0},{4,7},{5,6},{6,5},{7,4},{8,11},{9,10},{10,... | collective-permute-start | bytes 1179656 | tf_op jit(solution)/shard_map/ppermute | solution.py:447
  246.1 3.5 %copy-start.10 = (s32[1536]{0:T(1024)S(1)}, s32[1536]{0:T(1024)}, u32[]{:S(2)}) copy-start(s32[1536]{0:T(1024)} %param.12) | copy-start | bytes 18436
  249.9 1.2 collective-permute-start.8
  251.1 3.7 %collective-permute-start.9 = (f32[4,2,2,64]{3,2,0,1:T(2,128)S(1)}, f32[4,2,2,64]{3,2,0,1:T(2,128)S(1)}, u32[]{:S(2)}, u32[]{:S(2)}) collective-permute-start(f32[4,2,2,64]{3,2,0,1:T(2,128)S(1)} %copy_add_fusion), channel_id=1, source_target_pairs={{0,8},{4,12},{8,0},{12,4},{16,24},{20,28},{24,16},{28,20},{1,9},{5... | collective-permute-start | bytes 12296 | tf_op jit(solution)/shard_map/ppermute | solution.py:466
  254.8 3.7 %collective-permute-start.10 = (f32[4,2,2,64]{3,2,0,1:T(2,128)S(1)}, f32[4,2,2,64]{3,2,0,1:T(2,128)S(1)}, u32[]{:S(2)}, u32[]{:S(2)}) collective-permute-start(f32[4,2,2,64]{3,2,0,1:T(2,128)S(1)} %add.46), channel_id=1, source_target_pairs={{0,16},{4,20},{8,24},{12,28},{16,0},{20,4},{24,8},{28,12},{1,17},{... | collective-permute-start | bytes 12296 | tf_op jit(solution)/shard_map/ppermute | solution.py:466
  258.4 3.7 %collective-permute-start.11 = (f32[4,2,2,64]{3,2,0,1:T(2,128)S(1)}, f32[4,2,2,64]{3,2,0,1:T(2,128)S(1)}, u32[]{:S(2)}, u32[]{:S(2)}) collective-permute-start(f32[4,2,2,64]{3,2,0,1:T(2,128)S(1)} %add.47), channel_id=1, source_target_pairs={{0,1},{1,0},{2,3},{3,2},{4,5},{5,4},{6,7},{7,6},{8,9},{9,8},{10,11... | collective-permute-start | bytes 12296 | tf_op jit(solution)/shard_map/ppermute | solution.py:466
  262.1 4.5 %collective-permute-start.12 = (f32[4,2,2,64]{3,2,0,1:T(2,128)S(1)}, f32[4,2,2,64]{3,2,0,1:T(2,128)S(1)}, u32[]{:S(2)}, u32[]{:S(2)}) collective-permute-start(f32[4,2,2,64]{3,2,0,1:T(2,128)S(1)} %add.48), channel_id=1, source_target_pairs={{0,2},{1,3},{2,0},{3,1},{4,6},{5,7},{6,4},{7,5},{8,10},{9,11},{10,... | collective-permute-start | bytes 12296 | tf_op jit(solution)/shard_map/ppermute | solution.py:466

commit v4 on v3

--- a/solution.py
+++ b/solution.py
@@ -156,7 +156,7 @@
     return x
 
 
-def filter_lines(line_ref, wave_ref, table_ref):
+def filter_lines(line_ref, wave_ref, table_ref, table_copy):
     _, line_count, row_count, width = line_ref.shape
     pieces = width // LANES
     groups = row_count // PAD
@@ -178,15 +178,14 @@
         value = wave_ref[tile]
         high = value.astype(jnp.bfloat16)
         low = (value - high.astype(jnp.float32)).astype(jnp.bfloat16)
-        table_high, table_low = table_ref[tile, 0], table_ref[tile, 1]
-        wave_ref[tile] = (
-            jnp.dot(high, table_low, preferred_element_type=jnp.float32)
-            + jnp.dot(low, table_high, preferred_element_type=jnp.float32)
-            + jnp.dot(high, table_high, preferred_element_type=jnp.float32)
-        )
+        rows = high.shape[0]
+        both = jnp.dot(jnp.concatenate([high, low]), table_ref[tile, 0], preferred_element_type=jnp.float32)
+        rest = jnp.dot(high, table_ref[tile, 1], preferred_element_type=jnp.float32)
+        wave_ref[tile] = both[:rows] + both[rows:] + rest
         return 0
 
-    lax.fori_loop(0, TILES, middle, 0)
+    table_copy.wait()
+    lax.fori_loop(0, TILES, middle, 0, unroll=4)
 
     def backward(step, _):
         line, rows, spot = spots(step)
@@ -198,19 +197,19 @@
     lax.fori_loop(0, line_count * groups, backward, 0)
 
 
-def paired_kernel(me_ref, table_ref, field_ref, *refs):
-    line_ref, wave_ref, sems = refs[-3:]
-    count, _, row_count, _ = line_ref.shape
-    received, sent = refs[: count - 1], refs[count - 1 : 2 * count - 1]
-    me, mode, top = me_ref[0], me_ref[1], me_ref[2]
-    own = field_ref.at[mode, 0, :, pl.ds(pl.multiple_of(top, PAD), row_count)]
-    sources = (own,) + received
-    copies = [pltpu.make_async_copy(sources[x], line_ref.at[me ^ x], sems.at[x]) for x in range(count)]
+def filter_kernel(me_ref, table_hbm, lines_hbm, *refs):
+    line_ref, wave_ref, table_ref, table_sem, sems = refs[-5:]
+    sent = refs[:-5]
+    count = len(sent)
+    me = me_ref[0]
+    copies = [pltpu.make_async_copy(lines_hbm.at[x], line_ref.at[x], sems.at[x]) for x in range(count)]
     for copy in copies:
         copy.start()
+    table_copy = pltpu.make_async_copy(table_hbm, table_ref, table_sem)
+    table_copy.start()
     for copy in copies:
         copy.wait()
-    filter_lines(line_ref, wave_ref, table_ref)
+    filter_lines(line_ref, wave_ref, table_ref, table_copy)
     copies = [pltpu.make_async_copy(line_ref.at[me ^ x], sent[x], sems.at[x]) for x in range(count)]
     for copy in copies:
         copy.start()
@@ -218,51 +217,29 @@
         copy.wait()
 
 
-def filter_cost(count, rows, width):
+HBM = pl.BlockSpec(memory_space=pltpu.HBM)
+
+
+def filter_component(lines, spots, tables):
+    count, part_count, row_count, width = lines.shape
+    rows = part_count * row_count
     flops = 3 * 2 * TILES * rows * (2 * LANES) ** 2
-    return pl.CostEstimate(flops=flops, bytes_accessed=8 * count * rows * width, transcendentals=0)
-
-
-def filter_paired(field, received, spots, tables):
-    count = len(received) + 1
-    part_count, row_count, width = received[0].shape
-    rows = part_count * row_count
-    anywhere = pl.BlockSpec(memory_space=pl.ANY)
     return pl.pallas_call(
-        paired_kernel,
-        out_shape=[jax.ShapeDtypeStruct(received[0].shape, jnp.float32)] * count,
-        in_specs=[pl.BlockSpec(memory_space=pltpu.SMEM), pl.BlockSpec(memory_space=pltpu.VMEM)] + [anywhere] * count,
-        out_specs=[anywhere] * count,
+        filter_kernel,
+        out_shape=[jax.ShapeDtypeStruct(lines.shape[1:], jnp.float32)] * count,
+        in_specs=[pl.BlockSpec(memory_space=pltpu.SMEM), HBM, HBM],
+        out_specs=[HBM] * count,
         scratch_shapes=[
-            pltpu.VMEM((count, part_count, row_count, width), jnp.float32),
+            pltpu.VMEM(lines.shape, jnp.float32),
             pltpu.VMEM((TILES, rows, 2 * LANES), jnp.float32),
+            pltpu.VMEM(tables.shape, tables.dtype),
+            pltpu.SemaphoreType.DMA,
             pltpu.SemaphoreType.DMA((count,)),
         ],
         compiler_params=pltpu.CompilerParams(vmem_limit_bytes=24 << 20),
-        cost_estimate=filter_cost(count, rows, width),
-        name="filter_paired",
-    )(spots, tables, field, *received)
-
-
-def whole_kernel(table_ref, line_ref, out_ref, wave_ref):
-    out_ref[...] = line_ref[...]
-    filter_lines(out_ref, wave_ref, table_ref)
-
-
-def filter_whole(lines, tables):
-    count, line_count, row_count, width = lines.shape
-    rows = line_count * row_count
-    vector = pl.BlockSpec(memory_space=pltpu.VMEM)
-    return pl.pallas_call(
-        whole_kernel,
-        out_shape=jax.ShapeDtypeStruct(lines.shape, jnp.float32),
-        in_specs=[vector] * 2,
-        out_specs=vector,
-        scratch_shapes=[pltpu.VMEM((TILES, rows, 2 * LANES), jnp.float32)],
-        compiler_params=pltpu.CompilerParams(vmem_limit_bytes=24 << 20),
-        cost_estimate=filter_cost(count, rows, width),
-        name="filter_whole",
-    )(tables, lines)
+        cost_estimate=pl.CostEstimate(flops=flops, bytes_accessed=8 * lines.size, transcendentals=0),
+        name="filter_component",
+    )(spots, tables, lines)
 
 
 def local_kernel(rate_ref, coef_ref, flow_ref, field_ref, low_ref, high_ref, out_ref, pad_ref):
@@ -322,86 +299,59 @@
     )(rate, coef, flow, field, low, high)
 
 
-def add_paired_kernel(row_split, me_ref, weight_ref, base_ref, *refs):
-    buffer_ref, sems = refs[-2:]
-    count, part_count, row_count, _ = buffer_ref.shape
-    terms, out_ref, shear_ref = refs[:count], refs[count], refs[count + 1]
+def add_kernel(row_split, comp, me_ref, *refs):
+    weight_ref = refs[0] if comp == 0 else None
+    base_hbm, *refs = refs[1:] if comp == 0 else refs
+    base_ref, term_ref, base_sems, term_sems = refs[-4:]
+    count, part_count, row_count, _ = base_ref.shape
+    terms, out_hbm = refs[:count], refs[count]
     me = me_ref[0]
 
     def spot(ref, x):
         other = me ^ x
         top = pl.multiple_of(other % row_split * row_count, PAD)
-        return ref.at[other // row_split, 0, :, pl.ds(top, row_count)]
-
-    loads = [pltpu.make_async_copy(spot(base_ref, x), buffer_ref.at[x], sems.at[x]) for x in range(count)]
-    stores = [pltpu.make_async_copy(buffer_ref.at[x], spot(out_ref, x), sems.at[x]) for x in range(count)]
-    for load in loads:
-        load.start()
+        return ref.at[other // row_split, comp, :, pl.ds(top, row_count)]
+
+    loads = [pltpu.make_async_copy(spot(base_hbm, x), base_ref.at[x], base_sems.at[x]) for x in range(count)]
+    term_loads = [pltpu.make_async_copy(terms[x], term_ref.at[x], term_sems.at[x]) for x in range(count)]
+    stores = [pltpu.make_async_copy(base_ref.at[x], spot(out_hbm, x), base_sems.at[x]) for x in range(count)]
+    for x in range(count):
+        loads[x].start()
+        term_loads[x].start()
     for x in range(count):
         loads[x].wait()
-        buffer_ref[x] = buffer_ref[x] + terms[x][...]
+        term_loads[x].wait()
+        base_ref[x] = base_ref[x] + term_ref[x]
         stores[x].start()
-        for p in range(part_count):
-            lower, upper = buffer_ref[x, p, :PAD], buffer_ref[x, p, row_count - PAD :]
-            shear_ref[me ^ x, p] = jnp.sum(lower * weight_ref[x, 0][:, :1], axis=0)
-            shear_ref[me ^ x, part_count + p] = jnp.sum(upper * weight_ref[x, 1][:, :1], axis=0)
+        if comp == 0:
+            shear_ref = refs[count + 1]
+            for p in range(part_count):
+                lower, upper = base_ref[x, p, :PAD], base_ref[x, p, row_count - PAD :]
+                shear_ref[me ^ x, p] = jnp.sum(lower * weight_ref[x, 0][:, :1], axis=0)
+                shear_ref[me ^ x, part_count + p] = jnp.sum(upper * weight_ref[x, 1][:, :1], axis=0)
     for store in stores:
         store.wait()
 
 
-def add_paired(base, terms, weight, spots, row_split):
+def add_component(base, terms, spots, row_split, comp, weight):
     count = len(terms)
     part_count, _, width = terms[0].shape
     size = count * terms[0].size
-    anywhere, vector = pl.BlockSpec(memory_space=pl.ANY), pl.BlockSpec(memory_space=pltpu.VMEM)
+    vector = pl.BlockSpec(memory_space=pltpu.VMEM)
+    first = comp == 0
+    block = pltpu.VMEM((count,) + terms[0].shape, jnp.float32)
+    sums = jax.ShapeDtypeStruct((count, 2 * part_count, width), jnp.float32)
     return pl.pallas_call(
-        functools.partial(add_paired_kernel, row_split),
-        out_shape=(
-            jax.ShapeDtypeStruct(base.shape, jnp.float32),
-            jax.ShapeDtypeStruct((count, 2 * part_count, width), jnp.float32),
-        ),
-        in_specs=[pl.BlockSpec(memory_space=pltpu.SMEM), vector, anywhere] + [vector] * count,
-        out_specs=(anywhere, vector),
-        scratch_shapes=[pltpu.VMEM((count,) + terms[0].shape, jnp.float32), pltpu.SemaphoreType.DMA((count,))],
-        input_output_aliases={2: 0},
+        functools.partial(add_kernel, row_split, comp),
+        out_shape=[jax.ShapeDtypeStruct(base.shape, jnp.float32)] + [sums] * first,
+        in_specs=[pl.BlockSpec(memory_space=pltpu.SMEM)] + [vector] * first + [HBM] * (count + 1),
+        out_specs=[HBM] + [vector] * first,
+        scratch_shapes=[block, block, pltpu.SemaphoreType.DMA((count,)), pltpu.SemaphoreType.DMA((count,))],
+        input_output_aliases={1 + first: 0},
         compiler_params=pltpu.CompilerParams(vmem_limit_bytes=16 << 20),
         cost_estimate=pl.CostEstimate(flops=size, bytes_accessed=12 * size, transcendentals=0),
-        name="add_paired",
-    )(spots, weight, base, *terms)
-
-
-def add_whole_kernel(row_split, base_ref, term_ref, out_ref, buffer_ref, sems):
-    count, comps, _, row_count, _ = term_ref.shape
-
-    def spot(ref, source):
-        rows = pl.ds(source % row_split * row_count, row_count)
-        return ref.at[source // row_split, pl.ds(1, comps), :, rows]
-
-    loads = [pltpu.make_async_copy(spot(base_ref, x), buffer_ref.at[x], sems.at[x]) for x in range(count)]
-    stores = [pltpu.make_async_copy(buffer_ref.at[x], spot(out_ref, x), sems.at[x]) for x in range(count)]
-    for load in loads:
-        load.start()
-    for x in range(count):
-        loads[x].wait()
-        buffer_ref[x] = buffer_ref[x] + term_ref[x]
-        stores[x].start()
-    for store in stores:
-        store.wait()
-
-
-def add_whole(base, term, row_split):
-    anywhere, vector = pl.BlockSpec(memory_space=pl.ANY), pl.BlockSpec(memory_space=pltpu.VMEM)
-    return pl.pallas_call(
-        functools.partial(add_whole_kernel, row_split),
-        out_shape=jax.ShapeDtypeStruct(base.shape, jnp.float32),
-        in_specs=[anywhere, vector],
-        out_specs=anywhere,
-        scratch_shapes=[pltpu.VMEM(term.shape, jnp.float32), pltpu.SemaphoreType.DMA((term.shape[0],))],
-        input_output_aliases={0: 0},
-        compiler_params=pltpu.CompilerParams(vmem_limit_bytes=16 << 20),
-        cost_estimate=pl.CostEstimate(flops=term.size, bytes_accessed=12 * term.size, transcendentals=0),
-        name="add_whole",
-    )(base, term)
+        name="add_component",
+    )(spots, *[weight] * first, base, *terms)
 
 
 def after(value, *others):
@@ -421,32 +371,30 @@
     pairs = [[(i, i ^ x) for i in range(span)] for x in range(span)]
     spots = jnp.stack([me, me // row_split, me % row_split * line_rows]).astype(jnp.int32)
 
-    def block_of(x):
-        other = me ^ x
-        start = (other // row_split, 0, 0, other % row_split * line_rows, 0)
-        return lax.dynamic_slice(field, start, (1, 1, part_count, line_rows, width))[0, 0]
-
-    def exchange(lines):
+    def to_lines(comp):
+        lines = field[:, comp].reshape(mode_split, -1, row_split, line_rows, width)
+        lines = lines.transpose(0, 2, 1, 3, 4).reshape(span, -1, line_rows, width)
         return lax.all_to_all(lines, "span", split_axis=0, concat_axis=0)
+
+    def send_back(sent):
+        return [sent[0]] + [lax.ppermute(sent[x], "span", pairs[x]) for x in range(span - 1, 0, -1)][::-1]
 
     forward = [(i, i + 1) for i in range(wall_count - 1)]
     backward = [(i + 1, i) for i in range(wall_count - 1)]
-    first = [lax.ppermute(block_of(x), "span", pairs[x]) for x in range(span - 1, 0, -1)][::-1]
-    rest = field[:, 1:].reshape(mode_split, -1, row_split, line_rows, width)
-    rest = exchange(rest.transpose(0, 2, 1, 3, 4).reshape(span, -1, line_rows, width))
+    lines = [to_lines(comp) for comp in range(comp_count)]
     low = lax.ppermute(field[:, :, :, row_count - PAD :], "wall", forward)
     high = lax.ppermute(field[:, :, :, :PAD], "wall", backward)
+
+    sent = [filter_component(lines[0], spots, tables)]
+    terms = [send_back(sent[0])]
 
     rate = kx_index.astype(jnp.float32) * (0.25 * TAU)
     coef = jnp.broadcast_to(d2_coef[:, :, None], (STEN, row_count, LANES))
     flow = jnp.broadcast_to(mean_flow[:, :, None], (2, row_count, LANES))
-    base = local_terms(field, low, high, rate, coef, flow)
-
-    first = list(lax.optimization_barrier((tuple(first), base))[0])
-    sent = filter_paired(field, first, spots, tables)
-    terms = [sent[0]] + [lax.ppermute(sent[x], "span", pairs[x]) for x in range(span - 1, 0, -1)][::-1]
-    filtered = filter_whole(after(rest, sent[0]), tables)
-    back = exchange(filtered).reshape(span, comp_count - 1, part_count, line_rows, width)
+    base = local_terms(field, after(low, sent[0][0]), high, rate, coef, flow)
+
+    sent.append(filter_component(after(lines[1], base), spots, tables))
+    terms.append(send_back(sent[1]))
 
     lower = jnp.where(wall_index == 0, wall_coef[0], 0.0)
     upper = jnp.where(wall_index == wall_count - 1, wall_coef[1, ::-1], 0.0)
@@ -456,8 +404,8 @@
     )
     weight = jnp.broadcast_to(weight[..., None], (span, 2, PAD, LANES))
     onehot = (patch_of[:, None] == jnp.arange(PATCH, dtype=jnp.int32)[None, :]).astype(jnp.float32)
-    terms[0] = after(terms[0], filtered)
-    result, shear = add_paired(base, terms, weight, spots, row_split)
+    terms[0][0] = after(terms[0][0], sent[1][0])
+    result, shear = add_component(base, terms[0], spots, row_split, 0, weight)
     grad = jnp.einsum("swz,zq->swq", shear, onehot, precision=lax.Precision.HIGHEST)
     grad = grad.reshape(mode_count, row_split, 2, part_count, PATCH).sum(axis=1)
     for axis, count in (("wall", wall_count), ("span", span)):
@@ -465,7 +413,14 @@
         while distance < count:
             grad = grad + lax.ppermute(grad, axis, [(i, i ^ distance) for i in range(count)])
             distance *= 2
-    return (add_whole(result, back, row_split), grad.transpose(1, 0, 2, 3))
+
+    for comp in range(2, comp_count):
+        sent.append(filter_component(after(lines[comp], grad), spots, tables))
+        terms.append(send_back(sent[comp]))
+    for comp in range(1, comp_count):
+        terms[comp][0] = after(terms[comp][0], sent[-1][0])
+        (result,) = add_component(result, terms[comp], spots, row_split, comp, None)
+    return (result, grad.transpose(1, 0, 2, 3))
 
 
 def solution(mesh):

time: 272 us -> 245 us (0.901)
  waiting for transfers between devices: 184 us -> 72.1 us
  blocking collectives: 0 us -> 79.5 us
  starting transfers between devices: 26.3 us -> 32.4 us
    ppermute x6 -> x9, waiting for transfers between devices: 154 us -> 50.5 us  [send_back(): lax.ppermute(sent[x], 'span', pairs[x])]
    all_to_all x0 -> x2, blocking collectives: none -> 79.5 us  [to_lines(): return lax.all_to_all(lines, 'span', split_axis=0, concat_axis=0)]
    ppermute x6 -> x9, starting transfers between devices: 7.38 us -> 19.3 us  [send_back(): lax.ppermute(sent[x], 'span', pairs[x])]
    all_to_all x2 -> x1, starting transfers between devices: 12.5 us -> 5.34 us  [to_lines(): return lax.all_to_all(lines, 'span', split_axis=0, concat_axis=0)]
    ppermute x1, waiting for transfers between devices: 15.7 us -> 10.3 us  [on_device(): high = lax.ppermute(field[:, :, :, :PAD], 'wall', backward)]
    another operation x0 -> x1, local copies, waits for them, and re-layouts: none -> 4.03 us  [to_lines(): lines = lines.transpose(0, 2, 1, 3, 4).reshape(span, -1, line_rows, width)]
    slice x1 -> x0, local copies, waits for them, and re-layouts: 3.87 us -> none  [on_device(): rest = field[:, 1:].reshape(mode_split, -1, row_split, line_rows, width)]
    ppermute x5, waiting for transfers between devices: 14.6 us -> 11.2 us  [on_device(): lax.ppermute(grad, axis, [(i, i ^ distance) for i in range(count)])]
  transfers between devices with their start and end apart: 15 -> 17, of which waited for: 11 -> 12; matrix products, arithmetic and copies ran while one was open for 2% -> 2% of each run, Pallas kernels for 10% -> 16%
where the time goes in v4:
time: 245 us
  blocking collectives  79.5 us (32%)
  waiting for transfers between devices  72.1 us (29%)
  Pallas kernels  41.9 us (17%)
  starting transfers between devices  32.4 us (13%)
  local copies, waits for them, and re-layouts  17 us (7%)
    all_to_all x2, blocking collectives, to_lines(): return lax.all_to_all(lines, 'span', split_axis=0, concat_axis=0)  79.5 us
    ppermute x9, waiting for transfers between devices, send_back(): lax.ppermute(sent[x], 'span', pairs[x])  50.5 us
    ppermute x9, starting transfers between devices, send_back(): lax.ppermute(sent[x], 'span', pairs[x])  19.3 us
    pallas_call x3, Pallas kernels, filter_component(): pl.pallas_call(filter_kernel, out_shape=[jax.ShapeDtypeStruct(lines.shape...  17.1 us
    pallas_call x1, Pallas kernels, local_terms(): pl.pallas_call(local_kernel, grid=(mode_count,), out_shape=jax.ShapeDtype...  15.7 us
    ppermute x5, waiting for transfers between devices, on_device(): lax.ppermute(grad, axis, [(i, i ^ distance) for i in range(count)])  11.2 us
    ppermute x1, waiting for transfers between devices, on_device(): high = lax.ppermute(field[:, :, :, :PAD], 'wall', backward)  10.3 us
    unnamed x22, local copies, waits for them, and re-layouts  9.34 us
  transfers between devices with their start and end apart: 17, of which 12 were waited for; matrix products, arithmetic and copies ran while one was open for 2% of the time, Pallas kernels for 16%

profile of v4, /device:TPU:10, one launch (start us, length us, event | category | flops | bytes accessed | tf_op | source)
XLA Modules:
  0.0 244.8 jit_solution(7703177379396781181)
XLA Ops:
  0.6 4.0 %slice_bitcast_fusion = (f32[4,2,32,1536]{3,2,1,0:T(8,128)}, f32[4,2,32,1536]{3,2,1,0:T(8,128)S(1)}, f32[4,2,32,1536]{3,2,1,0:T(8,128)S(1)}) fusion(f32[4,3,2,32,1536]{4,3,2,1,0:T(8,128)} %field_ref.1), kind=kLoop, calls=%fused_computation | loop fusion | bytes 9437184 | tf_op jit(solution)/shard_map/reshape;transpose;reshape;squeeze | solution.py:376
  4.7 40.3 %all_to_all.15.lines_hbm = f32[4,2,32,1536]{3,2,1,0:T(8,128)S(1)} all-to-all(f32[4,2,32,1536]{3,2,1,0:T(8,128)S(1)} %get-tuple-element.43), channel_id=1, replica_groups=mesh['wall'=8,'span'=4] {'span'}, dimensions={0} | all-to-all | bytes 3145728 | tf_op jit(solution)/shard_map/all_to_all | solution.py:377
  44.9 39.3 %all_to_all.16.lines_hbm = f32[4,2,32,1536]{3,2,1,0:T(8,128)} all-to-all(f32[4,2,32,1536]{3,2,1,0:T(8,128)S(1)} %get-tuple-element.44), channel_id=1, replica_groups=mesh['wall'=8,'span'=4] {'span'}, dimensions={0} | all-to-all | bytes 3145728 | tf_op jit(solution)/shard_map/all_to_all | solution.py:377
  84.2 5.3 %all-to-all-start.2 = ((f32[4,2,32,1536]{3,2,1,0:T(8,128)}), f32[4,2,32,1536]{3,2,1,0:T(8,128)S(1)}, u32[]{:S(2)}, u32[]{:S(2)}) async-start(f32[4,2,32,1536]{3,2,1,0:T(8,128)} %get-tuple-element.42), calls=%async_computation.2 | async-start | bytes 3145728 | tf_op jit(solution)/shard_map/all_to_all | solution.py:377
  89.5 3.3 %fusion.6 = (f32[4,3,2,8,1536]{4,3,2,1,0:T(8,128)}, f32[4,3,2,8,1536]{4,3,2,1,0:T(8,128)}) fusion(f32[4,3,2,32,1536]{4,3,2,1,0:T(8,128)} %field_ref.1), kind=kLoop, calls=%fused_computation.15 | loop fusion | bytes 4718592 | tf_op jit(solution)/shard_map/slice | solution.py:386
  92.8 1.9 collective-permute-start
  94.7 3.6 %collective-permute-start.1 = (f32[4,3,2,8,1536]{4,3,2,1,0:T(8,128)}, f32[4,3,2,8,1536]{4,3,2,1,0:T(8,128)}, u32[]{:S(2)}, u32[]{:S(2)}) collective-permute-start(f32[4,3,2,8,1536]{4,3,2,1,0:T(8,128)} %get-tuple-element.45), channel_id=1, source_target_pairs={{4,0},{8,4},{12,8},{16,12},{20,16},{24,20},{28,24},{5,1},{9,5},{13... | collective-permute-start | bytes 3538952 | tf_op jit(solution)/shard_map/ppermute | solution.py:386
  98.4 0.0 copy-done.6
  98.4 0.1 rev.3
  98.5 0.1 pad_add_fusion.me_ref
  98.6 2.8 %copy-done = bf16[24,2,256,256]{3,2,1,0:T(8,128)(2,1)S(1)} copy-done((bf16[24,2,256,256]{3,2,1,0:T(8,128)(2,1)S(1)}, bf16[24,2,256,256]{3,2,1,0:T(8,128)(2,1)}, u32[]{:S(2)}) %copy-start) | copy-done | bytes 6291480
  101.4 1.4 copy-done.3
  102.8 5.5 %filter_component.3 = (f32[2,32,1536]{2,1,0:T(8,128)S(1)}, f32[2,32,1536]{2,1,0:T(8,128)S(1)}, f32[2,32,1536]{2,1,0:T(8,128)S(1)}, f32[2,32,1536]{2,1,0:T(8,128)S(1)}) custom-call(s32[3]{0:T(128)S(1)} %pad_add_fusion.me_ref, bf16[24,2,256,256]{3,2,1,0:T(8,128)(2,1)S(1)} %copy-done, f32[4,2,32,1536]{3,2,1,0:T(8,128)S(1)} %copy-done.3), custom_call_target="tpu_custom_call" | custom-call | flops 603979776 | bytes 3145728 | tf_op jit(solution)/shard_map/filter_component/pallas_call | solution.py:227
  108.3 0.1 collective-permute-start.2
  108.4 2.9 %collective-permute-start.3 = (f32[2,32,1536]{2,1,0:T(8,128)S(1)}, f32[2,32,1536]{2,1,0:T(8,128)S(1)}, u32[]{:S(2)}, u32[]{:S(2)}) collective-permute-start(f32[2,32,1536]{2,1,0:T(8,128)S(1)} %get-tuple-element.28), channel_id=1, source_target_pairs={{0,2},{1,3},{2,0},{3,1},{4,6},{5,7},{6,4},{7,5},{8,10},{9,11},{10,... | collective-permute-start | bytes 1179656 | tf_op jit(solution)/shard_map/ppermute | solution.py:380
  111.3 0.6 collective-permute-start.4
  111.9 0.0 copy-done.8
  111.9 0.0 collective-permute-done.low_ref
  111.9 10.3 %collective-permute-done.1.high_ref = f32[4,3,2,8,1536]{4,3,2,1,0:T(8,128)} collective-permute-done((f32[4,3,2,8,1536]{4,3,2,1,0:T(8,128)}, f32[4,3,2,8,1536]{4,3,2,1,0:T(8,128)}, u32[]{:S(2)}, u32[]{:S(2)}) %collective-permute-start.1) | collective-permute-done | bytes 1179680 | tf_op jit(solution)/shard_map/ppermute | solution.py:386
  122.3 0.0 copy-done.5
  122.3 0.1 broadcast_in_dim.51.flow_ref
  122.4 0.0 copy-done.4
  122.4 0.1 broadcast_in_dim.50.coef_ref
  122.5 0.0 copy-start.2
  122.5 2.3 copy-done.2
  124.8 15.7 %local_terms.1.refs_1_ = f32[4,3,2,32,1536]{4,3,2,1,0:T(8,128)} custom-call(f32[4]{0:T(128)S(1)} %convert_multiply_fusion.rate_ref, f32[15,32,128]{2,1,0:T(8,128)S(1)} %broadcast_in_dim.50.coef_ref, f32[2,32,128]{2,1,0:T(8,128)S(1)} %broadcast_in_dim.51.flow_ref, f32[4,3,2,32,1536]{4,3,2,1,0:T(8,128)S(1)} %copy-done.2, ...), custom_call_target="tpu_custom_call" | custom-call | flops 47185920 | bytes 11796480 | tf_op jit(solution)/shard_map/local_terms/pallas_call | solution.py:282
  140.5 0.0 slice-done
  140.5 0.0 slice-done.1
  140.5 6.0 %filter_component.4 = (f32[2,32,1536]{2,1,0:T(8,128)S(1)}, f32[2,32,1536]{2,1,0:T(8,128)}, f32[2,32,1536]{2,1,0:T(8,128)}, f32[2,32,1536]{2,1,0:T(8,128)}) custom-call(s32[3]{0:T(128)S(1)} %pad_add_fusion.me_ref, bf16[24,2,256,256]{3,2,1,0:T(8,128)(2,1)S(1)} %bitcast.24, f32[4,2,32,1536]{3,2,1,0:T(8,128)S(1)} %all_to_all.15.lines_hbm), custom_call_target="tpu_custom_call" | custom-call | flops 603979776 | bytes 3145728 | tf_op jit(solution)/shard_map/filter_component/pallas_call | solution.py:227
  146.5 0.1 collective-permute-start.10
  146.6 0.0 collective-permute-done.2.refs_3_
  146.6 3.3 %collective-permute-done.3.refs_4_ = f32[2,32,1536]{2,1,0:T(8,128)S(1)} collective-permute-done((f32[2,32,1536]{2,1,0:T(8,128)S(1)}, f32[2,32,1536]{2,1,0:T(8,128)S(1)}, u32[]{:S(2)}, u32[]{:S(2)}) %collective-permute-start.3) | collective-permute-done | bytes 393248 | tf_op jit(solution)/shard_map/ppermute | solution.py:380
  149.9 7.9 %collective-permute-done.4.refs_5_ = f32[2,32,1536]{2,1,0:T(8,128)S(1)} collective-permute-done((f32[2,32,1536]{2,1,0:T(8,128)S(1)}, f32[2,32,1536]{2,1,0:T(8,128)S(1)}, u32[]{:S(2)}, u32[]{:S(2)}) %collective-permute-start.4) | collective-permute-done | bytes 393248 | tf_op jit(solution)/shard_map/ppermute | solution.py:380
  157.8 0.1 broadcast_in_dim.49.refs_0_
  157.9 3.1 %add_component.3 = (f32[4,3,2,32,1536]{4,3,2,1,0:T(8,128)}, f32[4,4,1536]{2,1,0:T(4,128)S(1)}) custom-call(s32[3]{0:T(128)S(1)} %pad_add_fusion.me_ref, f32[4,2,8,128]{3,2,1,0:T(8,128)S(1)} %broadcast_in_dim.49.refs_0_, f32[4,3,2,32,1536]{4,3,2,1,0:T(8,128)} %local_terms.1.refs_1_, ...), custom_call_target="tpu_custom_call", output_to_operand_aliasing={{0}: (2, {})} | custom-call | flops 393216 | bytes 4718592 | tf_op jit(solution)/shard_map/add_component/pallas_call | solution.py:344
  161.0 0.0 copy-done.7
  161.0 0.3 fusion.1
  161.3 0.1 collective-permute-start.5
  161.4 1.2 collective-permute-done.5
  162.6 0.6 collective-permute-start.6
  163.1 3.1 %collective-permute-done.6 = f32[4,2,2,64]{3,2,0,1:T(2,128)S(1)} collective-permute-done((f32[4,2,2,64]{3,2,0,1:T(2,128)S(1)}, f32[4,2,2,64]{3,2,0,1:T(2,128)S(1)}, u32[]{:S(2)}, u32[]{:S(2)}) %collective-permute-start.6) | collective-permute-done | bytes 4128 | tf_op jit(solution)/shard_map/ppermute | solution.py:414
  166.2 1.6 collective-permute-start.7
  167.8 2.1 collective-permute-done.7
  169.9 0.0 collective-permute-start.8
  169.9 3.6 %collective-permute-done.8 = f32[4,2,2,64]{3,2,0,1:T(2,128)S(1)} collective-permute-done((f32[4,2,2,64]{3,2,0,1:T(2,128)S(1)}, f32[4,2,2,64]{3,2,0,1:T(2,128)S(1)}, u32[]{:S(2)}, u32[]{:S(2)}) %collective-permute-start.8) | collective-permute-done | bytes 4128 | tf_op jit(solution)/shard_map/ppermute | solution.py:414
  173.5 0.0 collective-permute-start.9
  173.6 2.9 %collective-permute-start.11 = (f32[2,32,1536]{2,1,0:T(8,128)}, f32[2,32,1536]{2,1,0:T(8,128)S(1)}, u32[]{:S(2)}, u32[]{:S(2)}) collective-permute-start(f32[2,32,1536]{2,1,0:T(8,128)} %get-tuple-element.36), channel_id=1, source_target_pairs={{0,2},{1,3},{2,0},{3,1},{4,6},{5,7},{6,4},{7,5},{8,10},{9,11},{10,... | collective-permute-start | bytes 1179656 | tf_op jit(solution)/shard_map/ppermute | solution.py:380
  176.5 0.6 collective-permute-start.12
  177.0 1.3 collective-permute-done.9
  178.3 0.6 add.28
  178.9 0.0 all-to-all-done.2.lines_hbm
  178.9 2.8 %copy-done.1 = bf16[24,2,256,256]{3,2,1,0:T(8,128)(2,1)S(1)} copy-done((bf16[24,2,256,256]{3,2,1,0:T(8,128)(2,1)S(1)}, bf16[24,2,256,256]{3,2,1,0:T(8,128)(2,1)}, u32[]{:S(2)}) %copy-start.1) | copy-done | bytes 6291480
  181.7 5.5 %filter_component.5 = (f32[2,32,1536]{2,1,0:T(8,128)S(1)}, f32[2,32,1536]{2,1,0:T(8,128)S(1)}, f32[2,32,1536]{2,1,0:T(8,128)S(1)}, f32[2,32,1536]{2,1,0:T(8,128)S(1)}) custom-call(s32[3]{0:T(128)S(1)} %pad_add_fusion.me_ref, bf16[24,2,256,256]{3,2,1,0:T(8,128)(2,1)S(1)} %copy-done.1, f32[4,2,32,1536]{3,2,1,0:T(8,128)S(1)} %all-to-all-done.2.lines_hbm), custom_call_target="tpu_custom_call" | custom-call | flops 603979776 | bytes 3145728 | tf_op jit(solution)/shard_map/filter_component/pallas_call | solution.py:227
  187.2 10.6 %collective-permute-start.13 = (f32[2,32,1536]{2,1,0:T(8,128)S(1)}, f32[2,32,1536]{2,1,0:T(8,128)S(1)}, u32[]{:S(2)}, u32[]{:S(2)}) collective-permute-start(f32[2,32,1536]{2,1,0:T(8,128)S(1)} %get-tuple-element.39), channel_id=1, source_target_pairs={{0,1},{1,0},{2,3},{3,2},{4,5},{5,4},{6,7},{7,6},{8,9},{9,8},{10,11... | collective-permute-start | bytes 1179656 | tf_op jit(solution)/shard_map/ppermute | solution.py:380
  197.8 0.9 collective-permute-start.14
  198.7 0.0 collective-permute-done.10.refs_2_
  198.7 0.6 collective-permute-start.15
  199.4 7.7 %collective-permute-done.11.refs_3_ = f32[2,32,1536]{2,1,0:T(8,128)S(1)} collective-permute-done((f32[2,32,1536]{2,1,0:T(8,128)}, f32[2,32,1536]{2,1,0:T(8,128)S(1)}, u32[]{:S(2)}, u32[]{:S(2)}) %collective-permute-start.11) | collective-permute-done | bytes 393248 | tf_op jit(solution)/shard_map/ppermute | solution.py:380
  207.1 18.0 %collective-permute-done.12.refs_4_ = f32[2,32,1536]{2,1,0:T(8,128)S(1)} collective-permute-done((f32[2,32,1536]{2,1,0:T(8,128)}, f32[2,32,1536]{2,1,0:T(8,128)S(1)}, u32[]{:S(2)}, u32[]{:S(2)}) %collective-permute-start.12) | collective-permute-done | bytes 393248 | tf_op jit(solution)/shard_map/ppermute | solution.py:380
  225.0 3.1 %add_component.4.refs_0_ = f32[4,3,2,32,1536]{4,3,2,1,0:T(8,128)} custom-call(s32[3]{0:T(128)S(1)} %pad_add_fusion.me_ref, f32[4,3,2,32,1536]{4,3,2,1,0:T(8,128)} %get-tuple-element.30.refs_0_, f32[2,32,1536]{2,1,0:T(8,128)S(1)} %get-tuple-element.34.refs_1_, f32[2,32,1536]{2,1,0:T(8,128)S(1)} %collective-permute-done.10.refs_2_, ...), custom_call_target="tpu_custom_call", output_to_operand_aliasing={{}: (1, {})} | custom-call | flops 393216 | bytes 4718592 | tf_op jit(solution)/shard_map/add_component/pallas_call | solution.py:344
  228.1 0.0 collective-permute-done.13.refs_2_
  228.1 4.3 %collective-permute-done.14.refs_3_ = f32[2,32,1536]{2,1,0:T(8,128)S(1)} collective-permute-done((f32[2,32,1536]{2,1,0:T(8,128)S(1)}, f32[2,32,1536]{2,1,0:T(8,128)S(1)}, u32[]{:S(2)}, u32[]{:S(2)}) %collective-permute-start.14) | collective-permute-done | bytes 393248 | tf_op jit(solution)/shard_map/ppermute | solution.py:380
  232.4 9.3 %collective-permute-done.15.refs_4_ = f32[2,32,1536]{2,1,0:T(8,128)S(1)} collective-permute-done((f32[2,32,1536]{2,1,0:T(8,128)S(1)}, f32[2,32,1536]{2,1,0:T(8,128)S(1)}, u32[]{:S(2)}, u32[]{:S(2)}) %collective-permute-start.15) | collective-permute-done | bytes 393248 | tf_op jit(solution)/shard_map/ppermute | solution.py:380
  241.7 3.1 %add_component.5 = f32[4,3,2,32,1536]{4,3,2,1,0:T(8,128)} custom-call(s32[3]{0:T(128)S(1)} %pad_add_fusion.me_ref, f32[4,3,2,32,1536]{4,3,2,1,0:T(8,128)} %add_component.4.refs_0_, f32[2,32,1536]{2,1,0:T(8,128)S(1)} %get-tuple-element.38.refs_1_, f32[2,32,1536]{2,1,0:T(8,128)S(1)} %collective-permute-done.13.refs_2_, ...), custom_call_target="tpu_custom_call", output_to_operand_aliasing={{}: (1, {})} | custom-call | flops 393216 | bytes 4718592 | tf_op jit(solution)/shard_map/add_component/pallas_call | solution.py:344
  (22 shorter events, 0.1 us)
Async XLA Ops:
  84.2 94.7 %all-to-all-start.2 = ((f32[4,2,32,1536]{3,2,1,0:T(8,128)}), f32[4,2,32,1536]{3,2,1,0:T(8,128)S(1)}, u32[]{:S(2)}, u32[]{:S(2)}) async-start(f32[4,2,32,1536]{3,2,1,0:T(8,128)} %get-tuple-element.42), calls=%async_computation.2 | async-start | bytes 3145728 | tf_op jit(solution)/shard_map/all_to_all | solution.py:377
  89.5 8.9 %copy-start.6 = (f32[2,8]{1,0:T(2,128)S(1)}, f32[2,8]{1,0:T(2,128)}, u32[]{:S(2)}) copy-start(f32[2,8]{1,0:T(2,128)} %param.10) | copy-start | bytes 196
  92.8 19.1 %collective-permute-start = (f32[4,3,2,8,1536]{4,3,2,1,0:T(8,128)}, f32[4,3,2,8,1536]{4,3,2,1,0:T(8,128)}, u32[]{:S(2)}, u32[]{:S(2)}) collective-permute-start(f32[4,3,2,8,1536]{4,3,2,1,0:T(8,128)} %get-tuple-element.46), channel_id=1, source_target_pairs={{0,4},{4,8},{8,12},{12,16},{16,20},{20,24},{24,28},{1,5},{5,9},{9,... | collective-permute-start | bytes 3538952 | tf_op jit(solution)/shard_map/ppermute | solution.py:385
  94.7 27.6 %collective-permute-start.1 = (f32[4,3,2,8,1536]{4,3,2,1,0:T(8,128)}, f32[4,3,2,8,1536]{4,3,2,1,0:T(8,128)}, u32[]{:S(2)}, u32[]{:S(2)}) collective-permute-start(f32[4,3,2,8,1536]{4,3,2,1,0:T(8,128)} %get-tuple-element.45), channel_id=1, source_target_pairs={{4,0},{8,4},{12,8},{16,12},{20,16},{24,20},{28,24},{5,1},{9,5},{13... | collective-permute-start | bytes 3538952 | tf_op jit(solution)/shard_map/ppermute | solution.py:386
  98.6 2.8 %copy-start = (bf16[24,2,256,256]{3,2,1,0:T(8,128)(2,1)S(1)}, bf16[24,2,256,256]{3,2,1,0:T(8,128)(2,1)}, u32[]{:S(2)}) copy-start(bf16[24,2,256,256]{3,2,1,0:T(8,128)(2,1)} %constant.55.clone.table_hbm) | copy-start | bytes 18874372
  101.4 1.4 copy-start.3
  102.8 9.1 %copy-start.8 = (s32[4]{0:T(128)S(1)}, s32[4]{0:T(128)}, u32[]{:S(2)}) copy-start(s32[4]{0:T(128)} %param.11) | copy-start | bytes 52
  102.8 19.5 %copy-start.5 = (f32[2,32]{1,0:T(2,128)S(1)}, f32[2,32]{1,0:T(2,128)}, u32[]{:S(2)}) copy-start(f32[2,32]{1,0:T(2,128)} %param.8) | copy-start | bytes 772
  102.8 19.6 %copy-start.4 = (f32[15,32]{1,0:T(8,128)S(1)}, f32[15,32]{1,0:T(8,128)}, u32[]{:S(2)}) copy-start(f32[15,32]{1,0:T(8,128)} %param.9) | copy-start | bytes 5764
  102.8 37.7 %slice-start = ((s8[6291456]{0:T(1024)(128)(4,1)}), s8[4194304]{0:T(1024)(128)(4,1)S(1)}, s32[]{:S(2)}) async-start(s8[6291456]{0:T(1024)(128)(4,1)} %bitcast.23), calls=%async_computation.3 | async-start | bytes 8388608
  108.3 38.3 %collective-permute-start.2 = (f32[2,32,1536]{2,1,0:T(8,128)S(1)}, f32[2,32,1536]{2,1,0:T(8,128)S(1)}, u32[]{:S(2)}, u32[]{:S(2)}) collective-permute-start(f32[2,32,1536]{2,1,0:T(8,128)S(1)} %get-tuple-element.27), channel_id=1, source_target_pairs={{0,1},{1,0},{2,3},{3,2},{4,5},{5,4},{6,7},{7,6},{8,9},{9,8},{10,11... | collective-permute-start | bytes 1179656 | tf_op jit(solution)/shard_map/ppermute | solution.py:380
  108.4 41.5 %collective-permute-start.3 = (f32[2,32,1536]{2,1,0:T(8,128)S(1)}, f32[2,32,1536]{2,1,0:T(8,128)S(1)}, u32[]{:S(2)}, u32[]{:S(2)}) collective-permute-start(f32[2,32,1536]{2,1,0:T(8,128)S(1)} %get-tuple-element.28), channel_id=1, source_target_pairs={{0,2},{1,3},{2,0},{3,1},{4,6},{5,7},{6,4},{7,5},{8,10},{9,11},{10,... | collective-permute-start | bytes 1179656 | tf_op jit(solution)/shard_map/ppermute | solution.py:380
  111.3 46.5 %collective-permute-start.4 = (f32[2,32,1536]{2,1,0:T(8,128)S(1)}, f32[2,32,1536]{2,1,0:T(8,128)S(1)}, u32[]{:S(2)}, u32[]{:S(2)}) collective-permute-start(f32[2,32,1536]{2,1,0:T(8,128)S(1)} %get-tuple-element.29), channel_id=1, source_target_pairs={{0,3},{1,2},{2,1},{3,0},{4,7},{5,6},{6,5},{7,4},{8,11},{9,10},{10,... | collective-permute-start | bytes 1179656 | tf_op jit(solution)/shard_map/ppermute | solution.py:380
  122.5 2.3 copy-start.2
  124.8 15.7 %slice-start.1 = ((s8[6291456]{0:T(1024)(128)(4,1)}), s8[2097152]{0:T(1024)(128)(4,1)S(1)}, s32[]{:S(2)}) async-start(s8[6291456]{0:T(1024)(128)(4,1)} %bitcast.23), calls=%async_computation.4 | async-start | bytes 4194304
  146.5 52.2 %collective-permute-start.10 = (f32[2,32,1536]{2,1,0:T(8,128)}, f32[2,32,1536]{2,1,0:T(8,128)S(1)}, u32[]{:S(2)}, u32[]{:S(2)}) collective-permute-start(f32[2,32,1536]{2,1,0:T(8,128)} %get-tuple-element.35), channel_id=1, source_target_pairs={{0,1},{1,0},{2,3},{3,2},{4,5},{5,4},{6,7},{7,6},{8,9},{9,8},{10,11... | collective-permute-start | bytes 1179656 | tf_op jit(solution)/shard_map/ppermute | solution.py:380
  157.9 3.1 %copy-start.7 = (s32[1536]{0:T(1024)S(1)}, s32[1536]{0:T(1024)}, u32[]{:S(2)}) copy-start(s32[1536]{0:T(1024)} %param.12) | copy-start | bytes 18436
  161.3 1.2 collective-permute-start.5
  162.6 3.7 %collective-permute-start.6 = (f32[4,2,2,64]{3,2,0,1:T(2,128)S(1)}, f32[4,2,2,64]{3,2,0,1:T(2,128)S(1)}, u32[]{:S(2)}, u32[]{:S(2)}) collective-permute-start(f32[4,2,2,64]{3,2,0,1:T(2,128)S(1)} %copy_add_fusion), channel_id=1, source_target_pairs={{0,8},{4,12},{8,0},{12,4},{16,24},{20,28},{24,16},{28,20},{1,9},{5... | collective-permute-start | bytes 12296 | tf_op jit(solution)/shard_map/ppermute | solution.py:414
  166.2 3.7 %collective-permute-start.7 = (f32[4,2,2,64]{3,2,0,1:T(2,128)S(1)}, f32[4,2,2,64]{3,2,0,1:T(2,128)S(1)}, u32[]{:S(2)}, u32[]{:S(2)}) collective-permute-start(f32[4,2,2,64]{3,2,0,1:T(2,128)S(1)} %add.25), channel_id=1, source_target_pairs={{0,16},{4,20},{8,24},{12,28},{16,0},{20,4},{24,8},{28,12},{1,17},{... | collective-permute-start | bytes 12296 | tf_op jit(solution)/shard_map/ppermute | solution.py:414
  169.9 3.7 %collective-permute-start.8 = (f32[4,2,2,64]{3,2,0,1:T(2,128)S(1)}, f32[4,2,2,64]{3,2,0,1:T(2,128)S(1)}, u32[]{:S(2)}, u32[]{:S(2)}) collective-permute-start(f32[4,2,2,64]{3,2,0,1:T(2,128)S(1)} %add.26), channel_id=1, source_target_pairs={{0,1},{1,0},{2,3},{3,2},{4,5},{5,4},{6,7},{7,6},{8,9},{9,8},{10,11... | collective-permute-start | bytes 12296 | tf_op jit(solution)/shard_map/ppermute | solution.py:414
  173.5 4.8 %collective-permute-start.9 = (f32[4,2,2,64]{3,2,0,1:T(2,128)S(1)}, f32[4,2,2,64]{3,2,0,1:T(2,128)S(1)}, u32[]{:S(2)}, u32[]{:S(2)}) collective-permute-start(f32[4,2,2,64]{3,2,0,1:T(2,128)S(1)} %add.27), channel_id=1, source_target_pairs={{0,2},{1,3},{2,0},{3,1},{4,6},{5,7},{6,4},{7,5},{8,10},{9,11},{10,... | collective-permute-start | bytes 12296 | tf_op jit(solution)/shard_map/ppermute | solution.py:414
  173.6 33.5 %collective-permute-start.11 = (f32[2,32,1536]{2,1,0:T(8,128)}, f32[2,32,1536]{2,1,0:T(8,128)S(1)}, u32[]{:S(2)}, u32[]{:S(2)}) collective-permute-start(f32[2,32,1536]{2,1,0:T(8,128)} %get-tuple-element.36), channel_id=1, source_target_pairs={{0,2},{1,3},{2,0},{3,1},{4,6},{5,7},{6,4},{7,5},{8,10},{9,11},{10,... | collective-permute-start | bytes 1179656 | tf_op jit(solution)/shard_map/ppermute | solution.py:380
  176.5 48.6 %collective-permute-start.12 = (f32[2,32,1536]{2,1,0:T(8,128)}, f32[2,32,1536]{2,1,0:T(8,128)S(1)}, u32[]{:S(2)}, u32[]{:S(2)}) collective-permute-start(f32[2,32,1536]{2,1,0:T(8,128)} %get-tuple-element.37), channel_id=1, source_target_pairs={{0,3},{1,2},{2,1},{3,0},{4,7},{5,6},{6,5},{7,4},{8,11},{9,10},{10,... | collective-permute-start | bytes 1179656 | tf_op jit(solution)/shard_map/ppermute | solution.py:380
  178.9 2.8 %copy-start.1 = (bf16[24,2,256,256]{3,2,1,0:T(8,128)(2,1)S(1)}, bf16[24,2,256,256]{3,2,1,0:T(8,128)(2,1)}, u32[]{:S(2)}) copy-start(bf16[24,2,256,256]{3,2,1,0:T(8,128)(2,1)} %constant.55.clone.table_hbm) | copy-start | bytes 18874372
  187.2 40.9 %collective-permute-start.13 = (f32[2,32,1536]{2,1,0:T(8,128)S(1)}, f32[2,32,1536]{2,1,0:T(8,128)S(1)}, u32[]{:S(2)}, u32[]{:S(2)}) collective-permute-start(f32[2,32,1536]{2,1,0:T(8,128)S(1)} %get-tuple-element.39), channel_id=1, source_target_pairs={{0,1},{1,0},{2,3},{3,2},{4,5},{5,4},{6,7},{7,6},{8,9},{9,8},{10,11... | collective-permute-start | bytes 1179656 | tf_op jit(solution)/shard_map/ppermute | solution.py:380
  197.8 34.5 %collective-permute-start.14 = (f32[2,32,1536]{2,1,0:T(8,128)S(1)}, f32[2,32,1536]{2,1,0:T(8,128)S(1)}, u32[]{:S(2)}, u32[]{:S(2)}) collective-permute-start(f32[2,32,1536]{2,1,0:T(8,128)S(1)} %get-tuple-element.40), channel_id=1, source_target_pairs={{0,2},{1,3},{2,0},{3,1},{4,6},{5,7},{6,4},{7,5},{8,10},{9,11},{10,... | collective-permute-start | bytes 1179656 | tf_op jit(solution)/shard_map/ppermute | solution.py:380
  198.7 43.0 %collective-permute-start.15 = (f32[2,32,1536]{2,1,0:T(8,128)S(1)}, f32[2,32,1536]{2,1,0:T(8,128)S(1)}, u32[]{:S(2)}, u32[]{:S(2)}) collective-permute-start(f32[2,32,1536]{2,1,0:T(8,128)S(1)} %get-tuple-element.41), channel_id=1, source_target_pairs={{0,3},{1,2},{2,1},{3,0},{4,7},{5,6},{6,5},{7,4},{8,11},{9,10},{10,... | collective-permute-start | bytes 1179656 | tf_op jit(solution)/shard_map/ppermute | solution.py:380

commit v5 on v4

--- a/solution.py
+++ b/solution.py
@@ -19,6 +19,7 @@
 OUTER = 48
 PAD = 8
 TILES = OUTER // 2
+FILTER_VMEM = 57_500_000
 
 QUARTER = (0, 4, 2, 1, 5, 9)
 KEPT = tuple(4 * q for q in QUARTER) + tuple(2 + 8 * t for t in range(6)) + tuple(4 * q + 1 for q in range(12))
@@ -236,7 +237,7 @@
             pltpu.SemaphoreType.DMA,
             pltpu.SemaphoreType.DMA((count,)),
         ],
-        compiler_params=pltpu.CompilerParams(vmem_limit_bytes=24 << 20),
+        compiler_params=pltpu.CompilerParams(vmem_limit_bytes=FILTER_VMEM),
         cost_estimate=pl.CostEstimate(flops=flops, bytes_accessed=8 * lines.size, transcendentals=0),
         name="filter_component",
     )(spots, tables, lines)
@@ -348,7 +349,7 @@
         out_specs=[HBM] + [vector] * first,
         scratch_shapes=[block, block, pltpu.SemaphoreType.DMA((count,)), pltpu.SemaphoreType.DMA((count,))],
         input_output_aliases={1 + first: 0},
-        compiler_params=pltpu.CompilerParams(vmem_limit_bytes=16 << 20),
+        compiler_params=pltpu.CompilerParams(vmem_limit_bytes=24 << 20),
         cost_estimate=pl.CostEstimate(flops=size, bytes_accessed=12 * size, transcendentals=0),
         name="add_component",
     )(spots, *[weight] * first, base, *terms)
@@ -371,22 +372,31 @@
     pairs = [[(i, i ^ x) for i in range(span)] for x in range(span)]
     spots = jnp.stack([me, me // row_split, me % row_split * line_rows]).astype(jnp.int32)
 
-    def to_lines(comp):
-        lines = field[:, comp].reshape(mode_split, -1, row_split, line_rows, width)
-        lines = lines.transpose(0, 2, 1, 3, 4).reshape(span, -1, line_rows, width)
+    def block_lines(source, comp):
+        lines = source[:, comp].reshape(mode_split, -1, row_split, line_rows, width)
+        return lines.transpose(0, 2, 1, 3, 4).reshape(span, -1, line_rows, width)
+
+    def exchange(lines):
         return lax.all_to_all(lines, "span", split_axis=0, concat_axis=0)
 
-    def send_back(sent):
+    def send_back(sent, *earlier):
+        if earlier:
+            sent = lax.optimization_barrier((tuple(sent), earlier))[0]
         return [sent[0]] + [lax.ppermute(sent[x], "span", pairs[x]) for x in range(span - 1, 0, -1)][::-1]
 
     forward = [(i, i + 1) for i in range(wall_count - 1)]
     backward = [(i + 1, i) for i in range(wall_count - 1)]
-    lines = [to_lines(comp) for comp in range(comp_count)]
+    own = [block_lines(field, 0)]
+    own.append(block_lines(after(field, own[0]), 1))
+    lines = [exchange(own[0]), exchange(own[1])]
     low = lax.ppermute(field[:, :, :, row_count - PAD :], "wall", forward)
     high = lax.ppermute(field[:, :, :, :PAD], "wall", backward)
 
-    sent = [filter_component(lines[0], spots, tables)]
+    sent = [filter_component(after(lines[0], low, high), spots, tables)]
     terms = [send_back(sent[0])]
+    for comp in range(2, comp_count):
+        own.append(block_lines(after(field, sent[0][0]), comp))
+        lines.append(exchange(own[comp]))
 
     rate = kx_index.astype(jnp.float32) * (0.25 * TAU)
     coef = jnp.broadcast_to(d2_coef[:, :, None], (STEN, row_count, LANES))
@@ -394,7 +404,11 @@
     base = local_terms(field, after(low, sent[0][0]), high, rate, coef, flow)
 
     sent.append(filter_component(after(lines[1], base), spots, tables))
-    terms.append(send_back(sent[1]))
+    terms.append(send_back(sent[1], *terms[0]))
+
+    for comp in range(2, comp_count):
+        sent.append(filter_component(after(lines[comp], sent[comp - 1][0]), spots, tables))
+        terms.append(send_back(sent[comp], *terms[comp - 1]))
 
     lower = jnp.where(wall_index == 0, wall_coef[0], 0.0)
     upper = jnp.where(wall_index == wall_count - 1, wall_coef[1, ::-1], 0.0)
@@ -404,7 +418,7 @@
     )
     weight = jnp.broadcast_to(weight[..., None], (span, 2, PAD, LANES))
     onehot = (patch_of[:, None] == jnp.arange(PATCH, dtype=jnp.int32)[None, :]).astype(jnp.float32)
-    terms[0][0] = after(terms[0][0], sent[1][0])
+    terms[0][0] = after(terms[0][0], terms[1][1])
     result, shear = add_component(base, terms[0], spots, row_split, 0, weight)
     grad = jnp.einsum("swz,zq->swq", shear, onehot, precision=lax.Precision.HIGHEST)
     grad = grad.reshape(mode_count, row_split, 2, part_count, PATCH).sum(axis=1)
@@ -414,9 +428,6 @@
             grad = grad + lax.ppermute(grad, axis, [(i, i ^ distance) for i in range(count)])
             distance *= 2
 
-    for comp in range(2, comp_count):
-        sent.append(filter_component(after(lines[comp], grad), spots, tables))
-        terms.append(send_back(sent[comp]))
     for comp in range(1, comp_count):
         terms[comp][0] = after(terms[comp][0], sent[-1][0])
         (result,) = add_component(result, terms[comp], spots, row_split, comp, None)

time: 245 us -> 251 us (1.024); the launches traced: 245 us -> 247 us
  blocking collectives: 79.5 us -> 0 us
  waiting for transfers between devices: 72.1 us -> 149 us
  Pallas kernels: 41.9 us -> 47.1 us
  local copies, waits for them, and re-layouts: 17 us -> 14.1 us
    all_to_all x2 -> x0, blocking collectives: 79.5 us -> none  [to_lines(): return lax.all_to_all(lines, 'span', split_axis=0, concat_axis=0)]
    all_to_all x1 -> x3, waiting for transfers between devices: 0.01 us -> 31 us  [exchange(): return lax.all_to_all(lines, 'span', split_axis=0, concat_axis=0)]
    ppermute x9, waiting for transfers between devices: 50.5 us -> 73 us  [send_back(): lax.ppermute(sent[x], 'span', pairs[x])]
    all_to_all x1 -> x3, starting transfers between devices: 5.34 us -> 18 us  [exchange(): return lax.all_to_all(lines, 'span', split_axis=0, concat_axis=0)]
    ppermute x1, waiting for transfers between devices: 0.01 us -> 11.5 us  [on_device(): low = lax.ppermute(field[:, :, :, row_count - PAD:], 'wall', forward)]
    ppermute x5, waiting for transfers between devices: 11.2 us -> 21.5 us  [on_device(): lax.ppermute(grad, axis, [(i, i ^ distance) for i in range(count)])]
    ppermute x9, starting transfers between devices: 19.3 us -> 10.5 us  [send_back(): lax.ppermute(sent[x], 'span', pairs[x])]
    unnamed x22 -> x24, local copies, waits for them, and re-layouts: 9.34 us -> 2.39 us
  transfers between devices with their start and end apart: 17 -> 19, of which waited for: 12 -> 13; matrix products, arithmetic and copies ran while one was open for 2% -> 4% of each run, Pallas kernels for 16% -> 18%
where the time goes in v5:
time: 251 us; the launch traced here: 247 us
  waiting for transfers between devices  149 us (59%)
  Pallas kernels  47.1 us (19%)
  starting transfers between devices  34.6 us (14%)
  local copies, waits for them, and re-layouts  14.1 us (6%)
    ppermute x9, waiting for transfers between devices, send_back(): lax.ppermute(sent[x], 'span', pairs[x])  73 us
    all_to_all x3, waiting for transfers between devices, exchange(): return lax.all_to_all(lines, 'span', split_axis=0, concat_axis=0)  31 us
    pallas_call x3, Pallas kernels, filter_component(): pl.pallas_call(filter_kernel, out_shape=[jax.ShapeDtypeStruct(lines.shape...  23 us
    ppermute x5, waiting for transfers between devices, on_device(): lax.ppermute(grad, axis, [(i, i ^ distance) for i in range(count)])  21.5 us
    all_to_all x3, starting transfers between devices, exchange(): return lax.all_to_all(lines, 'span', split_axis=0, concat_axis=0)  18 us
    pallas_call x1, Pallas kernels, local_terms(): pl.pallas_call(local_kernel, grid=(mode_count,), out_shape=jax.ShapeDtype...  15 us
    ppermute x1, waiting for transfers between devices, on_device(): high = lax.ppermute(field[:, :, :, :PAD], 'wall', backward)  11.8 us
    ppermute x1, waiting for transfers between devices, on_device(): low = lax.ppermute(field[:, :, :, row_count - PAD:], 'wall', forward)  11.5 us
  transfers between devices with their start and end apart: 19, of which 13 were waited for; matrix products, arithmetic and copies ran while one was open for 4% of the time, Pallas kernels for 18%

profile of v5, /device:TPU:10, one launch (start us, length us, event | category | flops | bytes accessed | tf_op | source)
XLA Modules:
  0.0 247.1 jit_solution(8379478249983965705)
XLA Ops:
  0.6 2.7 %slice_bitcast_fusion.2 = f32[4,2,32,1536]{3,2,1,0:T(8,128)} fusion(f32[4,3,2,32,1536]{4,3,2,1,0:T(8,128)} %field_ref.1), kind=kLoop, calls=%fused_computation.2 | loop fusion | bytes 3145728 | tf_op jit(solution)/shard_map/reshape;transpose;reshape;squeeze | solution.py:377
  3.3 5.3 %all-to-all-start = ((f32[4,2,32,1536]{3,2,1,0:T(8,128)}), f32[4,2,32,1536]{3,2,1,0:T(8,128)S(1)}, u32[]{:S(2)}, u32[]{:S(2)}) async-start(f32[4,2,32,1536]{3,2,1,0:T(8,128)} %slice_bitcast_fusion.2), calls=%async_computation | async-start | bytes 3145728 | tf_op jit(solution)/shard_map/all_to_all | solution.py:380
  8.6 2.7 %slice_bitcast_fusion.1 = f32[4,2,32,1536]{3,2,1,0:T(8,128)} fusion(f32[4,3,2,32,1536]{4,3,2,1,0:T(8,128)} %field_ref.1), kind=kLoop, calls=%fused_computation.1 | loop fusion | bytes 3145728 | tf_op jit(solution)/shard_map/reshape;transpose;reshape;squeeze | solution.py:377
  11.3 31.0 %all-to-all-done.lines_hbm = f32[4,2,32,1536]{3,2,1,0:T(8,128)S(1)} async-done(((f32[4,2,32,1536]{3,2,1,0:T(8,128)}), f32[4,2,32,1536]{3,2,1,0:T(8,128)S(1)}, u32[]{:S(2)}, u32[]{:S(2)}) %all-to-all-start) | async-done | bytes 1572896 | tf_op jit(solution)/shard_map/all_to_all | solution.py:380
  42.3 7.6 %all-to-all-start.1 = ((f32[4,2,32,1536]{3,2,1,0:T(8,128)}), f32[4,2,32,1536]{3,2,1,0:T(8,128)}, u32[]{:S(2)}, u32[]{:S(2)}) async-start(f32[4,2,32,1536]{3,2,1,0:T(8,128)} %slice_bitcast_fusion.1), calls=%async_computation.1 | async-start | bytes 3145728 | tf_op jit(solution)/shard_map/all_to_all | solution.py:380
  49.9 3.3 %fusion.6 = (f32[4,3,2,8,1536]{4,3,2,1,0:T(8,128)}, f32[4,3,2,8,1536]{4,3,2,1,0:T(8,128)}) fusion(f32[4,3,2,32,1536]{4,3,2,1,0:T(8,128)} %field_ref.1), kind=kLoop, calls=%fused_computation.16 | loop fusion | bytes 4718592 | tf_op jit(solution)/shard_map/slice | solution.py:393
  53.2 1.9 collective-permute-start
  55.1 3.6 %collective-permute-start.1 = (f32[4,3,2,8,1536]{4,3,2,1,0:T(8,128)}, f32[4,3,2,8,1536]{4,3,2,1,0:T(8,128)S(1)}, u32[]{:S(2)}, u32[]{:S(2)}) collective-permute-start(f32[4,3,2,8,1536]{4,3,2,1,0:T(8,128)} %get-tuple-element.64), channel_id=1, source_target_pairs={{4,0},{8,4},{12,8},{16,12},{20,16},{24,20},{28,24},{5,1},{9,5},{13... | collective-permute-start | bytes 3538952 | tf_op jit(solution)/shard_map/ppermute | solution.py:393
  58.7 0.7 pad_add_fusion.me_ref
  59.4 11.5 %collective-permute-done.low_ref = f32[4,3,2,8,1536]{4,3,2,1,0:T(8,128)S(1)} collective-permute-done((f32[4,3,2,8,1536]{4,3,2,1,0:T(8,128)}, f32[4,3,2,8,1536]{4,3,2,1,0:T(8,128)S(1)}, u32[]{:S(2)}, u32[]{:S(2)}) %collective-permute-start) | collective-permute-done | bytes 1179680 | tf_op jit(solution)/shard_map/ppermute | solution.py:392
  70.9 11.8 %collective-permute-done.1.high_ref = f32[4,3,2,8,1536]{4,3,2,1,0:T(8,128)S(1)} collective-permute-done((f32[4,3,2,8,1536]{4,3,2,1,0:T(8,128)}, f32[4,3,2,8,1536]{4,3,2,1,0:T(8,128)S(1)}, u32[]{:S(2)}, u32[]{:S(2)}) %collective-permute-start.1) | collective-permute-done | bytes 1179680 | tf_op jit(solution)/shard_map/ppermute | solution.py:393
  82.6 7.6 %filter_component.3 = (f32[2,32,1536]{2,1,0:T(8,128)}, f32[2,32,1536]{2,1,0:T(8,128)}, f32[2,32,1536]{2,1,0:T(8,128)}, f32[2,32,1536]{2,1,0:T(8,128)}) custom-call(s32[3]{0:T(128)} %pad_add_fusion.me_ref, bf16[24,2,256,256]{3,2,1,0:T(8,128)(2,1)} %constant.55.clone.table_hbm, f32[4,2,32,1536]{3,2,1,0:T(8,128)} %copy-done.6), custom_call_target="tpu_custom_call" | custom-call | flops 603979776 | bytes 3145728 | tf_op jit(solution)/shard_map/filter_component/pallas_call | solution.py:228
  90.2 0.0 copy-start.11
  90.2 0.0 copy-start.7
  90.2 0.0 copy-start.8
  90.3 2.7 %slice_bitcast_fusion = f32[4,2,32,1536]{3,2,1,0:T(8,128)} fusion(f32[4,3,2,32,1536]{4,3,2,1,0:T(8,128)} %field_ref.1), kind=kLoop, calls=%fused_computation | loop fusion | bytes 3145728 | tf_op jit(solution)/shard_map/reshape;transpose;reshape;squeeze | solution.py:377
  92.9 0.0 all-to-all-done.1.lines_hbm
  92.9 5.1 %all-to-all-start.2 = ((f32[4,2,32,1536]{3,2,1,0:T(8,128)}), f32[4,2,32,1536]{3,2,1,0:T(8,128)}, u32[]{:S(2)}, u32[]{:S(2)}) async-start(f32[4,2,32,1536]{3,2,1,0:T(8,128)} %slice_bitcast_fusion), calls=%async_computation.2 | async-start | bytes 3145728 | tf_op jit(solution)/shard_map/all_to_all | solution.py:380
  98.0 0.0 collective-permute-start.2
  98.1 2.9 %collective-permute-start.3 = (f32[2,32,1536]{2,1,0:T(8,128)}, f32[2,32,1536]{2,1,0:T(8,128)S(1)}, u32[]{:S(2)}, u32[]{:S(2)}) collective-permute-start(f32[2,32,1536]{2,1,0:T(8,128)} %get-tuple-element.43), channel_id=1, source_target_pairs={{0,2},{1,3},{2,0},{3,1},{4,6},{5,7},{6,4},{7,5},{8,10},{9,11},{10,... | collective-permute-start | bytes 1179656 | tf_op jit(solution)/shard_map/ppermute | solution.py:385
  101.0 0.6 collective-permute-start.4
  101.5 0.0 copy-done.7
  101.5 0.1 broadcast_in_dim.50.coef_ref
  101.7 0.1 broadcast_in_dim.51.flow_ref
  101.8 2.3 copy-done
  104.1 15.0 %local_terms.1.refs_1_ = f32[4,3,2,32,1536]{4,3,2,1,0:T(8,128)} custom-call(f32[4]{0:T(128)S(1)} %convert_multiply_fusion.rate_ref, f32[15,32,128]{2,1,0:T(8,128)S(1)} %broadcast_in_dim.50.coef_ref, f32[2,32,128]{2,1,0:T(8,128)S(1)} %broadcast_in_dim.51.flow_ref, f32[4,3,2,32,1536]{4,3,2,1,0:T(8,128)S(1)} %copy-done, ...), custom_call_target="tpu_custom_call" | custom-call | flops 47185920 | bytes 11796480 | tf_op jit(solution)/shard_map/local_terms/pallas_call | solution.py:283
  119.1 7.8 %filter_component.4 = (f32[2,32,1536]{2,1,0:T(8,128)}, f32[2,32,1536]{2,1,0:T(8,128)}, f32[2,32,1536]{2,1,0:T(8,128)}, f32[2,32,1536]{2,1,0:T(8,128)}) custom-call(s32[3]{0:T(128)} %pad_add_fusion.me_ref, bf16[24,2,256,256]{3,2,1,0:T(8,128)(2,1)} %constant.55.clone.table_hbm, f32[4,2,32,1536]{3,2,1,0:T(8,128)} %all-to-all-done.1.lines_hbm), custom_call_target="tpu_custom_call" | custom-call | flops 603979776 | bytes 3145728 | tf_op jit(solution)/shard_map/filter_component/pallas_call | solution.py:228
  126.9 0.0 copy-start.10
  126.9 6.0 %collective-permute-done.2.refs_3_ = f32[2,32,1536]{2,1,0:T(8,128)S(1)} collective-permute-done((f32[2,32,1536]{2,1,0:T(8,128)}, f32[2,32,1536]{2,1,0:T(8,128)S(1)}, u32[]{:S(2)}, u32[]{:S(2)}) %collective-permute-start.2) | collective-permute-done | bytes 393248 | tf_op jit(solution)/shard_map/ppermute | solution.py:385
  132.9 25.2 %collective-permute-done.3.refs_4_ = f32[2,32,1536]{2,1,0:T(8,128)S(1)} collective-permute-done((f32[2,32,1536]{2,1,0:T(8,128)}, f32[2,32,1536]{2,1,0:T(8,128)S(1)}, u32[]{:S(2)}, u32[]{:S(2)}) %collective-permute-start.3) | collective-permute-done | bytes 393248 | tf_op jit(solution)/shard_map/ppermute | solution.py:385
  158.1 10.2 %collective-permute-done.4.refs_5_ = f32[2,32,1536]{2,1,0:T(8,128)S(1)} collective-permute-done((f32[2,32,1536]{2,1,0:T(8,128)}, f32[2,32,1536]{2,1,0:T(8,128)S(1)}, u32[]{:S(2)}, u32[]{:S(2)}) %collective-permute-start.4) | collective-permute-done | bytes 393248 | tf_op jit(solution)/shard_map/ppermute | solution.py:385
  168.3 0.0 collective-permute-start.5
  168.4 0.1 rev.3
  168.5 2.0 collective-permute-start.6
  170.5 1.5 collective-permute-start.7
  172.0 12.8 %collective-permute-done.5.refs_2_ = f32[2,32,1536]{2,1,0:T(8,128)S(1)} collective-permute-done((f32[2,32,1536]{2,1,0:T(8,128)}, f32[2,32,1536]{2,1,0:T(8,128)S(1)}, u32[]{:S(2)}, u32[]{:S(2)}) %collective-permute-start.5) | collective-permute-done | bytes 393248 | tf_op jit(solution)/shard_map/ppermute | solution.py:385
  184.8 0.1 broadcast_in_dim.49.refs_0_
  184.9 3.1 %add_component.3 = (f32[4,3,2,32,1536]{4,3,2,1,0:T(8,128)}, f32[4,4,1536]{2,1,0:T(4,128)S(1)}) custom-call(s32[3]{0:T(128)S(1)} %copy-done.4, f32[4,2,8,128]{3,2,1,0:T(8,128)S(1)} %broadcast_in_dim.49.refs_0_, f32[4,3,2,32,1536]{4,3,2,1,0:T(8,128)} %local_terms.1.refs_1_, f32[2,32,1536]{2,1,0:T(8,128)S(1)} %copy-done.3, ...), custom_call_target="tpu_custom_call", output_to_operand_aliasing={{0}: (2, {})} | custom-call | flops 393216 | bytes 4718592 | tf_op jit(solution)/shard_map/add_component/pallas_call | solution.py:345
  188.0 0.0 copy-start.1
  188.0 0.0 copy-start.5
  188.0 0.3 fusion.1
  188.3 0.1 collective-permute-start.11
  188.4 0.0 all-to-all-done.2.lines_hbm
  188.4 7.6 %filter_component.5 = (f32[2,32,1536]{2,1,0:T(8,128)}, f32[2,32,1536]{2,1,0:T(8,128)}, f32[2,32,1536]{2,1,0:T(8,128)}, f32[2,32,1536]{2,1,0:T(8,128)}) custom-call(s32[3]{0:T(128)} %pad_add_fusion.me_ref, bf16[24,2,256,256]{3,2,1,0:T(8,128)(2,1)} %constant.55.clone.table_hbm, f32[4,2,32,1536]{3,2,1,0:T(8,128)} %all-to-all-done.2.lines_hbm), custom_call_target="tpu_custom_call" | custom-call | flops 603979776 | bytes 3145728 | tf_op jit(solution)/shard_map/filter_component/pallas_call | solution.py:228
  196.0 1.1 collective-permute-done.6.refs_3_
  197.2 17.6 %collective-permute-done.7.refs_4_ = f32[2,32,1536]{2,1,0:T(8,128)S(1)} collective-permute-done((f32[2,32,1536]{2,1,0:T(8,128)}, f32[2,32,1536]{2,1,0:T(8,128)S(1)}, u32[]{:S(2)}, u32[]{:S(2)}) %collective-permute-start.7) | collective-permute-done | bytes 393248 | tf_op jit(solution)/shard_map/ppermute | solution.py:385
  214.8 0.6 collective-permute-start.10
  215.3 0.0 collective-permute-start.8
  215.3 2.9 %collective-permute-start.9 = (f32[2,32,1536]{2,1,0:T(8,128)}, f32[2,32,1536]{2,1,0:T(8,128)S(1)}, u32[]{:S(2)}, u32[]{:S(2)}) collective-permute-start(f32[2,32,1536]{2,1,0:T(8,128)} %get-tuple-element.61), channel_id=1, source_target_pairs={{0,2},{1,3},{2,0},{3,1},{4,6},{5,7},{6,4},{7,5},{8,10},{9,11},{10,... | collective-permute-start | bytes 1179656 | tf_op jit(solution)/shard_map/ppermute | solution.py:385
  218.3 0.0 collective-permute-done.11
  218.3 0.1 collective-permute-start.12
  218.3 3.6 %collective-permute-done.12 = f32[4,2,2,64]{3,2,0,1:T(2,128)S(1)} collective-permute-done((f32[4,2,2,64]{3,2,0,1:T(2,128)S(1)}, f32[4,2,2,64]{3,2,0,1:T(2,128)S(1)}, u32[]{:S(2)}, u32[]{:S(2)}) %collective-permute-start.12) | collective-permute-done | bytes 4128 | tf_op jit(solution)/shard_map/ppermute | solution.py:428
  222.0 0.0 collective-permute-start.13
  222.0 3.6 %collective-permute-done.13 = f32[4,2,2,64]{3,2,0,1:T(2,128)S(1)} collective-permute-done((f32[4,2,2,64]{3,2,0,1:T(2,128)S(1)}, f32[4,2,2,64]{3,2,0,1:T(2,128)S(1)}, u32[]{:S(2)}, u32[]{:S(2)}) %collective-permute-start.13) | collective-permute-done | bytes 4128 | tf_op jit(solution)/shard_map/ppermute | solution.py:428
  225.7 0.0 collective-permute-start.14
  225.7 8.3 %collective-permute-done.14 = f32[4,2,2,64]{3,2,0,1:T(2,128)S(1)} collective-permute-done((f32[4,2,2,64]{3,2,0,1:T(2,128)S(1)}, f32[4,2,2,64]{3,2,0,1:T(2,128)S(1)}, u32[]{:S(2)}, u32[]{:S(2)}) %collective-permute-start.14) | collective-permute-done | bytes 4128 | tf_op jit(solution)/shard_map/ppermute | solution.py:428
  234.0 0.5 collective-permute-start.15
  234.4 5.9 %collective-permute-done.15 = f32[4,2,2,64]{3,2,0,1:T(2,128)S(1)} collective-permute-done((f32[4,2,2,64]{3,2,0,1:T(2,128)S(1)}, f32[4,2,2,64]{3,2,0,1:T(2,128)S(1)}, u32[]{:S(2)}, u32[]{:S(2)}) %collective-permute-start.15) | collective-permute-done | bytes 4128 | tf_op jit(solution)/shard_map/ppermute | solution.py:428
  240.3 0.6 add_bitcast_fusion
  241.0 3.1 %add_component.4.refs_0_ = f32[4,3,2,32,1536]{4,3,2,1,0:T(8,128)} custom-call(s32[3]{0:T(128)S(1)} %copy-done.5, f32[4,3,2,32,1536]{4,3,2,1,0:T(8,128)} %get-tuple-element.47.refs_0_, f32[2,32,1536]{2,1,0:T(8,128)S(1)} %copy-done.1, f32[2,32,1536]{2,1,0:T(8,128)S(1)} %collective-permute-done.5.refs_2_, ...), custom_call_target="tpu_custom_call", output_to_operand_aliasing={{}: (1, {})} | custom-call | flops 393216 | bytes 4718592 | tf_op jit(solution)/shard_map/add_component/pallas_call | solution.py:345
  244.0 0.0 collective-permute-done.10.refs_4_
  244.0 0.0 collective-permute-done.8.refs_2_
  244.0 0.0 collective-permute-done.9.refs_3_
  244.1 3.1 %add_component.5 = f32[4,3,2,32,1536]{4,3,2,1,0:T(8,128)} custom-call(s32[3]{0:T(128)S(1)} %copy-done.5, f32[4,3,2,32,1536]{4,3,2,1,0:T(8,128)} %add_component.4.refs_0_, f32[2,32,1536]{2,1,0:T(8,128)S(1)} %copy-done.2, f32[2,32,1536]{2,1,0:T(8,128)S(1)} %collective-permute-done.8.refs_2_, ...), custom_call_target="tpu_custom_call", output_to_operand_aliasing={{}: (1, {})} | custom-call | flops 393216 | bytes 4718592 | tf_op jit(solution)/shard_map/add_component/pallas_call | solution.py:345
  (27 shorter events, 0.1 us)
Async XLA Ops:
  3.3 39.0 %all-to-all-start = ((f32[4,2,32,1536]{3,2,1,0:T(8,128)}), f32[4,2,32,1536]{3,2,1,0:T(8,128)S(1)}, u32[]{:S(2)}, u32[]{:S(2)}) async-start(f32[4,2,32,1536]{3,2,1,0:T(8,128)} %slice_bitcast_fusion.2), calls=%async_computation | async-start | bytes 3145728 | tf_op jit(solution)/shard_map/all_to_all | solution.py:380
  42.3 10.9 %copy-start.6 = (f32[4,2,32,1536]{3,2,1,0:T(8,128)}, f32[4,2,32,1536]{3,2,1,0:T(8,128)S(1)}, u32[]{:S(2)}) copy-start(f32[4,2,32,1536]{3,2,1,0:T(8,128)S(1)} %all-to-all-done.lines_hbm) | copy-start | bytes 4718596
  42.3 50.6 %all-to-all-start.1 = ((f32[4,2,32,1536]{3,2,1,0:T(8,128)}), f32[4,2,32,1536]{3,2,1,0:T(8,128)}, u32[]{:S(2)}, u32[]{:S(2)}) async-start(f32[4,2,32,1536]{3,2,1,0:T(8,128)} %slice_bitcast_fusion.1), calls=%async_computation.1 | async-start | bytes 3145728 | tf_op jit(solution)/shard_map/all_to_all | solution.py:380
  53.2 17.7 %collective-permute-start = (f32[4,3,2,8,1536]{4,3,2,1,0:T(8,128)}, f32[4,3,2,8,1536]{4,3,2,1,0:T(8,128)S(1)}, u32[]{:S(2)}, u32[]{:S(2)}) collective-permute-start(f32[4,3,2,8,1536]{4,3,2,1,0:T(8,128)} %get-tuple-element.65), channel_id=1, source_target_pairs={{0,4},{4,8},{8,12},{12,16},{16,20},{20,24},{24,28},{1,5},{5,9},{9,... | collective-permute-start | bytes 3538952 | tf_op jit(solution)/shard_map/ppermute | solution.py:392
  55.1 27.6 %collective-permute-start.1 = (f32[4,3,2,8,1536]{4,3,2,1,0:T(8,128)}, f32[4,3,2,8,1536]{4,3,2,1,0:T(8,128)S(1)}, u32[]{:S(2)}, u32[]{:S(2)}) collective-permute-start(f32[4,3,2,8,1536]{4,3,2,1,0:T(8,128)} %get-tuple-element.64), channel_id=1, source_target_pairs={{4,0},{8,4},{12,8},{16,12},{20,16},{24,20},{28,24},{5,1},{9,5},{13... | collective-permute-start | bytes 3538952 | tf_op jit(solution)/shard_map/ppermute | solution.py:393
  90.2 11.3 %copy-start.11 = (s32[4]{0:T(128)S(1)}, s32[4]{0:T(128)}, u32[]{:S(2)}) copy-start(s32[4]{0:T(128)} %param.11) | copy-start | bytes 52
  90.2 11.3 %copy-start.7 = (f32[15,32]{1,0:T(8,128)S(1)}, f32[15,32]{1,0:T(8,128)}, u32[]{:S(2)}) copy-start(f32[15,32]{1,0:T(8,128)} %param.9) | copy-start | bytes 5764
  90.2 11.4 %copy-start.8 = (f32[2,32]{1,0:T(2,128)S(1)}, f32[2,32]{1,0:T(2,128)}, u32[]{:S(2)}) copy-start(f32[2,32]{1,0:T(2,128)} %param.8) | copy-start | bytes 772
  92.9 95.4 %all-to-all-start.2 = ((f32[4,2,32,1536]{3,2,1,0:T(8,128)}), f32[4,2,32,1536]{3,2,1,0:T(8,128)}, u32[]{:S(2)}, u32[]{:S(2)}) async-start(f32[4,2,32,1536]{3,2,1,0:T(8,128)} %slice_bitcast_fusion), calls=%async_computation.2 | async-start | bytes 3145728 | tf_op jit(solution)/shard_map/all_to_all | solution.py:380
  98.0 34.9 %collective-permute-start.2 = (f32[2,32,1536]{2,1,0:T(8,128)}, f32[2,32,1536]{2,1,0:T(8,128)S(1)}, u32[]{:S(2)}, u32[]{:S(2)}) collective-permute-start(f32[2,32,1536]{2,1,0:T(8,128)} %get-tuple-element.42), channel_id=1, source_target_pairs={{0,1},{1,0},{2,3},{3,2},{4,5},{5,4},{6,7},{7,6},{8,9},{9,8},{10,11... | collective-permute-start | bytes 1179656 | tf_op jit(solution)/shard_map/ppermute | solution.py:385
  98.1 60.0 %collective-permute-start.3 = (f32[2,32,1536]{2,1,0:T(8,128)}, f32[2,32,1536]{2,1,0:T(8,128)S(1)}, u32[]{:S(2)}, u32[]{:S(2)}) collective-permute-start(f32[2,32,1536]{2,1,0:T(8,128)} %get-tuple-element.43), channel_id=1, source_target_pairs={{0,2},{1,3},{2,0},{3,1},{4,6},{5,7},{6,4},{7,5},{8,10},{9,11},{10,... | collective-permute-start | bytes 1179656 | tf_op jit(solution)/shard_map/ppermute | solution.py:385
  101.0 67.4 %collective-permute-start.4 = (f32[2,32,1536]{2,1,0:T(8,128)}, f32[2,32,1536]{2,1,0:T(8,128)S(1)}, u32[]{:S(2)}, u32[]{:S(2)}) collective-permute-start(f32[2,32,1536]{2,1,0:T(8,128)} %get-tuple-element.44), channel_id=1, source_target_pairs={{0,3},{1,2},{2,1},{3,0},{4,7},{5,6},{6,5},{7,4},{8,11},{9,10},{10,... | collective-permute-start | bytes 1179656 | tf_op jit(solution)/shard_map/ppermute | solution.py:385
  101.8 2.3 copy-start
  119.1 49.3 %copy-start.9 = (f32[2,8]{1,0:T(2,128)S(1)}, f32[2,8]{1,0:T(2,128)}, u32[]{:S(2)}) copy-start(f32[2,8]{1,0:T(2,128)} %param.10) | copy-start | bytes 196
  119.1 65.8 %copy-start.3 = (f32[2,32,1536]{2,1,0:T(8,128)S(1)}, f32[2,32,1536]{2,1,0:T(8,128)}, u32[]{:S(2)}) copy-start(f32[2,32,1536]{2,1,0:T(8,128)} %get-tuple-element.46.refs_2_) | copy-start | bytes 1179652
  119.1 65.8 %copy-start.4 = (s32[3]{0:T(128)S(1)}, s32[3]{0:T(128)}, u32[]{:S(2)}) copy-start(s32[3]{0:T(128)} %pad_add_fusion.me_ref) | copy-start | bytes 40
  126.9 61.1 %copy-start.10 = (s32[1536]{0:T(1024)S(1)}, s32[1536]{0:T(1024)}, u32[]{:S(2)}) copy-start(s32[1536]{0:T(1024)} %param.12) | copy-start | bytes 18436
  168.3 16.5 %collective-permute-start.5 = (f32[2,32,1536]{2,1,0:T(8,128)}, f32[2,32,1536]{2,1,0:T(8,128)S(1)}, u32[]{:S(2)}, u32[]{:S(2)}) collective-permute-start(f32[2,32,1536]{2,1,0:T(8,128)} %get-tuple-element.45), channel_id=1, source_target_pairs={{0,1},{1,0},{2,3},{3,2},{4,5},{5,4},{6,7},{7,6},{8,9},{9,8},{10,11... | collective-permute-start | bytes 1179656 | tf_op jit(solution)/shard_map/ppermute | solution.py:385
  168.5 28.7 %collective-permute-start.6 = (f32[2,32,1536]{2,1,0:T(8,128)}, f32[2,32,1536]{2,1,0:T(8,128)S(1)}, u32[]{:S(2)}, u32[]{:S(2)}) collective-permute-start(f32[2,32,1536]{2,1,0:T(8,128)} %get-tuple-element.53), channel_id=1, source_target_pairs={{0,2},{1,3},{2,0},{3,1},{4,6},{5,7},{6,4},{7,5},{8,10},{9,11},{10,... | collective-permute-start | bytes 1179656 | tf_op jit(solution)/shard_map/ppermute | solution.py:385
  170.5 44.3 %collective-permute-start.7 = (f32[2,32,1536]{2,1,0:T(8,128)}, f32[2,32,1536]{2,1,0:T(8,128)S(1)}, u32[]{:S(2)}, u32[]{:S(2)}) collective-permute-start(f32[2,32,1536]{2,1,0:T(8,128)} %get-tuple-element.54), channel_id=1, source_target_pairs={{0,3},{1,2},{2,1},{3,0},{4,7},{5,6},{6,5},{7,4},{8,11},{9,10},{10,... | collective-permute-start | bytes 1179656 | tf_op jit(solution)/shard_map/ppermute | solution.py:385
  188.0 53.0 %copy-start.1 = (f32[2,32,1536]{2,1,0:T(8,128)S(1)}, f32[2,32,1536]{2,1,0:T(8,128)}, u32[]{:S(2)}) copy-start(f32[2,32,1536]{2,1,0:T(8,128)} %get-tuple-element.52.refs_1_) | copy-start | bytes 1179652
  188.0 53.0 %copy-start.5 = (s32[3]{0:T(128)S(1)}, s32[3]{0:T(128)}, u32[]{:S(2)}) copy-start(s32[3]{0:T(128)} %pad_add_fusion.me_ref) | copy-start | bytes 40
  188.3 29.9 %collective-permute-start.11 = (f32[4,2,2,64]{3,2,0,1:T(2,128)S(1)}, f32[4,2,2,64]{3,2,0,1:T(2,128)S(1)}, u32[]{:S(2)}, u32[]{:S(2)}) collective-permute-start(f32[4,2,2,64]{3,2,0,1:T(2,128)S(1)} %copy.16), channel_id=1, source_target_pairs={{0,4},{4,0},{8,12},{12,8},{16,20},{20,16},{24,28},{28,24},{1,5},{5... | collective-permute-start | bytes 12296 | tf_op jit(solution)/shard_map/ppermute | solution.py:428
  214.8 29.2 %collective-permute-start.10 = (f32[2,32,1536]{2,1,0:T(8,128)}, f32[2,32,1536]{2,1,0:T(8,128)S(1)}, u32[]{:S(2)}, u32[]{:S(2)}) collective-permute-start(f32[2,32,1536]{2,1,0:T(8,128)} %get-tuple-element.62), channel_id=1, source_target_pairs={{0,3},{1,2},{2,1},{3,0},{4,7},{5,6},{6,5},{7,4},{8,11},{9,10},{10,... | collective-permute-start | bytes 1179656 | tf_op jit(solution)/shard_map/ppermute | solution.py:385
  215.3 28.7 %collective-permute-start.8 = (f32[2,32,1536]{2,1,0:T(8,128)}, f32[2,32,1536]{2,1,0:T(8,128)S(1)}, u32[]{:S(2)}, u32[]{:S(2)}) collective-permute-start(f32[2,32,1536]{2,1,0:T(8,128)} %get-tuple-element.60), channel_id=1, source_target_pairs={{0,1},{1,0},{2,3},{3,2},{4,5},{5,4},{6,7},{7,6},{8,9},{9,8},{10,11... | collective-permute-start | bytes 1179656 | tf_op jit(solution)/shard_map/ppermute | solution.py:385
  215.3 28.7 %collective-permute-start.9 = (f32[2,32,1536]{2,1,0:T(8,128)}, f32[2,32,1536]{2,1,0:T(8,128)S(1)}, u32[]{:S(2)}, u32[]{:S(2)}) collective-permute-start(f32[2,32,1536]{2,1,0:T(8,128)} %get-tuple-element.61), channel_id=1, source_target_pairs={{0,2},{1,3},{2,0},{3,1},{4,6},{5,7},{6,4},{7,5},{8,10},{9,11},{10,... | collective-permute-start | bytes 1179656 | tf_op jit(solution)/shard_map/ppermute | solution.py:385
  218.3 3.7 %collective-permute-start.12 = (f32[4,2,2,64]{3,2,0,1:T(2,128)S(1)}, f32[4,2,2,64]{3,2,0,1:T(2,128)S(1)}, u32[]{:S(2)}, u32[]{:S(2)}) collective-permute-start(f32[4,2,2,64]{3,2,0,1:T(2,128)S(1)} %copy_add_fusion), channel_id=1, source_target_pairs={{0,8},{4,12},{8,0},{12,4},{16,24},{20,28},{24,16},{28,20},{1,9},{5... | collective-permute-start | bytes 12296 | tf_op jit(solution)/shard_map/ppermute | solution.py:428
  222.0 3.7 %collective-permute-start.13 = (f32[4,2,2,64]{3,2,0,1:T(2,128)S(1)}, f32[4,2,2,64]{3,2,0,1:T(2,128)S(1)}, u32[]{:S(2)}, u32[]{:S(2)}) collective-permute-start(f32[4,2,2,64]{3,2,0,1:T(2,128)S(1)} %add.25), channel_id=1, source_target_pairs={{0,16},{4,20},{8,24},{12,28},{16,0},{20,4},{24,8},{28,12},{1,17},{... | collective-permute-start | bytes 12296 | tf_op jit(solution)/shard_map/ppermute | solution.py:428
  225.7 8.3 %collective-permute-start.14 = (f32[4,2,2,64]{3,2,0,1:T(2,128)S(1)}, f32[4,2,2,64]{3,2,0,1:T(2,128)S(1)}, u32[]{:S(2)}, u32[]{:S(2)}) collective-permute-start(f32[4,2,2,64]{3,2,0,1:T(2,128)S(1)} %add.26), channel_id=1, source_target_pairs={{0,1},{1,0},{2,3},{3,2},{4,5},{5,4},{6,7},{7,6},{8,9},{9,8},{10,11... | collective-permute-start | bytes 12296 | tf_op jit(solution)/shard_map/ppermute | solution.py:428
  234.0 6.4 %collective-permute-start.15 = (f32[4,2,2,64]{3,2,0,1:T(2,128)S(1)}, f32[4,2,2,64]{3,2,0,1:T(2,128)S(1)}, u32[]{:S(2)}, u32[]{:S(2)}) collective-permute-start(f32[4,2,2,64]{3,2,0,1:T(2,128)S(1)} %add.27), channel_id=1, source_target_pairs={{0,2},{1,3},{2,0},{3,1},{4,6},{5,7},{6,4},{7,5},{8,10},{9,11},{10,... | collective-permute-start | bytes 12296 | tf_op jit(solution)/shard_map/ppermute | solution.py:428
  240.9 3.1 %copy-start.2 = (f32[2,32,1536]{2,1,0:T(8,128)S(1)}, f32[2,32,1536]{2,1,0:T(8,128)}, u32[]{:S(2)}) copy-start(f32[2,32,1536]{2,1,0:T(8,128)} %get-tuple-element.59.refs_1_) | copy-start | bytes 1179652

commit v6 on v4

--- a/solution.py
+++ b/solution.py
@@ -19,6 +19,7 @@
 OUTER = 48
 PAD = 8
 TILES = OUTER // 2
+FILTER_VMEM = 57_500_000
 
 QUARTER = (0, 4, 2, 1, 5, 9)
 KEPT = tuple(4 * q for q in QUARTER) + tuple(2 + 8 * t for t in range(6)) + tuple(4 * q + 1 for q in range(12))
@@ -197,52 +198,102 @@
     lax.fori_loop(0, line_count * groups, backward, 0)
 
 
-def filter_kernel(me_ref, table_hbm, lines_hbm, *refs):
-    line_ref, wave_ref, table_ref, table_sem, sems = refs[-5:]
-    sent = refs[:-5]
-    count = len(sent)
-    me = me_ref[0]
-    copies = [pltpu.make_async_copy(lines_hbm.at[x], line_ref.at[x], sems.at[x]) for x in range(count)]
+def start_all(copies):
     for copy in copies:
         copy.start()
+    return copies
+
+
+def wait_all(copies):
+    for copy in copies:
+        copy.wait()
+
+
+def wall_sums(block, weight):
+    row_count = block.shape[1]
+    lower = [jnp.sum(block[p, :PAD] * weight[0][:, :1], axis=0) for p in range(2)]
+    upper = [jnp.sum(block[p, row_count - PAD :] * weight[1][:, :1], axis=0) for p in range(2)]
+    return lower + upper
+
+
+def filter_main_kernel(me_ref, table_hbm, weight_ref, lines_hbm, out_hbm, shear_ref, *scratch):
+    line_ref, wave_ref, table_ref, table_sem, sems = scratch
+    count = line_ref.shape[0]
+    me = me_ref[0]
+    copies = start_all([pltpu.make_async_copy(lines_hbm.at[x], line_ref.at[x], sems.at[x]) for x in range(count)])
     table_copy = pltpu.make_async_copy(table_hbm, table_ref, table_sem)
     table_copy.start()
-    for copy in copies:
-        copy.wait()
+    wait_all(copies)
     filter_lines(line_ref, wave_ref, table_ref, table_copy)
-    copies = [pltpu.make_async_copy(line_ref.at[me ^ x], sent[x], sems.at[x]) for x in range(count)]
-    for copy in copies:
-        copy.start()
-    for copy in copies:
-        copy.wait()
+    copies = start_all([pltpu.make_async_copy(line_ref.at[x], out_hbm.at[x], sems.at[x]) for x in range(count)])
+    for x in range(count):
+        for spot, value in enumerate(wall_sums(line_ref.at[me ^ x], weight_ref)):
+            shear_ref[x, spot] = value
+    wait_all(copies)
+
+
+def filter_last_kernel(me_ref, table_hbm, field_hbm, *refs):
+    line_ref, wave_ref, table_ref, table_sem, sems = refs[-5:]
+    count, _, row_count, _ = line_ref.shape
+    received, sent = refs[: count - 1], refs[count - 1 : 2 * count - 1]
+    me, mode, top = me_ref[0], me_ref[1], me_ref[2]
+    comp = field_hbm.shape[1] - 1
+    sources = (field_hbm.at[mode, comp, :, pl.ds(pl.multiple_of(top, PAD), row_count)],) + received
+    copies = start_all([pltpu.make_async_copy(sources[x], line_ref.at[me ^ x], sems.at[x]) for x in range(count)])
+    table_copy = pltpu.make_async_copy(table_hbm, table_ref, table_sem)
+    table_copy.start()
+    wait_all(copies)
+    filter_lines(line_ref, wave_ref, table_ref, table_copy)
+    wait_all(start_all([pltpu.make_async_copy(line_ref.at[me ^ x], sent[x], sems.at[x]) for x in range(count)]))
 
 
 HBM = pl.BlockSpec(memory_space=pltpu.HBM)
-
-
-def filter_component(lines, spots, tables):
-    count, part_count, row_count, width = lines.shape
-    rows = part_count * row_count
+SCALARS = pl.BlockSpec(memory_space=pltpu.SMEM)
+WHOLE = pl.BlockSpec(memory_space=pltpu.VMEM)
+
+
+def filter_call(kernel, name, block, tables, in_specs, out_specs, out_shape):
+    count, line_count, row_count, width = block
+    rows = line_count * row_count
     flops = 3 * 2 * TILES * rows * (2 * LANES) ** 2
     return pl.pallas_call(
-        filter_kernel,
-        out_shape=[jax.ShapeDtypeStruct(lines.shape[1:], jnp.float32)] * count,
-        in_specs=[pl.BlockSpec(memory_space=pltpu.SMEM), HBM, HBM],
-        out_specs=[HBM] * count,
+        kernel,
+        out_shape=out_shape,
+        in_specs=in_specs,
+        out_specs=out_specs,
         scratch_shapes=[
-            pltpu.VMEM(lines.shape, jnp.float32),
+            pltpu.VMEM(block, jnp.float32),
             pltpu.VMEM((TILES, rows, 2 * LANES), jnp.float32),
             pltpu.VMEM(tables.shape, tables.dtype),
             pltpu.SemaphoreType.DMA,
             pltpu.SemaphoreType.DMA((count,)),
         ],
-        compiler_params=pltpu.CompilerParams(vmem_limit_bytes=24 << 20),
-        cost_estimate=pl.CostEstimate(flops=flops, bytes_accessed=8 * lines.size, transcendentals=0),
-        name="filter_component",
-    )(spots, tables, lines)
-
-
-def local_kernel(rate_ref, coef_ref, flow_ref, field_ref, low_ref, high_ref, out_ref, pad_ref):
+        compiler_params=pltpu.CompilerParams(vmem_limit_bytes=FILTER_VMEM),
+        cost_estimate=pl.CostEstimate(flops=flops, bytes_accessed=8 * count * rows * width, transcendentals=0),
+        name=name,
+    )
+
+
+def filter_main(lines, weight, spots, tables, part_count):
+    shear = jax.ShapeDtypeStruct((lines.shape[0], 2 * part_count, lines.shape[3]), jnp.float32)
+    out_shape = (jax.ShapeDtypeStruct(lines.shape, jnp.float32), shear)
+    ins = [SCALARS, HBM, WHOLE, HBM]
+    call = filter_call(
+        filter_main_kernel, "filter_main", lines.shape, tables, ins, (HBM, WHOLE), out_shape
+    )
+    return call(spots, tables, weight, lines)
+
+
+def filter_last(field, received, spots, tables):
+    count = len(received) + 1
+    shape = received[0].shape
+    out_shape = [jax.ShapeDtypeStruct(shape, jnp.float32)] * count
+    ins = [SCALARS] + [HBM] * (count + 1)
+    call = filter_call(filter_last_kernel, "filter_last", (count,) + shape, tables, ins, [HBM] * count, out_shape)
+    return call(spots, tables, field, *received)
+
+
+def local_kernel(rate_ref, coef_ref, flow_ref, weight_ref, field_ref, low_ref, high_ref, out_ref, shear_ref, pad_ref):
     _, comp_count, part_count, row_count, width = field_ref.shape
     pad_ref[:, :, :PAD] = low_ref[0]
     pad_ref[:, :, PAD : PAD + row_count] = field_ref[0]
@@ -269,9 +320,11 @@
         return 0
 
     lax.fori_loop(0, width // LANES, column, 0)
-
-
-def local_terms(field, low, high, rate, coef, flow):
+    for spot, value in enumerate(wall_sums(out_ref.at[0, 0], weight_ref)):
+        shear_ref[0, spot] = value
+
+
+def local_terms(field, low, high, rate, coef, flow, weight):
     mode_count, comp_count, part_count, row_count, width = field.shape
     block = (1, comp_count, part_count, row_count, width)
     edge = (1, comp_count, part_count, PAD, width)
@@ -282,38 +335,41 @@
     return pl.pallas_call(
         local_kernel,
         grid=(mode_count,),
-        out_shape=jax.ShapeDtypeStruct(field.shape, jnp.float32),
+        out_shape=(
+            jax.ShapeDtypeStruct(field.shape, jnp.float32),
+            jax.ShapeDtypeStruct((mode_count, 2 * part_count, width), jnp.float32),
+        ),
         in_specs=[
-            pl.BlockSpec(memory_space=pltpu.SMEM),
+            SCALARS,
             pl.BlockSpec(coef.shape, lambda m: (0, 0, 0)),
             pl.BlockSpec(flow.shape, lambda m: (0, 0, 0)),
+            pl.BlockSpec(weight.shape, lambda m: (0, 0, 0)),
             pl.BlockSpec(block, by_mode),
             pl.BlockSpec(edge, by_mode),
             pl.BlockSpec(edge, by_mode),
         ],
-        out_specs=pl.BlockSpec(block, by_mode),
+        out_specs=(pl.BlockSpec(block, by_mode), pl.BlockSpec((1, 2 * part_count, width), lambda m: (m, 0, 0))),
         scratch_shapes=[pltpu.VMEM((comp_count, part_count, row_count + 2 * PAD, width), jnp.float32)],
         compiler_params=pltpu.CompilerParams(vmem_limit_bytes=24 << 20),
         cost_estimate=pl.CostEstimate(flops=40 * field.size, bytes_accessed=10 * field.size, transcendentals=0),
         name="local_terms",
-    )(rate, coef, flow, field, low, high)
-
-
-def add_kernel(row_split, comp, me_ref, *refs):
-    weight_ref = refs[0] if comp == 0 else None
-    base_hbm, *refs = refs[1:] if comp == 0 else refs
+    )(rate, coef, flow, weight, field, low, high)
+
+
+def add_kernel(row_split, comps, me_ref, base_hbm, *refs):
     base_ref, term_ref, base_sems, term_sems = refs[-4:]
-    count, part_count, row_count, _ = base_ref.shape
-    terms, out_hbm = refs[:count], refs[count]
+    count, _, _, row_count, _ = base_ref.shape
+    *terms, out_hbm = refs[:-4]
     me = me_ref[0]
 
     def spot(ref, x):
         other = me ^ x
         top = pl.multiple_of(other % row_split * row_count, PAD)
-        return ref.at[other // row_split, comp, :, pl.ds(top, row_count)]
+        return ref.at[other // row_split, comps, :, pl.ds(top, row_count)]
 
     loads = [pltpu.make_async_copy(spot(base_hbm, x), base_ref.at[x], base_sems.at[x]) for x in range(count)]
-    term_loads = [pltpu.make_async_copy(terms[x], term_ref.at[x], term_sems.at[x]) for x in range(count)]
+    sources = [terms[0].at[me ^ x] if len(terms) == 1 else terms[x] for x in range(count)]
+    term_loads = [pltpu.make_async_copy(sources[x], term_ref.at[x], term_sems.at[x]) for x in range(count)]
     stores = [pltpu.make_async_copy(base_ref.at[x], spot(out_hbm, x), base_sems.at[x]) for x in range(count)]
     for x in range(count):
         loads[x].start()
@@ -323,35 +379,27 @@
         term_loads[x].wait()
         base_ref[x] = base_ref[x] + term_ref[x]
         stores[x].start()
-        if comp == 0:
-            shear_ref = refs[count + 1]
-            for p in range(part_count):
-                lower, upper = base_ref[x, p, :PAD], base_ref[x, p, row_count - PAD :]
-                shear_ref[me ^ x, p] = jnp.sum(lower * weight_ref[x, 0][:, :1], axis=0)
-                shear_ref[me ^ x, part_count + p] = jnp.sum(upper * weight_ref[x, 1][:, :1], axis=0)
-    for store in stores:
-        store.wait()
-
-
-def add_component(base, terms, spots, row_split, comp, weight):
-    count = len(terms)
-    part_count, _, width = terms[0].shape
-    size = count * terms[0].size
-    vector = pl.BlockSpec(memory_space=pltpu.VMEM)
-    first = comp == 0
-    block = pltpu.VMEM((count,) + terms[0].shape, jnp.float32)
-    sums = jax.ShapeDtypeStruct((count, 2 * part_count, width), jnp.float32)
+    wait_all(stores)
+
+
+def add_components(base, terms, spots, span, row_split, comps):
+    first, last = comps
+    mode_count, _, part_count, row_count, width = base.shape
+    block = (span, last - first, part_count, row_count // row_split, width)
+    terms = [term.reshape(block[1:] if len(terms) > 1 else block) for term in terms]
+    size = math.prod(block)
+    buffer, sems = pltpu.VMEM(block, jnp.float32), pltpu.SemaphoreType.DMA((span,))
     return pl.pallas_call(
-        functools.partial(add_kernel, row_split, comp),
-        out_shape=[jax.ShapeDtypeStruct(base.shape, jnp.float32)] + [sums] * first,
-        in_specs=[pl.BlockSpec(memory_space=pltpu.SMEM)] + [vector] * first + [HBM] * (count + 1),
-        out_specs=[HBM] + [vector] * first,
-        scratch_shapes=[block, block, pltpu.SemaphoreType.DMA((count,)), pltpu.SemaphoreType.DMA((count,))],
-        input_output_aliases={1 + first: 0},
-        compiler_params=pltpu.CompilerParams(vmem_limit_bytes=16 << 20),
+        functools.partial(add_kernel, row_split, pl.ds(first, last - first)),
+        out_shape=jax.ShapeDtypeStruct(base.shape, jnp.float32),
+        in_specs=[SCALARS] + [HBM] * (1 + len(terms)),
+        out_specs=HBM,
+        scratch_shapes=[buffer, buffer, sems, sems],
+        input_output_aliases={1: 0},
+        compiler_params=pltpu.CompilerParams(vmem_limit_bytes=24 << 20),
         cost_estimate=pl.CostEstimate(flops=size, bytes_accessed=12 * size, transcendentals=0),
-        name="add_component",
-    )(spots, *[weight] * first, base, *terms)
+        name="add_components",
+    )(spots, base, *terms)
 
 
 def after(value, *others):
@@ -371,56 +419,66 @@
     pairs = [[(i, i ^ x) for i in range(span)] for x in range(span)]
     spots = jnp.stack([me, me // row_split, me % row_split * line_rows]).astype(jnp.int32)
 
-    def to_lines(comp):
-        lines = field[:, comp].reshape(mode_split, -1, row_split, line_rows, width)
-        lines = lines.transpose(0, 2, 1, 3, 4).reshape(span, -1, line_rows, width)
+    last = comp_count - 1
+
+    def exchange(lines):
         return lax.all_to_all(lines, "span", split_axis=0, concat_axis=0)
 
-    def send_back(sent):
-        return [sent[0]] + [lax.ppermute(sent[x], "span", pairs[x]) for x in range(span - 1, 0, -1)][::-1]
+    def swap(blocks):
+        return [lax.ppermute(blocks[x], "span", pairs[x]) for x in range(span - 1, 0, -1)][::-1]
+
+    main = field[:, :last].reshape(mode_split, -1, row_split, line_rows, width)
+    main = exchange(main.transpose(0, 2, 1, 3, 4).reshape(span, -1, line_rows, width))
 
     forward = [(i, i + 1) for i in range(wall_count - 1)]
     backward = [(i + 1, i) for i in range(wall_count - 1)]
-    lines = [to_lines(comp) for comp in range(comp_count)]
     low = lax.ppermute(field[:, :, :, row_count - PAD :], "wall", forward)
     high = lax.ppermute(field[:, :, :, :PAD], "wall", backward)
-
-    sent = [filter_component(lines[0], spots, tables)]
-    terms = [send_back(sent[0])]
+    patches = jnp.stack([patch_of] + swap([patch_of] * span))
+    onehot = (patches[:, :, None] == jnp.arange(PATCH, dtype=jnp.int32)).astype(jnp.float32)
+
+    lower = jnp.where(wall_index == 0, wall_coef[0], 0.0)
+    upper = jnp.where(wall_index == wall_count - 1, wall_coef[1, ::-1], 0.0)
+    weight = jnp.broadcast_to(jnp.stack([lower, upper])[:, :, None], (2, PAD, LANES))
+    group = me % row_split
+    ends = jnp.stack([group == 0, group == row_split - 1])
+    line_weight = jnp.where(ends[:, None, None], weight, 0.0)
 
     rate = kx_index.astype(jnp.float32) * (0.25 * TAU)
     coef = jnp.broadcast_to(d2_coef[:, :, None], (STEN, row_count, LANES))
     flow = jnp.broadcast_to(mean_flow[:, :, None], (2, row_count, LANES))
-    base = local_terms(field, after(low, sent[0][0]), high, rate, coef, flow)
-
-    sent.append(filter_component(after(lines[1], base), spots, tables))
-    terms.append(send_back(sent[1]))
-
-    lower = jnp.where(wall_index == 0, wall_coef[0], 0.0)
-    upper = jnp.where(wall_index == wall_count - 1, wall_coef[1, ::-1], 0.0)
-    group = (me ^ jnp.arange(span)) % row_split
-    weight = jnp.stack(
-        [jnp.where((group == 0)[:, None], lower, 0.0), jnp.where((group == row_split - 1)[:, None], upper, 0.0)], axis=1
-    )
-    weight = jnp.broadcast_to(weight[..., None], (span, 2, PAD, LANES))
-    onehot = (patch_of[:, None] == jnp.arange(PATCH, dtype=jnp.int32)[None, :]).astype(jnp.float32)
-    terms[0][0] = after(terms[0][0], sent[1][0])
-    result, shear = add_component(base, terms[0], spots, row_split, 0, weight)
-    grad = jnp.einsum("swz,zq->swq", shear, onehot, precision=lax.Precision.HIGHEST)
-    grad = grad.reshape(mode_count, row_split, 2, part_count, PATCH).sum(axis=1)
+    base, shear = local_terms(field, low, high, rate, coef, flow, weight)
+
+    def last_block(x):
+        other = me ^ x
+        start = (other // row_split, last, 0, other % row_split * line_rows, 0)
+        return lax.dynamic_slice(field, start, (1, 1, part_count, line_rows, width))[0, 0]
+
+    blocks = [last_block(x) for x in range(1, span)]
+    blocks = list(lax.optimization_barrier((tuple(blocks), base))[0])
+    received = swap([None] + blocks)
+
+    filtered, line_shear = filter_main(after(main, received[0]), line_weight, spots, tables, part_count)
+    back = exchange(filtered)
+    received[0] = after(received[0], filtered)
+    sent = filter_last(field, received, spots, tables)
+    returned = [sent[0]] + swap(sent)
+
+    highest = lax.Precision.HIGHEST
+    grad = jnp.einsum("mwz,zq->mwq", shear, onehot[0], precision=highest)
+    line_grad = jnp.einsum("xwz,xzq->wq", line_shear, onehot, precision=highest)
+    mine = jnp.arange(mode_count) == me // row_split
+    grad = after(grad + jnp.where(mine[:, None, None], line_grad, 0.0), returned[1])
     for axis, count in (("wall", wall_count), ("span", span)):
         distance = 1
         while distance < count:
             grad = grad + lax.ppermute(grad, axis, [(i, i ^ distance) for i in range(count)])
             distance *= 2
-
-    for comp in range(2, comp_count):
-        sent.append(filter_component(after(lines[comp], grad), spots, tables))
-        terms.append(send_back(sent[comp]))
-    for comp in range(1, comp_count):
-        terms[comp][0] = after(terms[comp][0], sent[-1][0])
-        (result,) = add_component(result, terms[comp], spots, row_split, comp, None)
-    return (result, grad.transpose(1, 0, 2, 3))
+    wall_grad = grad.reshape(mode_count, 2, part_count, PATCH).transpose(1, 0, 2, 3)
+
+    result = add_components(base, [back], spots, span, row_split, (0, last))
+    result = add_components(result, returned, spots, span, row_split, (last, comp_count))
+    return (result, wall_grad)
 
 
 def solution(mesh):

time: 245 us -> 262 us (1.069); the launches traced: 245 us -> 257 us
  waiting for transfers between devices: 72.1 us -> 162 us
  blocking collectives: 79.5 us -> 0 us
    ppermute x9, waiting for transfers between devices: 50.5 us -> 133 us  [swap(): lax.ppermute(blocks[x], 'span', pairs[x])]
    all_to_all x2 -> x0, blocking collectives: 79.5 us -> none  [to_lines(): return lax.all_to_all(lines, 'span', split_axis=0, concat_axis=0)]
    ppermute x9, starting transfers between devices: 19.3 us -> 10.4 us  [swap(): lax.ppermute(blocks[x], 'span', pairs[x])]
    all_to_all x1 -> x2, starting transfers between devices: 5.34 us -> 14.1 us  [exchange(): return lax.all_to_all(lines, 'span', split_axis=0, concat_axis=0)]
    ppermute x1, waiting for transfers between devices: 10.3 us -> 15.8 us  [on_device(): high = lax.ppermute(field[:, :, :, :PAD], 'wall', backward)]
    unnamed x22 -> x28, local copies, waits for them, and re-layouts: 9.34 us -> 4.51 us
    another operation x1 -> x4, local copies, waits for them, and re-layouts: 4.03 us -> 0.02 us  [on_device(): patches = jnp.stack([patch_of] + swap([patch_of] * span))]
    slice x0 -> x1, local copies, waits for them, and re-layouts: none -> 3.8 us  [on_device(): main = field[:, :last].reshape(mode_split, -1, row_split, line_rows, width)]
  transfers between devices with their start and end apart: 17 -> 18, of which waited for: 12 -> 10; matrix products, arithmetic and copies ran while one was open for 2% -> 4% of each run, Pallas kernels for 16% -> 10%
where the time goes in v6:
time: 262 us; the launch traced here: 257 us
  waiting for transfers between devices  162 us (62%)
  Pallas kernels  40.3 us (15%)
  starting transfers between devices  34.2 us (13%)
  local copies, waits for them, and re-layouts  15.5 us (6%)
  other arithmetic  2.8 us (1%)
    ppermute x9, waiting for transfers between devices, swap(): lax.ppermute(blocks[x], 'span', pairs[x])  133 us
    ppermute x1, waiting for transfers between devices, on_device(): high = lax.ppermute(field[:, :, :, :PAD], 'wall', backward)  15.8 us
    pallas_call x1, Pallas kernels, local_terms(): pl.pallas_call(local_kernel, grid=(mode_count,), out_shape=(jax.ShapeDtyp...  15.3 us
    all_to_all x2, starting transfers between devices, exchange(): return lax.all_to_all(lines, 'span', split_axis=0, concat_axis=0)  14.1 us
    ppermute x5, waiting for transfers between devices, on_device(): lax.ppermute(grad, axis, [(i, i ^ distance) for i in range(count)])  13 us
    ppermute x9, starting transfers between devices, swap(): lax.ppermute(blocks[x], 'span', pairs[x])  10.4 us
    pallas_call x1, Pallas kernels, filter_main(): return call(spots, tables, weight, lines)  10.3 us
    pallas_call x1, Pallas kernels, filter_last(): return call(spots, tables, field, *received)  7.99 us
  transfers between devices with their start and end apart: 18, of which 10 were waited for; matrix products, arithmetic and copies ran while one was open for 4% of the time, Pallas kernels for 10%

profile of v6, /device:TPU:10, one launch (start us, length us, event | category | flops | bytes accessed | tf_op | source)
XLA Modules:
  0.0 256.8 jit_solution(660647965176488134)
XLA Ops:
  0.6 3.8 %slice.22 = f32[4,2,2,32,1536]{4,3,2,1,0:T(8,128)} slice(f32[4,3,2,32,1536]{4,3,2,1,0:T(8,128)} %field_hbm.1), slice={[0:4], [0:2], [0:2], [0:32], [0:1536]} | slice | bytes 6291456 | tf_op jit(solution)/shard_map/slice | solution.py:430
  4.4 5.3 %all-to-all-start = ((f32[4,4,32,1536]{3,2,1,0:T(8,128)}), f32[4,4,32,1536]{3,2,1,0:T(8,128)}, u32[]{:S(2)}, u32[]{:S(2)}) async-start(f32[4,4,32,1536]{3,2,1,0:T(8,128)} %bitcast.1), calls=%async_computation | async-start | bytes 6291456 | tf_op jit(solution)/shard_map/all_to_all | solution.py:425
  9.8 2.9 %fusion = (f32[4,3,2,8,1536]{4,3,2,1,0:T(8,128)}, f32[4,3,2,8,1536]{4,3,2,1,0:T(8,128)S(1)}) fusion(f32[4,3,2,32,1536]{4,3,2,1,0:T(8,128)} %field_hbm.1), kind=kLoop, calls=%fused_computation.15 | loop fusion | bytes 4718592 | tf_op jit(solution)/shard_map/slice | solution.py:436
  12.6 1.9 collective-permute-start.1
  14.6 2.4 collective-permute-start
  17.0 1.3 broadcast_select_fusion.1
  18.3 1.3 rev.3
  19.5 0.7 convert_multiply_fusion.rate_ref
  20.2 2.2 dynamic-slice_bitcast_fusion
  22.4 15.8 %collective-permute-done.1.high_ref = f32[4,3,2,8,1536]{4,3,2,1,0:T(8,128)S(1)} collective-permute-done((f32[4,3,2,8,1536]{4,3,2,1,0:T(8,128)}, f32[4,3,2,8,1536]{4,3,2,1,0:T(8,128)S(1)}, u32[]{:S(2)}, u32[]{:S(2)}) %collective-permute-start.1) | collective-permute-done | bytes 1179680 | tf_op jit(solution)/shard_map/ppermute | solution.py:436
  38.2 0.0 collective-permute-done.low_ref
  38.2 0.1 broadcast_in_dim.54.weight_ref
  38.3 0.1 broadcast_in_dim.52.flow_ref
  38.4 0.0 copy-done.10
  38.4 0.1 broadcast_in_dim.30.coef_ref
  38.5 0.0 copy-start
  38.5 2.3 copy-done
  40.8 15.3 %local_terms.1 = (f32[4,3,2,32,1536]{4,3,2,1,0:T(8,128)}, f32[4,4,1536]{2,1,0:T(4,128)S(1)}) custom-call(f32[4]{0:T(128)S(1)} %convert_multiply_fusion.rate_ref, f32[15,32,128]{2,1,0:T(8,128)S(1)} %broadcast_in_dim.30.coef_ref, f32[2,32,128]{2,1,0:T(8,128)S(1)} %broadcast_in_dim.52.flow_ref, f32[2,8,128]{2,1,0:T(8,128)S(1)} %broadcast_in_dim.54.weight_ref, ...), custom_call_target="tpu_custom_call" | custom-call | flops 47185920 | bytes 11796480 | tf_op jit(solution)/shard_map/local_terms/pallas_call | solution.py:335
  56.2 0.0 copy-done.2
  56.2 0.6 copy-done.4
  56.8 0.0 collective-permute-start.2
  56.8 0.6 pad_add_fusion.1.me_ref
  57.4 22.3 %collective-permute-done.2.refs_0_ = f32[2,32,1536]{2,1,0:T(8,128)S(1)} collective-permute-done((f32[2,32,1536]{2,1,0:T(8,128)S(1)}, f32[2,32,1536]{2,1,0:T(8,128)S(1)}, u32[]{:S(2)}, u32[]{:S(2)}) %collective-permute-start.2) | collective-permute-done | bytes 393248 | tf_op jit(solution)/shard_map/ppermute | solution.py:428
  79.7 0.0 all-to-all-done.lines_hbm
  79.7 10.3 %filter_main.1 = (f32[4,4,32,1536]{3,2,1,0:T(8,128)}, f32[4,4,1536]{2,1,0:T(4,128)}) custom-call(s32[3]{0:T(128)} %pad_add_fusion.1.me_ref, bf16[24,2,256,256]{3,2,1,0:T(8,128)(2,1)} %constant.93.clone.table_hbm, f32[2,8,128]{2,1,0:T(8,128)} %copy-done.2, f32[4,4,32,1536]{3,2,1,0:T(8,128)} %all-to-all-done.lines_hbm), custom_call_target="tpu_custom_call" | custom-call | flops 1207959552 | bytes 6291456 | tf_op jit(solution)/shard_map/filter_main/pallas_call | solution.py:284
  90.0 0.0 copy-start.11
  90.0 8.8 %all-to-all-start.1 = ((f32[4,4,32,1536]{3,2,1,0:T(8,128)}), f32[4,4,32,1536]{3,2,1,0:T(8,128)S(1)}, u32[]{:S(2)}, u32[]{:S(2)}) async-start(f32[4,4,32,1536]{3,2,1,0:T(8,128)} %get-tuple-element.19), calls=%async_computation.1 | async-start | bytes 6291456 | tf_op jit(solution)/shard_map/all_to_all | solution.py:425
  98.8 2.4 collective-permute-start.3
  101.2 0.0 copy-done.9
  101.2 0.0 collective-permute-start.4
  101.2 2.0 collective-permute-start.8
  103.2 1.5 collective-permute-start.10
  104.7 1.0 collective-permute-start.9
  105.7 62.1 %collective-permute-done.8 = s32[1536]{0:T(1024)S(1)} collective-permute-done((s32[1536]{0:T(1024)S(1)}, s32[1536]{0:T(1024)S(1)}, u32[]{:S(2)}, u32[]{:S(2)}) %collective-permute-start.8) | collective-permute-done | bytes 6176 | tf_op jit(solution)/shard_map/ppermute | solution.py:428
  167.8 35.7 %collective-permute-done.10 = s32[1536]{0:T(1024)S(1)} collective-permute-done((s32[1536]{0:T(1024)S(1)}, s32[1536]{0:T(1024)S(1)}, u32[]{:S(2)}, u32[]{:S(2)}) %collective-permute-start.10) | collective-permute-done | bytes 6176 | tf_op jit(solution)/shard_map/ppermute | solution.py:428
  203.5 0.0 collective-permute-done.9
  203.6 0.0 collective-permute-done.3.refs_1_
  203.6 0.0 collective-permute-done.4.refs_2_
  203.6 0.7 copy-done.7
  204.3 0.7 copy-done.8
  205.1 8.0 %filter_last.1 = (f32[2,32,1536]{2,1,0:T(8,128)}, f32[2,32,1536]{2,1,0:T(8,128)}, f32[2,32,1536]{2,1,0:T(8,128)}, f32[2,32,1536]{2,1,0:T(8,128)}) custom-call(s32[3]{0:T(128)} %pad_add_fusion.1.me_ref, bf16[24,2,256,256]{3,2,1,0:T(8,128)(2,1)} %constant.93.clone.table_hbm, f32[4,3,2,32,1536]{4,3,2,1,0:T(8,128)} %field_hbm.1, f32[2,32,1536]{2,1,0:T(8,128)} %copy-done.6, ...), custom_call_target="tpu_custom_call" | custom-call | flops 603979776 | bytes 3145728 | tf_op jit(solution)/shard_map/filter_last/pallas_call | solution.py:293
  213.1 1.7 collective-permute-start.5
  214.8 0.4 collective-permute-start.6
  215.2 1.5 collective-permute-start.7
  216.6 0.2 iota_compare_fusion
  216.8 0.8 convolution_bitcast_fusion
  217.7 0.3 convolution_add_fusion
  218.0 13.0 %collective-permute-done.5 = f32[2,32,1536]{2,1,0:T(8,128)S(1)} collective-permute-done((f32[2,32,1536]{2,1,0:T(8,128)}, f32[2,32,1536]{2,1,0:T(8,128)S(1)}, u32[]{:S(2)}, u32[]{:S(2)}) %collective-permute-start.5) | collective-permute-done | bytes 393248 | tf_op jit(solution)/shard_map/ppermute | solution.py:428
  231.0 0.0 collective-permute-start.11
  231.0 1.2 collective-permute-done.11
  232.2 0.0 collective-permute-start.12
  232.2 3.6 %collective-permute-done.12 = f32[4,4,64]{2,1,0:T(4,128)S(1)} collective-permute-done((f32[4,4,64]{2,1,0:T(4,128)S(1)}, f32[4,4,64]{2,1,0:T(4,128)S(1)}, u32[]{:S(2)}, u32[]{:S(2)}) %collective-permute-start.12) | collective-permute-done | bytes 4128 | tf_op jit(solution)/shard_map/ppermute | solution.py:475
  235.9 0.5 collective-permute-start.13
  236.4 3.1 %collective-permute-done.13 = f32[4,4,64]{2,1,0:T(4,128)S(1)} collective-permute-done((f32[4,4,64]{2,1,0:T(4,128)S(1)}, f32[4,4,64]{2,1,0:T(4,128)S(1)}, u32[]{:S(2)}, u32[]{:S(2)}) %collective-permute-start.13) | collective-permute-done | bytes 4128 | tf_op jit(solution)/shard_map/ppermute | solution.py:475
  239.5 2.4 collective-permute-start.14
  241.9 1.6 collective-permute-done.14
  243.5 2.5 collective-permute-start.15
  246.0 3.4 %collective-permute-done.15 = f32[4,4,64]{2,1,0:T(4,128)S(1)} collective-permute-done((f32[4,4,64]{2,1,0:T(4,128)S(1)}, f32[4,4,64]{2,1,0:T(4,128)S(1)}, u32[]{:S(2)}, u32[]{:S(2)}) %collective-permute-start.15) | collective-permute-done | bytes 4128 | tf_op jit(solution)/shard_map/ppermute | solution.py:475
  249.5 0.6 copy.13
  250.1 0.0 all-to-all-done.1
  250.1 3.5 %add_components.2.base_hbm = f32[4,3,2,32,1536]{4,3,2,1,0:T(8,128)} custom-call(s32[3]{0:T(128)S(1)} %copy-done.3, f32[4,3,2,32,1536]{4,3,2,1,0:T(8,128)} %get-tuple-element.16.base_hbm, f32[4,2,2,32,1536]{4,3,2,1,0:T(8,128)S(1)} %bitcast.25), custom_call_target="tpu_custom_call", output_to_operand_aliasing={{}: (1, {})} | custom-call | flops 786432 | bytes 9437184 | tf_op jit(solution)/shard_map/add_components/pallas_call | solution.py:392
  253.6 0.0 collective-permute-done.6
  253.6 0.0 collective-permute-done.7
  253.6 3.2 %add_components.3 = f32[4,3,2,32,1536]{4,3,2,1,0:T(8,128)} custom-call(s32[3]{0:T(128)S(1)} %copy-done.3, f32[4,3,2,32,1536]{4,3,2,1,0:T(8,128)} %add_components.2.base_hbm, f32[1,2,32,1536]{3,2,1,0:T(8,128)S(1)} %bitcast.26, f32[1,2,32,1536]{3,2,1,0:T(8,128)S(1)} %bitcast.27, f32[1,2,32,1536]{3,2,1,0:T(8,128)} %bitcast.8.refs_2_, ...), custom_call_target="tpu_custom_call", output_to_operand_aliasing={{}: (1, {})} | custom-call | flops 393216 | bytes 4718592 | tf_op jit(solution)/shard_map/add_components/pallas_call | solution.py:392
  (32 shorter events, 0.1 us)
Async XLA Ops:
  4.4 75.2 %all-to-all-start = ((f32[4,4,32,1536]{3,2,1,0:T(8,128)}), f32[4,4,32,1536]{3,2,1,0:T(8,128)}, u32[]{:S(2)}, u32[]{:S(2)}) async-start(f32[4,4,32,1536]{3,2,1,0:T(8,128)} %bitcast.1), calls=%async_computation | async-start | bytes 6291456 | tf_op jit(solution)/shard_map/all_to_all | solution.py:425
  9.7 28.5 %copy-start.12 = (f32[2,32]{1,0:T(2,128)S(1)}, f32[2,32]{1,0:T(2,128)}, u32[]{:S(2)}) copy-start(f32[2,32]{1,0:T(2,128)} %param.8) | copy-start | bytes 772
  9.7 28.6 %copy-start.10 = (f32[15,32]{1,0:T(8,128)S(1)}, f32[15,32]{1,0:T(8,128)}, u32[]{:S(2)}) copy-start(f32[15,32]{1,0:T(8,128)} %param.9) | copy-start | bytes 5764
  12.6 25.6 %collective-permute-start.1 = (f32[4,3,2,8,1536]{4,3,2,1,0:T(8,128)}, f32[4,3,2,8,1536]{4,3,2,1,0:T(8,128)S(1)}, u32[]{:S(2)}, u32[]{:S(2)}) collective-permute-start(f32[4,3,2,8,1536]{4,3,2,1,0:T(8,128)} %get-tuple-element.33), channel_id=1, source_target_pairs={{4,0},{8,4},{12,8},{16,12},{20,16},{24,20},{28,24},{5,1},{9,5},{13... | collective-permute-start | bytes 3538952 | tf_op jit(solution)/shard_map/ppermute | solution.py:436
  14.6 23.7 %collective-permute-start = (f32[4,3,2,8,1536]{4,3,2,1,0:T(8,128)S(1)}, f32[4,3,2,8,1536]{4,3,2,1,0:T(8,128)S(1)}, u32[]{:S(2)}, u32[]{:S(2)}) collective-permute-start(f32[4,3,2,8,1536]{4,3,2,1,0:T(8,128)S(1)} %get-tuple-element.34), channel_id=1, source_target_pairs={{0,4},{4,8},{8,12},{12,16},{16,20},{20,24},{24,28},{1,5},{5,9},{9,... | collective-permute-start | bytes 3538952 | tf_op jit(solution)/shard_map/ppermute | solution.py:435
  38.3 17.9 %copy-start.2 = (f32[2,8,128]{2,1,0:T(8,128)}, f32[2,8,128]{2,1,0:T(8,128)S(1)}, u32[]{:S(2)}) copy-start(f32[2,8,128]{2,1,0:T(8,128)S(1)} %broadcast_in_dim.54.weight_ref) | copy-start | bytes 24580
  38.5 2.3 copy-start
  56.2 0.6 copy-start.4
  56.8 22.8 %collective-permute-start.2 = (f32[2,32,1536]{2,1,0:T(8,128)S(1)}, f32[2,32,1536]{2,1,0:T(8,128)S(1)}, u32[]{:S(2)}, u32[]{:S(2)}) collective-permute-start(f32[2,32,1536]{2,1,0:T(8,128)S(1)} %get-tuple-element.17), channel_id=1, source_target_pairs={{0,1},{1,0},{2,3},{3,2},{4,5},{5,4},{6,7},{7,6},{8,9},{9,8},{10,11... | collective-permute-start | bytes 1179656 | tf_op jit(solution)/shard_map/ppermute | solution.py:428
  79.7 10.3 %copy-start.6 = (f32[2,32,1536]{2,1,0:T(8,128)}, f32[2,32,1536]{2,1,0:T(8,128)S(1)}, u32[]{:S(2)}) copy-start(f32[2,32,1536]{2,1,0:T(8,128)S(1)} %collective-permute-done.2.refs_0_) | copy-start | bytes 1179652
  90.0 11.2 %copy-start.9 = (f32[2,32,1536]{2,1,0:T(8,128)S(1)}, f32[2,32,1536]{2,1,0:T(8,128)}, u32[]{:S(2)}) copy-start(f32[2,32,1536]{2,1,0:T(8,128)} %get-tuple-element.22) | copy-start | bytes 1179652
  90.0 11.2 %copy-start.11 = (s32[1536]{0:T(1024)S(1)}, s32[1536]{0:T(1024)}, u32[]{:S(2)}) copy-start(s32[1536]{0:T(1024)} %param.12) | copy-start | bytes 18436
  90.0 160.1 %all-to-all-start.1 = ((f32[4,4,32,1536]{3,2,1,0:T(8,128)}), f32[4,4,32,1536]{3,2,1,0:T(8,128)S(1)}, u32[]{:S(2)}, u32[]{:S(2)}) async-start(f32[4,4,32,1536]{3,2,1,0:T(8,128)} %get-tuple-element.19), calls=%async_computation.1 | async-start | bytes 6291456 | tf_op jit(solution)/shard_map/all_to_all | solution.py:425
  98.8 104.7 %collective-permute-start.3 = (f32[2,32,1536]{2,1,0:T(8,128)}, f32[2,32,1536]{2,1,0:T(8,128)S(1)}, u32[]{:S(2)}, u32[]{:S(2)}) collective-permute-start(f32[2,32,1536]{2,1,0:T(8,128)} %get-tuple-element.21), channel_id=1, source_target_pairs={{0,2},{1,3},{2,0},{3,1},{4,6},{5,7},{6,4},{7,5},{8,10},{9,11},{10,... | collective-permute-start | bytes 1179656 | tf_op jit(solution)/shard_map/ppermute | solution.py:428
  101.2 102.4 %collective-permute-start.4 = (f32[2,32,1536]{2,1,0:T(8,128)S(1)}, f32[2,32,1536]{2,1,0:T(8,128)S(1)}, u32[]{:S(2)}, u32[]{:S(2)}) collective-permute-start(f32[2,32,1536]{2,1,0:T(8,128)S(1)} %copy-done.9), channel_id=1, source_target_pairs={{0,3},{1,2},{2,1},{3,0},{4,7},{5,6},{6,5},{7,4},{8,11},{9,10},{10,... | collective-permute-start | bytes 1179656 | tf_op jit(solution)/shard_map/ppermute | solution.py:428
  101.2 66.6 %collective-permute-start.8 = (s32[1536]{0:T(1024)S(1)}, s32[1536]{0:T(1024)S(1)}, u32[]{:S(2)}, u32[]{:S(2)}) collective-permute-start(s32[1536]{0:T(1024)S(1)} %copy-done.11), channel_id=1, source_target_pairs={{0,1},{1,0},{2,3},{3,2},{4,5},{5,4},{6,7},{7,6},{8,9},{9,8},{10,11... | collective-permute-start | bytes 18440 | tf_op jit(solution)/shard_map/ppermute | solution.py:428
  103.2 100.2 %collective-permute-start.10 = (s32[1536]{0:T(1024)S(1)}, s32[1536]{0:T(1024)S(1)}, u32[]{:S(2)}, u32[]{:S(2)}) collective-permute-start(s32[1536]{0:T(1024)S(1)} %copy-done.11), channel_id=1, source_target_pairs={{0,3},{1,2},{2,1},{3,0},{4,7},{5,6},{6,5},{7,4},{8,11},{9,10},{10,... | collective-permute-start | bytes 18440 | tf_op jit(solution)/shard_map/ppermute | solution.py:428
  104.7 98.8 %collective-permute-start.9 = (s32[1536]{0:T(1024)S(1)}, s32[1536]{0:T(1024)S(1)}, u32[]{:S(2)}, u32[]{:S(2)}) collective-permute-start(s32[1536]{0:T(1024)S(1)} %copy-done.11), channel_id=1, source_target_pairs={{0,2},{1,3},{2,0},{3,1},{4,6},{5,7},{6,4},{7,5},{8,10},{9,11},{10,... | collective-permute-start | bytes 18440 | tf_op jit(solution)/shard_map/ppermute | solution.py:428
  203.5 13.3 %copy-start.13 = (f32[4,4,1536]{2,1,0:T(4,128)S(1)}, f32[4,4,1536]{2,1,0:T(4,128)}, u32[]{:S(2)}) copy-start(f32[4,4,1536]{2,1,0:T(4,128)} %get-tuple-element.28) | copy-start | bytes 294916
  203.5 14.1 %copy-start.5 = (f32[4,4,1536]{2,1,0:T(4,128)S(1)}, f32[4,4,1536]{2,1,0:T(4,128)}, u32[]{:S(2)}) copy-start(f32[4,4,1536]{2,1,0:T(4,128)} %copy-done.4) | copy-start | bytes 294916
  203.5 46.5 %copy-start.3 = (s32[3]{0:T(128)S(1)}, s32[3]{0:T(128)}, u32[]{:S(2)}) copy-start(s32[3]{0:T(128)} %pad_add_fusion.1.me_ref) | copy-start | bytes 40
  203.6 0.8 copy-start.7
  204.3 0.7 copy-start.8
  213.1 17.9 %collective-permute-start.5 = (f32[2,32,1536]{2,1,0:T(8,128)}, f32[2,32,1536]{2,1,0:T(8,128)S(1)}, u32[]{:S(2)}, u32[]{:S(2)}) collective-permute-start(f32[2,32,1536]{2,1,0:T(8,128)} %get-tuple-element.24), channel_id=1, source_target_pairs={{0,1},{1,0},{2,3},{3,2},{4,5},{5,4},{6,7},{7,6},{8,9},{9,8},{10,11... | collective-permute-start | bytes 1179656 | tf_op jit(solution)/shard_map/ppermute | solution.py:428
  214.8 38.8 %collective-permute-start.6 = (f32[2,32,1536]{2,1,0:T(8,128)}, f32[2,32,1536]{2,1,0:T(8,128)}, u32[]{:S(2)}, u32[]{:S(2)}) collective-permute-start(f32[2,32,1536]{2,1,0:T(8,128)} %get-tuple-element.25), channel_id=1, source_target_pairs={{0,2},{1,3},{2,0},{3,1},{4,6},{5,7},{6,4},{7,5},{8,10},{9,11},{10,... | collective-permute-start | bytes 1179656 | tf_op jit(solution)/shard_map/ppermute | solution.py:428
  215.2 38.4 %collective-permute-start.7 = (f32[2,32,1536]{2,1,0:T(8,128)}, f32[2,32,1536]{2,1,0:T(8,128)}, u32[]{:S(2)}, u32[]{:S(2)}) collective-permute-start(f32[2,32,1536]{2,1,0:T(8,128)} %get-tuple-element.26), channel_id=1, source_target_pairs={{0,3},{1,2},{2,1},{3,0},{4,7},{5,6},{6,5},{7,4},{8,11},{9,10},{10,... | collective-permute-start | bytes 1179656 | tf_op jit(solution)/shard_map/ppermute | solution.py:428
  231.0 1.2 collective-permute-start.11
  232.2 3.7 %collective-permute-start.12 = (f32[4,4,64]{2,1,0:T(4,128)S(1)}, f32[4,4,64]{2,1,0:T(4,128)S(1)}, u32[]{:S(2)}, u32[]{:S(2)}) collective-permute-start(f32[4,4,64]{2,1,0:T(4,128)S(1)} %add.44), channel_id=1, source_target_pairs={{0,8},{4,12},{8,0},{12,4},{16,24},{20,28},{24,16},{28,20},{1,9},{5... | collective-permute-start | bytes 12296 | tf_op jit(solution)/shard_map/ppermute | solution.py:475
  235.9 3.7 %collective-permute-start.13 = (f32[4,4,64]{2,1,0:T(4,128)S(1)}, f32[4,4,64]{2,1,0:T(4,128)S(1)}, u32[]{:S(2)}, u32[]{:S(2)}) collective-permute-start(f32[4,4,64]{2,1,0:T(4,128)S(1)} %add.45), channel_id=1, source_target_pairs={{0,16},{4,20},{8,24},{12,28},{16,0},{20,4},{24,8},{28,12},{1,17},{... | collective-permute-start | bytes 12296 | tf_op jit(solution)/shard_map/ppermute | solution.py:475
  239.5 4.0 %collective-permute-start.14 = (f32[4,4,64]{2,1,0:T(4,128)S(1)}, f32[4,4,64]{2,1,0:T(4,128)S(1)}, u32[]{:S(2)}, u32[]{:S(2)}) collective-permute-start(f32[4,4,64]{2,1,0:T(4,128)S(1)} %add.46), channel_id=1, source_target_pairs={{0,1},{1,0},{2,3},{3,2},{4,5},{5,4},{6,7},{7,6},{8,9},{9,8},{10,11... | collective-permute-start | bytes 12296 | tf_op jit(solution)/shard_map/ppermute | solution.py:475
  243.5 5.9 %collective-permute-start.15 = (f32[4,4,64]{2,1,0:T(4,128)S(1)}, f32[4,4,64]{2,1,0:T(4,128)S(1)}, u32[]{:S(2)}, u32[]{:S(2)}) collective-permute-start(f32[4,4,64]{2,1,0:T(4,128)S(1)} %add.47), channel_id=1, source_target_pairs={{0,2},{1,3},{2,0},{3,1},{4,6},{5,7},{6,4},{7,5},{8,10},{9,11},{10,... | collective-permute-start | bytes 12296 | tf_op jit(solution)/shard_map/ppermute | solution.py:475
  250.1 3.5 %copy-start.1 = (f32[2,32,1536]{2,1,0:T(8,128)S(1)}, f32[2,32,1536]{2,1,0:T(8,128)}, u32[]{:S(2)}) copy-start(f32[2,32,1536]{2,1,0:T(8,128)} %get-tuple-element.23) | copy-start | bytes 1179652

commit v7 on v6

--- a/solution.py
+++ b/solution.py
@@ -216,11 +216,17 @@
     return lower + upper
 
 
-def filter_main_kernel(me_ref, table_hbm, weight_ref, lines_hbm, out_hbm, shear_ref, *scratch):
-    line_ref, wave_ref, table_ref, table_sem, sems = scratch
-    count = line_ref.shape[0]
-    me = me_ref[0]
-    copies = start_all([pltpu.make_async_copy(lines_hbm.at[x], line_ref.at[x], sems.at[x]) for x in range(count)])
+def filter_main_kernel(me_ref, table_hbm, weight_ref, field_hbm, *refs):
+    line_ref, wave_ref, table_ref, table_sem, sems = refs[-5:]
+    count, line_count, row_count, _ = line_ref.shape
+    received, (out_hbm, shear_ref) = refs[: count - 1], refs[count - 1 : count + 1]
+    me, mode, rows = me_ref[0], me_ref[1], pl.ds(pl.multiple_of(me_ref[2], PAD), row_count)
+    copies = [pltpu.make_async_copy(received[x - 1], line_ref.at[me ^ x], sems.at[x]) for x in range(1, count)]
+    for comp in range(line_count // 2):
+        target = line_ref.at[me, pl.ds(2 * comp, 2)]
+        sem = sems.at[0 if comp == 0 else count - 1 + comp]
+        copies.append(pltpu.make_async_copy(field_hbm.at[mode, comp, :, rows], target, sem))
+    start_all(copies)
     table_copy = pltpu.make_async_copy(table_hbm, table_ref, table_sem)
     table_copy.start()
     wait_all(copies)
@@ -232,14 +238,11 @@
     wait_all(copies)
 
 
-def filter_last_kernel(me_ref, table_hbm, field_hbm, *refs):
+def filter_last_kernel(me_ref, table_hbm, lines_hbm, *refs):
     line_ref, wave_ref, table_ref, table_sem, sems = refs[-5:]
-    count, _, row_count, _ = line_ref.shape
-    received, sent = refs[: count - 1], refs[count - 1 : 2 * count - 1]
-    me, mode, top = me_ref[0], me_ref[1], me_ref[2]
-    comp = field_hbm.shape[1] - 1
-    sources = (field_hbm.at[mode, comp, :, pl.ds(pl.multiple_of(top, PAD), row_count)],) + received
-    copies = start_all([pltpu.make_async_copy(sources[x], line_ref.at[me ^ x], sems.at[x]) for x in range(count)])
+    count = line_ref.shape[0]
+    sent, me = refs[:count], me_ref[0]
+    copies = start_all([pltpu.make_async_copy(lines_hbm.at[x], line_ref.at[x], sems.at[x]) for x in range(count)])
     table_copy = pltpu.make_async_copy(table_hbm, table_ref, table_sem)
     table_copy.start()
     wait_all(copies)
@@ -266,7 +269,7 @@
             pltpu.VMEM((TILES, rows, 2 * LANES), jnp.float32),
             pltpu.VMEM(tables.shape, tables.dtype),
             pltpu.SemaphoreType.DMA,
-            pltpu.SemaphoreType.DMA((count,)),
+            pltpu.SemaphoreType.DMA((count + line_count // 2,)),
         ],
         compiler_params=pltpu.CompilerParams(vmem_limit_bytes=FILTER_VMEM),
         cost_estimate=pl.CostEstimate(flops=flops, bytes_accessed=8 * count * rows * width, transcendentals=0),
@@ -274,23 +277,22 @@
     )
 
 
-def filter_main(lines, weight, spots, tables, part_count):
-    shear = jax.ShapeDtypeStruct((lines.shape[0], 2 * part_count, lines.shape[3]), jnp.float32)
-    out_shape = (jax.ShapeDtypeStruct(lines.shape, jnp.float32), shear)
-    ins = [SCALARS, HBM, WHOLE, HBM]
-    call = filter_call(
-        filter_main_kernel, "filter_main", lines.shape, tables, ins, (HBM, WHOLE), out_shape
-    )
-    return call(spots, tables, weight, lines)
-
-
-def filter_last(field, received, spots, tables):
+def filter_main(field, received, weight, spots, tables):
     count = len(received) + 1
-    shape = received[0].shape
-    out_shape = [jax.ShapeDtypeStruct(shape, jnp.float32)] * count
-    ins = [SCALARS] + [HBM] * (count + 1)
-    call = filter_call(filter_last_kernel, "filter_last", (count,) + shape, tables, ins, [HBM] * count, out_shape)
-    return call(spots, tables, field, *received)
+    block = (count,) + received[0].shape
+    shear = jax.ShapeDtypeStruct((count, 4, block[3]), jnp.float32)
+    out_shape = (jax.ShapeDtypeStruct(block, jnp.float32), shear)
+    ins = [SCALARS, HBM, WHOLE] + [HBM] * count
+    call = filter_call(filter_main_kernel, "filter_main", block, tables, ins, (HBM, WHOLE), out_shape)
+    return call(spots, tables, weight, field, *received)
+
+
+def filter_last(lines, spots, tables):
+    count = lines.shape[0]
+    out_shape = [jax.ShapeDtypeStruct(lines.shape[1:], jnp.float32)] * count
+    ins = [SCALARS, HBM, HBM]
+    call = filter_call(filter_last_kernel, "filter_last", lines.shape, tables, ins, [HBM] * count, out_shape)
+    return call(spots, tables, lines)
 
 
 def local_kernel(rate_ref, coef_ref, flow_ref, weight_ref, field_ref, low_ref, high_ref, out_ref, shear_ref, pad_ref):
@@ -427,15 +429,18 @@
     def swap(blocks):
         return [lax.ppermute(blocks[x], "span", pairs[x]) for x in range(span - 1, 0, -1)][::-1]
 
-    main = field[:, :last].reshape(mode_split, -1, row_split, line_rows, width)
-    main = exchange(main.transpose(0, 2, 1, 3, 4).reshape(span, -1, line_rows, width))
+    def main_block(x):
+        other = me ^ x
+        start = (other // row_split, 0, 0, other % row_split * line_rows, 0)
+        block = lax.dynamic_slice(field, start, (1, last, part_count, line_rows, width))
+        return block.reshape(-1, line_rows, width)
+
+    received = swap([None] + [main_block(x) for x in range(1, span)])
 
     forward = [(i, i + 1) for i in range(wall_count - 1)]
     backward = [(i + 1, i) for i in range(wall_count - 1)]
     low = lax.ppermute(field[:, :, :, row_count - PAD :], "wall", forward)
     high = lax.ppermute(field[:, :, :, :PAD], "wall", backward)
-    patches = jnp.stack([patch_of] + swap([patch_of] * span))
-    onehot = (patches[:, :, None] == jnp.arange(PATCH, dtype=jnp.int32)).astype(jnp.float32)
 
     lower = jnp.where(wall_index == 0, wall_coef[0], 0.0)
     upper = jnp.where(wall_index == wall_count - 1, wall_coef[1, ::-1], 0.0)
@@ -449,31 +454,32 @@
     flow = jnp.broadcast_to(mean_flow[:, :, None], (2, row_count, LANES))
     base, shear = local_terms(field, low, high, rate, coef, flow, weight)
 
-    def last_block(x):
-        other = me ^ x
-        start = (other // row_split, last, 0, other % row_split * line_rows, 0)
-        return lax.dynamic_slice(field, start, (1, 1, part_count, line_rows, width))[0, 0]
-
-    blocks = [last_block(x) for x in range(1, span)]
-    blocks = list(lax.optimization_barrier((tuple(blocks), base))[0])
-    received = swap([None] + blocks)
-
-    filtered, line_shear = filter_main(after(main, received[0]), line_weight, spots, tables, part_count)
+    lines = field[:, last].reshape(mode_split, -1, row_split, line_rows, width)
+    lines = lines.transpose(0, 2, 1, 3, 4).reshape(span, -1, line_rows, width)
+    lines = exchange(after(lines, base))
+
+    received[0] = after(received[0], base)
+    filtered, line_shear = filter_main(field, received, line_weight, spots, tables)
     back = exchange(filtered)
-    received[0] = after(received[0], filtered)
-    sent = filter_last(field, received, spots, tables)
-    returned = [sent[0]] + swap(sent)
+
+    patches, distance = after(patch_of, base)[None], 1
+    while distance < span:
+        patches = jnp.concatenate([patches, lax.ppermute(patches, "span", pairs[distance])])
+        distance *= 2
+    onehot = (patches[:, :, None] == jnp.arange(PATCH, dtype=jnp.int32)).astype(jnp.float32)
 
     highest = lax.Precision.HIGHEST
     grad = jnp.einsum("mwz,zq->mwq", shear, onehot[0], precision=highest)
     line_grad = jnp.einsum("xwz,xzq->wq", line_shear, onehot, precision=highest)
     mine = jnp.arange(mode_count) == me // row_split
-    grad = after(grad + jnp.where(mine[:, None, None], line_grad, 0.0), returned[1])
+    grad = after(grad + jnp.where(mine[:, None, None], line_grad, 0.0), lines)
     for axis, count in (("wall", wall_count), ("span", span)):
         distance = 1
         while distance < count:
             grad = grad + lax.ppermute(grad, axis, [(i, i ^ distance) for i in range(count)])
             distance *= 2
+    sent = filter_last(after(lines, grad), spots, tables)
+    returned = [sent[0]] + swap(sent)
     wall_grad = grad.reshape(mode_count, 2, part_count, PATCH).transpose(1, 0, 2, 3)
 
     result = add_components(base, [back], spots, span, row_split, (0, last))

time: 262 us -> 308 us (1.18); the launches traced: 257 us -> 306 us
  waiting for transfers between devices: 162 us -> 218 us
  starting transfers between devices: 34.2 us -> 30.9 us
    ppermute x0 -> x2, waiting for transfers between devices: none -> 67.1 us  [on_device(): lax.ppermute(patches, 'span', pairs[distance])]
    ppermute x9 -> x6, waiting for transfers between devices: 133 us -> 124 us  [swap(): lax.ppermute(blocks[x], 'span', pairs[x])]
    all_to_all x2, starting transfers between devices: 14.1 us -> 9.01 us  [exchange(): return lax.all_to_all(lines, 'span', split_axis=0, concat_axis=0)]
    slice x1 -> x0, local copies, waits for them, and re-layouts: 3.8 us -> none  [on_device(): main = field[:, :last].reshape(mode_split, -1, row_split, line_rows, width)]
    ppermute x5, waiting for transfers between devices: 13 us -> 9.36 us  [on_device(): lax.ppermute(grad, axis, [(i, i ^ distance) for i in range(count)])]
    ppermute x9 -> x6, starting transfers between devices: 10.4 us -> 7.13 us  [swap(): lax.ppermute(blocks[x], 'span', pairs[x])]
    ppermute x5, starting transfers between devices: 5.42 us -> 8.63 us  [on_device(): lax.ppermute(grad, axis, [(i, i ^ distance) for i in range(count)])]
  transfers between devices with their start and end apart: 18 -> 17, of which waited for: 10 -> 14; matrix products, arithmetic and copies ran while one was open for 4% -> 2% of each run, Pallas kernels for 10% -> 7%
where the time goes in v7:
time: 308 us; the launch traced here: 306 us
  waiting for transfers between devices  218 us (71%)
  Pallas kernels  41.1 us (13%)
  starting transfers between devices  30.9 us (10%)
  local copies, waits for them, and re-layouts  12.6 us (4%)
    ppermute x6, waiting for transfers between devices, swap(): lax.ppermute(blocks[x], 'span', pairs[x])  124 us
    ppermute x2, waiting for transfers between devices, on_device(): lax.ppermute(patches, 'span', pairs[distance])  67.1 us
    ppermute x1, waiting for transfers between devices, on_device(): high = lax.ppermute(field[:, :, :, :PAD], 'wall', backward)  17.8 us
    pallas_call x1, Pallas kernels, local_terms(): pl.pallas_call(local_kernel, grid=(mode_count,), out_shape=(jax.ShapeDtyp...  15.4 us
    pallas_call x1, Pallas kernels, filter_main(): return call(spots, tables, weight, field, *received)  11.3 us
    ppermute x5, waiting for transfers between devices, on_device(): lax.ppermute(grad, axis, [(i, i ^ distance) for i in range(count)])  9.36 us
    all_to_all x2, starting transfers between devices, exchange(): return lax.all_to_all(lines, 'span', split_axis=0, concat_axis=0)  9.01 us
    ppermute x5, starting transfers between devices, on_device(): lax.ppermute(grad, axis, [(i, i ^ distance) for i in range(count)])  8.63 us
  transfers between devices with their start and end apart: 17, of which 14 were waited for; matrix products, arithmetic and copies ran while one was open for 2% of the time, Pallas kernels for 7%

profile of v7, /device:TPU:10, one launch (start us, length us, event | category | flops | bytes accessed | tf_op | source)
XLA Modules:
  0.0 305.9 jit_solution(3538552375943363353)
XLA Ops:
  0.6 0.0 copy-start.11
  0.6 0.0 copy-start.13
  0.6 2.9 fusion
  3.5 1.9 collective-permute-start.1
  5.4 2.4 collective-permute-start
  7.8 0.0 copy-done.11
  7.9 0.1 rev.3
  8.0 0.0 copy-done.13
  8.0 0.0 copy-start.10
  8.0 0.0 copy-start.8
  8.0 2.7 slice_bitcast_fusion
  10.7 17.8 %collective-permute-done.1.high_ref = f32[4,3,2,8,1536]{4,3,2,1,0:T(8,128)S(1)} collective-permute-done((f32[4,3,2,8,1536]{4,3,2,1,0:T(8,128)}, f32[4,3,2,8,1536]{4,3,2,1,0:T(8,128)S(1)}, u32[]{:S(2)}, u32[]{:S(2)}) %collective-permute-start.1) | collective-permute-done | bytes 1179680 | tf_op jit(solution)/shard_map/ppermute | solution.py:443
  28.5 0.0 collective-permute-done.low_ref
  28.5 0.1 broadcast_in_dim.57.weight_ref
  28.6 0.1 broadcast_in_dim.55.flow_ref
  28.7 0.1 broadcast_in_dim.54.coef_ref
  28.8 0.0 copy-start
  28.8 2.3 copy-done
  31.2 15.4 %local_terms.1 = (f32[4,3,2,32,1536]{4,3,2,1,0:T(8,128)}, f32[4,4,1536]{2,1,0:T(4,128)S(1)}) custom-call(f32[4]{0:T(128)S(1)} %convert_multiply_fusion.rate_ref, f32[15,32,128]{2,1,0:T(8,128)S(1)} %broadcast_in_dim.54.coef_ref, f32[2,32,128]{2,1,0:T(8,128)S(1)} %broadcast_in_dim.55.flow_ref, f32[2,8,128]{2,1,0:T(8,128)S(1)} %broadcast_in_dim.57.weight_ref, ...), custom_call_target="tpu_custom_call" | custom-call | flops 47185920 | bytes 11796480 | tf_op jit(solution)/shard_map/local_terms/pallas_call | solution.py:337
  46.5 5.3 %all-to-all-start.1 = ((f32[4,2,32,1536]{3,2,1,0:T(8,128)}), f32[4,2,32,1536]{3,2,1,0:T(8,128)S(1)}, u32[]{:S(2)}, u32[]{:S(2)}) async-start(f32[4,2,32,1536]{3,2,1,0:T(8,128)} %slice_bitcast_fusion), calls=%async_computation.1 | async-start | bytes 3145728 | tf_op jit(solution)/shard_map/all_to_all | solution.py:427
  51.9 1.8 constant_dynamic-slice_fusion
  53.6 0.1 collective-permute-start.2
  53.7 2.9 collective-permute-start.3
  56.6 0.6 collective-permute-start.4
  57.2 0.6 pad_add_fusion.2.me_ref
  57.8 45.0 %collective-permute-done.2.refs_0_ = f32[4,32,1536]{2,1,0:T(8,128)S(1)} collective-permute-done((f32[4,32,1536]{2,1,0:T(8,128)S(1)}, f32[4,32,1536]{2,1,0:T(8,128)S(1)}, u32[]{:S(2)}, u32[]{:S(2)}) %collective-permute-start.2) | collective-permute-done | bytes 786464 | tf_op jit(solution)/shard_map/ppermute | solution.py:430
  102.7 31.7 %collective-permute-done.3.refs_1_ = f32[4,32,1536]{2,1,0:T(8,128)S(1)} collective-permute-done((f32[4,32,1536]{2,1,0:T(8,128)S(1)}, f32[4,32,1536]{2,1,0:T(8,128)S(1)}, u32[]{:S(2)}, u32[]{:S(2)}) %collective-permute-start.3) | collective-permute-done | bytes 786464 | tf_op jit(solution)/shard_map/ppermute | solution.py:430
  134.4 20.8 %collective-permute-done.4.refs_2_ = f32[4,32,1536]{2,1,0:T(8,128)S(1)} collective-permute-done((f32[4,32,1536]{2,1,0:T(8,128)S(1)}, f32[4,32,1536]{2,1,0:T(8,128)S(1)}, u32[]{:S(2)}, u32[]{:S(2)}) %collective-permute-start.4) | collective-permute-done | bytes 786464 | tf_op jit(solution)/shard_map/ppermute | solution.py:430
  155.2 0.0 copy-done.6
  155.2 0.9 copy-done.7
  156.0 11.3 %filter_main.1 = (f32[4,4,32,1536]{3,2,1,0:T(8,128)}, f32[4,4,1536]{2,1,0:T(4,128)}) custom-call(s32[3]{0:T(128)} %pad_add_fusion.2.me_ref, bf16[24,2,256,256]{3,2,1,0:T(8,128)(2,1)} %constant.93.clone.table_hbm, f32[2,8,128]{2,1,0:T(8,128)} %copy-done.2, f32[4,3,2,32,1536]{4,3,2,1,0:T(8,128)} %field_hbm.1, f32[4,32,1536]{2,1,0:T(8,128)} %copy-done.5, ...), custom_call_target="tpu_custom_call" | custom-call | flops 1207959552 | bytes 6291456 | tf_op jit(solution)/shard_map/filter_main/pallas_call | solution.py:287
  167.3 0.0 all-to-all-done.1.lines_hbm
  167.3 0.0 copy-start.4
  167.3 0.0 copy-start.9
  167.4 1.1 copy-done.4
  168.5 3.7 %all-to-all-start = ((f32[4,4,32,1536]{3,2,1,0:T(8,128)}), f32[4,4,32,1536]{3,2,1,0:T(8,128)S(1)}, u32[]{:S(2)}, u32[]{:S(2)}) async-start(f32[4,4,32,1536]{3,2,1,0:T(8,128)} %get-tuple-element.17), calls=%async_computation | async-start | bytes 6291456 | tf_op jit(solution)/shard_map/all_to_all | solution.py:427
  172.2 0.1 collective-permute-start.5
  172.3 51.9 %collective-permute-done.5 = s32[1,1536]{1,0:T(1,128)S(1)} collective-permute-done((s32[1,1536]{1,0:T(1,128)S(1)}, s32[1,1536]{1,0:T(1,128)S(1)}, u32[]{:S(2)}, u32[]{:S(2)}) %collective-permute-start.5) | collective-permute-done | bytes 6176 | tf_op jit(solution)/shard_map/ppermute | solution.py:467
  224.2 1.8 collective-permute-start.6
  226.0 15.2 %collective-permute-done.6 = s32[2,1536]{1,0:T(2,128)S(1)} collective-permute-done((s32[2,1536]{1,0:T(2,128)S(1)}, s32[2,1536]{1,0:T(2,128)S(1)}, u32[]{:S(2)}, u32[]{:S(2)}) %collective-permute-start.6) | collective-permute-done | bytes 12320 | tf_op jit(solution)/shard_map/ppermute | solution.py:467
  241.2 0.8 convolution_bitcast_fusion
  242.0 0.2 iota_compare_fusion
  242.3 0.3 convolution_add_fusion
  242.6 0.4 collective-permute-start.7
  243.0 0.8 collective-permute-done.7
  243.8 0.0 collective-permute-start.8
  243.8 3.6 %collective-permute-done.8 = f32[4,4,64]{2,1,0:T(4,128)S(1)} collective-permute-done((f32[4,4,64]{2,1,0:T(4,128)S(1)}, f32[4,4,64]{2,1,0:T(4,128)S(1)}, u32[]{:S(2)}, u32[]{:S(2)}) %collective-permute-start.8) | collective-permute-done | bytes 4128 | tf_op jit(solution)/shard_map/ppermute | solution.py:479
  247.5 2.8 collective-permute-start.9
  250.3 1.6 collective-permute-done.9
  251.9 2.4 collective-permute-start.10
  254.4 1.6 collective-permute-done.10
  256.0 3.0 collective-permute-start.11
  259.0 1.6 collective-permute-done.11
  260.6 7.8 %filter_last.1 = (f32[2,32,1536]{2,1,0:T(8,128)}, f32[2,32,1536]{2,1,0:T(8,128)}, f32[2,32,1536]{2,1,0:T(8,128)}, f32[2,32,1536]{2,1,0:T(8,128)}) custom-call(s32[3]{0:T(128)} %pad_add_fusion.2.me_ref, bf16[24,2,256,256]{3,2,1,0:T(8,128)(2,1)} %constant.93.clone.table_hbm, f32[4,2,32,1536]{3,2,1,0:T(8,128)} %copy-done.4), custom_call_target="tpu_custom_call" | custom-call | flops 603979776 | bytes 3145728 | tf_op jit(solution)/shard_map/filter_last/pallas_call | solution.py:295
  268.4 2.0 collective-permute-start.12
  270.4 1.0 collective-permute-start.13
  271.4 0.5 collective-permute-start.14
  272.0 0.6 copy.15
  272.6 0.0 all-to-all-done
  272.6 3.5 %add_components.2.base_hbm = f32[4,3,2,32,1536]{4,3,2,1,0:T(8,128)} custom-call(s32[3]{0:T(128)S(1)} %copy-done.3, f32[4,3,2,32,1536]{4,3,2,1,0:T(8,128)} %get-tuple-element.15.base_hbm, f32[4,2,2,32,1536]{4,3,2,1,0:T(8,128)S(1)} %bitcast.25), custom_call_target="tpu_custom_call", output_to_operand_aliasing={{}: (1, {})} | custom-call | flops 786432 | bytes 9437184 | tf_op jit(solution)/shard_map/add_components/pallas_call | solution.py:394
  276.1 7.0 %collective-permute-done.12 = f32[2,32,1536]{2,1,0:T(8,128)S(1)} collective-permute-done((f32[2,32,1536]{2,1,0:T(8,128)}, f32[2,32,1536]{2,1,0:T(8,128)S(1)}, u32[]{:S(2)}, u32[]{:S(2)}) %collective-permute-start.12) | collective-permute-done | bytes 393248 | tf_op jit(solution)/shard_map/ppermute | solution.py:430
  283.1 13.9 %collective-permute-done.13 = f32[2,32,1536]{2,1,0:T(8,128)} collective-permute-done((f32[2,32,1536]{2,1,0:T(8,128)}, f32[2,32,1536]{2,1,0:T(8,128)}, u32[]{:S(2)}, u32[]{:S(2)}) %collective-permute-start.13) | collective-permute-done | bytes 393248 | tf_op jit(solution)/shard_map/ppermute | solution.py:430
  297.0 5.7 %collective-permute-done.14 = f32[2,32,1536]{2,1,0:T(8,128)} collective-permute-done((f32[2,32,1536]{2,1,0:T(8,128)}, f32[2,32,1536]{2,1,0:T(8,128)}, u32[]{:S(2)}, u32[]{:S(2)}) %collective-permute-start.14) | collective-permute-done | bytes 393248 | tf_op jit(solution)/shard_map/ppermute | solution.py:430
  302.7 3.2 %add_components.3 = f32[4,3,2,32,1536]{4,3,2,1,0:T(8,128)} custom-call(s32[3]{0:T(128)S(1)} %copy-done.3, f32[4,3,2,32,1536]{4,3,2,1,0:T(8,128)} %add_components.2.base_hbm, f32[1,2,32,1536]{3,2,1,0:T(8,128)S(1)} %bitcast.26, f32[1,2,32,1536]{3,2,1,0:T(8,128)S(1)} %bitcast.27, f32[1,2,32,1536]{3,2,1,0:T(8,128)} %bitcast.11.refs_2_, ...), custom_call_target="tpu_custom_call", output_to_operand_aliasing={{}: (1, {})} | custom-call | flops 393216 | bytes 4718592 | tf_op jit(solution)/shard_map/add_components/pallas_call | solution.py:394
  (28 shorter events, 0.1 us)
Async XLA Ops:
  0.6 7.2 %copy-start.11 = (f32[2,8]{1,0:T(2,128)S(1)}, f32[2,8]{1,0:T(2,128)}, u32[]{:S(2)}) copy-start(f32[2,8]{1,0:T(2,128)} %param.10) | copy-start | bytes 196
  0.6 7.4 %copy-start.13 = (s32[4]{0:T(128)S(1)}, s32[4]{0:T(128)}, u32[]{:S(2)}) copy-start(s32[4]{0:T(128)} %param.11) | copy-start | bytes 52
  3.5 25.0 %collective-permute-start.1 = (f32[4,3,2,8,1536]{4,3,2,1,0:T(8,128)}, f32[4,3,2,8,1536]{4,3,2,1,0:T(8,128)S(1)}, u32[]{:S(2)}, u32[]{:S(2)}) collective-permute-start(f32[4,3,2,8,1536]{4,3,2,1,0:T(8,128)} %get-tuple-element.31), channel_id=1, source_target_pairs={{4,0},{8,4},{12,8},{16,12},{20,16},{24,20},{28,24},{5,1},{9,5},{13... | collective-permute-start | bytes 3538952 | tf_op jit(solution)/shard_map/ppermute | solution.py:443
  5.4 23.1 %collective-permute-start = (f32[4,3,2,8,1536]{4,3,2,1,0:T(8,128)S(1)}, f32[4,3,2,8,1536]{4,3,2,1,0:T(8,128)S(1)}, u32[]{:S(2)}, u32[]{:S(2)}) collective-permute-start(f32[4,3,2,8,1536]{4,3,2,1,0:T(8,128)S(1)} %get-tuple-element.32), channel_id=1, source_target_pairs={{0,4},{4,8},{8,12},{12,16},{16,20},{20,24},{24,28},{1,5},{5,9},{9,... | collective-permute-start | bytes 3538952 | tf_op jit(solution)/shard_map/ppermute | solution.py:442
  8.0 20.6 %copy-start.10 = (f32[2,32]{1,0:T(2,128)S(1)}, f32[2,32]{1,0:T(2,128)}, u32[]{:S(2)}) copy-start(f32[2,32]{1,0:T(2,128)} %param.8) | copy-start | bytes 772
  8.0 20.7 %copy-start.8 = (f32[15,32]{1,0:T(8,128)S(1)}, f32[15,32]{1,0:T(8,128)}, u32[]{:S(2)}) copy-start(f32[15,32]{1,0:T(8,128)} %param.9) | copy-start | bytes 5764
  28.6 17.9 %copy-start.2 = (f32[2,8,128]{2,1,0:T(8,128)}, f32[2,8,128]{2,1,0:T(8,128)S(1)}, u32[]{:S(2)}) copy-start(f32[2,8,128]{2,1,0:T(8,128)S(1)} %broadcast_in_dim.57.weight_ref) | copy-start | bytes 24580
  28.8 2.3 copy-start
  46.5 120.8 %all-to-all-start.1 = ((f32[4,2,32,1536]{3,2,1,0:T(8,128)}), f32[4,2,32,1536]{3,2,1,0:T(8,128)S(1)}, u32[]{:S(2)}, u32[]{:S(2)}) async-start(f32[4,2,32,1536]{3,2,1,0:T(8,128)} %slice_bitcast_fusion), calls=%async_computation.1 | async-start | bytes 3145728 | tf_op jit(solution)/shard_map/all_to_all | solution.py:427
  53.6 49.1 %collective-permute-start.2 = (f32[4,32,1536]{2,1,0:T(8,128)S(1)}, f32[4,32,1536]{2,1,0:T(8,128)S(1)}, u32[]{:S(2)}, u32[]{:S(2)}) collective-permute-start(f32[4,32,1536]{2,1,0:T(8,128)S(1)} %bitcast.30), channel_id=1, source_target_pairs={{0,1},{1,0},{2,3},{3,2},{4,5},{5,4},{6,7},{7,6},{8,9},{9,8},{10,11... | collective-permute-start | bytes 2359304 | tf_op jit(solution)/shard_map/ppermute | solution.py:430
  53.7 80.7 %collective-permute-start.3 = (f32[4,32,1536]{2,1,0:T(8,128)S(1)}, f32[4,32,1536]{2,1,0:T(8,128)S(1)}, u32[]{:S(2)}, u32[]{:S(2)}) collective-permute-start(f32[4,32,1536]{2,1,0:T(8,128)S(1)} %bitcast.29), channel_id=1, source_target_pairs={{0,2},{1,3},{2,0},{3,1},{4,6},{5,7},{6,4},{7,5},{8,10},{9,11},{10,... | collective-permute-start | bytes 2359304 | tf_op jit(solution)/shard_map/ppermute | solution.py:430
  56.6 98.6 %collective-permute-start.4 = (f32[4,32,1536]{2,1,0:T(8,128)S(1)}, f32[4,32,1536]{2,1,0:T(8,128)S(1)}, u32[]{:S(2)}, u32[]{:S(2)}) collective-permute-start(f32[4,32,1536]{2,1,0:T(8,128)S(1)} %bitcast.28), channel_id=1, source_target_pairs={{0,3},{1,2},{2,1},{3,0},{4,7},{5,6},{6,5},{7,4},{8,11},{9,10},{10,... | collective-permute-start | bytes 2359304 | tf_op jit(solution)/shard_map/ppermute | solution.py:430
  102.7 52.4 %copy-start.5 = (f32[4,32,1536]{2,1,0:T(8,128)}, f32[4,32,1536]{2,1,0:T(8,128)S(1)}, u32[]{:S(2)}) copy-start(f32[4,32,1536]{2,1,0:T(8,128)S(1)} %collective-permute-done.2.refs_0_) | copy-start | bytes 2359300
  134.4 20.8 %copy-start.6 = (f32[4,32,1536]{2,1,0:T(8,128)}, f32[4,32,1536]{2,1,0:T(8,128)S(1)}, u32[]{:S(2)}) copy-start(f32[4,32,1536]{2,1,0:T(8,128)S(1)} %collective-permute-done.3.refs_1_) | copy-start | bytes 2359300
  155.2 0.9 copy-start.7
  167.3 1.1 copy-start.4
  167.3 4.8 %copy-start.9 = (s32[1536]{0:T(1024)S(1)}, s32[1536]{0:T(1024)}, u32[]{:S(2)}) copy-start(s32[1536]{0:T(1024)} %param.12) | copy-start | bytes 18436
  167.4 73.9 %copy-start.12 = (f32[4,4,1536]{2,1,0:T(4,128)S(1)}, f32[4,4,1536]{2,1,0:T(4,128)}, u32[]{:S(2)}) copy-start(f32[4,4,1536]{2,1,0:T(4,128)} %get-tuple-element.21) | copy-start | bytes 294916
  168.5 104.1 %all-to-all-start = ((f32[4,4,32,1536]{3,2,1,0:T(8,128)}), f32[4,4,32,1536]{3,2,1,0:T(8,128)S(1)}, u32[]{:S(2)}, u32[]{:S(2)}) async-start(f32[4,4,32,1536]{3,2,1,0:T(8,128)} %get-tuple-element.17), calls=%async_computation | async-start | bytes 6291456 | tf_op jit(solution)/shard_map/all_to_all | solution.py:427
  172.2 52.0 %collective-permute-start.5 = (s32[1,1536]{1,0:T(1,128)S(1)}, s32[1,1536]{1,0:T(1,128)S(1)}, u32[]{:S(2)}, u32[]{:S(2)}) collective-permute-start(s32[1,1536]{1,0:T(1,128)S(1)} %broadcast_in_dim.58), channel_id=1, source_target_pairs={{0,1},{1,0},{2,3},{3,2},{4,5},{5,4},{6,7},{7,6},{8,9},{9,8},{10,11... | collective-permute-start | bytes 18440 | tf_op jit(solution)/shard_map/ppermute | solution.py:467
  224.2 17.0 %collective-permute-start.6 = (s32[2,1536]{1,0:T(2,128)S(1)}, s32[2,1536]{1,0:T(2,128)S(1)}, u32[]{:S(2)}, u32[]{:S(2)}) collective-permute-start(s32[2,1536]{1,0:T(2,128)S(1)} %pad_add_fusion.1), channel_id=1, source_target_pairs={{0,2},{1,3},{2,0},{3,1},{4,6},{5,7},{6,4},{7,5},{8,10},{9,11},{10,... | collective-permute-start | bytes 36872 | tf_op jit(solution)/shard_map/ppermute | solution.py:467
  242.6 1.2 collective-permute-start.7
  243.8 3.7 %collective-permute-start.8 = (f32[4,4,64]{2,1,0:T(4,128)S(1)}, f32[4,4,64]{2,1,0:T(4,128)S(1)}, u32[]{:S(2)}, u32[]{:S(2)}) collective-permute-start(f32[4,4,64]{2,1,0:T(4,128)S(1)} %add.44), channel_id=1, source_target_pairs={{0,8},{4,12},{8,0},{12,4},{16,24},{20,28},{24,16},{28,20},{1,9},{5... | collective-permute-start | bytes 12296 | tf_op jit(solution)/shard_map/ppermute | solution.py:479
  247.5 4.5 %collective-permute-start.9 = (f32[4,4,64]{2,1,0:T(4,128)S(1)}, f32[4,4,64]{2,1,0:T(4,128)S(1)}, u32[]{:S(2)}, u32[]{:S(2)}) collective-permute-start(f32[4,4,64]{2,1,0:T(4,128)S(1)} %add.45), channel_id=1, source_target_pairs={{0,16},{4,20},{8,24},{12,28},{16,0},{20,4},{24,8},{28,12},{1,17},{... | collective-permute-start | bytes 12296 | tf_op jit(solution)/shard_map/ppermute | solution.py:479
  251.9 4.1 %collective-permute-start.10 = (f32[4,4,64]{2,1,0:T(4,128)S(1)}, f32[4,4,64]{2,1,0:T(4,128)S(1)}, u32[]{:S(2)}, u32[]{:S(2)}) collective-permute-start(f32[4,4,64]{2,1,0:T(4,128)S(1)} %add.46), channel_id=1, source_target_pairs={{0,1},{1,0},{2,3},{3,2},{4,5},{5,4},{6,7},{7,6},{8,9},{9,8},{10,11... | collective-permute-start | bytes 12296 | tf_op jit(solution)/shard_map/ppermute | solution.py:479
  256.0 4.6 %collective-permute-start.11 = (f32[4,4,64]{2,1,0:T(4,128)S(1)}, f32[4,4,64]{2,1,0:T(4,128)S(1)}, u32[]{:S(2)}, u32[]{:S(2)}) collective-permute-start(f32[4,4,64]{2,1,0:T(4,128)S(1)} %add.47), channel_id=1, source_target_pairs={{0,2},{1,3},{2,0},{3,1},{4,6},{5,7},{6,4},{7,5},{8,10},{9,11},{10,... | collective-permute-start | bytes 12296 | tf_op jit(solution)/shard_map/ppermute | solution.py:479
  260.6 12.0 %copy-start.3 = (s32[3]{0:T(128)S(1)}, s32[3]{0:T(128)}, u32[]{:S(2)}) copy-start(s32[3]{0:T(128)} %pad_add_fusion.2.me_ref) | copy-start | bytes 40
  268.4 14.7 %collective-permute-start.12 = (f32[2,32,1536]{2,1,0:T(8,128)}, f32[2,32,1536]{2,1,0:T(8,128)S(1)}, u32[]{:S(2)}, u32[]{:S(2)}) collective-permute-start(f32[2,32,1536]{2,1,0:T(8,128)} %get-tuple-element.25), channel_id=1, source_target_pairs={{0,1},{1,0},{2,3},{3,2},{4,5},{5,4},{6,7},{7,6},{8,9},{9,8},{10,11... | collective-permute-start | bytes 1179656 | tf_op jit(solution)/shard_map/ppermute | solution.py:430
  270.4 26.6 %collective-permute-start.13 = (f32[2,32,1536]{2,1,0:T(8,128)}, f32[2,32,1536]{2,1,0:T(8,128)}, u32[]{:S(2)}, u32[]{:S(2)}) collective-permute-start(f32[2,32,1536]{2,1,0:T(8,128)} %get-tuple-element.26), channel_id=1, source_target_pairs={{0,2},{1,3},{2,0},{3,1},{4,6},{5,7},{6,4},{7,5},{8,10},{9,11},{10,... | collective-permute-start | bytes 1179656 | tf_op jit(solution)/shard_map/ppermute | solution.py:430
  271.4 31.3 %collective-permute-start.14 = (f32[2,32,1536]{2,1,0:T(8,128)}, f32[2,32,1536]{2,1,0:T(8,128)}, u32[]{:S(2)}, u32[]{:S(2)}) collective-permute-start(f32[2,32,1536]{2,1,0:T(8,128)} %get-tuple-element.27), channel_id=1, source_target_pairs={{0,3},{1,2},{2,1},{3,0},{4,7},{5,6},{6,5},{7,4},{8,11},{9,10},{10,... | collective-permute-start | bytes 1179656 | tf_op jit(solution)/shard_map/ppermute | solution.py:430
  272.6 30.2 %copy-start.1 = (f32[2,32,1536]{2,1,0:T(8,128)S(1)}, f32[2,32,1536]{2,1,0:T(8,128)}, u32[]{:S(2)}) copy-start(f32[2,32,1536]{2,1,0:T(8,128)} %get-tuple-element.24) | copy-start | bytes 1179652

commit v8 on v6

--- a/solution.py
+++ b/solution.py
@@ -20,6 +20,7 @@
 PAD = 8
 TILES = OUTER // 2
 FILTER_VMEM = 57_500_000
+TABLE_COPIES = 4
 
 QUARTER = (0, 4, 2, 1, 5, 9)
 KEPT = tuple(4 * q for q in QUARTER) + tuple(2 + 8 * t for t in range(6)) + tuple(4 * q + 1 for q in range(12))
@@ -157,7 +158,7 @@
     return x
 
 
-def filter_lines(line_ref, wave_ref, table_ref, table_copy):
+def filter_lines(line_ref, wave_ref, table_ref, table_copies):
     _, line_count, row_count, width = line_ref.shape
     pieces = width // LANES
     groups = row_count // PAD
@@ -185,8 +186,10 @@
         wave_ref[tile] = both[:rows] + both[rows:] + rest
         return 0
 
-    table_copy.wait()
-    lax.fori_loop(0, TILES, middle, 0, unroll=4)
+    step = TILES // len(table_copies)
+    for i, copy in enumerate(table_copies):
+        copy.wait()
+        lax.fori_loop(i * step, (i + 1) * step, middle, 0, unroll=3)
 
     def backward(step, _):
         line, rows, spot = spots(step)
@@ -216,15 +219,26 @@
     return lower + upper
 
 
-def filter_main_kernel(me_ref, table_hbm, weight_ref, lines_hbm, out_hbm, shear_ref, *scratch):
-    line_ref, wave_ref, table_ref, table_sem, sems = scratch
+def run_filter(table_hbm, lines_hbm, first, scratch):
+    line_ref, wave_ref, table_ref, table_sems, sems = scratch
+    count, line_count, _, _ = line_ref.shape
+    lines = pl.ds(first, line_count)
+    copies = [pltpu.make_async_copy(lines_hbm.at[x, lines], line_ref.at[x], sems.at[x]) for x in range(count)]
+    start_all(copies)
+    step = TILES // TABLE_COPIES
+    spans = [pl.ds(i * step, step) for i in range(TABLE_COPIES)]
+    table_copies = [
+        pltpu.make_async_copy(table_hbm.at[span], table_ref.at[span], table_sems.at[i]) for i, span in enumerate(spans)
+    ]
+    start_all(table_copies)
+    wait_all(copies)
+    filter_lines(line_ref, wave_ref, table_ref, table_copies)
+
+
+def filter_first_kernel(me_ref, table_hbm, weight_ref, lines_hbm, out_hbm, shear_ref, *scratch):
+    run_filter(table_hbm, lines_hbm, 0, scratch)
+    line_ref, sems, me = scratch[0], scratch[-1], me_ref[0]
     count = line_ref.shape[0]
-    me = me_ref[0]
-    copies = start_all([pltpu.make_async_copy(lines_hbm.at[x], line_ref.at[x], sems.at[x]) for x in range(count)])
-    table_copy = pltpu.make_async_copy(table_hbm, table_ref, table_sem)
-    table_copy.start()
-    wait_all(copies)
-    filter_lines(line_ref, wave_ref, table_ref, table_copy)
     copies = start_all([pltpu.make_async_copy(line_ref.at[x], out_hbm.at[x], sems.at[x]) for x in range(count)])
     for x in range(count):
         for spot, value in enumerate(wall_sums(line_ref.at[me ^ x], weight_ref)):
@@ -232,19 +246,12 @@
     wait_all(copies)
 
 
-def filter_last_kernel(me_ref, table_hbm, field_hbm, *refs):
-    line_ref, wave_ref, table_ref, table_sem, sems = refs[-5:]
-    count, _, row_count, _ = line_ref.shape
-    received, sent = refs[: count - 1], refs[count - 1 : 2 * count - 1]
-    me, mode, top = me_ref[0], me_ref[1], me_ref[2]
-    comp = field_hbm.shape[1] - 1
-    sources = (field_hbm.at[mode, comp, :, pl.ds(pl.multiple_of(top, PAD), row_count)],) + received
-    copies = start_all([pltpu.make_async_copy(sources[x], line_ref.at[me ^ x], sems.at[x]) for x in range(count)])
-    table_copy = pltpu.make_async_copy(table_hbm, table_ref, table_sem)
-    table_copy.start()
-    wait_all(copies)
-    filter_lines(line_ref, wave_ref, table_ref, table_copy)
-    wait_all(start_all([pltpu.make_async_copy(line_ref.at[me ^ x], sent[x], sems.at[x]) for x in range(count)]))
+def filter_rest_kernel(me_ref, table_hbm, lines_hbm, *refs):
+    sent, scratch = refs[:-5], refs[-5:]
+    line_ref, sems, me = scratch[0], scratch[-1], me_ref[0]
+    run_filter(table_hbm, lines_hbm, lines_hbm.shape[1] - line_ref.shape[1], scratch)
+    copies = [pltpu.make_async_copy(line_ref.at[me ^ x], sent[x], sems.at[x]) for x in range(len(sent))]
+    wait_all(start_all(copies))
 
 
 HBM = pl.BlockSpec(memory_space=pltpu.HBM)
@@ -265,7 +272,7 @@
             pltpu.VMEM(block, jnp.float32),
             pltpu.VMEM((TILES, rows, 2 * LANES), jnp.float32),
             pltpu.VMEM(tables.shape, tables.dtype),
-            pltpu.SemaphoreType.DMA,
+            pltpu.SemaphoreType.DMA((TABLE_COPIES,)),
             pltpu.SemaphoreType.DMA((count,)),
         ],
         compiler_params=pltpu.CompilerParams(vmem_limit_bytes=FILTER_VMEM),
@@ -274,23 +281,22 @@
     )
 
 
-def filter_main(lines, weight, spots, tables, part_count):
-    shear = jax.ShapeDtypeStruct((lines.shape[0], 2 * part_count, lines.shape[3]), jnp.float32)
-    out_shape = (jax.ShapeDtypeStruct(lines.shape, jnp.float32), shear)
+def filter_first(lines, weight, spots, tables):
+    block = (lines.shape[0], 2) + lines.shape[2:]
+    shear = jax.ShapeDtypeStruct((block[0], 4, block[3]), jnp.float32)
+    out_shape = (jax.ShapeDtypeStruct(block, jnp.float32), shear)
     ins = [SCALARS, HBM, WHOLE, HBM]
-    call = filter_call(
-        filter_main_kernel, "filter_main", lines.shape, tables, ins, (HBM, WHOLE), out_shape
-    )
+    call = filter_call(filter_first_kernel, "filter_first", block, tables, ins, (HBM, WHOLE), out_shape)
     return call(spots, tables, weight, lines)
 
 
-def filter_last(field, received, spots, tables):
-    count = len(received) + 1
-    shape = received[0].shape
-    out_shape = [jax.ShapeDtypeStruct(shape, jnp.float32)] * count
-    ins = [SCALARS] + [HBM] * (count + 1)
-    call = filter_call(filter_last_kernel, "filter_last", (count,) + shape, tables, ins, [HBM] * count, out_shape)
-    return call(spots, tables, field, *received)
+def filter_rest(lines, spots, tables):
+    count, line_count, row_count, width = lines.shape
+    block = (count, line_count - 2, row_count, width)
+    out_shape = [jax.ShapeDtypeStruct(block[1:], jnp.float32)] * count
+    ins = [SCALARS, HBM, HBM]
+    call = filter_call(filter_rest_kernel, "filter_rest", block, tables, ins, [HBM] * count, out_shape)
+    return call(spots, tables, lines)
 
 
 def local_kernel(rate_ref, coef_ref, flow_ref, weight_ref, field_ref, low_ref, high_ref, out_ref, shear_ref, pad_ref):
@@ -419,22 +425,24 @@
     pairs = [[(i, i ^ x) for i in range(span)] for x in range(span)]
     spots = jnp.stack([me, me // row_split, me % row_split * line_rows]).astype(jnp.int32)
 
-    last = comp_count - 1
-
     def exchange(lines):
         return lax.all_to_all(lines, "span", split_axis=0, concat_axis=0)
 
     def swap(blocks):
         return [lax.ppermute(blocks[x], "span", pairs[x]) for x in range(span - 1, 0, -1)][::-1]
 
-    main = field[:, :last].reshape(mode_split, -1, row_split, line_rows, width)
-    main = exchange(main.transpose(0, 2, 1, 3, 4).reshape(span, -1, line_rows, width))
+    lines = field.reshape(mode_split, -1, row_split, line_rows, width)
+    lines = exchange(lines.transpose(0, 2, 1, 3, 4).reshape(span, -1, line_rows, width))
 
     forward = [(i, i + 1) for i in range(wall_count - 1)]
     backward = [(i + 1, i) for i in range(wall_count - 1)]
     low = lax.ppermute(field[:, :, :, row_count - PAD :], "wall", forward)
     high = lax.ppermute(field[:, :, :, :PAD], "wall", backward)
-    patches = jnp.stack([patch_of] + swap([patch_of] * span))
+
+    patches, distance = patch_of[None], 1
+    while distance < span:
+        patches = jnp.concatenate([patches, lax.ppermute(patches, "span", pairs[distance])])
+        distance *= 2
     onehot = (patches[:, :, None] == jnp.arange(PATCH, dtype=jnp.int32)).astype(jnp.float32)
 
     lower = jnp.where(wall_index == 0, wall_coef[0], 0.0)
@@ -449,35 +457,22 @@
     flow = jnp.broadcast_to(mean_flow[:, :, None], (2, row_count, LANES))
     base, shear = local_terms(field, low, high, rate, coef, flow, weight)
 
-    def last_block(x):
-        other = me ^ x
-        start = (other // row_split, last, 0, other % row_split * line_rows, 0)
-        return lax.dynamic_slice(field, start, (1, 1, part_count, line_rows, width))[0, 0]
-
-    blocks = [last_block(x) for x in range(1, span)]
-    blocks = list(lax.optimization_barrier((tuple(blocks), base))[0])
-    received = swap([None] + blocks)
-
-    filtered, line_shear = filter_main(after(main, received[0]), line_weight, spots, tables, part_count)
+    lines = after(lines, base, patches)
+    filtered, line_shear = filter_first(lines, line_weight, spots, tables)
     back = exchange(filtered)
-    received[0] = after(received[0], filtered)
-    sent = filter_last(field, received, spots, tables)
+    sent = filter_rest(after(lines, line_shear), spots, tables)
     returned = [sent[0]] + swap(sent)
 
     highest = lax.Precision.HIGHEST
     grad = jnp.einsum("mwz,zq->mwq", shear, onehot[0], precision=highest)
     line_grad = jnp.einsum("xwz,xzq->wq", line_shear, onehot, precision=highest)
     mine = jnp.arange(mode_count) == me // row_split
-    grad = after(grad + jnp.where(mine[:, None, None], line_grad, 0.0), returned[1])
-    for axis, count in (("wall", wall_count), ("span", span)):
-        distance = 1
-        while distance < count:
-            grad = grad + lax.ppermute(grad, axis, [(i, i ^ distance) for i in range(count)])
-            distance *= 2
+    grad = after(grad + jnp.where(mine[:, None, None], line_grad, 0.0), sent[0])
+    grad = lax.psum(grad, ("wall", "span"))
     wall_grad = grad.reshape(mode_count, 2, part_count, PATCH).transpose(1, 0, 2, 3)
 
-    result = add_components(base, [back], spots, span, row_split, (0, last))
-    result = add_components(result, returned, spots, span, row_split, (last, comp_count))
+    result = add_components(base, [back], spots, span, row_split, (0, 1))
+    result = add_components(result, returned, spots, span, row_split, (1, comp_count))
     return (result, wall_grad)
 
 

time: 262 us -> 277 us (1.057)
  blocking collectives: 0 us -> 107 us
  waiting for transfers between devices: 162 us -> 88.9 us
  starting transfers between devices: 34.2 us -> 22 us
  local copies, waits for them, and re-layouts: 15.5 us -> 7.49 us
    ppermute x9 -> x3, waiting for transfers between devices: 133 us -> 0.01 us  [swap(): lax.ppermute(blocks[x], 'span', pairs[x])]
    psum x0 -> x1, blocking collectives: none -> 107 us  [on_device(): grad = lax.psum(grad, ('wall', 'span'))]
    ppermute x5 -> x2, waiting for transfers between devices: 13 us -> 88.9 us  [on_device(): lax.ppermute(patches, 'span', pairs[distance])]
    ppermute x1, waiting for transfers between devices: 15.8 us -> 0.01 us  [on_device(): high = lax.ppermute(field[:, :, :, :PAD], 'wall', backward)]
    ppermute x9 -> x3, starting transfers between devices: 10.4 us -> 3.55 us  [swap(): lax.ppermute(blocks[x], 'span', pairs[x])]
    slice x1 -> x0, local copies, waits for them, and re-layouts: 3.8 us -> none  [on_device(): main = field[:, :last].reshape(mode_split, -1, row_split, line_rows, width)]
    ppermute x5 -> x2, starting transfers between devices: 5.42 us -> 1.83 us  [on_device(): lax.ppermute(patches, 'span', pairs[distance])]
  transfers between devices with their start and end apart: 18 -> 9, of which waited for: 10 -> 2; matrix products, arithmetic and copies ran while one was open for 4% -> 4% of each run, Pallas kernels for 10% -> 11%
where the time goes in v8:
time: 277 us; the launch traced here: 274 us
  blocking collectives  107 us (39%)
  waiting for transfers between devices  88.9 us (32%)
  Pallas kernels  41.6 us (15%)
  starting transfers between devices  22 us (8%)
  local copies, waits for them, and re-layouts  7.49 us (3%)
  other arithmetic  4.72 us (2%)
    psum x1, blocking collectives, on_device(): grad = lax.psum(grad, ('wall', 'span'))  107 us
    ppermute x2, waiting for transfers between devices, on_device(): lax.ppermute(patches, 'span', pairs[distance])  88.9 us
    pallas_call x1, Pallas kernels, local_terms(): pl.pallas_call(local_kernel, grid=(mode_count,), out_shape=(jax.ShapeDtyp...  15.4 us
    all_to_all x2, starting transfers between devices, exchange(): return lax.all_to_all(lines, 'span', split_axis=0, concat_axis=0)  12.3 us
    pallas_call x1, Pallas kernels, filter_rest(): return call(spots, tables, lines)  11 us
    pallas_call x1, Pallas kernels, filter_first(): return call(spots, tables, weight, lines)  8.51 us
    pallas_call x2, Pallas kernels, add_components(): pl.pallas_call(functools.partial(add_kernel, row_split, pl.ds(first, last...  6.75 us
  transfers between devices with their start and end apart: 9, of which 2 were waited for; matrix products, arithmetic and copies ran while one was open for 4% of the time, Pallas kernels for 11%

profile of v8, /device:TPU:10, one launch (start us, length us, event | category | flops | bytes accessed | tf_op | source)
XLA Modules:
  0.0 273.8 jit_solution(7641680117687786610)
XLA Ops:
  0.6 0.0 copy-start.5
  0.6 5.4 %all-to-all-start = ((f32[4,6,32,1536]{3,2,1,0:T(8,128)}), f32[4,6,32,1536]{3,2,1,0:T(8,128)}, u32[]{:S(2)}, u32[]{:S(2)}) async-start(f32[4,6,32,1536]{3,2,1,0:T(8,128)} %bitcast.19), calls=%async_computation | async-start | bytes 9437184 | tf_op jit(solution)/shard_map/all_to_all | solution.py:429
  6.0 0.0 copy-done.5
  6.0 0.0 copy-start.6
  6.0 0.1 collective-permute-start.2
  6.2 2.9 %fusion = (f32[4,3,2,8,1536]{4,3,2,1,0:T(8,128)}, f32[4,3,2,8,1536]{4,3,2,1,0:T(8,128)S(1)}) fusion(f32[4,3,2,32,1536]{4,3,2,1,0:T(8,128)} %field_ref.1), kind=kLoop, calls=%fused_computation.13 | loop fusion | bytes 4718592 | tf_op jit(solution)/shard_map/slice | solution.py:440
  9.0 1.9 collective-permute-start.1
  10.9 2.4 collective-permute-start
  13.4 0.0 copy-done.6
  13.4 0.5 broadcast_select_fusion.1
  13.9 0.6 rev.3
  14.5 0.7 convert_multiply_fusion.rate_ref
  15.2 0.7 pad_maximum_fusion
  15.8 67.2 %collective-permute-done.2 = s32[1,1536]{1,0:T(1,128)} collective-permute-done((s32[1,1536]{1,0:T(1,128)S(1)}, s32[1,1536]{1,0:T(1,128)}, u32[]{:S(2)}, u32[]{:S(2)}) %collective-permute-start.2) | collective-permute-done | bytes 6176 | tf_op jit(solution)/shard_map/ppermute | solution.py:444
  83.1 0.7 pad_add_fusion.1
  83.8 1.7 collective-permute-start.3
  85.5 0.7 pad_add_fusion.2.me_ref
  86.1 21.7 %collective-permute-done.3 = s32[2,1536]{1,0:T(2,128)S(1)} collective-permute-done((s32[2,1536]{1,0:T(2,128)S(1)}, s32[2,1536]{1,0:T(2,128)S(1)}, u32[]{:S(2)}, u32[]{:S(2)}) %collective-permute-start.3) | collective-permute-done | bytes 12320 | tf_op jit(solution)/shard_map/ppermute | solution.py:444
  107.8 1.3 pad_add_fusion
  109.1 0.0 collective-permute-done.1.high_ref
  109.1 0.0 collective-permute-done.low_ref
  109.1 0.1 broadcast_in_dim.57.weight_ref
  109.2 0.0 copy-start.2
  109.2 0.8 broadcast_in_dim.55.flow_ref
  110.0 0.8 broadcast_in_dim.54.coef_ref
  110.8 0.0 copy-start
  110.8 2.3 copy-done
  113.1 15.4 %local_terms.1 = (f32[4,3,2,32,1536]{4,3,2,1,0:T(8,128)}, f32[4,4,1536]{2,1,0:T(4,128)S(1)}) custom-call(f32[4]{0:T(128)S(1)} %convert_multiply_fusion.rate_ref, f32[15,32,128]{2,1,0:T(8,128)S(1)} %broadcast_in_dim.54.coef_ref, f32[2,32,128]{2,1,0:T(8,128)S(1)} %broadcast_in_dim.55.flow_ref, f32[2,8,128]{2,1,0:T(8,128)S(1)} %broadcast_in_dim.57.weight_ref, ...), custom_call_target="tpu_custom_call" | custom-call | flops 47185920 | bytes 11796480 | tf_op jit(solution)/shard_map/local_terms/pallas_call | solution.py:341
  128.5 0.0 copy-done.2
  128.5 0.0 all-to-all-done.lines_hbm
  128.5 8.5 %filter_first.1 = (f32[4,2,32,1536]{3,2,1,0:T(8,128)}, f32[4,4,1536]{2,1,0:T(4,128)}) custom-call(s32[3]{0:T(128)} %pad_add_fusion.2.me_ref, bf16[24,2,256,256]{3,2,1,0:T(8,128)(2,1)} %constant.50.clone.table_hbm, f32[2,8,128]{2,1,0:T(8,128)} %copy-done.2, f32[4,6,32,1536]{3,2,1,0:T(8,128)} %all-to-all-done.lines_hbm), custom_call_target="tpu_custom_call" | custom-call | flops 603979776 | bytes 3145728 | tf_op jit(solution)/shard_map/filter_first/pallas_call | solution.py:290
  137.0 6.9 %all-to-all-start.1 = ((f32[4,2,32,1536]{3,2,1,0:T(8,128)}), f32[4,2,32,1536]{3,2,1,0:T(8,128)S(1)}, u32[]{:S(2)}, u32[]{:S(2)}) async-start(f32[4,2,32,1536]{3,2,1,0:T(8,128)} %get-tuple-element.15), calls=%async_computation.1 | async-start | bytes 3145728 | tf_op jit(solution)/shard_map/all_to_all | solution.py:429
  144.0 0.0 copy-start.4
  144.0 0.0 copy-start.7
  144.0 0.0 copy-start.3
  144.0 11.0 %filter_rest.1 = (f32[4,32,1536]{2,1,0:T(8,128)}, f32[4,32,1536]{2,1,0:T(8,128)}, f32[4,32,1536]{2,1,0:T(8,128)}, f32[4,32,1536]{2,1,0:T(8,128)}) custom-call(s32[3]{0:T(128)} %pad_add_fusion.2.me_ref, bf16[24,2,256,256]{3,2,1,0:T(8,128)(2,1)} %constant.50.clone.table_hbm, f32[4,6,32,1536]{3,2,1,0:T(8,128)} %all-to-all-done.lines_hbm), custom_call_target="tpu_custom_call" | custom-call | flops 1207959552 | bytes 6291456 | tf_op jit(solution)/shard_map/filter_rest/pallas_call | solution.py:299
  154.9 0.1 collective-permute-start.4
  155.1 2.9 %collective-permute-start.5 = (f32[4,32,1536]{2,1,0:T(8,128)}, f32[4,32,1536]{2,1,0:T(8,128)S(1)}, u32[]{:S(2)}, u32[]{:S(2)}) collective-permute-start(f32[4,32,1536]{2,1,0:T(8,128)} %get-tuple-element.20), channel_id=1, source_target_pairs={{0,2},{1,3},{2,0},{3,1},{4,6},{5,7},{6,4},{7,5},{8,10},{9,11},{10,... | collective-permute-start | bytes 2359304 | tf_op jit(solution)/shard_map/ppermute | solution.py:432
  157.9 0.6 collective-permute-start.6
  158.5 0.0 copy-done.4
  158.5 0.2 iota_compare_fusion
  158.7 0.0 copy-done.7
  158.7 0.8 convolution_bitcast_fusion
  159.5 0.3 convolution_add_fusion
  159.9 107.1 %psum.7 = f32[2,4,2,64]{3,2,1,0:T(2,128)} all-reduce(f32[2,4,2,64]{3,2,1,0:T(2,128)S(1)} %bitcast.24), channel_id=1, replica_groups=mesh['wall'=8,'span'=4] {'wall','span'}, use_global_device_ids=true, to_apply=%region_0.1 | all-reduce | flops 1024 | bytes 8192 | tf_op jit(solution)/shard_map/psum | solution.py:471
  267.0 0.0 all-to-all-done.1
  267.0 0.0 copy-done.3
  267.0 0.0 copy-start.1
  267.0 3.1 %add_components.2.base_hbm = f32[4,3,2,32,1536]{4,3,2,1,0:T(8,128)} custom-call(s32[3]{0:T(128)S(1)} %copy-done.3, f32[4,3,2,32,1536]{4,3,2,1,0:T(8,128)} %get-tuple-element.13.base_hbm, f32[4,1,2,32,1536]{4,3,2,1,0:T(8,128)S(1)} %bitcast.20), custom_call_target="tpu_custom_call", output_to_operand_aliasing={{}: (1, {})} | custom-call | flops 393216 | bytes 4718592 | tf_op jit(solution)/shard_map/add_components/pallas_call | solution.py:398
  270.0 0.0 collective-permute-done.4
  270.0 0.0 collective-permute-done.5
  270.1 0.0 collective-permute-done.6
  270.1 0.0 copy-done.1
  270.1 3.7 %add_components.3 = f32[4,3,2,32,1536]{4,3,2,1,0:T(8,128)} custom-call(s32[3]{0:T(128)S(1)} %copy-done.3, f32[4,3,2,32,1536]{4,3,2,1,0:T(8,128)} %add_components.2.base_hbm, f32[2,2,32,1536]{3,2,1,0:T(8,128)S(1)} %bitcast.21, f32[2,2,32,1536]{3,2,1,0:T(8,128)S(1)} %bitcast.22, f32[2,2,32,1536]{3,2,1,0:T(8,128)S(1)} %bitcast.23, ...), custom_call_target="tpu_custom_call", output_to_operand_aliasing={{}: (1, {})} | custom-call | flops 786432 | bytes 9437184 | tf_op jit(solution)/shard_map/add_components/pallas_call | solution.py:398
  (4 shorter events, 0.0 us)
Async XLA Ops:
  0.6 5.4 %copy-start.5 = (s32[1536]{0:T(1024)S(1)}, s32[1536]{0:T(1024)}, u32[]{:S(2)}) copy-start(s32[1536]{0:T(1024)} %param.12) | copy-start | bytes 18436
  0.6 127.9 %all-to-all-start = ((f32[4,6,32,1536]{3,2,1,0:T(8,128)}), f32[4,6,32,1536]{3,2,1,0:T(8,128)}, u32[]{:S(2)}, u32[]{:S(2)}) async-start(f32[4,6,32,1536]{3,2,1,0:T(8,128)} %bitcast.19), calls=%async_computation | async-start | bytes 9437184 | tf_op jit(solution)/shard_map/all_to_all | solution.py:429
  6.0 7.3 %copy-start.6 = (f32[2,8]{1,0:T(2,128)S(1)}, f32[2,8]{1,0:T(2,128)}, u32[]{:S(2)}) copy-start(f32[2,8]{1,0:T(2,128)} %param.10) | copy-start | bytes 196
  6.0 77.0 %collective-permute-start.2 = (s32[1,1536]{1,0:T(1,128)S(1)}, s32[1,1536]{1,0:T(1,128)}, u32[]{:S(2)}, u32[]{:S(2)}) collective-permute-start(s32[1,1536]{1,0:T(1,128)S(1)} %broadcast_in_dim.58), channel_id=1, source_target_pairs={{0,1},{1,0},{2,3},{3,2},{4,5},{5,4},{6,7},{7,6},{8,9},{9,8},{10,11... | collective-permute-start | bytes 18440 | tf_op jit(solution)/shard_map/ppermute | solution.py:444
  9.0 100.1 %collective-permute-start.1 = (f32[4,3,2,8,1536]{4,3,2,1,0:T(8,128)}, f32[4,3,2,8,1536]{4,3,2,1,0:T(8,128)S(1)}, u32[]{:S(2)}, u32[]{:S(2)}) collective-permute-start(f32[4,3,2,8,1536]{4,3,2,1,0:T(8,128)} %get-tuple-element.24), channel_id=1, source_target_pairs={{4,0},{8,4},{12,8},{16,12},{20,16},{24,20},{28,24},{5,1},{9,5},{13... | collective-permute-start | bytes 3538952 | tf_op jit(solution)/shard_map/ppermute | solution.py:440
  10.9 98.2 %collective-permute-start = (f32[4,3,2,8,1536]{4,3,2,1,0:T(8,128)S(1)}, f32[4,3,2,8,1536]{4,3,2,1,0:T(8,128)S(1)}, u32[]{:S(2)}, u32[]{:S(2)}) collective-permute-start(f32[4,3,2,8,1536]{4,3,2,1,0:T(8,128)S(1)} %get-tuple-element.25), channel_id=1, source_target_pairs={{0,4},{4,8},{8,12},{12,16},{16,20},{20,24},{24,28},{1,5},{5,9},{9,... | collective-permute-start | bytes 3538952 | tf_op jit(solution)/shard_map/ppermute | solution.py:439
  83.8 24.1 %collective-permute-start.3 = (s32[2,1536]{1,0:T(2,128)S(1)}, s32[2,1536]{1,0:T(2,128)S(1)}, u32[]{:S(2)}, u32[]{:S(2)}) collective-permute-start(s32[2,1536]{1,0:T(2,128)S(1)} %pad_add_fusion.1), channel_id=1, source_target_pairs={{0,2},{1,3},{2,0},{3,1},{4,6},{5,7},{6,4},{7,5},{8,10},{9,11},{10,... | collective-permute-start | bytes 36872 | tf_op jit(solution)/shard_map/ppermute | solution.py:444
  109.2 19.3 %copy-start.2 = (f32[2,8,128]{2,1,0:T(8,128)}, f32[2,8,128]{2,1,0:T(8,128)S(1)}, u32[]{:S(2)}) copy-start(f32[2,8,128]{2,1,0:T(8,128)S(1)} %broadcast_in_dim.57.weight_ref) | copy-start | bytes 24580
  110.8 2.3 copy-start
  137.0 129.9 %all-to-all-start.1 = ((f32[4,2,32,1536]{3,2,1,0:T(8,128)}), f32[4,2,32,1536]{3,2,1,0:T(8,128)S(1)}, u32[]{:S(2)}, u32[]{:S(2)}) async-start(f32[4,2,32,1536]{3,2,1,0:T(8,128)} %get-tuple-element.15), calls=%async_computation.1 | async-start | bytes 3145728 | tf_op jit(solution)/shard_map/all_to_all | solution.py:429
  144.0 14.5 %copy-start.4 = (s32[4,1536]{1,0:T(4,128)S(1)}, s32[4,1536]{1,0:T(4,128)}, u32[]{:S(2)}) copy-start(s32[4,1536]{1,0:T(4,128)} %pad_add_fusion) | copy-start | bytes 73732
  144.0 14.7 %copy-start.7 = (f32[4,4,1536]{2,1,0:T(4,128)S(1)}, f32[4,4,1536]{2,1,0:T(4,128)}, u32[]{:S(2)}) copy-start(f32[4,4,1536]{2,1,0:T(4,128)} %get-tuple-element.16) | copy-start | bytes 294916
  144.0 123.0 %copy-start.3 = (s32[3]{0:T(128)S(1)}, s32[3]{0:T(128)}, u32[]{:S(2)}) copy-start(s32[3]{0:T(128)} %pad_add_fusion.2.me_ref) | copy-start | bytes 40
  154.9 115.1 %collective-permute-start.4 = (f32[4,32,1536]{2,1,0:T(8,128)}, f32[4,32,1536]{2,1,0:T(8,128)S(1)}, u32[]{:S(2)}, u32[]{:S(2)}) collective-permute-start(f32[4,32,1536]{2,1,0:T(8,128)} %get-tuple-element.19), channel_id=1, source_target_pairs={{0,1},{1,0},{2,3},{3,2},{4,5},{5,4},{6,7},{7,6},{8,9},{9,8},{10,11... | collective-permute-start | bytes 2359304 | tf_op jit(solution)/shard_map/ppermute | solution.py:432
  155.1 115.0 %collective-permute-start.5 = (f32[4,32,1536]{2,1,0:T(8,128)}, f32[4,32,1536]{2,1,0:T(8,128)S(1)}, u32[]{:S(2)}, u32[]{:S(2)}) collective-permute-start(f32[4,32,1536]{2,1,0:T(8,128)} %get-tuple-element.20), channel_id=1, source_target_pairs={{0,2},{1,3},{2,0},{3,1},{4,6},{5,7},{6,4},{7,5},{8,10},{9,11},{10,... | collective-permute-start | bytes 2359304 | tf_op jit(solution)/shard_map/ppermute | solution.py:432
  157.9 112.1 %collective-permute-start.6 = (f32[4,32,1536]{2,1,0:T(8,128)}, f32[4,32,1536]{2,1,0:T(8,128)}, u32[]{:S(2)}, u32[]{:S(2)}) collective-permute-start(f32[4,32,1536]{2,1,0:T(8,128)} %get-tuple-element.21), channel_id=1, source_target_pairs={{0,3},{1,2},{2,1},{3,0},{4,7},{5,6},{6,5},{7,4},{8,11},{9,10},{10,... | collective-permute-start | bytes 2359304 | tf_op jit(solution)/shard_map/ppermute | solution.py:432
  267.0 3.1 %copy-start.1 = (f32[4,32,1536]{2,1,0:T(8,128)S(1)}, f32[4,32,1536]{2,1,0:T(8,128)}, u32[]{:S(2)}) copy-start(f32[4,32,1536]{2,1,0:T(8,128)} %get-tuple-element.18) | copy-start | bytes 2359300

commit v9 on v8

--- a/solution.py
+++ b/solution.py
@@ -235,15 +235,10 @@
     filter_lines(line_ref, wave_ref, table_ref, table_copies)
 
 
-def filter_first_kernel(me_ref, table_hbm, weight_ref, lines_hbm, out_hbm, shear_ref, *scratch):
+def filter_first_kernel(table_hbm, lines_hbm, out_hbm, *scratch):
     run_filter(table_hbm, lines_hbm, 0, scratch)
-    line_ref, sems, me = scratch[0], scratch[-1], me_ref[0]
-    count = line_ref.shape[0]
-    copies = start_all([pltpu.make_async_copy(line_ref.at[x], out_hbm.at[x], sems.at[x]) for x in range(count)])
-    for x in range(count):
-        for spot, value in enumerate(wall_sums(line_ref.at[me ^ x], weight_ref)):
-            shear_ref[x, spot] = value
-    wait_all(copies)
+    line_ref, sems = scratch[0], scratch[-1]
+    wait_all(start_all([pltpu.make_async_copy(line_ref.at[x], out_hbm.at[x], sems.at[x]) for x in range(sems.shape[0])]))
 
 
 def filter_rest_kernel(me_ref, table_hbm, lines_hbm, *refs):
@@ -281,13 +276,11 @@
     )
 
 
-def filter_first(lines, weight, spots, tables):
+def filter_first(lines, tables):
     block = (lines.shape[0], 2) + lines.shape[2:]
-    shear = jax.ShapeDtypeStruct((block[0], 4, block[3]), jnp.float32)
-    out_shape = (jax.ShapeDtypeStruct(block, jnp.float32), shear)
-    ins = [SCALARS, HBM, WHOLE, HBM]
-    call = filter_call(filter_first_kernel, "filter_first", block, tables, ins, (HBM, WHOLE), out_shape)
-    return call(spots, tables, weight, lines)
+    out_shape = jax.ShapeDtypeStruct(block, jnp.float32)
+    call = filter_call(filter_first_kernel, "filter_first", block, tables, [HBM, HBM], HBM, out_shape)
+    return call(tables, lines)
 
 
 def filter_rest(lines, spots, tables):
@@ -299,7 +292,7 @@
     return call(spots, tables, lines)
 
 
-def local_kernel(rate_ref, coef_ref, flow_ref, weight_ref, field_ref, low_ref, high_ref, out_ref, shear_ref, pad_ref):
+def local_kernel(rate_ref, coef_ref, flow_ref, field_ref, low_ref, high_ref, out_ref, pad_ref):
     _, comp_count, part_count, row_count, width = field_ref.shape
     pad_ref[:, :, :PAD] = low_ref[0]
     pad_ref[:, :, PAD : PAD + row_count] = field_ref[0]
@@ -326,11 +319,9 @@
         return 0
 
     lax.fori_loop(0, width // LANES, column, 0)
-    for spot, value in enumerate(wall_sums(out_ref.at[0, 0], weight_ref)):
-        shear_ref[0, spot] = value
-
-
-def local_terms(field, low, high, rate, coef, flow, weight):
+
+
+def local_terms(field, low, high, rate, coef, flow):
     mode_count, comp_count, part_count, row_count, width = field.shape
     block = (1, comp_count, part_count, row_count, width)
     edge = (1, comp_count, part_count, PAD, width)
@@ -341,31 +332,31 @@
     return pl.pallas_call(
         local_kernel,
         grid=(mode_count,),
-        out_shape=(
-            jax.ShapeDtypeStruct(field.shape, jnp.float32),
-            jax.ShapeDtypeStruct((mode_count, 2 * part_count, width), jnp.float32),
-        ),
+        out_shape=jax.ShapeDtypeStruct(field.shape, jnp.float32),
         in_specs=[
             SCALARS,
             pl.BlockSpec(coef.shape, lambda m: (0, 0, 0)),
             pl.BlockSpec(flow.shape, lambda m: (0, 0, 0)),
-            pl.BlockSpec(weight.shape, lambda m: (0, 0, 0)),
             pl.BlockSpec(block, by_mode),
             pl.BlockSpec(edge, by_mode),
             pl.BlockSpec(edge, by_mode),
         ],
-        out_specs=(pl.BlockSpec(block, by_mode), pl.BlockSpec((1, 2 * part_count, width), lambda m: (m, 0, 0))),
+        out_specs=pl.BlockSpec(block, by_mode),
         scratch_shapes=[pltpu.VMEM((comp_count, part_count, row_count + 2 * PAD, width), jnp.float32)],
         compiler_params=pltpu.CompilerParams(vmem_limit_bytes=24 << 20),
         cost_estimate=pl.CostEstimate(flops=40 * field.size, bytes_accessed=10 * field.size, transcendentals=0),
         name="local_terms",
-    )(rate, coef, flow, weight, field, low, high)
+    )(rate, coef, flow, field, low, high)
 
 
 def add_kernel(row_split, comps, me_ref, base_hbm, *refs):
     base_ref, term_ref, base_sems, term_sems = refs[-4:]
     count, _, _, row_count, _ = base_ref.shape
-    *terms, out_hbm = refs[:-4]
+    sums = comps.start == 0
+    if sums:
+        weight_ref, *terms, out_hbm, shear_ref = refs[:-4]
+    else:
+        *terms, out_hbm = refs[:-4]
     me = me_ref[0]
 
     def spot(ref, x):
@@ -385,27 +376,35 @@
         term_loads[x].wait()
         base_ref[x] = base_ref[x] + term_ref[x]
         stores[x].start()
+        if sums:
+            for place, value in enumerate(wall_sums(base_ref.at[x, 0], weight_ref[x])):
+                shear_ref[me ^ x, place] = value
     wait_all(stores)
 
 
-def add_components(base, terms, spots, span, row_split, comps):
+def add_components(base, terms, spots, row_split, comps, weight=None):
     first, last = comps
-    mode_count, _, part_count, row_count, width = base.shape
+    _, _, part_count, row_count, width = base.shape
+    span = weight.shape[0] if weight is not None else len(terms)
     block = (span, last - first, part_count, row_count // row_split, width)
     terms = [term.reshape(block[1:] if len(terms) > 1 else block) for term in terms]
     size = math.prod(block)
     buffer, sems = pltpu.VMEM(block, jnp.float32), pltpu.SemaphoreType.DMA((span,))
+    out_shape, out_specs, weights = jax.ShapeDtypeStruct(base.shape, jnp.float32), HBM, []
+    if weight is not None:
+        out_shape, out_specs = (out_shape, jax.ShapeDtypeStruct((span, 4, width), jnp.float32)), (HBM, WHOLE)
+        weights = [weight]
     return pl.pallas_call(
         functools.partial(add_kernel, row_split, pl.ds(first, last - first)),
-        out_shape=jax.ShapeDtypeStruct(base.shape, jnp.float32),
-        in_specs=[SCALARS] + [HBM] * (1 + len(terms)),
-        out_specs=HBM,
+        out_shape=out_shape,
+        in_specs=[SCALARS, HBM] + [WHOLE] * len(weights) + [HBM] * len(terms),
+        out_specs=out_specs,
         scratch_shapes=[buffer, buffer, sems, sems],
         input_output_aliases={1: 0},
         compiler_params=pltpu.CompilerParams(vmem_limit_bytes=24 << 20),
         cost_estimate=pl.CostEstimate(flops=size, bytes_accessed=12 * size, transcendentals=0),
         name="add_components",
-    )(spots, base, *terms)
+    )(spots, base, *weights, *terms)
 
 
 def after(value, *others):
@@ -439,40 +438,35 @@
     low = lax.ppermute(field[:, :, :, row_count - PAD :], "wall", forward)
     high = lax.ppermute(field[:, :, :, :PAD], "wall", backward)
 
-    patches, distance = patch_of[None], 1
-    while distance < span:
-        patches = jnp.concatenate([patches, lax.ppermute(patches, "span", pairs[distance])])
-        distance *= 2
-    onehot = (patches[:, :, None] == jnp.arange(PATCH, dtype=jnp.int32)).astype(jnp.float32)
-
-    lower = jnp.where(wall_index == 0, wall_coef[0], 0.0)
-    upper = jnp.where(wall_index == wall_count - 1, wall_coef[1, ::-1], 0.0)
-    weight = jnp.broadcast_to(jnp.stack([lower, upper])[:, :, None], (2, PAD, LANES))
-    group = me % row_split
-    ends = jnp.stack([group == 0, group == row_split - 1])
-    line_weight = jnp.where(ends[:, None, None], weight, 0.0)
-
     rate = kx_index.astype(jnp.float32) * (0.25 * TAU)
     coef = jnp.broadcast_to(d2_coef[:, :, None], (STEN, row_count, LANES))
     flow = jnp.broadcast_to(mean_flow[:, :, None], (2, row_count, LANES))
-    base, shear = local_terms(field, low, high, rate, coef, flow, weight)
-
-    lines = after(lines, base, patches)
-    filtered, line_shear = filter_first(lines, line_weight, spots, tables)
+    base = local_terms(field, low, high, rate, coef, flow)
+
+    lines = after(lines, base)
+    filtered = filter_first(lines, tables)
     back = exchange(filtered)
-    sent = filter_rest(after(lines, line_shear), spots, tables)
+    sent = filter_rest(after(lines, filtered), spots, tables)
     returned = [sent[0]] + swap(sent)
 
-    highest = lax.Precision.HIGHEST
-    grad = jnp.einsum("mwz,zq->mwq", shear, onehot[0], precision=highest)
-    line_grad = jnp.einsum("xwz,xzq->wq", line_shear, onehot, precision=highest)
-    mine = jnp.arange(mode_count) == me // row_split
-    grad = after(grad + jnp.where(mine[:, None, None], line_grad, 0.0), sent[0])
-    grad = lax.psum(grad, ("wall", "span"))
-    wall_grad = grad.reshape(mode_count, 2, part_count, PATCH).transpose(1, 0, 2, 3)
-
-    result = add_components(base, [back], spots, span, row_split, (0, 1))
-    result = add_components(result, returned, spots, span, row_split, (1, comp_count))
+    lower = jnp.where(wall_index == 0, wall_coef[0], 0.0)
+    upper = jnp.where(wall_index == wall_count - 1, wall_coef[1, ::-1], 0.0)
+    group = ((me ^ jnp.arange(span)) % row_split)[:, None]
+    ends = [jnp.where(group == 0, lower, 0.0), jnp.where(group == row_split - 1, upper, 0.0)]
+    weight = jnp.broadcast_to(jnp.stack(ends, axis=1)[..., None], (span, 2, PAD, LANES))
+    result, shear = add_components(base, [back], spots, row_split, (0, 1), weight)
+    onehot = (patch_of[:, None] == jnp.arange(PATCH, dtype=jnp.int32)[None, :]).astype(jnp.float32)
+    grad = jnp.einsum("swz,zq->swq", shear, onehot, precision=lax.Precision.HIGHEST)
+    grad = grad.reshape(mode_count, row_split, 2, part_count, PATCH).sum(axis=1)
+    distance = 1
+    while distance < wall_count:
+        grad = grad + lax.ppermute(grad, "wall", [(i, i ^ distance) for i in range(wall_count)])
+        distance *= 2
+    parts = jnp.stack([grad] + swap([grad] * span))
+    parts = [lax.dynamic_index_in_dim(parts, me ^ x, 0, keepdims=False) for x in range(span)]
+    wall_grad = functools.reduce(jnp.add, parts).transpose(1, 0, 2, 3)
+
+    result = add_components(result, returned, spots, row_split, (1, comp_count))
     return (result, wall_grad)
 
 

time: 277 us -> 230 us (0.83); the launches traced: 274 us -> 230 us
  blocking collectives: 107 us -> 0 us
  waiting for transfers between devices: 88.9 us -> 154 us
  starting transfers between devices: 22 us -> 28.5 us
  other arithmetic: 4.72 us -> 1.35 us
  local copies, waits for them, and re-layouts: 7.49 us -> 4.57 us
    psum x1 -> x0, blocking collectives: 107 us -> none  [on_device(): grad = lax.psum(grad, ('wall', 'span'))]
    ppermute x2 -> x3, waiting for transfers between devices: 88.9 us -> 6.47 us  [on_device(): lax.ppermute(grad, 'wall', [(i, i ^ distance) for i in range(wall_count)])]
    all_to_all x2, waiting for transfers between devices: 0.01 us -> 77.1 us  [exchange(): return lax.all_to_all(lines, 'span', split_axis=0, concat_axis=0)]
    ppermute x3 -> x6, waiting for transfers between devices: 0.01 us -> 49.6 us  [swap(): lax.ppermute(blocks[x], 'span', pairs[x])]
    ppermute x1, waiting for transfers between devices: 0.01 us -> 20.4 us  [on_device(): high = lax.ppermute(field[:, :, :, :PAD], 'wall', backward)]
    ppermute x3 -> x6, starting transfers between devices: 3.55 us -> 9.75 us  [swap(): lax.ppermute(blocks[x], 'span', pairs[x])]
  transfers between devices with their start and end apart: 9 -> 13, of which waited for: 2 -> 8; matrix products, arithmetic and copies ran while one was open for 4% -> 1% of each run, Pallas kernels for 11% -> 15%
where the time goes in v9:
time: 230 us
  waiting for transfers between devices  154 us (67%)
  Pallas kernels  40.6 us (18%)
  starting transfers between devices  28.5 us (12%)
  local copies, waits for them, and re-layouts  4.57 us (2%)
    all_to_all x2, waiting for transfers between devices, exchange(): return lax.all_to_all(lines, 'span', split_axis=0, concat_axis=0)  77.1 us
    ppermute x6, waiting for transfers between devices, swap(): lax.ppermute(blocks[x], 'span', pairs[x])  49.6 us
    ppermute x1, waiting for transfers between devices, on_device(): high = lax.ppermute(field[:, :, :, :PAD], 'wall', backward)  20.4 us
    pallas_call x1, Pallas kernels, local_terms(): pl.pallas_call(local_kernel, grid=(mode_count,), out_shape=jax.ShapeDtype...  15 us
    all_to_all x2, starting transfers between devices, exchange(): return lax.all_to_all(lines, 'span', split_axis=0, concat_axis=0)  12.3 us
    pallas_call x1, Pallas kernels, filter_rest(): return call(spots, tables, lines)  11 us
    ppermute x6, starting transfers between devices, swap(): lax.ppermute(blocks[x], 'span', pairs[x])  9.75 us
    pallas_call x2, Pallas kernels, add_components(): pl.pallas_call(functools.partial(add_kernel, row_split, pl.ds(first, last...  7.45 us
  transfers between devices with their start and end apart: 13, of which 8 were waited for; matrix products, arithmetic and copies ran while one was open for 1% of the time, Pallas kernels for 15%

profile of v9, /device:TPU:10, one launch (start us, length us, event | category | flops | bytes accessed | tf_op | source)
XLA Modules:
  0.0 229.7 jit_solution(7442129214219480787)
XLA Ops:
  0.6 5.4 %all-to-all-start = ((f32[4,6,32,1536]{3,2,1,0:T(8,128)}), f32[4,6,32,1536]{3,2,1,0:T(8,128)}, u32[]{:S(2)}, u32[]{:S(2)}) async-start(f32[4,6,32,1536]{3,2,1,0:T(8,128)} %bitcast.24), calls=%async_computation | async-start | bytes 9437184 | tf_op jit(solution)/shard_map/all_to_all | solution.py:428
  6.0 0.0 copy-start.7
  6.0 0.0 copy-start.4
  6.0 0.0 copy-start.3
  6.0 1.8 fusion.6
  7.9 1.9 collective-permute-start.1
  9.8 2.4 %collective-permute-start = (f32[4,3,2,8,1536]{4,3,2,1,0:T(8,128)S(1)}, f32[4,3,2,8,1536]{4,3,2,1,0:T(8,128)S(1)}, u32[]{:S(2)}, u32[]{:S(2)}) collective-permute-start(f32[4,3,2,8,1536]{4,3,2,1,0:T(8,128)S(1)} %get-tuple-element.19), channel_id=1, source_target_pairs={{0,4},{4,8},{8,12},{12,16},{16,20},{20,24},{24,28},{1,5},{5,9},{9,... | collective-permute-start | bytes 3538952 | tf_op jit(solution)/shard_map/ppermute | solution.py:438
  12.2 0.0 copy-done.7
  12.2 20.4 %collective-permute-done.1.high_ref = f32[4,3,2,8,1536]{4,3,2,1,0:T(8,128)S(1)} collective-permute-done((f32[4,3,2,8,1536]{4,3,2,1,0:T(8,128)S(1)}, f32[4,3,2,8,1536]{4,3,2,1,0:T(8,128)S(1)}, u32[]{:S(2)}, u32[]{:S(2)}) %collective-permute-start.1) | collective-permute-done | bytes 1179680 | tf_op jit(solution)/shard_map/ppermute | solution.py:439
  32.7 0.0 collective-permute-done.low_ref
  32.7 0.0 copy-done.4
  32.7 0.1 broadcast_in_dim.46.flow_ref
  32.7 0.0 copy-done.3
  32.7 0.1 broadcast_in_dim.45.coef_ref
  32.9 0.0 copy-start
  32.9 2.3 %copy-done = f32[4,3,2,32,1536]{4,3,2,1,0:T(8,128)S(1)} copy-done((f32[4,3,2,32,1536]{4,3,2,1,0:T(8,128)S(1)}, f32[4,3,2,32,1536]{4,3,2,1,0:T(8,128)}, u32[]{:S(2)}) %copy-start) | copy-done | bytes 4718616
  35.2 15.0 %local_terms.1.base_hbm = f32[4,3,2,32,1536]{4,3,2,1,0:T(8,128)} custom-call(f32[4]{0:T(128)S(1)} %convert_multiply_fusion.rate_ref, f32[15,32,128]{2,1,0:T(8,128)S(1)} %broadcast_in_dim.45.coef_ref, f32[2,32,128]{2,1,0:T(8,128)S(1)} %broadcast_in_dim.46.flow_ref, f32[4,3,2,32,1536]{4,3,2,1,0:T(8,128)S(1)} %copy-done, ...), custom_call_target="tpu_custom_call" | custom-call | flops 47185920 | bytes 11796480 | tf_op jit(solution)/shard_map/local_terms/pallas_call | solution.py:332
  50.2 57.2 %all-to-all-done.lines_hbm = f32[4,6,32,1536]{3,2,1,0:T(8,128)} async-done(((f32[4,6,32,1536]{3,2,1,0:T(8,128)}), f32[4,6,32,1536]{3,2,1,0:T(8,128)}, u32[]{:S(2)}, u32[]{:S(2)}) %all-to-all-start) | async-done | bytes 4718624 | tf_op jit(solution)/shard_map/all_to_all | solution.py:428
  107.4 7.2 %filter_first.1 = f32[4,2,32,1536]{3,2,1,0:T(8,128)} custom-call(bf16[24,2,256,256]{3,2,1,0:T(8,128)(2,1)} %constant.71.clone.table_hbm, f32[4,6,32,1536]{3,2,1,0:T(8,128)} %all-to-all-done.lines_hbm), custom_call_target="tpu_custom_call" | custom-call | flops 603979776 | bytes 3145728 | tf_op jit(solution)/shard_map/filter_first/pallas_call | solution.py:283
  114.6 0.0 copy-start.5
  114.6 6.9 %all-to-all-start.1 = ((f32[4,2,32,1536]{3,2,1,0:T(8,128)}), f32[4,2,32,1536]{3,2,1,0:T(8,128)S(1)}, u32[]{:S(2)}, u32[]{:S(2)}) async-start(f32[4,2,32,1536]{3,2,1,0:T(8,128)} %filter_first.1), calls=%async_computation.1 | async-start | bytes 3145728 | tf_op jit(solution)/shard_map/all_to_all | solution.py:428
  121.5 0.0 copy-done.5
  121.5 0.1 rev.3
  121.6 0.7 pad_add_fusion.me_ref
  122.3 0.0 copy-start.2
  122.3 11.0 %filter_rest.1 = (f32[4,32,1536]{2,1,0:T(8,128)}, f32[4,32,1536]{2,1,0:T(8,128)}, f32[4,32,1536]{2,1,0:T(8,128)}, f32[4,32,1536]{2,1,0:T(8,128)}) custom-call(s32[3]{0:T(128)} %pad_add_fusion.me_ref, bf16[24,2,256,256]{3,2,1,0:T(8,128)(2,1)} %constant.71.clone.table_hbm, f32[4,6,32,1536]{3,2,1,0:T(8,128)} %all-to-all-done.lines_hbm), custom_call_target="tpu_custom_call" | custom-call | flops 1207959552 | bytes 6291456 | tf_op jit(solution)/shard_map/filter_rest/pallas_call | solution.py:292
  133.3 0.1 collective-permute-start.2
  133.4 2.9 %collective-permute-start.3 = (f32[4,32,1536]{2,1,0:T(8,128)}, f32[4,32,1536]{2,1,0:T(8,128)}, u32[]{:S(2)}, u32[]{:S(2)}) collective-permute-start(f32[4,32,1536]{2,1,0:T(8,128)} %get-tuple-element.15), channel_id=1, source_target_pairs={{0,2},{1,3},{2,0},{3,1},{4,6},{5,7},{6,4},{7,5},{8,10},{9,11},{10,... | collective-permute-start | bytes 2359304 | tf_op jit(solution)/shard_map/ppermute | solution.py:431
  136.3 0.6 collective-permute-start.4
  136.9 19.9 %all-to-all-done.1 = f32[4,2,32,1536]{3,2,1,0:T(8,128)S(1)} async-done(((f32[4,2,32,1536]{3,2,1,0:T(8,128)}), f32[4,2,32,1536]{3,2,1,0:T(8,128)S(1)}, u32[]{:S(2)}, u32[]{:S(2)}) %all-to-all-start.1) | async-done | bytes 1572896 | tf_op jit(solution)/shard_map/all_to_all | solution.py:428
  156.7 0.1 broadcast_in_dim.50.refs_0_
  156.8 0.0 copy-done.2
  156.8 0.0 copy-start.6
  156.8 0.0 copy-start.1
  156.8 3.1 %add_components.2 = (f32[4,3,2,32,1536]{4,3,2,1,0:T(8,128)}, f32[4,4,1536]{2,1,0:T(4,128)S(1)}) custom-call(s32[3]{0:T(128)S(1)} %copy-done.2, f32[4,3,2,32,1536]{4,3,2,1,0:T(8,128)} %local_terms.1.base_hbm, f32[4,2,8,128]{3,2,1,0:T(8,128)S(1)} %broadcast_in_dim.50.refs_0_, f32[4,1,2,32,1536]{4,3,2,1,0:T(8,128)S(1)} %bitcast.25), custom_call_target="tpu_custom_call", output_to_operand_aliasing={{0}: (1, {})} | custom-call | flops 393216 | bytes 4718592 | tf_op jit(solution)/shard_map/add_components/pallas_call | solution.py:397
  159.9 0.0 copy-done.6
  159.9 0.3 fusion.1
  160.2 0.1 collective-permute-start.5
  160.3 1.2 collective-permute-done.5
  161.5 0.5 collective-permute-start.6
  161.9 3.2 %collective-permute-done.6 = f32[4,2,2,64]{3,2,0,1:T(2,128)S(1)} collective-permute-done((f32[4,2,2,64]{3,2,0,1:T(2,128)S(1)}, f32[4,2,2,64]{3,2,0,1:T(2,128)S(1)}, u32[]{:S(2)}, u32[]{:S(2)}) %collective-permute-start.6) | collective-permute-done | bytes 4128 | tf_op jit(solution)/shard_map/ppermute | solution.py:463
  165.1 1.5 collective-permute-start.7
  166.7 2.1 collective-permute-done.7
  168.8 0.6 collective-permute-start.10
  169.3 4.2 %collective-permute-start.9 = (f32[4,2,2,64]{3,2,0,1:T(2,128)S(1)}, f32[4,2,2,64]{3,2,0,1:T(2,128)S(1)}, u32[]{:S(2)}, u32[]{:S(2)}) collective-permute-start(f32[4,2,2,64]{3,2,0,1:T(2,128)S(1)} %add.47), channel_id=1, source_target_pairs={{0,2},{1,3},{2,0},{3,1},{4,6},{5,7},{6,4},{7,5},{8,10},{9,11},{10,... | collective-permute-start | bytes 12296 | tf_op jit(solution)/shard_map/ppermute | solution.py:431
  173.6 0.0 collective-permute-done.2
  173.6 1.4 collective-permute-start.8
  175.0 32.7 %collective-permute-done.3 = f32[4,32,1536]{2,1,0:T(8,128)} collective-permute-done((f32[4,32,1536]{2,1,0:T(8,128)}, f32[4,32,1536]{2,1,0:T(8,128)}, u32[]{:S(2)}, u32[]{:S(2)}) %collective-permute-start.3) | collective-permute-done | bytes 786464 | tf_op jit(solution)/shard_map/ppermute | solution.py:431
  207.7 17.0 %collective-permute-done.4 = f32[4,32,1536]{2,1,0:T(8,128)} collective-permute-done((f32[4,32,1536]{2,1,0:T(8,128)}, f32[4,32,1536]{2,1,0:T(8,128)}, u32[]{:S(2)}, u32[]{:S(2)}) %collective-permute-start.4) | collective-permute-done | bytes 786464 | tf_op jit(solution)/shard_map/ppermute | solution.py:431
  224.6 0.0 copy-done.1
  224.6 4.4 %add_components.3 = f32[4,3,2,32,1536]{4,3,2,1,0:T(8,128)} custom-call(s32[3]{0:T(128)S(1)} %copy-done.2, f32[4,3,2,32,1536]{4,3,2,1,0:T(8,128)} %get-tuple-element.11.base_hbm, f32[2,2,32,1536]{3,2,1,0:T(8,128)S(1)} %bitcast.26, f32[2,2,32,1536]{3,2,1,0:T(8,128)S(1)} %bitcast.27, ...), custom_call_target="tpu_custom_call", output_to_operand_aliasing={{}: (1, {})} | custom-call | flops 786432 | bytes 9437184 | tf_op jit(solution)/shard_map/add_components/pallas_call | solution.py:397
  229.0 0.0 collective-permute-done.10
  229.0 0.0 collective-permute-done.9
  229.0 0.0 collective-permute-done.8
  229.1 0.6 add_bitcast_fusion
  (11 shorter events, 0.1 us)
Async XLA Ops:
  0.6 106.8 %all-to-all-start = ((f32[4,6,32,1536]{3,2,1,0:T(8,128)}), f32[4,6,32,1536]{3,2,1,0:T(8,128)}, u32[]{:S(2)}, u32[]{:S(2)}) async-start(f32[4,6,32,1536]{3,2,1,0:T(8,128)} %bitcast.24), calls=%async_computation | async-start | bytes 9437184 | tf_op jit(solution)/shard_map/all_to_all | solution.py:428
  6.0 6.2 %copy-start.7 = (s32[4]{0:T(128)S(1)}, s32[4]{0:T(128)}, u32[]{:S(2)}) copy-start(s32[4]{0:T(128)} %param.11) | copy-start | bytes 52
  6.0 26.6 %copy-start.4 = (f32[2,32]{1,0:T(2,128)S(1)}, f32[2,32]{1,0:T(2,128)}, u32[]{:S(2)}) copy-start(f32[2,32]{1,0:T(2,128)} %param.8) | copy-start | bytes 772
  6.0 26.7 %copy-start.3 = (f32[15,32]{1,0:T(8,128)S(1)}, f32[15,32]{1,0:T(8,128)}, u32[]{:S(2)}) copy-start(f32[15,32]{1,0:T(8,128)} %param.9) | copy-start | bytes 5764
  7.9 24.8 %collective-permute-start.1 = (f32[4,3,2,8,1536]{4,3,2,1,0:T(8,128)S(1)}, f32[4,3,2,8,1536]{4,3,2,1,0:T(8,128)S(1)}, u32[]{:S(2)}, u32[]{:S(2)}) collective-permute-start(f32[4,3,2,8,1536]{4,3,2,1,0:T(8,128)S(1)} %get-tuple-element.18), channel_id=1, source_target_pairs={{4,0},{8,4},{12,8},{16,12},{20,16},{24,20},{28,24},{5,1},{9,5},{13... | collective-permute-start | bytes 3538952 | tf_op jit(solution)/shard_map/ppermute | solution.py:439
  9.8 22.9 %collective-permute-start = (f32[4,3,2,8,1536]{4,3,2,1,0:T(8,128)S(1)}, f32[4,3,2,8,1536]{4,3,2,1,0:T(8,128)S(1)}, u32[]{:S(2)}, u32[]{:S(2)}) collective-permute-start(f32[4,3,2,8,1536]{4,3,2,1,0:T(8,128)S(1)} %get-tuple-element.19), channel_id=1, source_target_pairs={{0,4},{4,8},{8,12},{12,16},{16,20},{20,24},{24,28},{1,5},{5,9},{9,... | collective-permute-start | bytes 3538952 | tf_op jit(solution)/shard_map/ppermute | solution.py:438
  32.9 2.3 %copy-start = (f32[4,3,2,32,1536]{4,3,2,1,0:T(8,128)S(1)}, f32[4,3,2,32,1536]{4,3,2,1,0:T(8,128)}, u32[]{:S(2)}) copy-start(f32[4,3,2,32,1536]{4,3,2,1,0:T(8,128)} %field_ref.1) | copy-start | bytes 14155780
  114.6 6.9 %copy-start.5 = (f32[2,8]{1,0:T(2,128)S(1)}, f32[2,8]{1,0:T(2,128)}, u32[]{:S(2)}) copy-start(f32[2,8]{1,0:T(2,128)} %param.10) | copy-start | bytes 196
  114.6 42.1 %all-to-all-start.1 = ((f32[4,2,32,1536]{3,2,1,0:T(8,128)}), f32[4,2,32,1536]{3,2,1,0:T(8,128)S(1)}, u32[]{:S(2)}, u32[]{:S(2)}) async-start(f32[4,2,32,1536]{3,2,1,0:T(8,128)} %filter_first.1), calls=%async_computation.1 | async-start | bytes 3145728 | tf_op jit(solution)/shard_map/all_to_all | solution.py:428
  122.3 34.5 %copy-start.2 = (s32[3]{0:T(128)S(1)}, s32[3]{0:T(128)}, u32[]{:S(2)}) copy-start(s32[3]{0:T(128)} %pad_add_fusion.me_ref) | copy-start | bytes 40
  133.3 40.3 %collective-permute-start.2 = (f32[4,32,1536]{2,1,0:T(8,128)}, f32[4,32,1536]{2,1,0:T(8,128)S(1)}, u32[]{:S(2)}, u32[]{:S(2)}) collective-permute-start(f32[4,32,1536]{2,1,0:T(8,128)} %get-tuple-element.14), channel_id=1, source_target_pairs={{0,1},{1,0},{2,3},{3,2},{4,5},{5,4},{6,7},{7,6},{8,9},{9,8},{10,11... | collective-permute-start | bytes 2359304 | tf_op jit(solution)/shard_map/ppermute | solution.py:431
  133.4 74.2 %collective-permute-start.3 = (f32[4,32,1536]{2,1,0:T(8,128)}, f32[4,32,1536]{2,1,0:T(8,128)}, u32[]{:S(2)}, u32[]{:S(2)}) collective-permute-start(f32[4,32,1536]{2,1,0:T(8,128)} %get-tuple-element.15), channel_id=1, source_target_pairs={{0,2},{1,3},{2,0},{3,1},{4,6},{5,7},{6,4},{7,5},{8,10},{9,11},{10,... | collective-permute-start | bytes 2359304 | tf_op jit(solution)/shard_map/ppermute | solution.py:431
  136.3 88.3 %collective-permute-start.4 = (f32[4,32,1536]{2,1,0:T(8,128)}, f32[4,32,1536]{2,1,0:T(8,128)}, u32[]{:S(2)}, u32[]{:S(2)}) collective-permute-start(f32[4,32,1536]{2,1,0:T(8,128)} %get-tuple-element.16), channel_id=1, source_target_pairs={{0,3},{1,2},{2,1},{3,0},{4,7},{5,6},{6,5},{7,4},{8,11},{9,10},{10,... | collective-permute-start | bytes 2359304 | tf_op jit(solution)/shard_map/ppermute | solution.py:431
  156.8 3.1 %copy-start.6 = (s32[1536]{0:T(1024)S(1)}, s32[1536]{0:T(1024)}, u32[]{:S(2)}) copy-start(s32[1536]{0:T(1024)} %param.12) | copy-start | bytes 18436
  156.8 67.8 %copy-start.1 = (f32[4,32,1536]{2,1,0:T(8,128)S(1)}, f32[4,32,1536]{2,1,0:T(8,128)}, u32[]{:S(2)}) copy-start(f32[4,32,1536]{2,1,0:T(8,128)} %get-tuple-element.13) | copy-start | bytes 2359300
  160.2 1.2 collective-permute-start.5
  161.5 3.7 %collective-permute-start.6 = (f32[4,2,2,64]{3,2,0,1:T(2,128)S(1)}, f32[4,2,2,64]{3,2,0,1:T(2,128)S(1)}, u32[]{:S(2)}, u32[]{:S(2)}) collective-permute-start(f32[4,2,2,64]{3,2,0,1:T(2,128)S(1)} %copy_add_fusion), channel_id=1, source_target_pairs={{0,8},{4,12},{8,0},{12,4},{16,24},{20,28},{24,16},{28,20},{1,9},{5... | collective-permute-start | bytes 12296 | tf_op jit(solution)/shard_map/ppermute | solution.py:463
  165.1 3.7 %collective-permute-start.7 = (f32[4,2,2,64]{3,2,0,1:T(2,128)S(1)}, f32[4,2,2,64]{3,2,0,1:T(2,128)S(1)}, u32[]{:S(2)}, u32[]{:S(2)}) collective-permute-start(f32[4,2,2,64]{3,2,0,1:T(2,128)S(1)} %add.46), channel_id=1, source_target_pairs={{0,16},{4,20},{8,24},{12,28},{16,0},{20,4},{24,8},{28,12},{1,17},{... | collective-permute-start | bytes 12296 | tf_op jit(solution)/shard_map/ppermute | solution.py:463
  168.8 60.2 %collective-permute-start.10 = (f32[4,2,2,64]{3,2,0,1:T(2,128)S(1)}, f32[4,2,2,64]{3,2,0,1:T(2,128)S(1)}, u32[]{:S(2)}, u32[]{:S(2)}) collective-permute-start(f32[4,2,2,64]{3,2,0,1:T(2,128)S(1)} %add.47), channel_id=1, source_target_pairs={{0,3},{1,2},{2,1},{3,0},{4,7},{5,6},{6,5},{7,4},{8,11},{9,10},{10,... | collective-permute-start | bytes 12296 | tf_op jit(solution)/shard_map/ppermute | solution.py:431
  169.3 59.7 %collective-permute-start.9 = (f32[4,2,2,64]{3,2,0,1:T(2,128)S(1)}, f32[4,2,2,64]{3,2,0,1:T(2,128)S(1)}, u32[]{:S(2)}, u32[]{:S(2)}) collective-permute-start(f32[4,2,2,64]{3,2,0,1:T(2,128)S(1)} %add.47), channel_id=1, source_target_pairs={{0,2},{1,3},{2,0},{3,1},{4,6},{5,7},{6,4},{7,5},{8,10},{9,11},{10,... | collective-permute-start | bytes 12296 | tf_op jit(solution)/shard_map/ppermute | solution.py:431
  173.6 55.5 %collective-permute-start.8 = (f32[4,2,2,64]{3,2,0,1:T(2,128)S(1)}, f32[4,2,2,64]{3,2,0,1:T(2,128)S(1)}, u32[]{:S(2)}, u32[]{:S(2)}) collective-permute-start(f32[4,2,2,64]{3,2,0,1:T(2,128)S(1)} %add.47), channel_id=1, source_target_pairs={{0,1},{1,0},{2,3},{3,2},{4,5},{5,4},{6,7},{7,6},{8,9},{9,8},{10,11... | collective-permute-start | bytes 12296 | tf_op jit(solution)/shard_map/ppermute | solution.py:431

commit v10 on v9

--- a/solution.py
+++ b/solution.py
@@ -158,23 +158,59 @@
     return x
 
 
-def filter_lines(line_ref, wave_ref, table_ref, table_copies):
-    _, line_count, row_count, width = line_ref.shape
-    pieces = width // LANES
-    groups = row_count // PAD
-
-    def spots(step):
-        return step // groups, pl.ds(pl.multiple_of(step % groups * PAD, PAD), PAD), pl.ds(pl.multiple_of(step * PAD, PAD), PAD)
-
-    def forward(step, _):
-        line, rows, spot = spots(step)
-        values = [line_ref[n1 // pieces, line, rows, pl.ds(n1 % pieces * LANES, LANES)] for n1 in range(OUTER)]
-        for tile, (re, im) in enumerate(real_forward(values)):
-            wave_ref[tile, spot, :LANES] = re
-            wave_ref[tile, spot, LANES:] = im
-        return 0
-
-    lax.fori_loop(0, line_count * groups, forward, 0)
+def group_count(piece):
+    return piece[1] * piece[3]
+
+
+def piece_at(ref, piece):
+    return ref.at[:, pl.ds(piece[0], piece[1]), pl.ds(piece[2], piece[3])]
+
+
+def start_all(copies):
+    for copy in copies:
+        copy.start()
+    return copies
+
+
+def wait_all(copies):
+    for copy in copies:
+        copy.wait()
+
+
+def run_filter(pieces, table_hbm, lines_hbm, send, scratch):
+    *line_refs, wave_ref, table_ref, table_sems, sems = scratch
+    copies = [
+        pltpu.make_async_copy(piece_at(lines_hbm, piece), line_ref, sems.at[i])
+        for i, (piece, line_ref) in enumerate(zip(pieces, line_refs))
+    ]
+    start_all(copies)
+    step = TILES // TABLE_COPIES
+    spans = [pl.ds(i * step, step) for i in range(TABLE_COPIES)]
+    table_copies = [
+        pltpu.make_async_copy(table_hbm.at[span], table_ref.at[span], table_sems.at[i]) for i, span in enumerate(spans)
+    ]
+    start_all(table_copies)
+    offsets = [sum(map(group_count, pieces[:i])) for i in range(len(pieces))]
+    per_source = lines_hbm.shape[4] // LANES
+
+    def spot(number):
+        return pl.ds(pl.multiple_of(number * PAD, PAD), PAD)
+
+    for piece, line_ref, offset, copy in zip(pieces, line_refs, offsets, copies):
+        copy.wait()
+
+        def forward(number, _, groups=piece[3], line_ref=line_ref, offset=offset):
+            pair, group = number // groups, number % groups
+            values = []
+            for n1 in range(OUTER):
+                lanes = pl.ds(n1 % per_source * LANES, LANES)
+                values.append(line_ref[n1 // per_source, pair, group, :, lanes])
+            for tile, (re, im) in enumerate(real_forward(values)):
+                wave_ref[tile, spot(offset + number), :LANES] = re
+                wave_ref[tile, spot(offset + number), LANES:] = im
+            return 0
+
+        lax.fori_loop(0, group_count(piece), forward, 0)
 
     def middle(tile, _):
         value = wave_ref[tile]
@@ -186,67 +222,61 @@
         wave_ref[tile] = both[:rows] + both[rows:] + rest
         return 0
 
-    step = TILES // len(table_copies)
     for i, copy in enumerate(table_copies):
         copy.wait()
         lax.fori_loop(i * step, (i + 1) * step, middle, 0, unroll=3)
 
-    def backward(step, _):
-        line, rows, spot = spots(step)
-        tiles = [(wave_ref[tile, spot, :LANES], wave_ref[tile, spot, LANES:]) for tile in range(TILES)]
-        for n1, value in enumerate(real_backward(tiles)):
-            line_ref[n1 // pieces, line, rows, pl.ds(n1 % pieces * LANES, LANES)] = value
-        return 0
-
-    lax.fori_loop(0, line_count * groups, backward, 0)
-
-
-def start_all(copies):
-    for copy in copies:
-        copy.start()
-    return copies
-
-
-def wait_all(copies):
-    for copy in copies:
-        copy.wait()
-
-
-def wall_sums(block, weight):
-    row_count = block.shape[1]
-    lower = [jnp.sum(block[p, :PAD] * weight[0][:, :1], axis=0) for p in range(2)]
-    upper = [jnp.sum(block[p, row_count - PAD :] * weight[1][:, :1], axis=0) for p in range(2)]
-    return lower + upper
-
-
-def run_filter(table_hbm, lines_hbm, first, scratch):
-    line_ref, wave_ref, table_ref, table_sems, sems = scratch
-    count, line_count, _, _ = line_ref.shape
-    lines = pl.ds(first, line_count)
-    copies = [pltpu.make_async_copy(lines_hbm.at[x, lines], line_ref.at[x], sems.at[x]) for x in range(count)]
-    start_all(copies)
-    step = TILES // TABLE_COPIES
-    spans = [pl.ds(i * step, step) for i in range(TABLE_COPIES)]
-    table_copies = [
-        pltpu.make_async_copy(table_hbm.at[span], table_ref.at[span], table_sems.at[i]) for i, span in enumerate(spans)
-    ]
-    start_all(table_copies)
-    wait_all(copies)
-    filter_lines(line_ref, wave_ref, table_ref, table_copies)
-
-
-def filter_first_kernel(table_hbm, lines_hbm, out_hbm, *scratch):
-    run_filter(table_hbm, lines_hbm, 0, scratch)
-    line_ref, sems = scratch[0], scratch[-1]
-    wait_all(start_all([pltpu.make_async_copy(line_ref.at[x], out_hbm.at[x], sems.at[x]) for x in range(sems.shape[0])]))
-
-
-def filter_rest_kernel(me_ref, table_hbm, lines_hbm, *refs):
-    sent, scratch = refs[:-5], refs[-5:]
-    line_ref, sems, me = scratch[0], scratch[-1], me_ref[0]
-    run_filter(table_hbm, lines_hbm, lines_hbm.shape[1] - line_ref.shape[1], scratch)
-    copies = [pltpu.make_async_copy(line_ref.at[me ^ x], sent[x], sems.at[x]) for x in range(len(sent))]
-    wait_all(start_all(copies))
+    away = []
+    for i, (piece, line_ref, offset) in enumerate(zip(pieces, line_refs, offsets)):
+
+        def backward(number, _, groups=piece[3], line_ref=line_ref, offset=offset):
+            pair, group = number // groups, number % groups
+            row = spot(offset + number)
+            tiles = [(wave_ref[tile, row, :LANES], wave_ref[tile, row, LANES:]) for tile in range(TILES)]
+            for n1, value in enumerate(real_backward(tiles)):
+                line_ref[n1 // per_source, pair, group, :, pl.ds(n1 % per_source * LANES, LANES)] = value
+            return 0
+
+        lax.fori_loop(0, group_count(piece), backward, 0)
+        away += start_all(send(i, line_ref))
+    wait_all(away)
+
+
+def filter_first_kernel(pieces, table_hbm, lines_hbm, out_hbm, *scratch):
+    *scratch, out_sems = scratch
+
+    def send(i, line_ref):
+        return [pltpu.make_async_copy(line_ref.at[:, :, 0], out_hbm.at[:, i], out_sems.at[i])]
+
+    run_filter(pieces, table_hbm, lines_hbm, send, scratch)
+
+
+def filter_rest_kernel(pieces, me_ref, table_hbm, lines_hbm, *refs):
+    count, me = lines_hbm.shape[0], me_ref[0]
+    sent, scratch, out_sems = refs[:count], refs[count:-1], refs[-1]
+    places = rest_places(pieces)
+
+    def send(i, line_ref):
+        copies = []
+        for pair in range(pieces[i][1]):
+            number, first = places[i][pair]
+            target = pl.ds(first, pieces[i][3])
+            for x in range(count):
+                sem = out_sems.at[number * count + x]
+                copies.append(pltpu.make_async_copy(line_ref.at[me ^ x, pair], sent[x].at[target], sem))
+        return copies
+
+    run_filter(pieces, table_hbm, lines_hbm, send, scratch)
+
+
+def rest_places(pieces):
+    places, number, first = [], 0, 0
+    for piece in pieces:
+        places.append([])
+        for _ in range(piece[1]):
+            places[-1].append((number, first))
+            number, first = number + 1, first + piece[3]
+    return places
 
 
 HBM = pl.BlockSpec(memory_space=pltpu.HBM)
@@ -254,21 +284,22 @@
 WHOLE = pl.BlockSpec(memory_space=pltpu.VMEM)
 
 
-def filter_call(kernel, name, block, tables, in_specs, out_specs, out_shape):
-    count, line_count, row_count, width = block
-    rows = line_count * row_count
+def filter_call(kernel, name, pieces, lines, tables, in_specs, out_specs, out_shape, out_sems):
+    count, _, _, _, width = lines.shape
+    rows = sum(map(group_count, pieces)) * PAD
     flops = 3 * 2 * TILES * rows * (2 * LANES) ** 2
     return pl.pallas_call(
-        kernel,
+        functools.partial(kernel, pieces),
         out_shape=out_shape,
         in_specs=in_specs,
         out_specs=out_specs,
-        scratch_shapes=[
-            pltpu.VMEM(block, jnp.float32),
+        scratch_shapes=[pltpu.VMEM((count, piece[1], piece[3], PAD, width), jnp.float32) for piece in pieces]
+        + [
             pltpu.VMEM((TILES, rows, 2 * LANES), jnp.float32),
             pltpu.VMEM(tables.shape, tables.dtype),
             pltpu.SemaphoreType.DMA((TABLE_COPIES,)),
-            pltpu.SemaphoreType.DMA((count,)),
+            pltpu.SemaphoreType.DMA((len(pieces),)),
+            pltpu.SemaphoreType.DMA((out_sems,)),
         ],
         compiler_params=pltpu.CompilerParams(vmem_limit_bytes=FILTER_VMEM),
         cost_estimate=pl.CostEstimate(flops=flops, bytes_accessed=8 * count * rows * width, transcendentals=0),
@@ -276,19 +307,22 @@
     )
 
 
-def filter_first(lines, tables):
-    block = (lines.shape[0], 2) + lines.shape[2:]
-    out_shape = jax.ShapeDtypeStruct(block, jnp.float32)
-    call = filter_call(filter_first_kernel, "filter_first", block, tables, [HBM, HBM], HBM, out_shape)
+def filter_first(lines, tables, pieces):
+    count, _, _, _, width = lines.shape
+    out_shape = jax.ShapeDtypeStruct((count, len(pieces), 2, PAD, width), jnp.float32)
+    call = filter_call(
+        filter_first_kernel, "filter_first", pieces, lines, tables, [HBM, HBM], HBM, out_shape, len(pieces)
+    )
     return call(tables, lines)
 
 
-def filter_rest(lines, spots, tables):
-    count, line_count, row_count, width = lines.shape
-    block = (count, line_count - 2, row_count, width)
-    out_shape = [jax.ShapeDtypeStruct(block[1:], jnp.float32)] * count
+def filter_rest(lines, spots, tables, pieces):
+    count, _, _, _, width = lines.shape
+    shape = (sum(map(group_count, pieces)), PAD, width)
+    out_shape = [jax.ShapeDtypeStruct(shape, jnp.float32)] * count
+    sems = count * sum(piece[1] for piece in pieces)
     ins = [SCALARS, HBM, HBM]
-    call = filter_call(filter_rest_kernel, "filter_rest", block, tables, ins, [HBM] * count, out_shape)
+    call = filter_call(filter_rest_kernel, "filter_rest", pieces, lines, tables, ins, [HBM] * count, out_shape, sems)
     return call(spots, tables, lines)
 
 
@@ -349,62 +383,108 @@
     )(rate, coef, flow, field, low, high)
 
 
-def add_kernel(row_split, comps, me_ref, base_hbm, *refs):
-    base_ref, term_ref, base_sems, term_sems = refs[-4:]
-    count, _, _, row_count, _ = base_ref.shape
-    sums = comps.start == 0
-    if sums:
-        weight_ref, *terms, out_hbm, shear_ref = refs[:-4]
-    else:
-        *terms, out_hbm = refs[:-4]
-    me = me_ref[0]
-
-    def spot(ref, x):
+def add_first_kernel(pieces, me_ref, base_hbm, weight_ref, term_hbm, out_hbm, shear_ref, *scratch):
+    base_ref, term_ref, base_sems, term_sems = scratch
+    count, split, me = term_hbm.shape[0], base_hbm.shape[2], me_ref[0]
+
+    def spot(ref, x, i):
         other = me ^ x
-        top = pl.multiple_of(other % row_split * row_count, PAD)
-        return ref.at[other // row_split, comps, :, pl.ds(top, row_count)]
-
-    loads = [pltpu.make_async_copy(spot(base_hbm, x), base_ref.at[x], base_sems.at[x]) for x in range(count)]
-    sources = [terms[0].at[me ^ x] if len(terms) == 1 else terms[x] for x in range(count)]
-    term_loads = [pltpu.make_async_copy(sources[x], term_ref.at[x], term_sems.at[x]) for x in range(count)]
-    stores = [pltpu.make_async_copy(base_ref.at[x], spot(out_hbm, x), base_sems.at[x]) for x in range(count)]
+        return ref.at[other // split, pl.ds(0, 2), other % split, pieces[i][2]]
+
+    spots = [(x, i) for x in range(count) for i in range(len(pieces))]
+    sem = [base_sems.at[x * len(pieces) + i] for x, i in spots]
+    loads = [pltpu.make_async_copy(spot(base_hbm, *at), base_ref.at[at], sem[n]) for n, at in enumerate(spots)]
+    stores = [pltpu.make_async_copy(base_ref.at[at], spot(out_hbm, *at), sem[n]) for n, at in enumerate(spots)]
+    terms = [pltpu.make_async_copy(term_hbm.at[me ^ x], term_ref.at[x], term_sems.at[x]) for x in range(count)]
+    start_all(loads)
+    start_all(terms)
+    wait_all(terms)
+    wait_all(loads)
     for x in range(count):
-        loads[x].start()
-        term_loads[x].start()
-    for x in range(count):
-        loads[x].wait()
-        term_loads[x].wait()
         base_ref[x] = base_ref[x] + term_ref[x]
-        stores[x].start()
-        if sums:
-            for place, value in enumerate(wall_sums(base_ref.at[x, 0], weight_ref[x])):
-                shear_ref[me ^ x, place] = value
+        start_all(stores[x * len(pieces) : (x + 1) * len(pieces)])
+        for p in range(2):
+            shear_ref[me ^ x, p] = jnp.sum(base_ref[x, 0, p] * weight_ref[x, 0][:, :1], axis=0)
+            shear_ref[me ^ x, 2 + p] = jnp.sum(base_ref[x, len(pieces) - 1, p] * weight_ref[x, 1][:, :1], axis=0)
     wait_all(stores)
 
 
-def add_components(base, terms, spots, row_split, comps, weight=None):
-    first, last = comps
-    _, _, part_count, row_count, width = base.shape
-    span = weight.shape[0] if weight is not None else len(terms)
-    block = (span, last - first, part_count, row_count // row_split, width)
-    terms = [term.reshape(block[1:] if len(terms) > 1 else block) for term in terms]
-    size = math.prod(block)
-    buffer, sems = pltpu.VMEM(block, jnp.float32), pltpu.SemaphoreType.DMA((span,))
-    out_shape, out_specs, weights = jax.ShapeDtypeStruct(base.shape, jnp.float32), HBM, []
-    if weight is not None:
-        out_shape, out_specs = (out_shape, jax.ShapeDtypeStruct((span, 4, width), jnp.float32)), (HBM, WHOLE)
-        weights = [weight]
+def add_first(base, term, weight, spots, pieces):
+    count, width = term.shape[0], term.shape[4]
+    buffer = pltpu.VMEM(term.shape, jnp.float32)
     return pl.pallas_call(
-        functools.partial(add_kernel, row_split, pl.ds(first, last - first)),
-        out_shape=out_shape,
-        in_specs=[SCALARS, HBM] + [WHOLE] * len(weights) + [HBM] * len(terms),
-        out_specs=out_specs,
-        scratch_shapes=[buffer, buffer, sems, sems],
+        functools.partial(add_first_kernel, pieces),
+        out_shape=(
+            jax.ShapeDtypeStruct(base.shape, jnp.float32),
+            jax.ShapeDtypeStruct((count, 4, width), jnp.float32),
+        ),
+        in_specs=[SCALARS, HBM, WHOLE, HBM],
+        out_specs=(HBM, WHOLE),
+        scratch_shapes=[
+            buffer,
+            buffer,
+            pltpu.SemaphoreType.DMA((count * len(pieces),)),
+            pltpu.SemaphoreType.DMA((count,)),
+        ],
+        input_output_aliases={1: 0},
+        compiler_params=pltpu.CompilerParams(vmem_limit_bytes=24 << 20),
+        cost_estimate=pl.CostEstimate(flops=term.size, bytes_accessed=12 * term.size, transcendentals=0),
+        name="add_first",
+    )(spots, base, weight, term)
+
+
+def add_rest_kernel(pieces, partners, me_ref, base_hbm, *refs):
+    count = len(partners)
+    terms, out_hbm = refs[:count], refs[count]
+    base_ref, term_ref, base_sems, term_sems = refs[count + 1 :]
+    split, me = base_hbm.shape[2], me_ref[0]
+    places = rest_places(pieces)
+    spots = []
+    for n, x in enumerate(partners):
+        for piece, pairs in zip(pieces, places):
+            for pair, (number, first) in enumerate(pairs):
+                spots.append((n, x, piece[0] + pair, pl.ds(piece[2], piece[3]), pl.ds(first, piece[3])))
+
+    def far(ref, spot):
+        other = me ^ spot[1]
+        return ref.at[other // split, spot[2], other % split, spot[3]]
+
+    def near(spot):
+        return base_ref.at[spot[0], spot[4]]
+
+    loads = [pltpu.make_async_copy(far(base_hbm, at), near(at), base_sems.at[n]) for n, at in enumerate(spots)]
+    stores = [pltpu.make_async_copy(near(at), far(out_hbm, at), base_sems.at[n]) for n, at in enumerate(spots)]
+    copies = [pltpu.make_async_copy(terms[n], term_ref.at[n], term_sems.at[n]) for n in range(count)]
+    start_all(copies)
+    start_all(loads)
+    wait_all(copies)
+    for load, store, at in zip(loads, stores, spots):
+        load.wait()
+        base_ref[at[0], at[4]] = base_ref[at[0], at[4]] + term_ref[at[0], at[4]]
+        store.start()
+    wait_all(stores)
+
+
+def add_rest(base, terms, partners, spots, pieces):
+    buffer = pltpu.VMEM((len(terms),) + terms[0].shape, jnp.float32)
+    size = len(terms) * terms[0].size
+    copies = len(terms) * sum(piece[1] for piece in pieces)
+    return pl.pallas_call(
+        functools.partial(add_rest_kernel, pieces, partners),
+        out_shape=jax.ShapeDtypeStruct(base.shape, jnp.float32),
+        in_specs=[SCALARS, HBM] + [HBM] * len(terms),
+        out_specs=HBM,
+        scratch_shapes=[
+            buffer,
+            buffer,
+            pltpu.SemaphoreType.DMA((copies,)),
+            pltpu.SemaphoreType.DMA((len(terms),)),
+        ],
         input_output_aliases={1: 0},
         compiler_params=pltpu.CompilerParams(vmem_limit_bytes=24 << 20),
         cost_estimate=pl.CostEstimate(flops=size, bytes_accessed=12 * size, transcendentals=0),
-        name="add_components",
-    )(spots, base, *weights, *terms)
+        name="add_rest",
+    )(spots, base, *terms)
 
 
 def after(value, *others):
@@ -422,7 +502,7 @@
     line_rows = row_count // row_split
     tables = jnp.asarray(spectral_tables(width * span))
     pairs = [[(i, i ^ x) for i in range(span)] for x in range(span)]
-    spots = jnp.stack([me, me // row_split, me % row_split * line_rows]).astype(jnp.int32)
+    spots = jnp.stack([me]).astype(jnp.int32)
 
     def exchange(lines):
         return lax.all_to_all(lines, "span", split_axis=0, concat_axis=0)
@@ -430,8 +510,15 @@
     def swap(blocks):
         return [lax.ppermute(blocks[x], "span", pairs[x]) for x in range(span - 1, 0, -1)][::-1]
 
-    lines = field.reshape(mode_split, -1, row_split, line_rows, width)
-    lines = exchange(lines.transpose(0, 2, 1, 3, 4).reshape(span, -1, line_rows, width))
+    pairs_count, groups = comp_count * part_count, line_rows // PAD
+    shares = (mode_split, pairs_count, row_split, groups, PAD, width)
+    lines = field.reshape(shares).transpose(0, 2, 1, 3, 4, 5)
+    lines = exchange(lines.reshape(span, pairs_count, groups, PAD, width))
+    wall_groups = sorted({0, groups - 1})
+    first_pieces = tuple((0, 2, group, 1) for group in wall_groups)
+    rest_pieces = tuple((2 * comp, 2, 0, groups) for comp in range(1, comp_count))
+    if groups > 2:
+        rest_pieces = ((0, 2, 1, groups - 2),) + rest_pieces
 
     forward = [(i, i + 1) for i in range(wall_count - 1)]
     backward = [(i + 1, i) for i in range(wall_count - 1)]
@@ -444,9 +531,9 @@
     base = local_terms(field, low, high, rate, coef, flow)
 
     lines = after(lines, base)
-    filtered = filter_first(lines, tables)
+    filtered = filter_first(lines, tables, first_pieces)
     back = exchange(filtered)
-    sent = filter_rest(after(lines, filtered), spots, tables)
+    sent = filter_rest(after(lines, filtered), spots, tables, rest_pieces)
     returned = [sent[0]] + swap(sent)
 
     lower = jnp.where(wall_index == 0, wall_coef[0], 0.0)
@@ -454,7 +541,7 @@
     group = ((me ^ jnp.arange(span)) % row_split)[:, None]
     ends = [jnp.where(group == 0, lower, 0.0), jnp.where(group == row_split - 1, upper, 0.0)]
     weight = jnp.broadcast_to(jnp.stack(ends, axis=1)[..., None], (span, 2, PAD, LANES))
-    result, shear = add_components(base, [back], spots, row_split, (0, 1), weight)
+    result, shear = add_first(base.reshape(shares), back, weight, spots, first_pieces)
     onehot = (patch_of[:, None] == jnp.arange(PATCH, dtype=jnp.int32)[None, :]).astype(jnp.float32)
     grad = jnp.einsum("swz,zq->swq", shear, onehot, precision=lax.Precision.HIGHEST)
     grad = grad.reshape(mode_count, row_split, 2, part_count, PATCH).sum(axis=1)
@@ -466,8 +553,11 @@
     parts = [lax.dynamic_index_in_dim(parts, me ^ x, 0, keepdims=False) for x in range(span)]
     wall_grad = functools.reduce(jnp.add, parts).transpose(1, 0, 2, 3)
 
-    result = add_components(result, returned, spots, row_split, (1, comp_count))
-    return (result, wall_grad)
+    cuts = [0, span // 2, 3 * span // 4, span]
+    for low_cut, high_cut in zip(cuts, cuts[1:]):
+        partners = range(low_cut, high_cut)
+        result = add_rest(result, returned[low_cut:high_cut], partners, spots, rest_pieces)
+    return (result.reshape(field.shape), wall_grad)
 
 
 def solution(mesh):

time: 230 us -> 226 us (0.983)
  waiting for transfers between devices: 154 us -> 151 us
    all_to_all x2, waiting for transfers between devices: 77.1 us -> 63.8 us  [exchange(): return lax.all_to_all(lines, 'span', split_axis=0, concat_axis=0)]
    ppermute x6, waiting for transfers between devices: 49.6 us -> 60.7 us  [swap(): lax.ppermute(blocks[x], 'span', pairs[x])]
    pallas_call x2 -> x4, Pallas kernels: 7.45 us -> 10.4 us  [the longest x3 8.15 us: add_rest(): pl.pallas_call(functools.partial(add_rest_kernel, pieces, partners), out_...]
    pallas_call x1, Pallas kernels: 7.18 us -> 4.77 us  [filter_first(): return call(tables, lines)]
    unnamed x16 -> x14, local copies, waits for them, and re-layouts: 2.36 us -> 0.03 us
  transfers between devices with their start and end apart: 13 -> 13, of which waited for: 8 -> 9; matrix products, arithmetic and copies ran while one was open for 1% -> 1% of each run, Pallas kernels for 15% -> 16%
where the time goes in v10:
time: 226 us; the launch traced here: 225 us
  waiting for transfers between devices  151 us (67%)
  Pallas kernels  40.3 us (18%)
  starting transfers between devices  29.6 us (13%)
  local copies, waits for them, and re-layouts  2.35 us (1%)
    all_to_all x2, waiting for transfers between devices, exchange(): return lax.all_to_all(lines, 'span', split_axis=0, concat_axis=0)  63.8 us
    ppermute x6, waiting for transfers between devices, swap(): lax.ppermute(blocks[x], 'span', pairs[x])  60.7 us
    ppermute x1, waiting for transfers between devices, on_device(): high = lax.ppermute(field[:, :, :, :PAD], 'wall', backward)  20.4 us
    pallas_call x1, Pallas kernels, local_terms(): pl.pallas_call(local_kernel, grid=(mode_count,), out_shape=jax.ShapeDtype...  15.1 us
    all_to_all x2, starting transfers between devices, exchange(): return lax.all_to_all(lines, 'span', split_axis=0, concat_axis=0)  12.4 us
    ppermute x6, starting transfers between devices, swap(): lax.ppermute(blocks[x], 'span', pairs[x])  10.7 us
    pallas_call x1, Pallas kernels, filter_rest(): return call(spots, tables, lines)  10.1 us
    pallas_call x3, Pallas kernels, add_rest(): pl.pallas_call(functools.partial(add_rest_kernel, pieces, partners), out_...  8.15 us
  transfers between devices with their start and end apart: 13, of which 9 were waited for; matrix products, arithmetic and copies ran while one was open for 1% of the time, Pallas kernels for 16%

profile of v10, /device:TPU:10, one launch (start us, length us, event | category | flops | bytes accessed | tf_op | source)
XLA Modules:
  0.0 225.5 jit_solution(3390547633912631138)
XLA Ops:
  0.6 0.0 copy-start.6
  0.6 0.0 copy-start.3
  0.7 5.5 %all-to-all-start = ((f32[4,6,4,8,1536]{4,3,2,1,0:T(8,128)}), f32[4,6,4,8,1536]{4,3,2,1,0:T(8,128)}, u32[]{:S(2)}, u32[]{:S(2)}) async-start(f32[4,6,4,8,1536]{4,3,2,1,0:T(8,128)} %bitcast.21), calls=%async_computation | async-start | bytes 9437184 | tf_op jit(solution)/shard_map/all_to_all | solution.py:508
  6.2 0.0 copy-start.2
  6.2 0.0 copy-start
  6.2 1.9 fusion.6
  8.1 2.1 collective-permute-start.1
  10.2 2.4 %collective-permute-start = (f32[4,3,2,8,1536]{4,3,2,1,0:T(8,128)S(1)}, f32[4,3,2,8,1536]{4,3,2,1,0:T(8,128)S(1)}, u32[]{:S(2)}, u32[]{:S(2)}) collective-permute-start(f32[4,3,2,8,1536]{4,3,2,1,0:T(8,128)S(1)} %get-tuple-element.19), channel_id=1, source_target_pairs={{0,4},{4,8},{8,12},{12,16},{16,20},{20,24},{24,28},{1,5},{5,9},{9,... | collective-permute-start | bytes 3538952 | tf_op jit(solution)/shard_map/ppermute | solution.py:525
  12.6 0.0 copy-done.6
  12.6 20.4 %collective-permute-done.1.high_ref = f32[4,3,2,8,1536]{4,3,2,1,0:T(8,128)S(1)} collective-permute-done((f32[4,3,2,8,1536]{4,3,2,1,0:T(8,128)S(1)}, f32[4,3,2,8,1536]{4,3,2,1,0:T(8,128)S(1)}, u32[]{:S(2)}, u32[]{:S(2)}) %collective-permute-start.1) | collective-permute-done | bytes 1179680 | tf_op jit(solution)/shard_map/ppermute | solution.py:526
  33.0 0.0 collective-permute-done.low_ref
  33.0 0.0 copy-done.3
  33.0 0.1 broadcast_in_dim.46.flow_ref
  33.1 0.0 copy-done.2
  33.1 0.1 broadcast_in_dim.45.coef_ref
  33.2 0.0 copy-done
  33.3 15.1 %local_terms.1 = f32[4,3,2,32,1536]{4,3,2,1,0:T(8,128)} custom-call(f32[4]{0:T(128)S(1)} %convert_multiply_fusion.rate_ref, f32[15,32,128]{2,1,0:T(8,128)S(1)} %broadcast_in_dim.45.coef_ref, f32[2,32,128]{2,1,0:T(8,128)S(1)} %broadcast_in_dim.46.flow_ref, f32[4,3,2,32,1536]{4,3,2,1,0:T(8,128)S(1)} %copy-done, ...), custom_call_target="tpu_custom_call" | custom-call | flops 47185920 | bytes 11796480 | tf_op jit(solution)/shard_map/local_terms/pallas_call | solution.py:366
  48.3 59.2 %all-to-all-done.lines_hbm = f32[4,6,4,8,1536]{4,3,2,1,0:T(8,128)} async-done(((f32[4,6,4,8,1536]{4,3,2,1,0:T(8,128)}), f32[4,6,4,8,1536]{4,3,2,1,0:T(8,128)}, u32[]{:S(2)}, u32[]{:S(2)}) %all-to-all-start) | async-done | bytes 4718624 | tf_op jit(solution)/shard_map/all_to_all | solution.py:508
  107.5 4.8 %filter_first.1 = f32[4,2,2,8,1536]{4,3,2,1,0:T(8,128)} custom-call(bf16[24,2,256,256]{3,2,1,0:T(8,128)(2,1)} %constant.50.clone.table_hbm, f32[4,6,4,8,1536]{4,3,2,1,0:T(8,128)} %all-to-all-done.lines_hbm), custom_call_target="tpu_custom_call" | custom-call | flops 301989888 | bytes 1572864 | tf_op jit(solution)/shard_map/filter_first/pallas_call | solution.py:316
  112.3 6.9 %all-to-all-start.1 = ((f32[4,2,2,8,1536]{4,3,2,1,0:T(8,128)}), f32[4,2,2,8,1536]{4,3,2,1,0:T(8,128)S(1)}, u32[]{:S(2)}, u32[]{:S(2)}) async-start(f32[4,2,2,8,1536]{4,3,2,1,0:T(8,128)} %filter_first.1), calls=%async_computation.1 | async-start | bytes 1572864 | tf_op jit(solution)/shard_map/all_to_all | solution.py:508
  119.2 0.0 copy-start.4
  119.2 10.1 %filter_rest.1 = (f32[20,8,1536]{2,1,0:T(8,128)}, f32[20,8,1536]{2,1,0:T(8,128)}, f32[20,8,1536]{2,1,0:T(8,128)}, f32[20,8,1536]{2,1,0:T(8,128)}) custom-call(s32[1]{0:T(128)} %bitcast.me_ref, bf16[24,2,256,256]{3,2,1,0:T(8,128)(2,1)} %constant.50.clone.table_hbm, f32[4,6,4,8,1536]{4,3,2,1,0:T(8,128)} %all-to-all-done.lines_hbm), custom_call_target="tpu_custom_call" | custom-call | flops 1509949440 | bytes 7864320 | tf_op jit(solution)/shard_map/filter_rest/pallas_call | solution.py:326
  129.3 0.0 copy-start.5
  129.3 0.0 copy-start.1
  129.3 0.1 collective-permute-start.2
  129.4 2.9 %collective-permute-start.3 = (f32[20,8,1536]{2,1,0:T(8,128)}, f32[20,8,1536]{2,1,0:T(8,128)}, u32[]{:S(2)}, u32[]{:S(2)}) collective-permute-start(f32[20,8,1536]{2,1,0:T(8,128)} %get-tuple-element.15), channel_id=1, source_target_pairs={{0,2},{1,3},{2,0},{3,1},{4,6},{5,7},{6,4},{7,5},{8,10},{9,11},{10,... | collective-permute-start | bytes 2949128 | tf_op jit(solution)/shard_map/ppermute | solution.py:511
  132.3 0.6 collective-permute-start.4
  132.8 0.0 copy-done.4
  132.8 0.1 rev.3
  133.0 4.6 %all-to-all-done.1.term_hbm = f32[4,2,2,8,1536]{4,3,2,1,0:T(8,128)S(1)} async-done(((f32[4,2,2,8,1536]{4,3,2,1,0:T(8,128)}), f32[4,2,2,8,1536]{4,3,2,1,0:T(8,128)S(1)}, u32[]{:S(2)}, u32[]{:S(2)}) %all-to-all-start.1) | async-done | bytes 786464 | tf_op jit(solution)/shard_map/all_to_all | solution.py:508
  137.5 0.1 broadcast_in_dim.50.weight_ref
  137.6 2.3 %add_first.1 = (f32[4,6,1,4,8,1536]{5,4,3,2,1,0:T(8,128)}, f32[4,4,1536]{2,1,0:T(4,128)S(1)}) custom-call(s32[1]{0:T(128)} %bitcast.me_ref, f32[4,6,1,4,8,1536]{5,4,3,2,1,0:T(8,128)} %bitcast.22, f32[4,2,8,128]{3,2,1,0:T(8,128)S(1)} %broadcast_in_dim.50.weight_ref, f32[4,2,2,8,1536]{4,3,2,1,0:T(8,128)S(1)} %all-to-all-done.1.term_hbm), custom_call_target="tpu_custom_call", output_to_operand_aliasing={{0}: (1, {})} | custom-call | flops 196608 | bytes 2359296 | tf_op jit(solution)/shard_map/add_first/pallas_call | solution.py:415
  139.9 0.0 copy-done.5
  139.9 0.3 fusion.1
  140.2 0.1 collective-permute-start.5
  140.3 1.2 collective-permute-done.5
  141.5 0.5 collective-permute-start.6
  142.0 3.2 %collective-permute-done.6 = f32[4,2,2,64]{3,2,0,1:T(2,128)S(1)} collective-permute-done((f32[4,2,2,64]{3,2,0,1:T(2,128)S(1)}, f32[4,2,2,64]{3,2,0,1:T(2,128)S(1)}, u32[]{:S(2)}, u32[]{:S(2)}) %collective-permute-start.6) | collective-permute-done | bytes 4128 | tf_op jit(solution)/shard_map/ppermute | solution.py:550
  145.1 1.5 collective-permute-start.7
  146.7 2.1 collective-permute-done.7
  148.8 0.5 collective-permute-start.10
  149.3 4.2 %collective-permute-start.9 = (f32[4,2,2,64]{3,2,0,1:T(2,128)S(1)}, f32[4,2,2,64]{3,2,0,1:T(2,128)S(1)}, u32[]{:S(2)}, u32[]{:S(2)}) collective-permute-start(f32[4,2,2,64]{3,2,0,1:T(2,128)S(1)} %add.44), channel_id=1, source_target_pairs={{0,2},{1,3},{2,0},{3,1},{4,6},{5,7},{6,4},{7,5},{8,10},{9,11},{10,... | collective-permute-start | bytes 12296 | tf_op jit(solution)/shard_map/ppermute | solution.py:511
  153.5 18.0 %collective-permute-done.2.refs_1_ = f32[20,8,1536]{2,1,0:T(8,128)S(1)} collective-permute-done((f32[20,8,1536]{2,1,0:T(8,128)}, f32[20,8,1536]{2,1,0:T(8,128)S(1)}, u32[]{:S(2)}, u32[]{:S(2)}) %collective-permute-start.2) | collective-permute-done | bytes 983072 | tf_op jit(solution)/shard_map/ppermute | solution.py:511
  171.6 2.4 %collective-permute-start.8 = (f32[4,2,2,64]{3,2,0,1:T(2,128)S(1)}, f32[4,2,2,64]{3,2,0,1:T(2,128)S(1)}, u32[]{:S(2)}, u32[]{:S(2)}) collective-permute-start(f32[4,2,2,64]{3,2,0,1:T(2,128)S(1)} %add.44), channel_id=1, source_target_pairs={{0,1},{1,0},{2,3},{3,2},{4,5},{5,4},{6,7},{7,6},{8,9},{9,8},{10,11... | collective-permute-start | bytes 12296 | tf_op jit(solution)/shard_map/ppermute | solution.py:511
  173.9 0.0 copy-done.1
  173.9 3.0 %add_rest.3.base_hbm = f32[4,6,1,4,8,1536]{5,4,3,2,1,0:T(8,128)} custom-call(s32[1]{0:T(128)} %bitcast.me_ref, f32[4,6,1,4,8,1536]{5,4,3,2,1,0:T(8,128)} %get-tuple-element.11.base_hbm, f32[20,8,1536]{2,1,0:T(8,128)S(1)} %copy-done.1, f32[20,8,1536]{2,1,0:T(8,128)S(1)} %collective-permute-done.2.refs_1_), custom_call_target="tpu_custom_call", output_to_operand_aliasing={{}: (1, {})} | custom-call | flops 491520 | bytes 5898240 | tf_op jit(solution)/shard_map/add_rest/pallas_call | solution.py:472
  177.0 24.1 %collective-permute-done.3.refs_0_ = f32[20,8,1536]{2,1,0:T(8,128)} collective-permute-done((f32[20,8,1536]{2,1,0:T(8,128)}, f32[20,8,1536]{2,1,0:T(8,128)}, u32[]{:S(2)}, u32[]{:S(2)}) %collective-permute-start.3) | collective-permute-done | bytes 983072 | tf_op jit(solution)/shard_map/ppermute | solution.py:511
  201.1 2.6 %add_rest.4.base_hbm = f32[4,6,1,4,8,1536]{5,4,3,2,1,0:T(8,128)} custom-call(s32[1]{0:T(128)} %bitcast.me_ref, f32[4,6,1,4,8,1536]{5,4,3,2,1,0:T(8,128)} %add_rest.3.base_hbm, f32[20,8,1536]{2,1,0:T(8,128)} %collective-permute-done.3.refs_0_), custom_call_target="tpu_custom_call", output_to_operand_aliasing={{}: (1, {})} | custom-call | flops 245760 | bytes 2949120 | tf_op jit(solution)/shard_map/add_rest/pallas_call | solution.py:472
  203.7 18.5 %collective-permute-done.4.refs_0_ = f32[20,8,1536]{2,1,0:T(8,128)} collective-permute-done((f32[20,8,1536]{2,1,0:T(8,128)}, f32[20,8,1536]{2,1,0:T(8,128)}, u32[]{:S(2)}, u32[]{:S(2)}) %collective-permute-start.4) | collective-permute-done | bytes 983072 | tf_op jit(solution)/shard_map/ppermute | solution.py:511
  222.2 2.6 %add_rest.5 = f32[4,6,1,4,8,1536]{5,4,3,2,1,0:T(8,128)} custom-call(s32[1]{0:T(128)} %bitcast.me_ref, f32[4,6,1,4,8,1536]{5,4,3,2,1,0:T(8,128)} %add_rest.4.base_hbm, f32[20,8,1536]{2,1,0:T(8,128)} %collective-permute-done.4.refs_0_), custom_call_target="tpu_custom_call", output_to_operand_aliasing={{}: (1, {})} | custom-call | flops 245760 | bytes 2949120 | tf_op jit(solution)/shard_map/add_rest/pallas_call | solution.py:472
  224.8 0.0 collective-permute-done.10
  224.8 0.0 collective-permute-done.9
  224.8 0.0 collective-permute-done.8
  224.8 0.6 add_bitcast_fusion
  (11 shorter events, 0.1 us)
Async XLA Ops:
  0.6 12.0 %copy-start.6 = (s32[4]{0:T(128)S(1)}, s32[4]{0:T(128)}, u32[]{:S(2)}) copy-start(s32[4]{0:T(128)} %param.11) | copy-start | bytes 52
  0.6 32.4 %copy-start.3 = (f32[2,32]{1,0:T(2,128)S(1)}, f32[2,32]{1,0:T(2,128)}, u32[]{:S(2)}) copy-start(f32[2,32]{1,0:T(2,128)} %param.8) | copy-start | bytes 772
  0.7 106.9 %all-to-all-start = ((f32[4,6,4,8,1536]{4,3,2,1,0:T(8,128)}), f32[4,6,4,8,1536]{4,3,2,1,0:T(8,128)}, u32[]{:S(2)}, u32[]{:S(2)}) async-start(f32[4,6,4,8,1536]{4,3,2,1,0:T(8,128)} %bitcast.21), calls=%async_computation | async-start | bytes 9437184 | tf_op jit(solution)/shard_map/all_to_all | solution.py:508
  6.2 27.0 %copy-start.2 = (f32[15,32]{1,0:T(8,128)S(1)}, f32[15,32]{1,0:T(8,128)}, u32[]{:S(2)}) copy-start(f32[15,32]{1,0:T(8,128)} %param.9) | copy-start | bytes 5764
  6.2 27.1 %copy-start = (f32[4,3,2,32,1536]{4,3,2,1,0:T(8,128)S(1)}, f32[4,3,2,32,1536]{4,3,2,1,0:T(8,128)}, u32[]{:S(2)}) copy-start(f32[4,3,2,32,1536]{4,3,2,1,0:T(8,128)} %field_ref.1) | copy-start | bytes 14155780
  8.1 24.9 %collective-permute-start.1 = (f32[4,3,2,8,1536]{4,3,2,1,0:T(8,128)S(1)}, f32[4,3,2,8,1536]{4,3,2,1,0:T(8,128)S(1)}, u32[]{:S(2)}, u32[]{:S(2)}) collective-permute-start(f32[4,3,2,8,1536]{4,3,2,1,0:T(8,128)S(1)} %get-tuple-element.18), channel_id=1, source_target_pairs={{4,0},{8,4},{12,8},{16,12},{20,16},{24,20},{28,24},{5,1},{9,5},{13... | collective-permute-start | bytes 3538952 | tf_op jit(solution)/shard_map/ppermute | solution.py:526
  10.2 22.9 %collective-permute-start = (f32[4,3,2,8,1536]{4,3,2,1,0:T(8,128)S(1)}, f32[4,3,2,8,1536]{4,3,2,1,0:T(8,128)S(1)}, u32[]{:S(2)}, u32[]{:S(2)}) collective-permute-start(f32[4,3,2,8,1536]{4,3,2,1,0:T(8,128)S(1)} %get-tuple-element.19), channel_id=1, source_target_pairs={{0,4},{4,8},{8,12},{12,16},{16,20},{20,24},{24,28},{1,5},{5,9},{9,... | collective-permute-start | bytes 3538952 | tf_op jit(solution)/shard_map/ppermute | solution.py:525
  112.3 25.2 %all-to-all-start.1 = ((f32[4,2,2,8,1536]{4,3,2,1,0:T(8,128)}), f32[4,2,2,8,1536]{4,3,2,1,0:T(8,128)S(1)}, u32[]{:S(2)}, u32[]{:S(2)}) async-start(f32[4,2,2,8,1536]{4,3,2,1,0:T(8,128)} %filter_first.1), calls=%async_computation.1 | async-start | bytes 1572864 | tf_op jit(solution)/shard_map/all_to_all | solution.py:508
  119.2 13.7 %copy-start.4 = (f32[2,8]{1,0:T(2,128)S(1)}, f32[2,8]{1,0:T(2,128)}, u32[]{:S(2)}) copy-start(f32[2,8]{1,0:T(2,128)} %param.10) | copy-start | bytes 196
  129.3 10.6 %copy-start.5 = (s32[1536]{0:T(1024)S(1)}, s32[1536]{0:T(1024)}, u32[]{:S(2)}) copy-start(s32[1536]{0:T(1024)} %param.12) | copy-start | bytes 18436
  129.3 44.7 %copy-start.1 = (f32[20,8,1536]{2,1,0:T(8,128)S(1)}, f32[20,8,1536]{2,1,0:T(8,128)}, u32[]{:S(2)}) copy-start(f32[20,8,1536]{2,1,0:T(8,128)} %get-tuple-element.13.refs_0_) | copy-start | bytes 2949124
  129.3 42.3 %collective-permute-start.2 = (f32[20,8,1536]{2,1,0:T(8,128)}, f32[20,8,1536]{2,1,0:T(8,128)S(1)}, u32[]{:S(2)}, u32[]{:S(2)}) collective-permute-start(f32[20,8,1536]{2,1,0:T(8,128)} %get-tuple-element.14), channel_id=1, source_target_pairs={{0,1},{1,0},{2,3},{3,2},{4,5},{5,4},{6,7},{7,6},{8,9},{9,8},{10,11... | collective-permute-start | bytes 2949128 | tf_op jit(solution)/shard_map/ppermute | solution.py:511
  129.4 71.7 %collective-permute-start.3 = (f32[20,8,1536]{2,1,0:T(8,128)}, f32[20,8,1536]{2,1,0:T(8,128)}, u32[]{:S(2)}, u32[]{:S(2)}) collective-permute-start(f32[20,8,1536]{2,1,0:T(8,128)} %get-tuple-element.15), channel_id=1, source_target_pairs={{0,2},{1,3},{2,0},{3,1},{4,6},{5,7},{6,4},{7,5},{8,10},{9,11},{10,... | collective-permute-start | bytes 2949128 | tf_op jit(solution)/shard_map/ppermute | solution.py:511
  132.3 89.9 %collective-permute-start.4 = (f32[20,8,1536]{2,1,0:T(8,128)}, f32[20,8,1536]{2,1,0:T(8,128)}, u32[]{:S(2)}, u32[]{:S(2)}) collective-permute-start(f32[20,8,1536]{2,1,0:T(8,128)} %get-tuple-element.16), channel_id=1, source_target_pairs={{0,3},{1,2},{2,1},{3,0},{4,7},{5,6},{6,5},{7,4},{8,11},{9,10},{10,... | collective-permute-start | bytes 2949128 | tf_op jit(solution)/shard_map/ppermute | solution.py:511
  140.2 1.2 collective-permute-start.5
  141.5 3.7 %collective-permute-start.6 = (f32[4,2,2,64]{3,2,0,1:T(2,128)S(1)}, f32[4,2,2,64]{3,2,0,1:T(2,128)S(1)}, u32[]{:S(2)}, u32[]{:S(2)}) collective-permute-start(f32[4,2,2,64]{3,2,0,1:T(2,128)S(1)} %copy_add_fusion), channel_id=1, source_target_pairs={{0,8},{4,12},{8,0},{12,4},{16,24},{20,28},{24,16},{28,20},{1,9},{5... | collective-permute-start | bytes 12296 | tf_op jit(solution)/shard_map/ppermute | solution.py:550
  145.1 3.7 %collective-permute-start.7 = (f32[4,2,2,64]{3,2,0,1:T(2,128)S(1)}, f32[4,2,2,64]{3,2,0,1:T(2,128)S(1)}, u32[]{:S(2)}, u32[]{:S(2)}) collective-permute-start(f32[4,2,2,64]{3,2,0,1:T(2,128)S(1)} %add.43), channel_id=1, source_target_pairs={{0,16},{4,20},{8,24},{12,28},{16,0},{20,4},{24,8},{28,12},{1,17},{... | collective-permute-start | bytes 12296 | tf_op jit(solution)/shard_map/ppermute | solution.py:550
  148.8 76.0 %collective-permute-start.10 = (f32[4,2,2,64]{3,2,0,1:T(2,128)S(1)}, f32[4,2,2,64]{3,2,0,1:T(2,128)S(1)}, u32[]{:S(2)}, u32[]{:S(2)}) collective-permute-start(f32[4,2,2,64]{3,2,0,1:T(2,128)S(1)} %add.44), channel_id=1, source_target_pairs={{0,3},{1,2},{2,1},{3,0},{4,7},{5,6},{6,5},{7,4},{8,11},{9,10},{10,... | collective-permute-start | bytes 12296 | tf_op jit(solution)/shard_map/ppermute | solution.py:511
  149.3 75.5 %collective-permute-start.9 = (f32[4,2,2,64]{3,2,0,1:T(2,128)S(1)}, f32[4,2,2,64]{3,2,0,1:T(2,128)S(1)}, u32[]{:S(2)}, u32[]{:S(2)}) collective-permute-start(f32[4,2,2,64]{3,2,0,1:T(2,128)S(1)} %add.44), channel_id=1, source_target_pairs={{0,2},{1,3},{2,0},{3,1},{4,6},{5,7},{6,4},{7,5},{8,10},{9,11},{10,... | collective-permute-start | bytes 12296 | tf_op jit(solution)/shard_map/ppermute | solution.py:511
  171.6 53.3 %collective-permute-start.8 = (f32[4,2,2,64]{3,2,0,1:T(2,128)S(1)}, f32[4,2,2,64]{3,2,0,1:T(2,128)S(1)}, u32[]{:S(2)}, u32[]{:S(2)}) collective-permute-start(f32[4,2,2,64]{3,2,0,1:T(2,128)S(1)} %add.44), channel_id=1, source_target_pairs={{0,1},{1,0},{2,3},{3,2},{4,5},{5,4},{6,7},{7,6},{8,9},{9,8},{10,11... | collective-permute-start | bytes 12296 | tf_op jit(solution)/shard_map/ppermute | solution.py:511

commit v11 on v10

--- a/solution.py
+++ b/solution.py
@@ -162,8 +162,17 @@
     return piece[1] * piece[3]
 
 
-def piece_at(ref, piece):
-    return ref.at[:, pl.ds(piece[0], piece[1]), pl.ds(piece[2], piece[3])]
+def line_copies(pieces, me_ref, field_hbm, received, line_refs, sems):
+    count, split, me = len(received) + 1, field_hbm.shape[2], me_ref[0]
+    copies = []
+    for i, (piece, line_ref) in enumerate(zip(pieces, line_refs)):
+        pairs, groups = pl.ds(piece[0], piece[1]), pl.ds(piece[2], piece[3])
+        sources = [field_hbm.at[me // split, pairs, me % split, groups]]
+        sources += [block.at[pairs, groups] for block in received]
+        copies.append(
+            [pltpu.make_async_copy(sources[x], line_ref.at[me ^ x], sems.at[i * count + x]) for x in range(count)]
+        )
+    return copies
 
 
 def start_all(copies):
@@ -177,13 +186,11 @@
         copy.wait()
 
 
-def run_filter(pieces, table_hbm, lines_hbm, send, scratch):
+def run_filter(pieces, me_ref, table_hbm, field_hbm, received, send, scratch):
     *line_refs, wave_ref, table_ref, table_sems, sems = scratch
-    copies = [
-        pltpu.make_async_copy(piece_at(lines_hbm, piece), line_ref, sems.at[i])
-        for i, (piece, line_ref) in enumerate(zip(pieces, line_refs))
-    ]
-    start_all(copies)
+    copies = line_copies(pieces, me_ref, field_hbm, received, line_refs, sems)
+    for piece_copies in copies:
+        start_all(piece_copies)
     step = TILES // TABLE_COPIES
     spans = [pl.ds(i * step, step) for i in range(TABLE_COPIES)]
     table_copies = [
@@ -191,13 +198,13 @@
     ]
     start_all(table_copies)
     offsets = [sum(map(group_count, pieces[:i])) for i in range(len(pieces))]
-    per_source = lines_hbm.shape[4] // LANES
+    per_source = field_hbm.shape[5] // LANES
 
     def spot(number):
         return pl.ds(pl.multiple_of(number * PAD, PAD), PAD)
 
     for piece, line_ref, offset, copy in zip(pieces, line_refs, offsets, copies):
-        copy.wait()
+        wait_all(copy)
 
         def forward(number, _, groups=piece[3], line_ref=line_ref, offset=offset):
             pair, group = number // groups, number % groups
@@ -242,18 +249,19 @@
     wait_all(away)
 
 
-def filter_first_kernel(pieces, table_hbm, lines_hbm, out_hbm, *scratch):
-    *scratch, out_sems = scratch
+def filter_first_kernel(pieces, count, me_ref, table_hbm, field_hbm, *refs):
+    received, out_hbm, scratch, out_sems = refs[: count - 1], refs[count - 1], refs[count:-1], refs[-1]
 
     def send(i, line_ref):
         return [pltpu.make_async_copy(line_ref.at[:, :, 0], out_hbm.at[:, i], out_sems.at[i])]
 
-    run_filter(pieces, table_hbm, lines_hbm, send, scratch)
-
-
-def filter_rest_kernel(pieces, me_ref, table_hbm, lines_hbm, *refs):
-    count, me = lines_hbm.shape[0], me_ref[0]
-    sent, scratch, out_sems = refs[:count], refs[count:-1], refs[-1]
+    run_filter(pieces, me_ref, table_hbm, field_hbm, received, send, scratch)
+
+
+def filter_rest_kernel(pieces, count, me_ref, table_hbm, field_hbm, *refs):
+    me = me_ref[0]
+    received, sent = refs[: count - 1], refs[count - 1 : 2 * count - 1]
+    scratch, out_sems = refs[2 * count - 1 : -1], refs[-1]
     places = rest_places(pieces)
 
     def send(i, line_ref):
@@ -266,7 +274,7 @@
                 copies.append(pltpu.make_async_copy(line_ref.at[me ^ x, pair], sent[x].at[target], sem))
         return copies
 
-    run_filter(pieces, table_hbm, lines_hbm, send, scratch)
+    run_filter(pieces, me_ref, table_hbm, field_hbm, received, send, scratch)
 
 
 def rest_places(pieces):
@@ -284,46 +292,43 @@
 WHOLE = pl.BlockSpec(memory_space=pltpu.VMEM)
 
 
-def filter_call(kernel, name, pieces, lines, tables, in_specs, out_specs, out_shape, out_sems):
-    count, _, _, _, width = lines.shape
+def filter_call(kernel, name, pieces, field, received, spots, tables, out_shape, out_sems):
+    count, width = len(received) + 1, field.shape[5]
     rows = sum(map(group_count, pieces)) * PAD
     flops = 3 * 2 * TILES * rows * (2 * LANES) ** 2
     return pl.pallas_call(
-        functools.partial(kernel, pieces),
+        functools.partial(kernel, pieces, count),
         out_shape=out_shape,
-        in_specs=in_specs,
-        out_specs=out_specs,
+        in_specs=[SCALARS] + [HBM] * (count + 1),
+        out_specs=[HBM] * len(out_shape),
         scratch_shapes=[pltpu.VMEM((count, piece[1], piece[3], PAD, width), jnp.float32) for piece in pieces]
         + [
             pltpu.VMEM((TILES, rows, 2 * LANES), jnp.float32),
             pltpu.VMEM(tables.shape, tables.dtype),
             pltpu.SemaphoreType.DMA((TABLE_COPIES,)),
-            pltpu.SemaphoreType.DMA((len(pieces),)),
+            pltpu.SemaphoreType.DMA((len(pieces) * count,)),
             pltpu.SemaphoreType.DMA((out_sems,)),
         ],
         compiler_params=pltpu.CompilerParams(vmem_limit_bytes=FILTER_VMEM),
         cost_estimate=pl.CostEstimate(flops=flops, bytes_accessed=8 * count * rows * width, transcendentals=0),
         name=name,
-    )
-
-
-def filter_first(lines, tables, pieces):
-    count, _, _, _, width = lines.shape
-    out_shape = jax.ShapeDtypeStruct((count, len(pieces), 2, PAD, width), jnp.float32)
-    call = filter_call(
-        filter_first_kernel, "filter_first", pieces, lines, tables, [HBM, HBM], HBM, out_shape, len(pieces)
-    )
-    return call(tables, lines)
-
-
-def filter_rest(lines, spots, tables, pieces):
-    count, _, _, _, width = lines.shape
+    )(spots, tables, field, *received)
+
+
+def filter_first(field, received, spots, tables, pieces):
+    count, width = len(received) + 1, field.shape[5]
+    out_shape = [jax.ShapeDtypeStruct((count, len(pieces), 2, PAD, width), jnp.float32)]
+    return filter_call(
+        filter_first_kernel, "filter_first", pieces, field, received, spots, tables, out_shape, len(pieces)
+    )[0]
+
+
+def filter_rest(field, received, spots, tables, pieces):
+    count, width = len(received) + 1, field.shape[5]
     shape = (sum(map(group_count, pieces)), PAD, width)
     out_shape = [jax.ShapeDtypeStruct(shape, jnp.float32)] * count
     sems = count * sum(piece[1] for piece in pieces)
-    ins = [SCALARS, HBM, HBM]
-    call = filter_call(filter_rest_kernel, "filter_rest", pieces, lines, tables, ins, [HBM] * count, out_shape, sems)
-    return call(spots, tables, lines)
+    return filter_call(filter_rest_kernel, "filter_rest", pieces, field, received, spots, tables, out_shape, sems)
 
 
 def local_kernel(rate_ref, coef_ref, flow_ref, field_ref, low_ref, high_ref, out_ref, pad_ref):
@@ -512,29 +517,39 @@
 
     pairs_count, groups = comp_count * part_count, line_rows // PAD
     shares = (mode_split, pairs_count, row_split, groups, PAD, width)
-    lines = field.reshape(shares).transpose(0, 2, 1, 3, 4, 5)
-    lines = exchange(lines.reshape(span, pairs_count, groups, PAD, width))
+    shared = field.reshape(shares)
+    blocks = [None] * span
+    source = shared
+    for x in range(span - 1, 0, -1):
+        other = me ^ x
+        start = (other // row_split, 0, other % row_split, 0, 0, 0)
+        block = lax.dynamic_slice(source, start, (1, pairs_count, 1, groups, PAD, width))
+        blocks[x] = block.reshape(pairs_count, groups, PAD, width)
+        source = after(shared, blocks[x])
+    received = swap(blocks)
     wall_groups = sorted({0, groups - 1})
     first_pieces = tuple((0, 2, group, 1) for group in wall_groups)
     rest_pieces = tuple((2 * comp, 2, 0, groups) for comp in range(1, comp_count))
     if groups > 2:
         rest_pieces = ((0, 2, 1, groups - 2),) + rest_pieces
 
+    filtered = filter_first(shared, received, spots, tables, first_pieces)
+    back = exchange(filtered)
+    received[0] = after(received[0], filtered)
+    sent = filter_rest(shared, received, spots, tables, rest_pieces)
+    returned = [sent[0]] + swap(sent)
+
     forward = [(i, i + 1) for i in range(wall_count - 1)]
     backward = [(i + 1, i) for i in range(wall_count - 1)]
-    low = lax.ppermute(field[:, :, :, row_count - PAD :], "wall", forward)
-    high = lax.ppermute(field[:, :, :, :PAD], "wall", backward)
+    late = after(field, back)
+    low = lax.ppermute(late[:, :, :, row_count - PAD :], "wall", forward)
+    high = lax.ppermute(late[:, :, :, :PAD], "wall", backward)
 
     rate = kx_index.astype(jnp.float32) * (0.25 * TAU)
     coef = jnp.broadcast_to(d2_coef[:, :, None], (STEN, row_count, LANES))
     flow = jnp.broadcast_to(mean_flow[:, :, None], (2, row_count, LANES))
     base = local_terms(field, low, high, rate, coef, flow)
 
-    lines = after(lines, base)
-    filtered = filter_first(lines, tables, first_pieces)
-    back = exchange(filtered)
-    sent = filter_rest(after(lines, filtered), spots, tables, rest_pieces)
-    returned = [sent[0]] + swap(sent)
 
     lower = jnp.where(wall_index == 0, wall_coef[0], 0.0)
     upper = jnp.where(wall_index == wall_count - 1, wall_coef[1, ::-1], 0.0)

time: 226 us -> 251 us (1.11)
  blocking collectives: 0 us -> 21.5 us
  starting transfers between devices: 29.6 us -> 22.2 us
  local copies, waits for them, and re-layouts: 2.35 us -> 9.39 us
    ppermute x6 -> x9, waiting for transfers between devices: 60.7 us -> 140 us  [swap(): lax.ppermute(blocks[x], 'span', pairs[x])]
    all_to_all x2 -> x0, waiting for transfers between devices: 63.8 us -> none  [exchange(): return lax.all_to_all(lines, 'span', split_axis=0, concat_axis=0)]
    all_to_all x0 -> x1, blocking collectives: none -> 21.5 us  [exchange(): return lax.all_to_all(lines, 'span', split_axis=0, concat_axis=0)]
    ppermute x2, waiting for transfers between devices: 20.4 us -> 7.24 us  [the longest x1 7.24 us: on_device(): high = lax.ppermute(late[:, :, :, :PAD], 'wall', backward)]
    all_to_all x2 -> x0, starting transfers between devices: 12.4 us -> none  [exchange(): return lax.all_to_all(lines, 'span', split_axis=0, concat_axis=0)]
    reshape x0 -> x3, local copies, waits for them, and re-layouts: none -> 6.31 us  [on_device(): blocks[x] = block.reshape(pairs_count, groups, PAD, width)]
    ppermute x3, starting transfers between devices: 2.08 us -> 5.82 us  [on_device(): lax.ppermute(grad, 'wall', [(i, i ^ distance) for i in range(wall_count)])]
    ppermute x6 -> x9, starting transfers between devices: 10.7 us -> 12.1 us  [swap(): lax.ppermute(blocks[x], 'span', pairs[x])]
  transfers between devices with their start and end apart: 13 -> 14, of which waited for: 9 -> 9; matrix products, arithmetic and copies ran while one was open for 1% -> 0% of each run, Pallas kernels for 16% -> 15%
where the time goes in v11:
time: 251 us; the launch traced here: 250 us
  waiting for transfers between devices  153 us (61%)
  Pallas kernels  42.2 us (17%)
  starting transfers between devices  22.2 us (9%)
  blocking collectives  21.5 us (9%)
  local copies, waits for them, and re-layouts  9.39 us (4%)
    ppermute x9, waiting for transfers between devices, swap(): lax.ppermute(blocks[x], 'span', pairs[x])  140 us
    all_to_all x1, blocking collectives, exchange(): return lax.all_to_all(lines, 'span', split_axis=0, concat_axis=0)  21.5 us
    pallas_call x2, Pallas kernels, filter_call(): pl.pallas_call(functools.partial(kernel, pieces, count), out_shape=out_sh...  16.2 us
    pallas_call x1, Pallas kernels, local_terms(): pl.pallas_call(local_kernel, grid=(mode_count,), out_shape=jax.ShapeDtype...  15.5 us
    ppermute x9, starting transfers between devices, swap(): lax.ppermute(blocks[x], 'span', pairs[x])  12.1 us
    pallas_call x3, Pallas kernels, add_rest(): pl.pallas_call(functools.partial(add_rest_kernel, pieces, partners), out_...  8.15 us
    ppermute x1, waiting for transfers between devices, on_device(): high = lax.ppermute(late[:, :, :, :PAD], 'wall', backward)  7.24 us
    reshape x3, local copies, waits for them, and re-layouts, on_device(): blocks[x] = block.reshape(pairs_count, groups, PAD, width)  6.31 us
  transfers between devices with their start and end apart: 14, of which 9 were waited for; matrix products, arithmetic and copies ran while one was open for 0% of the time, Pallas kernels for 15%

profile of v11, /device:TPU:10, one launch (start us, length us, event | category | flops | bytes accessed | tf_op | source)
XLA Modules:
  0.0 250.3 jit_solution(7504838603092690048)
XLA Ops:
  0.6 2.4 dynamic-slice_bitcast_fusion.2
  3.1 2.4 dynamic-slice_bitcast_fusion.1
  5.4 0.0 slice-start
  5.4 1.5 dynamic-slice_bitcast_fusion
  7.0 0.5 collective-permute-start
  7.5 2.6 %collective-permute-start.1 = (f32[6,4,8,1536]{3,2,1,0:T(8,128)}, f32[6,4,8,1536]{3,2,1,0:T(8,128)S(1)}, u32[]{:S(2)}, u32[]{:S(2)}) collective-permute-start(f32[6,4,8,1536]{3,2,1,0:T(8,128)} %dynamic-slice_bitcast_fusion.1), channel_id=1, source_target_pairs={{0,2},{1,3},{2,0},{3,1},{4,6},{5,7},{6,4},{7,5},{8,10},{9,11},{10,... | collective-permute-start | bytes 3538952 | tf_op jit(solution)/shard_map/ppermute | solution.py:516
  10.1 0.5 collective-permute-start.2
  10.5 46.6 %collective-permute-done.refs_0_ = f32[6,4,8,1536]{3,2,1,0:T(8,128)S(1)} collective-permute-done((f32[6,4,8,1536]{3,2,1,0:T(8,128)S(1)}, f32[6,4,8,1536]{3,2,1,0:T(8,128)S(1)}, u32[]{:S(2)}, u32[]{:S(2)}) %collective-permute-start) | collective-permute-done | bytes 1179680 | tf_op jit(solution)/shard_map/ppermute | solution.py:516
  57.1 0.0 copy-start.1
  57.1 30.2 %collective-permute-done.1.refs_1_ = f32[6,4,8,1536]{3,2,1,0:T(8,128)S(1)} collective-permute-done((f32[6,4,8,1536]{3,2,1,0:T(8,128)}, f32[6,4,8,1536]{3,2,1,0:T(8,128)S(1)}, u32[]{:S(2)}, u32[]{:S(2)}) %collective-permute-start.1) | collective-permute-done | bytes 1179680 | tf_op jit(solution)/shard_map/ppermute | solution.py:516
  87.4 0.0 copy-start.2
  87.4 24.7 %collective-permute-done.2.refs_2_ = f32[6,4,8,1536]{3,2,1,0:T(8,128)S(1)} collective-permute-done((f32[6,4,8,1536]{3,2,1,0:T(8,128)}, f32[6,4,8,1536]{3,2,1,0:T(8,128)S(1)}, u32[]{:S(2)}, u32[]{:S(2)}) %collective-permute-start.2) | collective-permute-done | bytes 1179680 | tf_op jit(solution)/shard_map/ppermute | solution.py:516
  112.0 0.0 copy-start.3
  112.0 0.0 copy-done.1
  112.0 0.0 copy-done.2
  112.0 1.0 copy-done.3
  113.1 5.9 %filter_first.1 = f32[4,2,2,8,1536]{4,3,2,1,0:T(8,128)} custom-call(s32[1]{0:T(128)} %bitcast.me_ref, bf16[24,2,256,256]{3,2,1,0:T(8,128)(2,1)} %constant.92.clone.table_hbm, f32[4,6,1,4,8,1536]{5,4,3,2,1,0:T(8,128)} %bitcast.30, f32[6,4,8,1536]{3,2,1,0:T(8,128)} %copy-done.1, f32[6,4,8,1536]{3,2,1,0:T(8,128)} %copy-done.2, f32[6,4,8,1536]{3,2,1,0:T(8,128)} %copy-done.3), custom_call_target="tpu_custom_call" | custom-call | flops 301989888 | bytes 1572864 | tf_op jit(solution)/shard_map/filter_first/pallas_call | solution.py:299
  119.0 21.5 %all_to_all.5.term_hbm = f32[4,2,2,8,1536]{4,3,2,1,0:T(8,128)S(1)} all-to-all(f32[4,2,2,8,1536]{4,3,2,1,0:T(8,128)} %filter_first.1), channel_id=1, replica_groups=mesh['wall'=8,'span'=4] {'span'}, dimensions={0} | all-to-all | bytes 1572864 | tf_op jit(solution)/shard_map/all_to_all | solution.py:513
  140.4 0.0 slice-done
  140.4 0.0 slice-done.1
  140.5 1.6 fusion.6
  142.1 1.9 collective-permute-start.4
  144.0 2.4 collective-permute-start.3
  146.4 0.0 copy-done.6
  146.4 0.0 slice-start.2
  146.5 0.1 rev.3
  146.6 10.3 %filter_rest.1 = (f32[20,8,1536]{2,1,0:T(8,128)}, f32[20,8,1536]{2,1,0:T(8,128)}, f32[20,8,1536]{2,1,0:T(8,128)}, f32[20,8,1536]{2,1,0:T(8,128)}) custom-call(s32[1]{0:T(128)} %bitcast.me_ref, bf16[24,2,256,256]{3,2,1,0:T(8,128)(2,1)} %constant.92.clone.table_hbm, f32[4,6,1,4,8,1536]{5,4,3,2,1,0:T(8,128)} %bitcast.31, f32[6,4,8,1536]{3,2,1,0:T(8,128)} %copy-done.1, ...), custom_call_target="tpu_custom_call" | custom-call | flops 1509949440 | bytes 7864320 | tf_op jit(solution)/shard_map/filter_rest/pallas_call | solution.py:299
  156.9 1.9 collective-permute-start.5
  158.8 0.2 collective-permute-start.6
  159.0 1.5 collective-permute-start.7
  160.5 0.0 copy-done.8
  160.5 7.2 %collective-permute-done.4.high_ref = f32[4,3,2,8,1536]{4,3,2,1,0:T(8,128)S(1)} collective-permute-done((f32[4,3,2,8,1536]{4,3,2,1,0:T(8,128)}, f32[4,3,2,8,1536]{4,3,2,1,0:T(8,128)S(1)}, u32[]{:S(2)}, u32[]{:S(2)}) %collective-permute-start.4) | collective-permute-done | bytes 1179680 | tf_op jit(solution)/shard_map/ppermute | solution.py:546
  167.8 0.0 collective-permute-done.3.low_ref
  167.8 0.0 copy-done.5
  167.8 0.1 broadcast_in_dim.46.flow_ref
  167.8 0.0 copy-done.4
  167.8 0.1 broadcast_in_dim.45.coef_ref
  168.0 0.0 slice-done.2
  168.0 0.0 slice-done.3
  168.0 15.5 %local_terms.1 = f32[4,3,2,32,1536]{4,3,2,1,0:T(8,128)} custom-call(f32[4]{0:T(128)S(1)} %convert_multiply_fusion.rate_ref, f32[15,32,128]{2,1,0:T(8,128)S(1)} %broadcast_in_dim.45.coef_ref, f32[2,32,128]{2,1,0:T(8,128)S(1)} %broadcast_in_dim.46.flow_ref, f32[4,3,2,32,1536]{4,3,2,1,0:T(8,128)S(1)} %bitcast.35, ...), custom_call_target="tpu_custom_call" | custom-call | flops 47185920 | bytes 11796480 | tf_op jit(solution)/shard_map/local_terms/pallas_call | solution.py:371
  183.5 0.1 broadcast_in_dim.50.weight_ref
  183.5 2.4 add_first.1
  185.9 0.0 copy-done.7
  185.9 0.3 fusion.1
  186.3 3.1 %collective-permute-start.8 = (f32[4,2,2,64]{3,2,0,1:T(2,128)S(1)}, f32[4,2,2,64]{3,2,0,1:T(2,128)S(1)}, u32[]{:S(2)}, u32[]{:S(2)}) collective-permute-start(f32[4,2,2,64]{3,2,0,1:T(2,128)S(1)} %copy.14), channel_id=1, source_target_pairs={{0,4},{4,0},{8,12},{12,8},{16,20},{20,16},{24,28},{28,24},{1,5},{5... | collective-permute-start | bytes 12296 | tf_op jit(solution)/shard_map/ppermute | solution.py:565
  189.3 0.8 collective-permute-done.8
  190.2 0.0 collective-permute-start.9
  190.2 3.6 %collective-permute-done.9 = f32[4,2,2,64]{3,2,0,1:T(2,128)S(1)} collective-permute-done((f32[4,2,2,64]{3,2,0,1:T(2,128)S(1)}, f32[4,2,2,64]{3,2,0,1:T(2,128)S(1)}, u32[]{:S(2)}, u32[]{:S(2)}) %collective-permute-start.9) | collective-permute-done | bytes 4128 | tf_op jit(solution)/shard_map/ppermute | solution.py:565
  193.8 2.7 %collective-permute-start.10 = (f32[4,2,2,64]{3,2,0,1:T(2,128)S(1)}, f32[4,2,2,64]{3,2,0,1:T(2,128)S(1)}, u32[]{:S(2)}, u32[]{:S(2)}) collective-permute-start(f32[4,2,2,64]{3,2,0,1:T(2,128)S(1)} %add.59), channel_id=1, source_target_pairs={{0,16},{4,20},{8,24},{12,28},{16,0},{20,4},{24,8},{28,12},{1,17},{... | collective-permute-start | bytes 12296 | tf_op jit(solution)/shard_map/ppermute | solution.py:565
  196.6 1.6 collective-permute-done.10
  198.2 0.6 collective-permute-start.13
  198.8 3.6 %collective-permute-start.12 = (f32[4,2,2,64]{3,2,0,1:T(2,128)S(1)}, f32[4,2,2,64]{3,2,0,1:T(2,128)S(1)}, u32[]{:S(2)}, u32[]{:S(2)}) collective-permute-start(f32[4,2,2,64]{3,2,0,1:T(2,128)S(1)} %add.60), channel_id=1, source_target_pairs={{0,2},{1,3},{2,0},{3,1},{4,6},{5,7},{6,4},{7,5},{8,10},{9,11},{10,... | collective-permute-start | bytes 12296 | tf_op jit(solution)/shard_map/ppermute | solution.py:516
  202.4 0.0 collective-permute-done.5.refs_1_
  202.4 0.8 collective-permute-start.11
  203.2 0.0 copy-done
  203.2 3.0 %add_rest.3.base_hbm = f32[4,6,1,4,8,1536]{5,4,3,2,1,0:T(8,128)} custom-call(s32[1]{0:T(128)} %bitcast.me_ref, f32[4,6,1,4,8,1536]{5,4,3,2,1,0:T(8,128)} %get-tuple-element.15.base_hbm, f32[20,8,1536]{2,1,0:T(8,128)S(1)} %copy-done, f32[20,8,1536]{2,1,0:T(8,128)S(1)} %collective-permute-done.5.refs_1_), custom_call_target="tpu_custom_call", output_to_operand_aliasing={{}: (1, {})} | custom-call | flops 491520 | bytes 5898240 | tf_op jit(solution)/shard_map/add_rest/pallas_call | solution.py:477
  206.2 17.9 %collective-permute-done.6.refs_0_ = f32[20,8,1536]{2,1,0:T(8,128)} collective-permute-done((f32[20,8,1536]{2,1,0:T(8,128)}, f32[20,8,1536]{2,1,0:T(8,128)}, u32[]{:S(2)}, u32[]{:S(2)}) %collective-permute-start.6) | collective-permute-done | bytes 983072 | tf_op jit(solution)/shard_map/ppermute | solution.py:516
  224.1 2.6 %add_rest.4.base_hbm = f32[4,6,1,4,8,1536]{5,4,3,2,1,0:T(8,128)} custom-call(s32[1]{0:T(128)} %bitcast.me_ref, f32[4,6,1,4,8,1536]{5,4,3,2,1,0:T(8,128)} %add_rest.3.base_hbm, f32[20,8,1536]{2,1,0:T(8,128)} %collective-permute-done.6.refs_0_), custom_call_target="tpu_custom_call", output_to_operand_aliasing={{}: (1, {})} | custom-call | flops 245760 | bytes 2949120 | tf_op jit(solution)/shard_map/add_rest/pallas_call | solution.py:477
  226.6 20.4 %collective-permute-done.7.refs_0_ = f32[20,8,1536]{2,1,0:T(8,128)} collective-permute-done((f32[20,8,1536]{2,1,0:T(8,128)}, f32[20,8,1536]{2,1,0:T(8,128)}, u32[]{:S(2)}, u32[]{:S(2)}) %collective-permute-start.7) | collective-permute-done | bytes 983072 | tf_op jit(solution)/shard_map/ppermute | solution.py:516
  247.0 2.6 %add_rest.5 = f32[4,6,1,4,8,1536]{5,4,3,2,1,0:T(8,128)} custom-call(s32[1]{0:T(128)} %bitcast.me_ref, f32[4,6,1,4,8,1536]{5,4,3,2,1,0:T(8,128)} %add_rest.4.base_hbm, f32[20,8,1536]{2,1,0:T(8,128)} %collective-permute-done.7.refs_0_), custom_call_target="tpu_custom_call", output_to_operand_aliasing={{}: (1, {})} | custom-call | flops 245760 | bytes 2949120 | tf_op jit(solution)/shard_map/add_rest/pallas_call | solution.py:477
  249.6 0.0 collective-permute-done.13
  249.6 0.0 collective-permute-done.12
  249.6 0.0 collective-permute-done.11
  249.6 0.6 add_bitcast_fusion
  (21 shorter events, 0.1 us)
Async XLA Ops:
  5.4 135.0 %slice-start = ((s8[4718592]{0:T(1024)(128)(4,1)}), s8[4194304]{0:T(1024)(128)(4,1)S(1)}, s32[]{:S(2)}) async-start(s8[4718592]{0:T(1024)(128)(4,1)} %bitcast.32), calls=%async_computation.1 | async-start | bytes 8388608
  7.0 50.1 %collective-permute-start = (f32[6,4,8,1536]{3,2,1,0:T(8,128)S(1)}, f32[6,4,8,1536]{3,2,1,0:T(8,128)S(1)}, u32[]{:S(2)}, u32[]{:S(2)}) collective-permute-start(f32[6,4,8,1536]{3,2,1,0:T(8,128)S(1)} %dynamic-slice_bitcast_fusion), channel_id=1, source_target_pairs={{0,1},{1,0},{2,3},{3,2},{4,5},{5,4},{6,7},{7,6},{8,9},{9,8},{10,11... | collective-permute-start | bytes 3538952 | tf_op jit(solution)/shard_map/ppermute | solution.py:516
  7.5 79.9 %collective-permute-start.1 = (f32[6,4,8,1536]{3,2,1,0:T(8,128)}, f32[6,4,8,1536]{3,2,1,0:T(8,128)S(1)}, u32[]{:S(2)}, u32[]{:S(2)}) collective-permute-start(f32[6,4,8,1536]{3,2,1,0:T(8,128)} %dynamic-slice_bitcast_fusion.1), channel_id=1, source_target_pairs={{0,2},{1,3},{2,0},{3,1},{4,6},{5,7},{6,4},{7,5},{8,10},{9,11},{10,... | collective-permute-start | bytes 3538952 | tf_op jit(solution)/shard_map/ppermute | solution.py:516
  10.1 101.9 %collective-permute-start.2 = (f32[6,4,8,1536]{3,2,1,0:T(8,128)}, f32[6,4,8,1536]{3,2,1,0:T(8,128)S(1)}, u32[]{:S(2)}, u32[]{:S(2)}) collective-permute-start(f32[6,4,8,1536]{3,2,1,0:T(8,128)} %dynamic-slice_bitcast_fusion.2), channel_id=1, source_target_pairs={{0,3},{1,2},{2,1},{3,0},{4,7},{5,6},{6,5},{7,4},{8,11},{9,10},{10,... | collective-permute-start | bytes 3538952 | tf_op jit(solution)/shard_map/ppermute | solution.py:516
  57.1 54.9 %copy-start.1 = (f32[6,4,8,1536]{3,2,1,0:T(8,128)}, f32[6,4,8,1536]{3,2,1,0:T(8,128)S(1)}, u32[]{:S(2)}) copy-start(f32[6,4,8,1536]{3,2,1,0:T(8,128)S(1)} %collective-permute-done.refs_0_) | copy-start | bytes 3538948
  87.4 24.7 %copy-start.2 = (f32[6,4,8,1536]{3,2,1,0:T(8,128)}, f32[6,4,8,1536]{3,2,1,0:T(8,128)S(1)}, u32[]{:S(2)}) copy-start(f32[6,4,8,1536]{3,2,1,0:T(8,128)S(1)} %collective-permute-done.1.refs_1_) | copy-start | bytes 3538948
  112.0 1.1 copy-start.3
  113.1 27.4 %slice-start.1 = ((s8[4718592]{0:T(1024)(128)(4,1)}), s8[524288]{0:T(1024)(128)(4,1)S(1)}, s32[]{:S(2)}) async-start(s8[4718592]{0:T(1024)(128)(4,1)} %bitcast.32), calls=%async_computation.2 | async-start | bytes 1048576
  140.5 6.0 %copy-start.6 = (f32[2,8]{1,0:T(2,128)S(1)}, f32[2,8]{1,0:T(2,128)}, u32[]{:S(2)}) copy-start(f32[2,8]{1,0:T(2,128)} %param.10) | copy-start | bytes 196
  142.1 25.7 %collective-permute-start.4 = (f32[4,3,2,8,1536]{4,3,2,1,0:T(8,128)}, f32[4,3,2,8,1536]{4,3,2,1,0:T(8,128)S(1)}, u32[]{:S(2)}, u32[]{:S(2)}) collective-permute-start(f32[4,3,2,8,1536]{4,3,2,1,0:T(8,128)} %get-tuple-element.22), channel_id=1, source_target_pairs={{4,0},{8,4},{12,8},{16,12},{20,16},{24,20},{28,24},{5,1},{9,5},{13... | collective-permute-start | bytes 3538952 | tf_op jit(solution)/shard_map/ppermute | solution.py:546
  144.0 23.8 %collective-permute-start.3 = (f32[4,3,2,8,1536]{4,3,2,1,0:T(8,128)}, f32[4,3,2,8,1536]{4,3,2,1,0:T(8,128)}, u32[]{:S(2)}, u32[]{:S(2)}) collective-permute-start(f32[4,3,2,8,1536]{4,3,2,1,0:T(8,128)} %get-tuple-element.23), channel_id=1, source_target_pairs={{0,4},{4,8},{8,12},{12,16},{16,20},{20,24},{24,28},{1,5},{5,9},{9,... | collective-permute-start | bytes 3538952 | tf_op jit(solution)/shard_map/ppermute | solution.py:545
  146.4 21.5 %slice-start.2 = ((s8[4718592]{0:T(1024)(128)(4,1)}), s8[524288]{0:T(1024)(128)(4,1)S(1)}, s32[]{:S(2)}) async-start(s8[4718592]{0:T(1024)(128)(4,1)} %bitcast.34), calls=%async_computation.3 | async-start | bytes 1048576
  146.6 13.9 %copy-start.8 = (s32[4]{0:T(128)S(1)}, s32[4]{0:T(128)}, u32[]{:S(2)}) copy-start(s32[4]{0:T(128)} %param.11) | copy-start | bytes 52
  146.6 21.2 %copy-start.5 = (f32[2,32]{1,0:T(2,128)S(1)}, f32[2,32]{1,0:T(2,128)}, u32[]{:S(2)}) copy-start(f32[2,32]{1,0:T(2,128)} %param.8) | copy-start | bytes 772
  146.6 21.3 %copy-start.4 = (f32[15,32]{1,0:T(8,128)S(1)}, f32[15,32]{1,0:T(8,128)}, u32[]{:S(2)}) copy-start(f32[15,32]{1,0:T(8,128)} %param.9) | copy-start | bytes 5764
  146.6 21.4 %slice-start.3 = ((s8[4718592]{0:T(1024)(128)(4,1)}), s8[4194304]{0:T(1024)(128)(4,1)S(1)}, s32[]{:S(2)}) async-start(s8[4718592]{0:T(1024)(128)(4,1)} %bitcast.34), calls=%async_computation.4 | async-start | bytes 8388608
  156.9 45.5 %collective-permute-start.5 = (f32[20,8,1536]{2,1,0:T(8,128)}, f32[20,8,1536]{2,1,0:T(8,128)S(1)}, u32[]{:S(2)}, u32[]{:S(2)}) collective-permute-start(f32[20,8,1536]{2,1,0:T(8,128)} %get-tuple-element.18), channel_id=1, source_target_pairs={{0,1},{1,0},{2,3},{3,2},{4,5},{5,4},{6,7},{7,6},{8,9},{9,8},{10,11... | collective-permute-start | bytes 2949128 | tf_op jit(solution)/shard_map/ppermute | solution.py:516
  158.8 65.3 %collective-permute-start.6 = (f32[20,8,1536]{2,1,0:T(8,128)}, f32[20,8,1536]{2,1,0:T(8,128)}, u32[]{:S(2)}, u32[]{:S(2)}) collective-permute-start(f32[20,8,1536]{2,1,0:T(8,128)} %get-tuple-element.19), channel_id=1, source_target_pairs={{0,2},{1,3},{2,0},{3,1},{4,6},{5,7},{6,4},{7,5},{8,10},{9,11},{10,... | collective-permute-start | bytes 2949128 | tf_op jit(solution)/shard_map/ppermute | solution.py:516
  159.0 88.0 %collective-permute-start.7 = (f32[20,8,1536]{2,1,0:T(8,128)}, f32[20,8,1536]{2,1,0:T(8,128)}, u32[]{:S(2)}, u32[]{:S(2)}) collective-permute-start(f32[20,8,1536]{2,1,0:T(8,128)} %get-tuple-element.20), channel_id=1, source_target_pairs={{0,3},{1,2},{2,1},{3,0},{4,7},{5,6},{6,5},{7,4},{8,11},{9,10},{10,... | collective-permute-start | bytes 2949128 | tf_op jit(solution)/shard_map/ppermute | solution.py:516
  183.5 2.4 copy-start.7
  183.5 19.6 %copy-start = (f32[20,8,1536]{2,1,0:T(8,128)S(1)}, f32[20,8,1536]{2,1,0:T(8,128)}, u32[]{:S(2)}) copy-start(f32[20,8,1536]{2,1,0:T(8,128)} %get-tuple-element.17.refs_0_) | copy-start | bytes 2949124
  186.3 3.9 %collective-permute-start.8 = (f32[4,2,2,64]{3,2,0,1:T(2,128)S(1)}, f32[4,2,2,64]{3,2,0,1:T(2,128)S(1)}, u32[]{:S(2)}, u32[]{:S(2)}) collective-permute-start(f32[4,2,2,64]{3,2,0,1:T(2,128)S(1)} %copy.14), channel_id=1, source_target_pairs={{0,4},{4,0},{8,12},{12,8},{16,20},{20,16},{24,28},{28,24},{1,5},{5... | collective-permute-start | bytes 12296 | tf_op jit(solution)/shard_map/ppermute | solution.py:565
  190.2 3.7 %collective-permute-start.9 = (f32[4,2,2,64]{3,2,0,1:T(2,128)S(1)}, f32[4,2,2,64]{3,2,0,1:T(2,128)S(1)}, u32[]{:S(2)}, u32[]{:S(2)}) collective-permute-start(f32[4,2,2,64]{3,2,0,1:T(2,128)S(1)} %copy_add_fusion), channel_id=1, source_target_pairs={{0,8},{4,12},{8,0},{12,4},{16,24},{20,28},{24,16},{28,20},{1,9},{5... | collective-permute-start | bytes 12296 | tf_op jit(solution)/shard_map/ppermute | solution.py:565
  193.8 4.4 %collective-permute-start.10 = (f32[4,2,2,64]{3,2,0,1:T(2,128)S(1)}, f32[4,2,2,64]{3,2,0,1:T(2,128)S(1)}, u32[]{:S(2)}, u32[]{:S(2)}) collective-permute-start(f32[4,2,2,64]{3,2,0,1:T(2,128)S(1)} %add.59), channel_id=1, source_target_pairs={{0,16},{4,20},{8,24},{12,28},{16,0},{20,4},{24,8},{28,12},{1,17},{... | collective-permute-start | bytes 12296 | tf_op jit(solution)/shard_map/ppermute | solution.py:565
  198.2 51.4 %collective-permute-start.13 = (f32[4,2,2,64]{3,2,0,1:T(2,128)S(1)}, f32[4,2,2,64]{3,2,0,1:T(2,128)S(1)}, u32[]{:S(2)}, u32[]{:S(2)}) collective-permute-start(f32[4,2,2,64]{3,2,0,1:T(2,128)S(1)} %add.60), channel_id=1, source_target_pairs={{0,3},{1,2},{2,1},{3,0},{4,7},{5,6},{6,5},{7,4},{8,11},{9,10},{10,... | collective-permute-start | bytes 12296 | tf_op jit(solution)/shard_map/ppermute | solution.py:516
  198.8 50.8 %collective-permute-start.12 = (f32[4,2,2,64]{3,2,0,1:T(2,128)S(1)}, f32[4,2,2,64]{3,2,0,1:T(2,128)S(1)}, u32[]{:S(2)}, u32[]{:S(2)}) collective-permute-start(f32[4,2,2,64]{3,2,0,1:T(2,128)S(1)} %add.60), channel_id=1, source_target_pairs={{0,2},{1,3},{2,0},{3,1},{4,6},{5,7},{6,4},{7,5},{8,10},{9,11},{10,... | collective-permute-start | bytes 12296 | tf_op jit(solution)/shard_map/ppermute | solution.py:516
  202.4 47.2 %collective-permute-start.11 = (f32[4,2,2,64]{3,2,0,1:T(2,128)S(1)}, f32[4,2,2,64]{3,2,0,1:T(2,128)S(1)}, u32[]{:S(2)}, u32[]{:S(2)}) collective-permute-start(f32[4,2,2,64]{3,2,0,1:T(2,128)S(1)} %add.60), channel_id=1, source_target_pairs={{0,1},{1,0},{2,3},{3,2},{4,5},{5,4},{6,7},{7,6},{8,9},{9,8},{10,11... | collective-permute-start | bytes 12296 | tf_op jit(solution)/shard_map/ppermute | solution.py:516

commit v12 on v10

--- a/solution.py
+++ b/solution.py
@@ -177,13 +177,9 @@
         copy.wait()
 
 
-def run_filter(pieces, table_hbm, lines_hbm, send, scratch):
+def run_filter(pieces, table_hbm, bring, send, scratch):
     *line_refs, wave_ref, table_ref, table_sems, sems = scratch
-    copies = [
-        pltpu.make_async_copy(piece_at(lines_hbm, piece), line_ref, sems.at[i])
-        for i, (piece, line_ref) in enumerate(zip(pieces, line_refs))
-    ]
-    start_all(copies)
+    copies = [start_all(bring(i, line_ref, sems)) for i, line_ref in enumerate(line_refs)]
     step = TILES // TABLE_COPIES
     spans = [pl.ds(i * step, step) for i in range(TABLE_COPIES)]
     table_copies = [
@@ -191,13 +187,13 @@
     ]
     start_all(table_copies)
     offsets = [sum(map(group_count, pieces[:i])) for i in range(len(pieces))]
-    per_source = lines_hbm.shape[4] // LANES
+    per_source = line_refs[0].shape[4] // LANES
 
     def spot(number):
         return pl.ds(pl.multiple_of(number * PAD, PAD), PAD)
 
     for piece, line_ref, offset, copy in zip(pieces, line_refs, offsets, copies):
-        copy.wait()
+        wait_all(copy)
 
         def forward(number, _, groups=piece[3], line_ref=line_ref, offset=offset):
             pair, group = number // groups, number % groups
@@ -245,16 +241,27 @@
 def filter_first_kernel(pieces, table_hbm, lines_hbm, out_hbm, *scratch):
     *scratch, out_sems = scratch
 
+    def bring(i, line_ref, sems):
+        return [pltpu.make_async_copy(piece_at(lines_hbm, pieces[i]), line_ref, sems.at[i])]
+
     def send(i, line_ref):
         return [pltpu.make_async_copy(line_ref.at[:, :, 0], out_hbm.at[:, i], out_sems.at[i])]
 
-    run_filter(pieces, table_hbm, lines_hbm, send, scratch)
-
-
-def filter_rest_kernel(pieces, me_ref, table_hbm, lines_hbm, *refs):
-    count, me = lines_hbm.shape[0], me_ref[0]
-    sent, scratch, out_sems = refs[:count], refs[count:-1], refs[-1]
+    run_filter(pieces, table_hbm, bring, send, scratch)
+
+
+def filter_rest_kernel(pieces, me_ref, table_hbm, lines_hbm, field_hbm, *refs):
+    count, split, me = lines_hbm.shape[0], field_hbm.shape[2], me_ref[0]
+    received, sent, scratch, out_sems = refs[: count - 1], refs[count - 1 : 2 * count - 1], refs[2 * count - 1 : -1], refs[-1]
     places = rest_places(pieces)
+    final = len(pieces) - 1
+
+    def bring(i, line_ref, sems):
+        if i < final:
+            return [pltpu.make_async_copy(piece_at(lines_hbm, pieces[i]), line_ref, sems.at[i])]
+        own = field_hbm.at[me // split, pl.ds(pieces[i][0], pieces[i][1]), me % split]
+        sources = (own,) + received
+        return [pltpu.make_async_copy(sources[x], line_ref.at[me ^ x], sems.at[i + x]) for x in range(count)]
 
     def send(i, line_ref):
         copies = []
@@ -266,7 +273,7 @@
                 copies.append(pltpu.make_async_copy(line_ref.at[me ^ x, pair], sent[x].at[target], sem))
         return copies
 
-    run_filter(pieces, table_hbm, lines_hbm, send, scratch)
+    run_filter(pieces, table_hbm, bring, send, scratch)
 
 
 def rest_places(pieces):
@@ -284,10 +291,9 @@
 WHOLE = pl.BlockSpec(memory_space=pltpu.VMEM)
 
 
-def filter_call(kernel, name, pieces, lines, tables, in_specs, out_specs, out_shape, out_sems):
+def filter_call(kernel, name, pieces, lines, tables, in_specs, out_specs, out_shape, sems, flops):
     count, _, _, _, width = lines.shape
     rows = sum(map(group_count, pieces)) * PAD
-    flops = 3 * 2 * TILES * rows * (2 * LANES) ** 2
     return pl.pallas_call(
         functools.partial(kernel, pieces),
         out_shape=out_shape,
@@ -298,11 +304,11 @@
             pltpu.VMEM((TILES, rows, 2 * LANES), jnp.float32),
             pltpu.VMEM(tables.shape, tables.dtype),
             pltpu.SemaphoreType.DMA((TABLE_COPIES,)),
-            pltpu.SemaphoreType.DMA((len(pieces),)),
-            pltpu.SemaphoreType.DMA((out_sems,)),
+            pltpu.SemaphoreType.DMA((sems[0],)),
+            pltpu.SemaphoreType.DMA((sems[1],)),
         ],
         compiler_params=pltpu.CompilerParams(vmem_limit_bytes=FILTER_VMEM),
-        cost_estimate=pl.CostEstimate(flops=flops, bytes_accessed=8 * count * rows * width, transcendentals=0),
+        cost_estimate=pl.CostEstimate(flops=flops, bytes_accessed=0, transcendentals=0),
         name=name,
     )
 
@@ -310,20 +316,23 @@
 def filter_first(lines, tables, pieces):
     count, _, _, _, width = lines.shape
     out_shape = jax.ShapeDtypeStruct((count, len(pieces), 2, PAD, width), jnp.float32)
+    sems = (len(pieces), len(pieces))
     call = filter_call(
-        filter_first_kernel, "filter_first", pieces, lines, tables, [HBM, HBM], HBM, out_shape, len(pieces)
+        filter_first_kernel, "filter_first", pieces, lines, tables, [HBM, HBM], HBM, out_shape, sems, 10**6
     )
     return call(tables, lines)
 
 
-def filter_rest(lines, spots, tables, pieces):
+def filter_rest(lines, field, received, spots, tables, pieces):
     count, _, _, _, width = lines.shape
     shape = (sum(map(group_count, pieces)), PAD, width)
     out_shape = [jax.ShapeDtypeStruct(shape, jnp.float32)] * count
-    sems = count * sum(piece[1] for piece in pieces)
-    ins = [SCALARS, HBM, HBM]
-    call = filter_call(filter_rest_kernel, "filter_rest", pieces, lines, tables, ins, [HBM] * count, out_shape, sems)
-    return call(spots, tables, lines)
+    sems = (len(pieces) - 1 + count, count * sum(piece[1] for piece in pieces))
+    ins = [SCALARS] + [HBM] * (count + 2)
+    call = filter_call(
+        filter_rest_kernel, "filter_rest", pieces, lines, tables, ins, [HBM] * count, out_shape, sems, 10**11
+    )
+    return call(spots, tables, lines, field, *received)
 
 
 def local_kernel(rate_ref, coef_ref, flow_ref, field_ref, low_ref, high_ref, out_ref, pad_ref):
@@ -512,8 +521,10 @@
 
     pairs_count, groups = comp_count * part_count, line_rows // PAD
     shares = (mode_split, pairs_count, row_split, groups, PAD, width)
-    lines = field.reshape(shares).transpose(0, 2, 1, 3, 4, 5)
-    lines = exchange(lines.reshape(span, pairs_count, groups, PAD, width))
+    shared = field.reshape(shares)
+    last = pairs_count - part_count
+    lines = exchange(shared[:, :last].transpose(0, 2, 1, 3, 4, 5).reshape(span, last, groups, PAD, width))
+
     wall_groups = sorted({0, groups - 1})
     first_pieces = tuple((0, 2, group, 1) for group in wall_groups)
     rest_pieces = tuple((2 * comp, 2, 0, groups) for comp in range(1, comp_count))
@@ -530,10 +541,19 @@
     flow = jnp.broadcast_to(mean_flow[:, :, None], (2, row_count, LANES))
     base = local_terms(field, low, high, rate, coef, flow)
 
+    def last_block(x):
+        other = me ^ x
+        start = (other // row_split, last, other % row_split, 0, 0, 0)
+        block = lax.dynamic_slice(shared, start, (1, part_count, 1, groups, PAD, width))
+        return block.reshape(part_count, groups, PAD, width)
+
+    blocks = tuple(last_block(x) for x in range(1, span))
+    received = swap((None,) + lax.optimization_barrier((blocks, base))[0])
     lines = after(lines, base)
     filtered = filter_first(lines, tables, first_pieces)
     back = exchange(filtered)
-    sent = filter_rest(after(lines, filtered), spots, tables, rest_pieces)
+    received[0] = after(received[0], filtered)
+    sent = filter_rest(lines, shared, received, spots, tables, rest_pieces)
     returned = [sent[0]] + swap(sent)
 
     lower = jnp.where(wall_index == 0, wall_coef[0], 0.0)

time: 226 us -> 223 us (0.987)
  waiting for transfers between devices: 151 us -> 136 us
  local copies, waits for them, and re-layouts: 2.35 us -> 12.5 us
    all_to_all x2, waiting for transfers between devices: 63.8 us -> 36.3 us  [exchange(): return lax.all_to_all(lines, 'span', split_axis=0, concat_axis=0)]
    ppermute x6 -> x9, waiting for transfers between devices: 60.7 us -> 74 us  [swap(): lax.ppermute(blocks[x], 'span', pairs[x])]
    another operation x0 -> x1, local copies, waits for them, and re-layouts: none -> 3.85 us  [on_device(): shared[:, :last].transpose(0, 2, 1, 3, 4, 5)]
    unnamed x14 -> x20, local copies, waits for them, and re-layouts: 0.03 us -> 3.14 us
    reshape x0 -> x1, local copies, waits for them, and re-layouts: none -> 2.3 us  [last_block(): return block.reshape(part_count, groups, PAD, width)]
    ppermute x6 -> x9, starting transfers between devices: 10.7 us -> 12.7 us  [swap(): lax.ppermute(blocks[x], 'span', pairs[x])]
  transfers between devices with their start and end apart: 13 -> 16, of which waited for: 9 -> 9; matrix products, arithmetic and copies ran while one was open for 1% -> 3% of each run, Pallas kernels for 16% -> 18%
where the time goes in v12:
time: 223 us; the launch traced here: 221 us
  waiting for transfers between devices  136 us (61%)
  Pallas kernels  40.2 us (18%)
  starting transfers between devices  31.2 us (14%)
  local copies, waits for them, and re-layouts  12.5 us (6%)
    ppermute x9, waiting for transfers between devices, swap(): lax.ppermute(blocks[x], 'span', pairs[x])  74 us
    all_to_all x2, waiting for transfers between devices, exchange(): return lax.all_to_all(lines, 'span', split_axis=0, concat_axis=0)  36.3 us
    ppermute x1, waiting for transfers between devices, on_device(): high = lax.ppermute(field[:, :, :, :PAD], 'wall', backward)  18.9 us
    pallas_call x1, Pallas kernels, local_terms(): pl.pallas_call(local_kernel, grid=(mode_count,), out_shape=jax.ShapeDtype...  15 us
    ppermute x9, starting transfers between devices, swap(): lax.ppermute(blocks[x], 'span', pairs[x])  12.7 us
    all_to_all x2, starting transfers between devices, exchange(): return lax.all_to_all(lines, 'span', split_axis=0, concat_axis=0)  12 us
    pallas_call x1, Pallas kernels, filter_rest(): return call(spots, tables, lines, field, *received)  10 us
    pallas_call x3, Pallas kernels, add_rest(): pl.pallas_call(functools.partial(add_rest_kernel, pieces, partners), out_...  8.15 us
  transfers between devices with their start and end apart: 16, of which 9 were waited for; matrix products, arithmetic and copies ran while one was open for 3% of the time, Pallas kernels for 18%

profile of v12, /device:TPU:10, one launch (start us, length us, event | category | flops | bytes accessed | tf_op | source)
XLA Modules:
  0.0 221.3 jit_solution(12857122437366250667)
XLA Ops:
  0.6 3.9 %slice_bitcast_fusion = f32[4,4,4,8,1536]{4,3,2,1,0:T(8,128)} fusion(f32[4,6,1,4,8,1536]{5,4,3,2,1,0:T(8,128)} %bitcast.29), kind=kLoop, calls=%fused_computation | loop fusion | bytes 6291456 | tf_op jit(solution)/shard_map/reshape;transpose | solution.py:526
  4.5 0.0 copy-start.9
  4.5 5.4 %all-to-all-start = ((f32[4,4,4,8,1536]{4,3,2,1,0:T(8,128)}), f32[4,4,4,8,1536]{4,3,2,1,0:T(8,128)}, u32[]{:S(2)}, u32[]{:S(2)}) async-start(f32[4,4,4,8,1536]{4,3,2,1,0:T(8,128)} %slice_bitcast_fusion), calls=%async_computation | async-start | bytes 6291456 | tf_op jit(solution)/shard_map/all_to_all | solution.py:517
  9.9 0.0 copy-start.3
  9.9 2.9 %fusion.6 = (f32[4,3,2,8,1536]{4,3,2,1,0:T(8,128)}, f32[4,3,2,8,1536]{4,3,2,1,0:T(8,128)S(1)}) fusion(f32[4,3,2,32,1536]{4,3,2,1,0:T(8,128)} %field_ref.1), kind=kLoop, calls=%fused_computation.17 | loop fusion | bytes 4718592 | tf_op jit(solution)/shard_map/slice | solution.py:537
  12.8 1.9 collective-permute-start.1
  14.7 2.4 %collective-permute-start = (f32[4,3,2,8,1536]{4,3,2,1,0:T(8,128)S(1)}, f32[4,3,2,8,1536]{4,3,2,1,0:T(8,128)S(1)}, u32[]{:S(2)}, u32[]{:S(2)}) collective-permute-start(f32[4,3,2,8,1536]{4,3,2,1,0:T(8,128)S(1)} %get-tuple-element.28), channel_id=1, source_target_pairs={{0,4},{4,8},{8,12},{12,16},{16,20},{20,24},{24,28},{1,5},{5,9},{9,... | collective-permute-start | bytes 3538952 | tf_op jit(solution)/shard_map/ppermute | solution.py:536
  17.2 0.0 copy-done.9
  17.2 2.3 %dynamic-slice_bitcast_fusion = (f32[2,4,8,1536]{3,2,1,0:T(8,128)}, f32[2,4,8,1536]{3,2,1,0:T(8,128)}, f32[2,4,8,1536]{3,2,1,0:T(8,128)}) fusion(f32[4,6,1,4,8,1536]{5,4,3,2,1,0:T(8,128)} %bitcast.30, s32[]{:T(128)S(6)} %select_n.72, s32[]{:T(128)S(6)} %select_n.71, s32[]{:T(128)S(6)} %select_n.70), kind=kLoop, calls=%fused_computation.2 | loop fusion | bytes 2359308 | tf_op jit(solution)/shard_map/reshape | solution.py:548
  19.5 18.9 %collective-permute-done.1.high_ref = f32[4,3,2,8,1536]{4,3,2,1,0:T(8,128)S(1)} collective-permute-done((f32[4,3,2,8,1536]{4,3,2,1,0:T(8,128)}, f32[4,3,2,8,1536]{4,3,2,1,0:T(8,128)S(1)}, u32[]{:S(2)}, u32[]{:S(2)}) %collective-permute-start.1) | collective-permute-done | bytes 1179680 | tf_op jit(solution)/shard_map/ppermute | solution.py:537
  38.4 0.0 collective-permute-done.low_ref
  38.4 0.0 copy-done.3
  38.4 0.1 broadcast_in_dim.46.flow_ref
  38.4 0.0 copy-done.2
  38.4 0.1 broadcast_in_dim.45.coef_ref
  38.6 0.0 copy-start
  38.6 2.3 %copy-done = f32[4,3,2,32,1536]{4,3,2,1,0:T(8,128)S(1)} copy-done((f32[4,3,2,32,1536]{4,3,2,1,0:T(8,128)S(1)}, f32[4,3,2,32,1536]{4,3,2,1,0:T(8,128)}, u32[]{:S(2)}) %copy-start) | copy-done | bytes 4718616
  40.9 15.0 %local_terms.1 = f32[4,3,2,32,1536]{4,3,2,1,0:T(8,128)} custom-call(f32[4]{0:T(128)S(1)} %convert_multiply_fusion.rate_ref, f32[15,32,128]{2,1,0:T(8,128)S(1)} %broadcast_in_dim.45.coef_ref, f32[2,32,128]{2,1,0:T(8,128)S(1)} %broadcast_in_dim.46.flow_ref, f32[4,3,2,32,1536]{4,3,2,1,0:T(8,128)S(1)} %copy-done, ...), custom_call_target="tpu_custom_call" | custom-call | flops 47185920 | bytes 11796480 | tf_op jit(solution)/shard_map/local_terms/pallas_call | solution.py:375
  55.9 0.0 collective-permute-start.2
  55.9 2.9 %collective-permute-start.3 = (f32[2,4,8,1536]{3,2,1,0:T(8,128)}, f32[2,4,8,1536]{3,2,1,0:T(8,128)S(1)}, u32[]{:S(2)}, u32[]{:S(2)}) collective-permute-start(f32[2,4,8,1536]{3,2,1,0:T(8,128)} %get-tuple-element.17), channel_id=1, source_target_pairs={{0,2},{1,3},{2,0},{3,1},{4,6},{5,7},{6,4},{7,5},{8,10},{9,11},{10,... | collective-permute-start | bytes 1179656 | tf_op jit(solution)/shard_map/ppermute | solution.py:520
  58.8 0.6 collective-permute-start.4
  59.4 36.3 %all-to-all-done.lines_hbm = f32[4,4,4,8,1536]{4,3,2,1,0:T(8,128)} async-done(((f32[4,4,4,8,1536]{4,3,2,1,0:T(8,128)}), f32[4,4,4,8,1536]{4,3,2,1,0:T(8,128)}, u32[]{:S(2)}, u32[]{:S(2)}) %all-to-all-start) | async-done | bytes 3145760 | tf_op jit(solution)/shard_map/all_to_all | solution.py:517
  95.7 4.8 %filter_first.1 = f32[4,2,2,8,1536]{4,3,2,1,0:T(8,128)} custom-call(bf16[24,2,256,256]{3,2,1,0:T(8,128)(2,1)} %constant.92.clone.table_hbm, f32[4,4,4,8,1536]{4,3,2,1,0:T(8,128)} %all-to-all-done.lines_hbm), custom_call_target="tpu_custom_call" | custom-call | flops 1000000 | tf_op jit(solution)/shard_map/filter_first/pallas_call | solution.py:323
  100.5 6.5 %all-to-all-start.1 = ((f32[4,2,2,8,1536]{4,3,2,1,0:T(8,128)}), f32[4,2,2,8,1536]{4,3,2,1,0:T(8,128)S(1)}, u32[]{:S(2)}, u32[]{:S(2)}) async-start(f32[4,2,2,8,1536]{4,3,2,1,0:T(8,128)} %filter_first.1), calls=%async_computation.1 | async-start | bytes 1572864 | tf_op jit(solution)/shard_map/all_to_all | solution.py:517
  107.0 0.0 collective-permute-done.2.refs_0_
  107.0 0.0 collective-permute-done.3.refs_1_
  107.0 0.0 copy-start.6
  107.0 15.5 %collective-permute-done.4.refs_2_ = f32[2,4,8,1536]{3,2,1,0:T(8,128)S(1)} collective-permute-done((f32[2,4,8,1536]{3,2,1,0:T(8,128)}, f32[2,4,8,1536]{3,2,1,0:T(8,128)S(1)}, u32[]{:S(2)}, u32[]{:S(2)}) %collective-permute-start.4) | collective-permute-done | bytes 393248 | tf_op jit(solution)/shard_map/ppermute | solution.py:520
  122.4 0.0 copy-done.5
  122.4 0.0 copy-done.6
  122.4 0.8 copy-done.7
  123.2 10.0 %filter_rest.1 = (f32[20,8,1536]{2,1,0:T(8,128)}, f32[20,8,1536]{2,1,0:T(8,128)}, f32[20,8,1536]{2,1,0:T(8,128)}, f32[20,8,1536]{2,1,0:T(8,128)}) custom-call(s32[1]{0:T(128)} %bitcast.me_ref, bf16[24,2,256,256]{3,2,1,0:T(8,128)(2,1)} %constant.92.clone.table_hbm, f32[4,4,4,8,1536]{4,3,2,1,0:T(8,128)} %all-to-all-done.lines_hbm, ...), custom_call_target="tpu_custom_call" | custom-call | flops 99999997952 | tf_op jit(solution)/shard_map/filter_rest/pallas_call | solution.py:335
  133.3 0.0 copy-start.8
  133.3 0.0 copy-start.1
  133.3 0.1 collective-permute-start.5
  133.4 2.4 %collective-permute-start.6 = (f32[20,8,1536]{2,1,0:T(8,128)}, f32[20,8,1536]{2,1,0:T(8,128)}, u32[]{:S(2)}, u32[]{:S(2)}) collective-permute-start(f32[20,8,1536]{2,1,0:T(8,128)} %get-tuple-element.21), channel_id=1, source_target_pairs={{0,2},{1,3},{2,0},{3,1},{4,6},{5,7},{6,4},{7,5},{8,10},{9,11},{10,... | collective-permute-start | bytes 2949128 | tf_op jit(solution)/shard_map/ppermute | solution.py:520
  135.7 1.1 collective-permute-start.7
  136.8 0.0 copy-done.4
  136.8 0.1 rev.3
  137.0 0.0 all-to-all-done.1.term_hbm
  137.0 0.1 broadcast_in_dim.50.weight_ref
  137.0 2.3 %add_first.1 = (f32[4,6,1,4,8,1536]{5,4,3,2,1,0:T(8,128)}, f32[4,4,1536]{2,1,0:T(4,128)S(1)}) custom-call(s32[1]{0:T(128)} %bitcast.me_ref, f32[4,6,1,4,8,1536]{5,4,3,2,1,0:T(8,128)} %bitcast.32, f32[4,2,8,128]{3,2,1,0:T(8,128)S(1)} %broadcast_in_dim.50.weight_ref, f32[4,2,2,8,1536]{4,3,2,1,0:T(8,128)S(1)} %all-to-all-done.1.term_hbm), custom_call_target="tpu_custom_call", output_to_operand_aliasing={{0}: (1, {})} | custom-call | flops 196608 | bytes 2359296 | tf_op jit(solution)/shard_map/add_first/pallas_call | solution.py:424
  139.3 0.0 copy-done.8
  139.3 0.3 fusion.1
  139.7 0.1 collective-permute-start.8
  139.8 1.2 collective-permute-done.8
  140.9 0.5 collective-permute-start.9
  141.5 3.1 %collective-permute-done.9 = f32[4,2,2,64]{3,2,0,1:T(2,128)S(1)} collective-permute-done((f32[4,2,2,64]{3,2,0,1:T(2,128)S(1)}, f32[4,2,2,64]{3,2,0,1:T(2,128)S(1)}, u32[]{:S(2)}, u32[]{:S(2)}) %collective-permute-start.9) | collective-permute-done | bytes 4128 | tf_op jit(solution)/shard_map/ppermute | solution.py:570
  144.6 1.5 collective-permute-start.10
  146.1 2.1 collective-permute-done.10
  148.2 0.9 collective-permute-start.13
  149.1 2.4 %collective-permute-start.12 = (f32[4,2,2,64]{3,2,0,1:T(2,128)S(1)}, f32[4,2,2,64]{3,2,0,1:T(2,128)S(1)}, u32[]{:S(2)}, u32[]{:S(2)}) collective-permute-start(f32[4,2,2,64]{3,2,0,1:T(2,128)S(1)} %add.60), channel_id=1, source_target_pairs={{0,2},{1,3},{2,0},{3,1},{4,6},{5,7},{6,4},{7,5},{8,10},{9,11},{10,... | collective-permute-start | bytes 12296 | tf_op jit(solution)/shard_map/ppermute | solution.py:520
  151.6 18.0 %collective-permute-done.5.refs_1_ = f32[20,8,1536]{2,1,0:T(8,128)S(1)} collective-permute-done((f32[20,8,1536]{2,1,0:T(8,128)}, f32[20,8,1536]{2,1,0:T(8,128)S(1)}, u32[]{:S(2)}, u32[]{:S(2)}) %collective-permute-start.5) | collective-permute-done | bytes 983072 | tf_op jit(solution)/shard_map/ppermute | solution.py:520
  169.6 2.4 %collective-permute-start.11 = (f32[4,2,2,64]{3,2,0,1:T(2,128)S(1)}, f32[4,2,2,64]{3,2,0,1:T(2,128)S(1)}, u32[]{:S(2)}, u32[]{:S(2)}) collective-permute-start(f32[4,2,2,64]{3,2,0,1:T(2,128)S(1)} %add.60), channel_id=1, source_target_pairs={{0,1},{1,0},{2,3},{3,2},{4,5},{5,4},{6,7},{7,6},{8,9},{9,8},{10,11... | collective-permute-start | bytes 12296 | tf_op jit(solution)/shard_map/ppermute | solution.py:520
  172.0 0.0 copy-done.1
  172.0 3.0 %add_rest.3.base_hbm = f32[4,6,1,4,8,1536]{5,4,3,2,1,0:T(8,128)} custom-call(s32[1]{0:T(128)} %bitcast.me_ref, f32[4,6,1,4,8,1536]{5,4,3,2,1,0:T(8,128)} %get-tuple-element.14.base_hbm, f32[20,8,1536]{2,1,0:T(8,128)S(1)} %copy-done.1, f32[20,8,1536]{2,1,0:T(8,128)S(1)} %collective-permute-done.5.refs_1_), custom_call_target="tpu_custom_call", output_to_operand_aliasing={{}: (1, {})} | custom-call | flops 491520 | bytes 5898240 | tf_op jit(solution)/shard_map/add_rest/pallas_call | solution.py:481
  175.0 25.7 %collective-permute-done.6.refs_0_ = f32[20,8,1536]{2,1,0:T(8,128)} collective-permute-done((f32[20,8,1536]{2,1,0:T(8,128)}, f32[20,8,1536]{2,1,0:T(8,128)}, u32[]{:S(2)}, u32[]{:S(2)}) %collective-permute-start.6) | collective-permute-done | bytes 983072 | tf_op jit(solution)/shard_map/ppermute | solution.py:520
  200.7 2.6 %add_rest.4.base_hbm = f32[4,6,1,4,8,1536]{5,4,3,2,1,0:T(8,128)} custom-call(s32[1]{0:T(128)} %bitcast.me_ref, f32[4,6,1,4,8,1536]{5,4,3,2,1,0:T(8,128)} %add_rest.3.base_hbm, f32[20,8,1536]{2,1,0:T(8,128)} %collective-permute-done.6.refs_0_), custom_call_target="tpu_custom_call", output_to_operand_aliasing={{}: (1, {})} | custom-call | flops 245760 | bytes 2949120 | tf_op jit(solution)/shard_map/add_rest/pallas_call | solution.py:481
  203.3 14.8 %collective-permute-done.7.refs_0_ = f32[20,8,1536]{2,1,0:T(8,128)} collective-permute-done((f32[20,8,1536]{2,1,0:T(8,128)}, f32[20,8,1536]{2,1,0:T(8,128)}, u32[]{:S(2)}, u32[]{:S(2)}) %collective-permute-start.7) | collective-permute-done | bytes 983072 | tf_op jit(solution)/shard_map/ppermute | solution.py:520
  218.1 2.6 %add_rest.5 = f32[4,6,1,4,8,1536]{5,4,3,2,1,0:T(8,128)} custom-call(s32[1]{0:T(128)} %bitcast.me_ref, f32[4,6,1,4,8,1536]{5,4,3,2,1,0:T(8,128)} %add_rest.4.base_hbm, f32[20,8,1536]{2,1,0:T(8,128)} %collective-permute-done.7.refs_0_), custom_call_target="tpu_custom_call", output_to_operand_aliasing={{}: (1, {})} | custom-call | flops 245760 | bytes 2949120 | tf_op jit(solution)/shard_map/add_rest/pallas_call | solution.py:481
  220.7 0.0 collective-permute-done.13
  220.7 0.0 collective-permute-done.12
  220.7 0.0 collective-permute-done.11
  220.7 0.6 add_bitcast_fusion
  (15 shorter events, 0.1 us)
Async XLA Ops:
  4.5 12.7 %copy-start.9 = (s32[4]{0:T(128)S(1)}, s32[4]{0:T(128)}, u32[]{:S(2)}) copy-start(s32[4]{0:T(128)} %param.11) | copy-start | bytes 52
  4.5 91.2 %all-to-all-start = ((f32[4,4,4,8,1536]{4,3,2,1,0:T(8,128)}), f32[4,4,4,8,1536]{4,3,2,1,0:T(8,128)}, u32[]{:S(2)}, u32[]{:S(2)}) async-start(f32[4,4,4,8,1536]{4,3,2,1,0:T(8,128)} %slice_bitcast_fusion), calls=%async_computation | async-start | bytes 6291456 | tf_op jit(solution)/shard_map/all_to_all | solution.py:517
  9.9 28.4 %copy-start.3 = (f32[2,32]{1,0:T(2,128)S(1)}, f32[2,32]{1,0:T(2,128)}, u32[]{:S(2)}) copy-start(f32[2,32]{1,0:T(2,128)} %param.8) | copy-start | bytes 772
  9.9 28.5 %copy-start.2 = (f32[15,32]{1,0:T(8,128)S(1)}, f32[15,32]{1,0:T(8,128)}, u32[]{:S(2)}) copy-start(f32[15,32]{1,0:T(8,128)} %param.9) | copy-start | bytes 5764
  12.8 25.6 %collective-permute-start.1 = (f32[4,3,2,8,1536]{4,3,2,1,0:T(8,128)}, f32[4,3,2,8,1536]{4,3,2,1,0:T(8,128)S(1)}, u32[]{:S(2)}, u32[]{:S(2)}) collective-permute-start(f32[4,3,2,8,1536]{4,3,2,1,0:T(8,128)} %get-tuple-element.27), channel_id=1, source_target_pairs={{4,0},{8,4},{12,8},{16,12},{20,16},{24,20},{28,24},{5,1},{9,5},{13... | collective-permute-start | bytes 3538952 | tf_op jit(solution)/shard_map/ppermute | solution.py:537
  14.7 23.6 %collective-permute-start = (f32[4,3,2,8,1536]{4,3,2,1,0:T(8,128)S(1)}, f32[4,3,2,8,1536]{4,3,2,1,0:T(8,128)S(1)}, u32[]{:S(2)}, u32[]{:S(2)}) collective-permute-start(f32[4,3,2,8,1536]{4,3,2,1,0:T(8,128)S(1)} %get-tuple-element.28), channel_id=1, source_target_pairs={{0,4},{4,8},{8,12},{12,16},{16,20},{20,24},{24,28},{1,5},{5,9},{9,... | collective-permute-start | bytes 3538952 | tf_op jit(solution)/shard_map/ppermute | solution.py:536
  38.6 2.3 %copy-start = (f32[4,3,2,32,1536]{4,3,2,1,0:T(8,128)S(1)}, f32[4,3,2,32,1536]{4,3,2,1,0:T(8,128)}, u32[]{:S(2)}) copy-start(f32[4,3,2,32,1536]{4,3,2,1,0:T(8,128)} %field_ref.1) | copy-start | bytes 14155780
  55.9 51.1 %collective-permute-start.2 = (f32[2,4,8,1536]{3,2,1,0:T(8,128)}, f32[2,4,8,1536]{3,2,1,0:T(8,128)S(1)}, u32[]{:S(2)}, u32[]{:S(2)}) collective-permute-start(f32[2,4,8,1536]{3,2,1,0:T(8,128)} %get-tuple-element.15), channel_id=1, source_target_pairs={{0,1},{1,0},{2,3},{3,2},{4,5},{5,4},{6,7},{7,6},{8,9},{9,8},{10,11... | collective-permute-start | bytes 1179656 | tf_op jit(solution)/shard_map/ppermute | solution.py:520
  55.9 51.1 %collective-permute-start.3 = (f32[2,4,8,1536]{3,2,1,0:T(8,128)}, f32[2,4,8,1536]{3,2,1,0:T(8,128)S(1)}, u32[]{:S(2)}, u32[]{:S(2)}) collective-permute-start(f32[2,4,8,1536]{3,2,1,0:T(8,128)} %get-tuple-element.17), channel_id=1, source_target_pairs={{0,2},{1,3},{2,0},{3,1},{4,6},{5,7},{6,4},{7,5},{8,10},{9,11},{10,... | collective-permute-start | bytes 1179656 | tf_op jit(solution)/shard_map/ppermute | solution.py:520
  58.8 63.6 %collective-permute-start.4 = (f32[2,4,8,1536]{3,2,1,0:T(8,128)}, f32[2,4,8,1536]{3,2,1,0:T(8,128)S(1)}, u32[]{:S(2)}, u32[]{:S(2)}) collective-permute-start(f32[2,4,8,1536]{3,2,1,0:T(8,128)} %get-tuple-element.18), channel_id=1, source_target_pairs={{0,3},{1,2},{2,1},{3,0},{4,7},{5,6},{6,5},{7,4},{8,11},{9,10},{10,... | collective-permute-start | bytes 1179656 | tf_op jit(solution)/shard_map/ppermute | solution.py:520
  100.5 36.5 %all-to-all-start.1 = ((f32[4,2,2,8,1536]{4,3,2,1,0:T(8,128)}), f32[4,2,2,8,1536]{4,3,2,1,0:T(8,128)S(1)}, u32[]{:S(2)}, u32[]{:S(2)}) async-start(f32[4,2,2,8,1536]{4,3,2,1,0:T(8,128)} %filter_first.1), calls=%async_computation.1 | async-start | bytes 1572864 | tf_op jit(solution)/shard_map/all_to_all | solution.py:517
  107.0 15.5 %copy-start.5 = (f32[2,4,8,1536]{3,2,1,0:T(8,128)}, f32[2,4,8,1536]{3,2,1,0:T(8,128)S(1)}, u32[]{:S(2)}) copy-start(f32[2,4,8,1536]{3,2,1,0:T(8,128)S(1)} %collective-permute-done.2.refs_0_) | copy-start | bytes 1179652
  107.0 15.5 %copy-start.6 = (f32[2,4,8,1536]{3,2,1,0:T(8,128)}, f32[2,4,8,1536]{3,2,1,0:T(8,128)S(1)}, u32[]{:S(2)}) copy-start(f32[2,4,8,1536]{3,2,1,0:T(8,128)S(1)} %collective-permute-done.3.refs_1_) | copy-start | bytes 1179652
  122.4 0.8 copy-start.7
  123.2 13.6 %copy-start.4 = (f32[2,8]{1,0:T(2,128)S(1)}, f32[2,8]{1,0:T(2,128)}, u32[]{:S(2)}) copy-start(f32[2,8]{1,0:T(2,128)} %param.10) | copy-start | bytes 196
  133.3 6.1 %copy-start.8 = (s32[1536]{0:T(1024)S(1)}, s32[1536]{0:T(1024)}, u32[]{:S(2)}) copy-start(s32[1536]{0:T(1024)} %param.12) | copy-start | bytes 18436
  133.3 38.7 %copy-start.1 = (f32[20,8,1536]{2,1,0:T(8,128)S(1)}, f32[20,8,1536]{2,1,0:T(8,128)}, u32[]{:S(2)}) copy-start(f32[20,8,1536]{2,1,0:T(8,128)} %get-tuple-element.19.refs_0_) | copy-start | bytes 2949124
  133.3 36.3 %collective-permute-start.5 = (f32[20,8,1536]{2,1,0:T(8,128)}, f32[20,8,1536]{2,1,0:T(8,128)S(1)}, u32[]{:S(2)}, u32[]{:S(2)}) collective-permute-start(f32[20,8,1536]{2,1,0:T(8,128)} %get-tuple-element.20), channel_id=1, source_target_pairs={{0,1},{1,0},{2,3},{3,2},{4,5},{5,4},{6,7},{7,6},{8,9},{9,8},{10,11... | collective-permute-start | bytes 2949128 | tf_op jit(solution)/shard_map/ppermute | solution.py:520
  133.4 67.4 %collective-permute-start.6 = (f32[20,8,1536]{2,1,0:T(8,128)}, f32[20,8,1536]{2,1,0:T(8,128)}, u32[]{:S(2)}, u32[]{:S(2)}) collective-permute-start(f32[20,8,1536]{2,1,0:T(8,128)} %get-tuple-element.21), channel_id=1, source_target_pairs={{0,2},{1,3},{2,0},{3,1},{4,6},{5,7},{6,4},{7,5},{8,10},{9,11},{10,... | collective-permute-start | bytes 2949128 | tf_op jit(solution)/shard_map/ppermute | solution.py:520
  135.7 82.4 %collective-permute-start.7 = (f32[20,8,1536]{2,1,0:T(8,128)}, f32[20,8,1536]{2,1,0:T(8,128)}, u32[]{:S(2)}, u32[]{:S(2)}) collective-permute-start(f32[20,8,1536]{2,1,0:T(8,128)} %get-tuple-element.22), channel_id=1, source_target_pairs={{0,3},{1,2},{2,1},{3,0},{4,7},{5,6},{6,5},{7,4},{8,11},{9,10},{10,... | collective-permute-start | bytes 2949128 | tf_op jit(solution)/shard_map/ppermute | solution.py:520
  139.7 1.2 collective-permute-start.8
  140.9 3.7 %collective-permute-start.9 = (f32[4,2,2,64]{3,2,0,1:T(2,128)S(1)}, f32[4,2,2,64]{3,2,0,1:T(2,128)S(1)}, u32[]{:S(2)}, u32[]{:S(2)}) collective-permute-start(f32[4,2,2,64]{3,2,0,1:T(2,128)S(1)} %copy_add_fusion), channel_id=1, source_target_pairs={{0,8},{4,12},{8,0},{12,4},{16,24},{20,28},{24,16},{28,20},{1,9},{5... | collective-permute-start | bytes 12296 | tf_op jit(solution)/shard_map/ppermute | solution.py:570
  144.6 3.7 %collective-permute-start.10 = (f32[4,2,2,64]{3,2,0,1:T(2,128)S(1)}, f32[4,2,2,64]{3,2,0,1:T(2,128)S(1)}, u32[]{:S(2)}, u32[]{:S(2)}) collective-permute-start(f32[4,2,2,64]{3,2,0,1:T(2,128)S(1)} %add.59), channel_id=1, source_target_pairs={{0,16},{4,20},{8,24},{12,28},{16,0},{20,4},{24,8},{28,12},{1,17},{... | collective-permute-start | bytes 12296 | tf_op jit(solution)/shard_map/ppermute | solution.py:570
  148.2 72.4 %collective-permute-start.13 = (f32[4,2,2,64]{3,2,0,1:T(2,128)S(1)}, f32[4,2,2,64]{3,2,0,1:T(2,128)S(1)}, u32[]{:S(2)}, u32[]{:S(2)}) collective-permute-start(f32[4,2,2,64]{3,2,0,1:T(2,128)S(1)} %add.60), channel_id=1, source_target_pairs={{0,3},{1,2},{2,1},{3,0},{4,7},{5,6},{6,5},{7,4},{8,11},{9,10},{10,... | collective-permute-start | bytes 12296 | tf_op jit(solution)/shard_map/ppermute | solution.py:520
  149.1 71.5 %collective-permute-start.12 = (f32[4,2,2,64]{3,2,0,1:T(2,128)S(1)}, f32[4,2,2,64]{3,2,0,1:T(2,128)S(1)}, u32[]{:S(2)}, u32[]{:S(2)}) collective-permute-start(f32[4,2,2,64]{3,2,0,1:T(2,128)S(1)} %add.60), channel_id=1, source_target_pairs={{0,2},{1,3},{2,0},{3,1},{4,6},{5,7},{6,4},{7,5},{8,10},{9,11},{10,... | collective-permute-start | bytes 12296 | tf_op jit(solution)/shard_map/ppermute | solution.py:520
  169.6 51.1 %collective-permute-start.11 = (f32[4,2,2,64]{3,2,0,1:T(2,128)S(1)}, f32[4,2,2,64]{3,2,0,1:T(2,128)S(1)}, u32[]{:S(2)}, u32[]{:S(2)}) collective-permute-start(f32[4,2,2,64]{3,2,0,1:T(2,128)S(1)} %add.60), channel_id=1, source_target_pairs={{0,1},{1,0},{2,3},{3,2},{4,5},{5,4},{6,7},{7,6},{8,9},{9,8},{10,11... | collective-permute-start | bytes 12296 | tf_op jit(solution)/shard_map/ppermute | solution.py:520

commit v13 on v12

--- a/solution.py
+++ b/solution.py
@@ -525,11 +525,8 @@
     last = pairs_count - part_count
     lines = exchange(shared[:, :last].transpose(0, 2, 1, 3, 4, 5).reshape(span, last, groups, PAD, width))
 
-    wall_groups = sorted({0, groups - 1})
-    first_pieces = tuple((0, 2, group, 1) for group in wall_groups)
+    first_pieces = tuple((0, 2, group, 1) for group in range(groups))
     rest_pieces = tuple((2 * comp, 2, 0, groups) for comp in range(1, comp_count))
-    if groups > 2:
-        rest_pieces = ((0, 2, 1, groups - 2),) + rest_pieces
 
     forward = [(i, i + 1) for i in range(wall_count - 1)]
     backward = [(i + 1, i) for i in range(wall_count - 1)]

time: 223 us -> 218 us (0.978)
  waiting for transfers between devices: 136 us -> 132 us
    ppermute x9, waiting for transfers between devices: 74 us -> 59.9 us  [swap(): lax.ppermute(blocks[x], 'span', pairs[x])]
    all_to_all x2, waiting for transfers between devices: 36.3 us -> 46.4 us  [exchange(): return lax.all_to_all(lines, 'span', split_axis=0, concat_axis=0)]
where the time goes in v13:
time: 218 us; the launch traced here: 217 us
  waiting for transfers between devices  132 us (61%)
  Pallas kernels  39.2 us (18%)
  starting transfers between devices  30.7 us (14%)
  local copies, waits for them, and re-layouts  13.7 us (6%)
    ppermute x9, waiting for transfers between devices, swap(): lax.ppermute(blocks[x], 'span', pairs[x])  59.9 us
    all_to_all x2, waiting for transfers between devices, exchange(): return lax.all_to_all(lines, 'span', split_axis=0, concat_axis=0)  46.4 us
    ppermute x1, waiting for transfers between devices, on_device(): high = lax.ppermute(field[:, :, :, :PAD], 'wall', backward)  18.9 us
    pallas_call x1, Pallas kernels, local_terms(): pl.pallas_call(local_kernel, grid=(mode_count,), out_shape=jax.ShapeDtype...  15 us
    ppermute x9, starting transfers between devices, swap(): lax.ppermute(blocks[x], 'span', pairs[x])  12.5 us
    all_to_all x2, starting transfers between devices, exchange(): return lax.all_to_all(lines, 'span', split_axis=0, concat_axis=0)  11.9 us
    pallas_call x1, Pallas kernels, filter_rest(): return call(spots, tables, lines, field, *received)  9.16 us
    pallas_call x3, Pallas kernels, add_rest(): pl.pallas_call(functools.partial(add_rest_kernel, pieces, partners), out_...  6.97 us
  transfers between devices with their start and end apart: 16, of which 9 were waited for; matrix products, arithmetic and copies ran while one was open for 3% of the time, Pallas kernels for 18%

profile of v13, /device:TPU:10, one launch (start us, length us, event | category | flops | bytes accessed | tf_op | source)
XLA Modules:
  0.0 217.2 jit_solution(11294814181141164601)
XLA Ops:
  0.6 3.9 %slice_bitcast_fusion = f32[4,4,4,8,1536]{4,3,2,1,0:T(8,128)} fusion(f32[4,6,1,4,8,1536]{5,4,3,2,1,0:T(8,128)} %bitcast.29), kind=kLoop, calls=%fused_computation | loop fusion | bytes 6291456 | tf_op jit(solution)/shard_map/reshape;transpose | solution.py:526
  4.5 5.3 %all-to-all-start = ((f32[4,4,4,8,1536]{4,3,2,1,0:T(8,128)}), f32[4,4,4,8,1536]{4,3,2,1,0:T(8,128)}, u32[]{:S(2)}, u32[]{:S(2)}) async-start(f32[4,4,4,8,1536]{4,3,2,1,0:T(8,128)} %slice_bitcast_fusion), calls=%async_computation | async-start | bytes 6291456 | tf_op jit(solution)/shard_map/all_to_all | solution.py:517
  9.8 0.0 copy-start.9
  9.8 0.0 copy-start.3
  9.8 0.0 copy-start.2
  9.8 2.9 %fusion.6 = (f32[4,3,2,8,1536]{4,3,2,1,0:T(8,128)}, f32[4,3,2,8,1536]{4,3,2,1,0:T(8,128)S(1)}) fusion(f32[4,3,2,32,1536]{4,3,2,1,0:T(8,128)} %field_ref.1), kind=kLoop, calls=%fused_computation.17 | loop fusion | bytes 4718592 | tf_op jit(solution)/shard_map/slice | solution.py:534
  12.7 1.9 collective-permute-start.1
  14.6 2.4 %collective-permute-start = (f32[4,3,2,8,1536]{4,3,2,1,0:T(8,128)S(1)}, f32[4,3,2,8,1536]{4,3,2,1,0:T(8,128)S(1)}, u32[]{:S(2)}, u32[]{:S(2)}) collective-permute-start(f32[4,3,2,8,1536]{4,3,2,1,0:T(8,128)S(1)} %get-tuple-element.28), channel_id=1, source_target_pairs={{0,4},{4,8},{8,12},{12,16},{16,20},{20,24},{24,28},{1,5},{5,9},{9,... | collective-permute-start | bytes 3538952 | tf_op jit(solution)/shard_map/ppermute | solution.py:533
  17.0 0.0 copy-done.9
  17.1 2.3 %dynamic-slice_bitcast_fusion = (f32[2,4,8,1536]{3,2,1,0:T(8,128)}, f32[2,4,8,1536]{3,2,1,0:T(8,128)}, f32[2,4,8,1536]{3,2,1,0:T(8,128)}) fusion(f32[4,6,1,4,8,1536]{5,4,3,2,1,0:T(8,128)} %bitcast.30, s32[]{:T(128)S(6)} %select_n.72, s32[]{:T(128)S(6)} %select_n.71, s32[]{:T(128)S(6)} %select_n.70), kind=kLoop, calls=%fused_computation.2 | loop fusion | bytes 2359308 | tf_op jit(solution)/shard_map/reshape | solution.py:545
  19.3 18.9 %collective-permute-done.1.high_ref = f32[4,3,2,8,1536]{4,3,2,1,0:T(8,128)S(1)} collective-permute-done((f32[4,3,2,8,1536]{4,3,2,1,0:T(8,128)}, f32[4,3,2,8,1536]{4,3,2,1,0:T(8,128)S(1)}, u32[]{:S(2)}, u32[]{:S(2)}) %collective-permute-start.1) | collective-permute-done | bytes 1179680 | tf_op jit(solution)/shard_map/ppermute | solution.py:534
  38.3 0.0 collective-permute-done.low_ref
  38.3 0.0 copy-done.3
  38.3 0.1 broadcast_in_dim.46.flow_ref
  38.3 0.0 copy-done.2
  38.3 0.1 broadcast_in_dim.45.coef_ref
  38.5 0.0 copy-start
  38.5 2.3 %copy-done = f32[4,3,2,32,1536]{4,3,2,1,0:T(8,128)S(1)} copy-done((f32[4,3,2,32,1536]{4,3,2,1,0:T(8,128)S(1)}, f32[4,3,2,32,1536]{4,3,2,1,0:T(8,128)}, u32[]{:S(2)}) %copy-start) | copy-done | bytes 4718616
  40.8 0.0 copy-start.4
  40.8 15.0 %local_terms.1 = f32[4,3,2,32,1536]{4,3,2,1,0:T(8,128)} custom-call(f32[4]{0:T(128)S(1)} %convert_multiply_fusion.rate_ref, f32[15,32,128]{2,1,0:T(8,128)S(1)} %broadcast_in_dim.45.coef_ref, f32[2,32,128]{2,1,0:T(8,128)S(1)} %broadcast_in_dim.46.flow_ref, f32[4,3,2,32,1536]{4,3,2,1,0:T(8,128)S(1)} %copy-done, ...), custom_call_target="tpu_custom_call" | custom-call | flops 47185920 | bytes 11796480 | tf_op jit(solution)/shard_map/local_terms/pallas_call | solution.py:375
  55.8 0.0 collective-permute-start.2
  55.8 2.9 %collective-permute-start.3 = (f32[2,4,8,1536]{3,2,1,0:T(8,128)}, f32[2,4,8,1536]{3,2,1,0:T(8,128)S(1)}, u32[]{:S(2)}, u32[]{:S(2)}) collective-permute-start(f32[2,4,8,1536]{3,2,1,0:T(8,128)} %get-tuple-element.17), channel_id=1, source_target_pairs={{0,2},{1,3},{2,0},{3,1},{4,6},{5,7},{6,4},{7,5},{8,10},{9,11},{10,... | collective-permute-start | bytes 1179656 | tf_op jit(solution)/shard_map/ppermute | solution.py:520
  58.7 0.6 collective-permute-start.4
  59.3 0.0 copy-done.4
  59.3 0.1 rev.3
  59.4 36.2 %all-to-all-done.lines_hbm = f32[4,4,4,8,1536]{4,3,2,1,0:T(8,128)} async-done(((f32[4,4,4,8,1536]{4,3,2,1,0:T(8,128)}), f32[4,4,4,8,1536]{4,3,2,1,0:T(8,128)}, u32[]{:S(2)}, u32[]{:S(2)}) %all-to-all-start) | async-done | bytes 3145760 | tf_op jit(solution)/shard_map/all_to_all | solution.py:517
  95.6 5.3 %filter_first.1 = f32[4,4,2,8,1536]{4,3,2,1,0:T(8,128)} custom-call(bf16[24,2,256,256]{3,2,1,0:T(8,128)(2,1)} %constant.92.clone.table_hbm, f32[4,4,4,8,1536]{4,3,2,1,0:T(8,128)} %all-to-all-done.lines_hbm), custom_call_target="tpu_custom_call" | custom-call | flops 1000000 | tf_op jit(solution)/shard_map/filter_first/pallas_call | solution.py:323
  100.9 6.6 %all-to-all-start.1 = ((f32[4,4,2,8,1536]{4,3,2,1,0:T(8,128)}), f32[4,4,2,8,1536]{4,3,2,1,0:T(8,128)S(1)}, u32[]{:S(2)}, u32[]{:S(2)}) async-start(f32[4,4,2,8,1536]{4,3,2,1,0:T(8,128)} %filter_first.1), calls=%async_computation.1 | async-start | bytes 3145728 | tf_op jit(solution)/shard_map/all_to_all | solution.py:517
  107.5 0.0 collective-permute-done.2.refs_0_
  107.5 0.0 collective-permute-done.3.refs_1_
  107.5 0.0 copy-start.6
  107.5 14.8 %collective-permute-done.4.refs_2_ = f32[2,4,8,1536]{3,2,1,0:T(8,128)S(1)} collective-permute-done((f32[2,4,8,1536]{3,2,1,0:T(8,128)}, f32[2,4,8,1536]{3,2,1,0:T(8,128)S(1)}, u32[]{:S(2)}, u32[]{:S(2)}) %collective-permute-start.4) | collective-permute-done | bytes 393248 | tf_op jit(solution)/shard_map/ppermute | solution.py:520
  122.3 0.0 copy-done.5
  122.3 0.0 copy-done.6
  122.3 0.8 copy-done.7
  123.1 9.2 %filter_rest.1 = (f32[16,8,1536]{2,1,0:T(8,128)}, f32[16,8,1536]{2,1,0:T(8,128)}, f32[16,8,1536]{2,1,0:T(8,128)}, f32[16,8,1536]{2,1,0:T(8,128)}) custom-call(s32[1]{0:T(128)} %bitcast.me_ref, bf16[24,2,256,256]{3,2,1,0:T(8,128)(2,1)} %constant.92.clone.table_hbm, f32[4,4,4,8,1536]{4,3,2,1,0:T(8,128)} %all-to-all-done.lines_hbm, ...), custom_call_target="tpu_custom_call" | custom-call | flops 99999997952 | tf_op jit(solution)/shard_map/filter_rest/pallas_call | solution.py:335
  132.3 0.1 collective-permute-start.5
  132.3 1.1 collective-permute-start.6
  133.4 2.4 %collective-permute-start.7 = (f32[16,8,1536]{2,1,0:T(8,128)}, f32[16,8,1536]{2,1,0:T(8,128)S(1)}, u32[]{:S(2)}, u32[]{:S(2)}) collective-permute-start(f32[16,8,1536]{2,1,0:T(8,128)} %get-tuple-element.22), channel_id=1, source_target_pairs={{0,3},{1,2},{2,1},{3,0},{4,7},{5,6},{6,5},{7,4},{8,11},{9,10},{10,... | collective-permute-start | bytes 2359304 | tf_op jit(solution)/shard_map/ppermute | solution.py:520
  135.8 10.3 %all-to-all-done.1.term_hbm = f32[4,4,2,8,1536]{4,3,2,1,0:T(8,128)S(1)} async-done(((f32[4,4,2,8,1536]{4,3,2,1,0:T(8,128)}), f32[4,4,2,8,1536]{4,3,2,1,0:T(8,128)S(1)}, u32[]{:S(2)}, u32[]{:S(2)}) %all-to-all-start.1) | async-done | bytes 1572896 | tf_op jit(solution)/shard_map/all_to_all | solution.py:517
  146.1 0.1 broadcast_in_dim.50.weight_ref
  146.2 2.8 %add_first.1 = (f32[4,6,1,4,8,1536]{5,4,3,2,1,0:T(8,128)}, f32[4,4,1536]{2,1,0:T(4,128)S(1)}) custom-call(s32[1]{0:T(128)} %bitcast.me_ref, f32[4,6,1,4,8,1536]{5,4,3,2,1,0:T(8,128)} %bitcast.32, f32[4,2,8,128]{3,2,1,0:T(8,128)S(1)} %broadcast_in_dim.50.weight_ref, f32[4,4,2,8,1536]{4,3,2,1,0:T(8,128)S(1)} %all-to-all-done.1.term_hbm), custom_call_target="tpu_custom_call", output_to_operand_aliasing={{0}: (1, {})} | custom-call | flops 393216 | bytes 4718592 | tf_op jit(solution)/shard_map/add_first/pallas_call | solution.py:424
  149.0 0.0 copy-done.8
  149.0 0.3 fusion.1
  149.3 0.1 collective-permute-start.8
  149.4 1.2 collective-permute-done.8
  150.6 0.5 collective-permute-start.9
  151.0 3.2 %collective-permute-done.9 = f32[4,2,2,64]{3,2,0,1:T(2,128)S(1)} collective-permute-done((f32[4,2,2,64]{3,2,0,1:T(2,128)S(1)}, f32[4,2,2,64]{3,2,0,1:T(2,128)S(1)}, u32[]{:S(2)}, u32[]{:S(2)}) %collective-permute-start.9) | collective-permute-done | bytes 4128 | tf_op jit(solution)/shard_map/ppermute | solution.py:567
  154.2 1.5 collective-permute-start.10
  155.7 2.1 collective-permute-done.10
  157.9 1.2 collective-permute-start.13
  159.1 4.2 %collective-permute-start.12 = (f32[4,2,2,64]{3,2,0,1:T(2,128)S(1)}, f32[4,2,2,64]{3,2,0,1:T(2,128)S(1)}, u32[]{:S(2)}, u32[]{:S(2)}) collective-permute-start(f32[4,2,2,64]{3,2,0,1:T(2,128)S(1)} %add.60), channel_id=1, source_target_pairs={{0,2},{1,3},{2,0},{3,1},{4,6},{5,7},{6,4},{7,5},{8,10},{9,11},{10,... | collective-permute-start | bytes 12296 | tf_op jit(solution)/shard_map/ppermute | solution.py:520
  163.3 0.0 collective-permute-done.5.refs_1_
  163.3 0.0 collective-permute-start.11
  163.3 1.1 copy-done.1
  164.4 3.0 %add_rest.3.base_hbm = f32[4,6,1,4,8,1536]{5,4,3,2,1,0:T(8,128)} custom-call(s32[1]{0:T(128)} %bitcast.me_ref, f32[4,6,1,4,8,1536]{5,4,3,2,1,0:T(8,128)} %get-tuple-element.14.base_hbm, f32[16,8,1536]{2,1,0:T(8,128)S(1)} %copy-done.1, f32[16,8,1536]{2,1,0:T(8,128)} %collective-permute-done.5.refs_1_), custom_call_target="tpu_custom_call", output_to_operand_aliasing={{}: (1, {})} | custom-call | flops 393216 | bytes 4718592 | tf_op jit(solution)/shard_map/add_rest/pallas_call | solution.py:481
  167.4 29.7 %collective-permute-done.6.refs_0_ = f32[16,8,1536]{2,1,0:T(8,128)S(1)} collective-permute-done((f32[16,8,1536]{2,1,0:T(8,128)}, f32[16,8,1536]{2,1,0:T(8,128)S(1)}, u32[]{:S(2)}, u32[]{:S(2)}) %collective-permute-start.6) | collective-permute-done | bytes 786464 | tf_op jit(solution)/shard_map/ppermute | solution.py:520
  197.1 2.0 add_rest.4.base_hbm
  199.1 15.4 %collective-permute-done.7.refs_0_ = f32[16,8,1536]{2,1,0:T(8,128)S(1)} collective-permute-done((f32[16,8,1536]{2,1,0:T(8,128)}, f32[16,8,1536]{2,1,0:T(8,128)S(1)}, u32[]{:S(2)}, u32[]{:S(2)}) %collective-permute-start.7) | collective-permute-done | bytes 786464 | tf_op jit(solution)/shard_map/ppermute | solution.py:520
  214.5 2.0 add_rest.5
  216.5 0.0 collective-permute-done.13
  216.5 0.0 collective-permute-done.12
  216.5 0.0 collective-permute-done.11
  216.6 0.6 add_bitcast_fusion
  (15 shorter events, 0.1 us)
Async XLA Ops:
  4.5 91.1 %all-to-all-start = ((f32[4,4,4,8,1536]{4,3,2,1,0:T(8,128)}), f32[4,4,4,8,1536]{4,3,2,1,0:T(8,128)}, u32[]{:S(2)}, u32[]{:S(2)}) async-start(f32[4,4,4,8,1536]{4,3,2,1,0:T(8,128)} %slice_bitcast_fusion), calls=%async_computation | async-start | bytes 6291456 | tf_op jit(solution)/shard_map/all_to_all | solution.py:517
  9.8 7.3 %copy-start.9 = (s32[4]{0:T(128)S(1)}, s32[4]{0:T(128)}, u32[]{:S(2)}) copy-start(s32[4]{0:T(128)} %param.11) | copy-start | bytes 52
  9.8 28.5 %copy-start.3 = (f32[2,32]{1,0:T(2,128)S(1)}, f32[2,32]{1,0:T(2,128)}, u32[]{:S(2)}) copy-start(f32[2,32]{1,0:T(2,128)} %param.8) | copy-start | bytes 772
  9.8 28.5 %copy-start.2 = (f32[15,32]{1,0:T(8,128)S(1)}, f32[15,32]{1,0:T(8,128)}, u32[]{:S(2)}) copy-start(f32[15,32]{1,0:T(8,128)} %param.9) | copy-start | bytes 5764
  12.7 25.6 %collective-permute-start.1 = (f32[4,3,2,8,1536]{4,3,2,1,0:T(8,128)}, f32[4,3,2,8,1536]{4,3,2,1,0:T(8,128)S(1)}, u32[]{:S(2)}, u32[]{:S(2)}) collective-permute-start(f32[4,3,2,8,1536]{4,3,2,1,0:T(8,128)} %get-tuple-element.27), channel_id=1, source_target_pairs={{4,0},{8,4},{12,8},{16,12},{20,16},{24,20},{28,24},{5,1},{9,5},{13... | collective-permute-start | bytes 3538952 | tf_op jit(solution)/shard_map/ppermute | solution.py:534
  14.6 23.6 %collective-permute-start = (f32[4,3,2,8,1536]{4,3,2,1,0:T(8,128)S(1)}, f32[4,3,2,8,1536]{4,3,2,1,0:T(8,128)S(1)}, u32[]{:S(2)}, u32[]{:S(2)}) collective-permute-start(f32[4,3,2,8,1536]{4,3,2,1,0:T(8,128)S(1)} %get-tuple-element.28), channel_id=1, source_target_pairs={{0,4},{4,8},{8,12},{12,16},{16,20},{20,24},{24,28},{1,5},{5,9},{9,... | collective-permute-start | bytes 3538952 | tf_op jit(solution)/shard_map/ppermute | solution.py:533
  38.5 2.3 %copy-start = (f32[4,3,2,32,1536]{4,3,2,1,0:T(8,128)S(1)}, f32[4,3,2,32,1536]{4,3,2,1,0:T(8,128)}, u32[]{:S(2)}) copy-start(f32[4,3,2,32,1536]{4,3,2,1,0:T(8,128)} %field_ref.1) | copy-start | bytes 14155780
  40.8 18.5 %copy-start.4 = (f32[2,8]{1,0:T(2,128)S(1)}, f32[2,8]{1,0:T(2,128)}, u32[]{:S(2)}) copy-start(f32[2,8]{1,0:T(2,128)} %param.10) | copy-start | bytes 196
  55.8 51.7 %collective-permute-start.2 = (f32[2,4,8,1536]{3,2,1,0:T(8,128)}, f32[2,4,8,1536]{3,2,1,0:T(8,128)S(1)}, u32[]{:S(2)}, u32[]{:S(2)}) collective-permute-start(f32[2,4,8,1536]{3,2,1,0:T(8,128)} %get-tuple-element.15), channel_id=1, source_target_pairs={{0,1},{1,0},{2,3},{3,2},{4,5},{5,4},{6,7},{7,6},{8,9},{9,8},{10,11... | collective-permute-start | bytes 1179656 | tf_op jit(solution)/shard_map/ppermute | solution.py:520
  55.8 51.7 %collective-permute-start.3 = (f32[2,4,8,1536]{3,2,1,0:T(8,128)}, f32[2,4,8,1536]{3,2,1,0:T(8,128)S(1)}, u32[]{:S(2)}, u32[]{:S(2)}) collective-permute-start(f32[2,4,8,1536]{3,2,1,0:T(8,128)} %get-tuple-element.17), channel_id=1, source_target_pairs={{0,2},{1,3},{2,0},{3,1},{4,6},{5,7},{6,4},{7,5},{8,10},{9,11},{10,... | collective-permute-start | bytes 1179656 | tf_op jit(solution)/shard_map/ppermute | solution.py:520
  58.7 63.6 %collective-permute-start.4 = (f32[2,4,8,1536]{3,2,1,0:T(8,128)}, f32[2,4,8,1536]{3,2,1,0:T(8,128)S(1)}, u32[]{:S(2)}, u32[]{:S(2)}) collective-permute-start(f32[2,4,8,1536]{3,2,1,0:T(8,128)} %get-tuple-element.18), channel_id=1, source_target_pairs={{0,3},{1,2},{2,1},{3,0},{4,7},{5,6},{6,5},{7,4},{8,11},{9,10},{10,... | collective-permute-start | bytes 1179656 | tf_op jit(solution)/shard_map/ppermute | solution.py:520
  100.9 45.2 %all-to-all-start.1 = ((f32[4,4,2,8,1536]{4,3,2,1,0:T(8,128)}), f32[4,4,2,8,1536]{4,3,2,1,0:T(8,128)S(1)}, u32[]{:S(2)}, u32[]{:S(2)}) async-start(f32[4,4,2,8,1536]{4,3,2,1,0:T(8,128)} %filter_first.1), calls=%async_computation.1 | async-start | bytes 3145728 | tf_op jit(solution)/shard_map/all_to_all | solution.py:517
  107.5 14.8 %copy-start.5 = (f32[2,4,8,1536]{3,2,1,0:T(8,128)}, f32[2,4,8,1536]{3,2,1,0:T(8,128)S(1)}, u32[]{:S(2)}) copy-start(f32[2,4,8,1536]{3,2,1,0:T(8,128)S(1)} %collective-permute-done.2.refs_0_) | copy-start | bytes 1179652
  107.5 14.8 %copy-start.6 = (f32[2,4,8,1536]{3,2,1,0:T(8,128)}, f32[2,4,8,1536]{3,2,1,0:T(8,128)S(1)}, u32[]{:S(2)}) copy-start(f32[2,4,8,1536]{3,2,1,0:T(8,128)S(1)} %collective-permute-done.3.refs_1_) | copy-start | bytes 1179652
  122.3 0.8 copy-start.7
  132.3 31.0 %collective-permute-start.5 = (f32[16,8,1536]{2,1,0:T(8,128)}, f32[16,8,1536]{2,1,0:T(8,128)}, u32[]{:S(2)}, u32[]{:S(2)}) collective-permute-start(f32[16,8,1536]{2,1,0:T(8,128)} %get-tuple-element.20), channel_id=1, source_target_pairs={{0,1},{1,0},{2,3},{3,2},{4,5},{5,4},{6,7},{7,6},{8,9},{9,8},{10,11... | collective-permute-start | bytes 2359304 | tf_op jit(solution)/shard_map/ppermute | solution.py:520
  132.3 64.7 %collective-permute-start.6 = (f32[16,8,1536]{2,1,0:T(8,128)}, f32[16,8,1536]{2,1,0:T(8,128)S(1)}, u32[]{:S(2)}, u32[]{:S(2)}) collective-permute-start(f32[16,8,1536]{2,1,0:T(8,128)} %get-tuple-element.21), channel_id=1, source_target_pairs={{0,2},{1,3},{2,0},{3,1},{4,6},{5,7},{6,4},{7,5},{8,10},{9,11},{10,... | collective-permute-start | bytes 2359304 | tf_op jit(solution)/shard_map/ppermute | solution.py:520
  133.4 81.0 %collective-permute-start.7 = (f32[16,8,1536]{2,1,0:T(8,128)}, f32[16,8,1536]{2,1,0:T(8,128)S(1)}, u32[]{:S(2)}, u32[]{:S(2)}) collective-permute-start(f32[16,8,1536]{2,1,0:T(8,128)} %get-tuple-element.22), channel_id=1, source_target_pairs={{0,3},{1,2},{2,1},{3,0},{4,7},{5,6},{6,5},{7,4},{8,11},{9,10},{10,... | collective-permute-start | bytes 2359304 | tf_op jit(solution)/shard_map/ppermute | solution.py:520
  146.2 2.8 %copy-start.8 = (s32[1536]{0:T(1024)S(1)}, s32[1536]{0:T(1024)}, u32[]{:S(2)}) copy-start(s32[1536]{0:T(1024)} %param.12) | copy-start | bytes 18436
  149.3 1.2 collective-permute-start.8
  150.6 3.7 %collective-permute-start.9 = (f32[4,2,2,64]{3,2,0,1:T(2,128)S(1)}, f32[4,2,2,64]{3,2,0,1:T(2,128)S(1)}, u32[]{:S(2)}, u32[]{:S(2)}) collective-permute-start(f32[4,2,2,64]{3,2,0,1:T(2,128)S(1)} %copy_add_fusion), channel_id=1, source_target_pairs={{0,8},{4,12},{8,0},{12,4},{16,24},{20,28},{24,16},{28,20},{1,9},{5... | collective-permute-start | bytes 12296 | tf_op jit(solution)/shard_map/ppermute | solution.py:567
  154.2 3.7 %collective-permute-start.10 = (f32[4,2,2,64]{3,2,0,1:T(2,128)S(1)}, f32[4,2,2,64]{3,2,0,1:T(2,128)S(1)}, u32[]{:S(2)}, u32[]{:S(2)}) collective-permute-start(f32[4,2,2,64]{3,2,0,1:T(2,128)S(1)} %add.59), channel_id=1, source_target_pairs={{0,16},{4,20},{8,24},{12,28},{16,0},{20,4},{24,8},{28,12},{1,17},{... | collective-permute-start | bytes 12296 | tf_op jit(solution)/shard_map/ppermute | solution.py:567
  157.9 58.6 %collective-permute-start.13 = (f32[4,2,2,64]{3,2,0,1:T(2,128)S(1)}, f32[4,2,2,64]{3,2,0,1:T(2,128)S(1)}, u32[]{:S(2)}, u32[]{:S(2)}) collective-permute-start(f32[4,2,2,64]{3,2,0,1:T(2,128)S(1)} %add.60), channel_id=1, source_target_pairs={{0,3},{1,2},{2,1},{3,0},{4,7},{5,6},{6,5},{7,4},{8,11},{9,10},{10,... | collective-permute-start | bytes 12296 | tf_op jit(solution)/shard_map/ppermute | solution.py:520
  159.1 57.4 %collective-permute-start.12 = (f32[4,2,2,64]{3,2,0,1:T(2,128)S(1)}, f32[4,2,2,64]{3,2,0,1:T(2,128)S(1)}, u32[]{:S(2)}, u32[]{:S(2)}) collective-permute-start(f32[4,2,2,64]{3,2,0,1:T(2,128)S(1)} %add.60), channel_id=1, source_target_pairs={{0,2},{1,3},{2,0},{3,1},{4,6},{5,7},{6,4},{7,5},{8,10},{9,11},{10,... | collective-permute-start | bytes 12296 | tf_op jit(solution)/shard_map/ppermute | solution.py:520
  163.3 53.2 %collective-permute-start.11 = (f32[4,2,2,64]{3,2,0,1:T(2,128)S(1)}, f32[4,2,2,64]{3,2,0,1:T(2,128)S(1)}, u32[]{:S(2)}, u32[]{:S(2)}) collective-permute-start(f32[4,2,2,64]{3,2,0,1:T(2,128)S(1)} %add.60), channel_id=1, source_target_pairs={{0,1},{1,0},{2,3},{3,2},{4,5},{5,4},{6,7},{7,6},{8,9},{9,8},{10,11... | collective-permute-start | bytes 12296 | tf_op jit(solution)/shard_map/ppermute | solution.py:520
  163.3 1.1 copy-start.1

commit v14 on v13

--- a/solution.py
+++ b/solution.py
@@ -238,6 +238,31 @@
     wait_all(away)
 
 
+def gather_kernel(field_hbm, out_hbm, sems):
+    count, pairs = out_hbm.shape[:2]
+    split = field_hbm.shape[2]
+    copies = []
+    for x in range(count):
+        for pair in range(pairs):
+            source = field_hbm.at[x // split, pair, x % split]
+            copies.append(pltpu.make_async_copy(source, out_hbm.at[x, pair], sems.at[x * pairs + pair]))
+    wait_all(start_all(copies))
+
+
+def gather_lines(field, count, pairs):
+    anywhere = pl.BlockSpec(memory_space=pl.ANY)
+    shape = (count, pairs) + field.shape[3:]
+    return pl.pallas_call(
+        gather_kernel,
+        out_shape=jax.ShapeDtypeStruct(shape, jnp.float32),
+        in_specs=[anywhere],
+        out_specs=anywhere,
+        scratch_shapes=[pltpu.SemaphoreType.DMA((count * pairs,))],
+        cost_estimate=pl.CostEstimate(flops=0, bytes_accessed=8 * math.prod(shape), transcendentals=0),
+        name="gather_lines",
+    )(field)
+
+
 def filter_first_kernel(pieces, table_hbm, lines_hbm, out_hbm, *scratch):
     *scratch, out_sems = scratch
 
@@ -523,7 +548,7 @@
     shares = (mode_split, pairs_count, row_split, groups, PAD, width)
     shared = field.reshape(shares)
     last = pairs_count - part_count
-    lines = exchange(shared[:, :last].transpose(0, 2, 1, 3, 4, 5).reshape(span, last, groups, PAD, width))
+    lines = exchange(gather_lines(shared, span, last))
 
     first_pieces = tuple((0, 2, group, 1) for group in range(groups))
     rest_pieces = tuple((2 * comp, 2, 0, groups) for comp in range(1, comp_count))

time: 218 us -> 311 us (1.43)
  Pallas kernels: 39.2 us -> 136 us
  local copies, waits for them, and re-layouts: 13.7 us -> 9.8 us
    pallas_call x0 -> x1, Pallas kernels: none -> 96.5 us  [gather_lines(): pl.pallas_call(gather_kernel, out_shape=jax.ShapeDtypeStruct(shape, jnp.f...]
    another operation x1 -> x0, local copies, waits for them, and re-layouts: 3.85 us -> none  [on_device(): shared[:, :last].transpose(0, 2, 1, 3, 4, 5)]
  transfers between devices with their start and end apart: 16 -> 16, of which waited for: 9 -> 9; matrix products, arithmetic and copies ran while one was open for 3% -> 2% of each run, Pallas kernels for 18% -> 13%
where the time goes in v14:
time: 311 us; the launch traced here: 310 us
  Pallas kernels  136 us (44%)
  waiting for transfers between devices  132 us (42%)
  starting transfers between devices  30.7 us (10%)
  local copies, waits for them, and re-layouts  9.8 us (3%)
    pallas_call x1, Pallas kernels, gather_lines(): pl.pallas_call(gather_kernel, out_shape=jax.ShapeDtypeStruct(shape, jnp.f...  96.5 us
    ppermute x9, waiting for transfers between devices, swap(): lax.ppermute(blocks[x], 'span', pairs[x])  59.9 us
    all_to_all x2, waiting for transfers between devices, exchange(): return lax.all_to_all(lines, 'span', split_axis=0, concat_axis=0)  46.4 us
    ppermute x1, waiting for transfers between devices, on_device(): high = lax.ppermute(field[:, :, :, :PAD], 'wall', backward)  18.9 us
    pallas_call x1, Pallas kernels, local_terms(): pl.pallas_call(local_kernel, grid=(mode_count,), out_shape=jax.ShapeDtype...  15 us
    ppermute x9, starting transfers between devices, swap(): lax.ppermute(blocks[x], 'span', pairs[x])  12.5 us
    all_to_all x2, starting transfers between devices, exchange(): return lax.all_to_all(lines, 'span', split_axis=0, concat_axis=0)  11.9 us
    pallas_call x1, Pallas kernels, filter_rest(): return call(spots, tables, lines, field, *received)  9.16 us
  transfers between devices with their start and end apart: 16, of which 9 were waited for; matrix products, arithmetic and copies ran while one was open for 2% of the time, Pallas kernels for 13%

profile of v14, /device:TPU:10, one launch (start us, length us, event | category | flops | bytes accessed | tf_op | source)
XLA Modules:
  0.0 309.9 jit_solution(11905731932575577626)
XLA Ops:
  0.6 96.5 %gather_lines.1 = f32[4,4,4,8,1536]{4,3,2,1,0:T(8,128)} custom-call(f32[4,6,1,4,8,1536]{5,4,3,2,1,0:T(8,128)} %bitcast.27), custom_call_target="tpu_custom_call" | custom-call | bytes 6291456 | tf_op jit(solution)/shard_map/gather_lines/pallas_call | solution.py:255
  97.2 5.3 %all-to-all-start = ((f32[4,4,4,8,1536]{4,3,2,1,0:T(8,128)}), f32[4,4,4,8,1536]{4,3,2,1,0:T(8,128)}, u32[]{:S(2)}, u32[]{:S(2)}) async-start(f32[4,4,4,8,1536]{4,3,2,1,0:T(8,128)} %gather_lines.1), calls=%async_computation | async-start | bytes 6291456 | tf_op jit(solution)/shard_map/all_to_all | solution.py:542
  102.5 0.0 copy-start.9
  102.5 0.0 copy-start.3
  102.5 0.0 copy-start.2
  102.5 2.9 fusion.6
  105.4 1.9 collective-permute-start.1
  107.3 2.4 collective-permute-start
  109.8 0.0 copy-done.9
  109.8 2.3 dynamic-slice_bitcast_fusion
  112.0 18.9 %collective-permute-done.1.high_ref = f32[4,3,2,8,1536]{4,3,2,1,0:T(8,128)S(1)} collective-permute-done((f32[4,3,2,8,1536]{4,3,2,1,0:T(8,128)}, f32[4,3,2,8,1536]{4,3,2,1,0:T(8,128)S(1)}, u32[]{:S(2)}, u32[]{:S(2)}) %collective-permute-start.1) | collective-permute-done | bytes 1179680 | tf_op jit(solution)/shard_map/ppermute | solution.py:559
  131.0 0.0 collective-permute-done.low_ref
  131.0 0.0 copy-done.3
  131.0 0.1 broadcast_in_dim.46.flow_ref
  131.0 0.0 copy-done.2
  131.0 0.1 broadcast_in_dim.45.coef_ref
  131.2 0.0 copy-start
  131.2 2.3 copy-done
  133.5 0.0 copy-start.4
  133.5 15.0 %local_terms.1 = f32[4,3,2,32,1536]{4,3,2,1,0:T(8,128)} custom-call(f32[4]{0:T(128)S(1)} %convert_multiply_fusion.rate_ref, f32[15,32,128]{2,1,0:T(8,128)S(1)} %broadcast_in_dim.45.coef_ref, f32[2,32,128]{2,1,0:T(8,128)S(1)} %broadcast_in_dim.46.flow_ref, f32[4,3,2,32,1536]{4,3,2,1,0:T(8,128)S(1)} %copy-done, ...), custom_call_target="tpu_custom_call" | custom-call | flops 47185920 | bytes 11796480 | tf_op jit(solution)/shard_map/local_terms/pallas_call | solution.py:400
  148.5 0.0 collective-permute-start.2
  148.5 2.9 collective-permute-start.3
  151.4 0.6 collective-permute-start.4
  152.0 0.0 copy-done.4
  152.0 0.1 rev.3
  152.1 36.2 %all-to-all-done.lines_hbm = f32[4,4,4,8,1536]{4,3,2,1,0:T(8,128)} async-done(((f32[4,4,4,8,1536]{4,3,2,1,0:T(8,128)}), f32[4,4,4,8,1536]{4,3,2,1,0:T(8,128)}, u32[]{:S(2)}, u32[]{:S(2)}) %all-to-all-start) | async-done | bytes 3145760 | tf_op jit(solution)/shard_map/all_to_all | solution.py:542
  188.3 5.3 %filter_first.1 = f32[4,4,2,8,1536]{4,3,2,1,0:T(8,128)} custom-call(bf16[24,2,256,256]{3,2,1,0:T(8,128)(2,1)} %constant.92.clone.table_hbm, f32[4,4,4,8,1536]{4,3,2,1,0:T(8,128)} %all-to-all-done.lines_hbm), custom_call_target="tpu_custom_call" | custom-call | flops 1000000 | tf_op jit(solution)/shard_map/filter_first/pallas_call | solution.py:348
  193.6 6.6 %all-to-all-start.1 = ((f32[4,4,2,8,1536]{4,3,2,1,0:T(8,128)}), f32[4,4,2,8,1536]{4,3,2,1,0:T(8,128)S(1)}, u32[]{:S(2)}, u32[]{:S(2)}) async-start(f32[4,4,2,8,1536]{4,3,2,1,0:T(8,128)} %filter_first.1), calls=%async_computation.1 | async-start | bytes 3145728 | tf_op jit(solution)/shard_map/all_to_all | solution.py:542
  200.2 0.0 collective-permute-done.2.refs_0_
  200.2 0.0 collective-permute-done.3.refs_1_
  200.2 0.0 copy-start.6
  200.2 14.8 %collective-permute-done.4.refs_2_ = f32[2,4,8,1536]{3,2,1,0:T(8,128)S(1)} collective-permute-done((f32[2,4,8,1536]{3,2,1,0:T(8,128)}, f32[2,4,8,1536]{3,2,1,0:T(8,128)S(1)}, u32[]{:S(2)}, u32[]{:S(2)}) %collective-permute-start.4) | collective-permute-done | bytes 393248 | tf_op jit(solution)/shard_map/ppermute | solution.py:545
  215.0 0.0 copy-done.5
  215.0 0.0 copy-done.6
  215.0 0.8 copy-done.7
  215.8 9.2 %filter_rest.1 = (f32[16,8,1536]{2,1,0:T(8,128)}, f32[16,8,1536]{2,1,0:T(8,128)}, f32[16,8,1536]{2,1,0:T(8,128)}, f32[16,8,1536]{2,1,0:T(8,128)}) custom-call(s32[1]{0:T(128)} %bitcast.me_ref, bf16[24,2,256,256]{3,2,1,0:T(8,128)(2,1)} %constant.92.clone.table_hbm, f32[4,4,4,8,1536]{4,3,2,1,0:T(8,128)} %all-to-all-done.lines_hbm, ...), custom_call_target="tpu_custom_call" | custom-call | flops 99999997952 | tf_op jit(solution)/shard_map/filter_rest/pallas_call | solution.py:360
  225.0 0.1 collective-permute-start.5
  225.0 1.1 collective-permute-start.6
  226.1 2.4 collective-permute-start.7
  228.5 10.3 %all-to-all-done.1.term_hbm = f32[4,4,2,8,1536]{4,3,2,1,0:T(8,128)S(1)} async-done(((f32[4,4,2,8,1536]{4,3,2,1,0:T(8,128)}), f32[4,4,2,8,1536]{4,3,2,1,0:T(8,128)S(1)}, u32[]{:S(2)}, u32[]{:S(2)}) %all-to-all-start.1) | async-done | bytes 1572896 | tf_op jit(solution)/shard_map/all_to_all | solution.py:542
  238.8 0.1 broadcast_in_dim.50.weight_ref
  238.9 2.8 add_first.1
  241.7 0.0 copy-done.8
  241.7 0.3 fusion.1
  242.0 0.1 collective-permute-start.8
  242.1 1.2 collective-permute-done.8
  243.3 0.5 collective-permute-start.9
  243.7 3.2 %collective-permute-done.9 = f32[4,2,2,64]{3,2,0,1:T(2,128)S(1)} collective-permute-done((f32[4,2,2,64]{3,2,0,1:T(2,128)S(1)}, f32[4,2,2,64]{3,2,0,1:T(2,128)S(1)}, u32[]{:S(2)}, u32[]{:S(2)}) %collective-permute-start.9) | collective-permute-done | bytes 4128 | tf_op jit(solution)/shard_map/ppermute | solution.py:592
  246.9 1.5 collective-permute-start.10
  248.4 2.1 collective-permute-done.10
  250.6 1.2 collective-permute-start.13
  251.8 4.2 %collective-permute-start.12 = (f32[4,2,2,64]{3,2,0,1:T(2,128)S(1)}, f32[4,2,2,64]{3,2,0,1:T(2,128)S(1)}, u32[]{:S(2)}, u32[]{:S(2)}) collective-permute-start(f32[4,2,2,64]{3,2,0,1:T(2,128)S(1)} %add.60), channel_id=1, source_target_pairs={{0,2},{1,3},{2,0},{3,1},{4,6},{5,7},{6,4},{7,5},{8,10},{9,11},{10,... | collective-permute-start | bytes 12296 | tf_op jit(solution)/shard_map/ppermute | solution.py:545
  256.0 0.0 collective-permute-done.5.refs_1_
  256.0 0.0 collective-permute-start.11
  256.0 1.1 copy-done.1
  257.1 3.0 add_rest.3.base_hbm
  260.1 29.7 %collective-permute-done.6.refs_0_ = f32[16,8,1536]{2,1,0:T(8,128)S(1)} collective-permute-done((f32[16,8,1536]{2,1,0:T(8,128)}, f32[16,8,1536]{2,1,0:T(8,128)S(1)}, u32[]{:S(2)}, u32[]{:S(2)}) %collective-permute-start.6) | collective-permute-done | bytes 786464 | tf_op jit(solution)/shard_map/ppermute | solution.py:545
  289.8 2.0 add_rest.4.base_hbm
  291.8 15.4 %collective-permute-done.7.refs_0_ = f32[16,8,1536]{2,1,0:T(8,128)S(1)} collective-permute-done((f32[16,8,1536]{2,1,0:T(8,128)}, f32[16,8,1536]{2,1,0:T(8,128)S(1)}, u32[]{:S(2)}, u32[]{:S(2)}) %collective-permute-start.7) | collective-permute-done | bytes 786464 | tf_op jit(solution)/shard_map/ppermute | solution.py:545
  307.2 2.0 add_rest.5
  309.2 0.0 collective-permute-done.13
  309.2 0.0 collective-permute-done.12
  309.2 0.0 collective-permute-done.11
  309.3 0.6 add_bitcast_fusion
  (15 shorter events, 0.1 us)
Async XLA Ops:
  97.2 91.1 %all-to-all-start = ((f32[4,4,4,8,1536]{4,3,2,1,0:T(8,128)}), f32[4,4,4,8,1536]{4,3,2,1,0:T(8,128)}, u32[]{:S(2)}, u32[]{:S(2)}) async-start(f32[4,4,4,8,1536]{4,3,2,1,0:T(8,128)} %gather_lines.1), calls=%async_computation | async-start | bytes 6291456 | tf_op jit(solution)/shard_map/all_to_all | solution.py:542
  102.5 7.3 %copy-start.9 = (s32[4]{0:T(128)S(1)}, s32[4]{0:T(128)}, u32[]{:S(2)}) copy-start(s32[4]{0:T(128)} %param.11) | copy-start | bytes 52
  102.5 28.5 %copy-start.3 = (f32[2,32]{1,0:T(2,128)S(1)}, f32[2,32]{1,0:T(2,128)}, u32[]{:S(2)}) copy-start(f32[2,32]{1,0:T(2,128)} %param.8) | copy-start | bytes 772
  102.5 28.5 %copy-start.2 = (f32[15,32]{1,0:T(8,128)S(1)}, f32[15,32]{1,0:T(8,128)}, u32[]{:S(2)}) copy-start(f32[15,32]{1,0:T(8,128)} %param.9) | copy-start | bytes 5764
  105.4 25.6 %collective-permute-start.1 = (f32[4,3,2,8,1536]{4,3,2,1,0:T(8,128)}, f32[4,3,2,8,1536]{4,3,2,1,0:T(8,128)S(1)}, u32[]{:S(2)}, u32[]{:S(2)}) collective-permute-start(f32[4,3,2,8,1536]{4,3,2,1,0:T(8,128)} %get-tuple-element.27), channel_id=1, source_target_pairs={{4,0},{8,4},{12,8},{16,12},{20,16},{24,20},{28,24},{5,1},{9,5},{13... | collective-permute-start | bytes 3538952 | tf_op jit(solution)/shard_map/ppermute | solution.py:559
  107.3 23.6 %collective-permute-start = (f32[4,3,2,8,1536]{4,3,2,1,0:T(8,128)S(1)}, f32[4,3,2,8,1536]{4,3,2,1,0:T(8,128)S(1)}, u32[]{:S(2)}, u32[]{:S(2)}) collective-permute-start(f32[4,3,2,8,1536]{4,3,2,1,0:T(8,128)S(1)} %get-tuple-element.28), channel_id=1, source_target_pairs={{0,4},{4,8},{8,12},{12,16},{16,20},{20,24},{24,28},{1,5},{5,9},{9,... | collective-permute-start | bytes 3538952 | tf_op jit(solution)/shard_map/ppermute | solution.py:558
  131.2 2.3 copy-start
  133.5 18.5 %copy-start.4 = (f32[2,8]{1,0:T(2,128)S(1)}, f32[2,8]{1,0:T(2,128)}, u32[]{:S(2)}) copy-start(f32[2,8]{1,0:T(2,128)} %param.10) | copy-start | bytes 196
  148.5 51.7 %collective-permute-start.2 = (f32[2,4,8,1536]{3,2,1,0:T(8,128)}, f32[2,4,8,1536]{3,2,1,0:T(8,128)S(1)}, u32[]{:S(2)}, u32[]{:S(2)}) collective-permute-start(f32[2,4,8,1536]{3,2,1,0:T(8,128)} %get-tuple-element.15), channel_id=1, source_target_pairs={{0,1},{1,0},{2,3},{3,2},{4,5},{5,4},{6,7},{7,6},{8,9},{9,8},{10,11... | collective-permute-start | bytes 1179656 | tf_op jit(solution)/shard_map/ppermute | solution.py:545
  148.5 51.7 %collective-permute-start.3 = (f32[2,4,8,1536]{3,2,1,0:T(8,128)}, f32[2,4,8,1536]{3,2,1,0:T(8,128)S(1)}, u32[]{:S(2)}, u32[]{:S(2)}) collective-permute-start(f32[2,4,8,1536]{3,2,1,0:T(8,128)} %get-tuple-element.17), channel_id=1, source_target_pairs={{0,2},{1,3},{2,0},{3,1},{4,6},{5,7},{6,4},{7,5},{8,10},{9,11},{10,... | collective-permute-start | bytes 1179656 | tf_op jit(solution)/shard_map/ppermute | solution.py:545
  151.4 63.6 %collective-permute-start.4 = (f32[2,4,8,1536]{3,2,1,0:T(8,128)}, f32[2,4,8,1536]{3,2,1,0:T(8,128)S(1)}, u32[]{:S(2)}, u32[]{:S(2)}) collective-permute-start(f32[2,4,8,1536]{3,2,1,0:T(8,128)} %get-tuple-element.18), channel_id=1, source_target_pairs={{0,3},{1,2},{2,1},{3,0},{4,7},{5,6},{6,5},{7,4},{8,11},{9,10},{10,... | collective-permute-start | bytes 1179656 | tf_op jit(solution)/shard_map/ppermute | solution.py:545
  193.6 45.2 %all-to-all-start.1 = ((f32[4,4,2,8,1536]{4,3,2,1,0:T(8,128)}), f32[4,4,2,8,1536]{4,3,2,1,0:T(8,128)S(1)}, u32[]{:S(2)}, u32[]{:S(2)}) async-start(f32[4,4,2,8,1536]{4,3,2,1,0:T(8,128)} %filter_first.1), calls=%async_computation.1 | async-start | bytes 3145728 | tf_op jit(solution)/shard_map/all_to_all | solution.py:542
  200.2 14.8 %copy-start.5 = (f32[2,4,8,1536]{3,2,1,0:T(8,128)}, f32[2,4,8,1536]{3,2,1,0:T(8,128)S(1)}, u32[]{:S(2)}) copy-start(f32[2,4,8,1536]{3,2,1,0:T(8,128)S(1)} %collective-permute-done.2.refs_0_) | copy-start | bytes 1179652
  200.2 14.8 %copy-start.6 = (f32[2,4,8,1536]{3,2,1,0:T(8,128)}, f32[2,4,8,1536]{3,2,1,0:T(8,128)S(1)}, u32[]{:S(2)}) copy-start(f32[2,4,8,1536]{3,2,1,0:T(8,128)S(1)} %collective-permute-done.3.refs_1_) | copy-start | bytes 1179652
  215.0 0.8 copy-start.7
  225.0 31.0 %collective-permute-start.5 = (f32[16,8,1536]{2,1,0:T(8,128)}, f32[16,8,1536]{2,1,0:T(8,128)}, u32[]{:S(2)}, u32[]{:S(2)}) collective-permute-start(f32[16,8,1536]{2,1,0:T(8,128)} %get-tuple-element.20), channel_id=1, source_target_pairs={{0,1},{1,0},{2,3},{3,2},{4,5},{5,4},{6,7},{7,6},{8,9},{9,8},{10,11... | collective-permute-start | bytes 2359304 | tf_op jit(solution)/shard_map/ppermute | solution.py:545
  225.0 64.7 %collective-permute-start.6 = (f32[16,8,1536]{2,1,0:T(8,128)}, f32[16,8,1536]{2,1,0:T(8,128)S(1)}, u32[]{:S(2)}, u32[]{:S(2)}) collective-permute-start(f32[16,8,1536]{2,1,0:T(8,128)} %get-tuple-element.21), channel_id=1, source_target_pairs={{0,2},{1,3},{2,0},{3,1},{4,6},{5,7},{6,4},{7,5},{8,10},{9,11},{10,... | collective-permute-start | bytes 2359304 | tf_op jit(solution)/shard_map/ppermute | solution.py:545
  226.1 81.1 %collective-permute-start.7 = (f32[16,8,1536]{2,1,0:T(8,128)}, f32[16,8,1536]{2,1,0:T(8,128)S(1)}, u32[]{:S(2)}, u32[]{:S(2)}) collective-permute-start(f32[16,8,1536]{2,1,0:T(8,128)} %get-tuple-element.22), channel_id=1, source_target_pairs={{0,3},{1,2},{2,1},{3,0},{4,7},{5,6},{6,5},{7,4},{8,11},{9,10},{10,... | collective-permute-start | bytes 2359304 | tf_op jit(solution)/shard_map/ppermute | solution.py:545
  238.9 2.8 copy-start.8
  242.0 1.2 collective-permute-start.8
  243.3 3.7 %collective-permute-start.9 = (f32[4,2,2,64]{3,2,0,1:T(2,128)S(1)}, f32[4,2,2,64]{3,2,0,1:T(2,128)S(1)}, u32[]{:S(2)}, u32[]{:S(2)}) collective-permute-start(f32[4,2,2,64]{3,2,0,1:T(2,128)S(1)} %copy_add_fusion), channel_id=1, source_target_pairs={{0,8},{4,12},{8,0},{12,4},{16,24},{20,28},{24,16},{28,20},{1,9},{5... | collective-permute-start | bytes 12296 | tf_op jit(solution)/shard_map/ppermute | solution.py:592
  246.9 3.7 %collective-permute-start.10 = (f32[4,2,2,64]{3,2,0,1:T(2,128)S(1)}, f32[4,2,2,64]{3,2,0,1:T(2,128)S(1)}, u32[]{:S(2)}, u32[]{:S(2)}) collective-permute-start(f32[4,2,2,64]{3,2,0,1:T(2,128)S(1)} %add.59), channel_id=1, source_target_pairs={{0,16},{4,20},{8,24},{12,28},{16,0},{20,4},{24,8},{28,12},{1,17},{... | collective-permute-start | bytes 12296 | tf_op jit(solution)/shard_map/ppermute | solution.py:592
  250.6 58.6 %collective-permute-start.13 = (f32[4,2,2,64]{3,2,0,1:T(2,128)S(1)}, f32[4,2,2,64]{3,2,0,1:T(2,128)S(1)}, u32[]{:S(2)}, u32[]{:S(2)}) collective-permute-start(f32[4,2,2,64]{3,2,0,1:T(2,128)S(1)} %add.60), channel_id=1, source_target_pairs={{0,3},{1,2},{2,1},{3,0},{4,7},{5,6},{6,5},{7,4},{8,11},{9,10},{10,... | collective-permute-start | bytes 12296 | tf_op jit(solution)/shard_map/ppermute | solution.py:545
  251.8 57.4 %collective-permute-start.12 = (f32[4,2,2,64]{3,2,0,1:T(2,128)S(1)}, f32[4,2,2,64]{3,2,0,1:T(2,128)S(1)}, u32[]{:S(2)}, u32[]{:S(2)}) collective-permute-start(f32[4,2,2,64]{3,2,0,1:T(2,128)S(1)} %add.60), channel_id=1, source_target_pairs={{0,2},{1,3},{2,0},{3,1},{4,6},{5,7},{6,4},{7,5},{8,10},{9,11},{10,... | collective-permute-start | bytes 12296 | tf_op jit(solution)/shard_map/ppermute | solution.py:545
  256.0 53.2 %collective-permute-start.11 = (f32[4,2,2,64]{3,2,0,1:T(2,128)S(1)}, f32[4,2,2,64]{3,2,0,1:T(2,128)S(1)}, u32[]{:S(2)}, u32[]{:S(2)}) collective-permute-start(f32[4,2,2,64]{3,2,0,1:T(2,128)S(1)} %add.60), channel_id=1, source_target_pairs={{0,1},{1,0},{2,3},{3,2},{4,5},{5,4},{6,7},{7,6},{8,9},{9,8},{10,11... | collective-permute-start | bytes 12296 | tf_op jit(solution)/shard_map/ppermute | solution.py:545
  256.0 1.1 copy-start.1

commit v15 on v14

--- a/solution.py
+++ b/solution.py
@@ -238,15 +238,20 @@
     wait_all(away)
 
 
-def gather_kernel(field_hbm, out_hbm, sems):
+def gather_kernel(field_hbm, out_hbm, buffer_ref, in_sems, out_sems):
     count, pairs = out_hbm.shape[:2]
     split = field_hbm.shape[2]
-    copies = []
+    loads, stores = [], []
     for x in range(count):
         for pair in range(pairs):
-            source = field_hbm.at[x // split, pair, x % split]
-            copies.append(pltpu.make_async_copy(source, out_hbm.at[x, pair], sems.at[x * pairs + pair]))
-    wait_all(start_all(copies))
+            source, number = field_hbm.at[x // split, pair, x % split], x * pairs + pair
+            loads.append(pltpu.make_async_copy(source, buffer_ref.at[x, pair], in_sems.at[number]))
+            stores.append(pltpu.make_async_copy(buffer_ref.at[x, pair], out_hbm.at[x, pair], out_sems.at[number]))
+    start_all(loads)
+    for load, store in zip(loads, stores):
+        load.wait()
+        store.start()
+    wait_all(stores)
 
 
 def gather_lines(field, count, pairs):
@@ -257,7 +262,12 @@
         out_shape=jax.ShapeDtypeStruct(shape, jnp.float32),
         in_specs=[anywhere],
         out_specs=anywhere,
-        scratch_shapes=[pltpu.SemaphoreType.DMA((count * pairs,))],
+        scratch_shapes=[
+            pltpu.VMEM(shape, jnp.float32),
+            pltpu.SemaphoreType.DMA((count * pairs,)),
+            pltpu.SemaphoreType.DMA((count * pairs,)),
+        ],
+        compiler_params=pltpu.CompilerParams(vmem_limit_bytes=FILTER_VMEM),
         cost_estimate=pl.CostEstimate(flops=0, bytes_accessed=8 * math.prod(shape), transcendentals=0),
         name="gather_lines",
     )(field)

time: 311 us -> 218 us (0.70)
  Pallas kernels: 136 us -> 42.4 us
    pallas_call x1, Pallas kernels: 96.5 us -> 3.18 us  [gather_lines(): pl.pallas_call(gather_kernel, out_shape=jax.ShapeDtypeStruct(shape, jnp.f...]
  transfers between devices with their start and end apart: 16 -> 16, of which waited for: 9 -> 9; matrix products, arithmetic and copies ran while one was open for 2% -> 3% of each run, Pallas kernels for 13% -> 18%
where the time goes in v15:
time: 218 us; the launch traced here: 217 us
  waiting for transfers between devices  132 us (61%)
  Pallas kernels  42.4 us (19%)
  starting transfers between devices  30.8 us (14%)
  local copies, waits for them, and re-layouts  9.8 us (4%)
    ppermute x9, waiting for transfers between devices, swap(): lax.ppermute(blocks[x], 'span', pairs[x])  59.9 us
    all_to_all x2, waiting for transfers between devices, exchange(): return lax.all_to_all(lines, 'span', split_axis=0, concat_axis=0)  46.4 us
    ppermute x1, waiting for transfers between devices, on_device(): high = lax.ppermute(field[:, :, :, :PAD], 'wall', backward)  18.9 us
    pallas_call x1, Pallas kernels, local_terms(): pl.pallas_call(local_kernel, grid=(mode_count,), out_shape=jax.ShapeDtype...  15 us
    ppermute x9, starting transfers between devices, swap(): lax.ppermute(blocks[x], 'span', pairs[x])  12.5 us
    all_to_all x2, starting transfers between devices, exchange(): return lax.all_to_all(lines, 'span', split_axis=0, concat_axis=0)  11.9 us
    pallas_call x1, Pallas kernels, filter_rest(): return call(spots, tables, lines, field, *received)  9.16 us
    pallas_call x3, Pallas kernels, add_rest(): pl.pallas_call(functools.partial(add_rest_kernel, pieces, partners), out_...  6.97 us
  transfers between devices with their start and end apart: 16, of which 9 were waited for; matrix products, arithmetic and copies ran while one was open for 3% of the time, Pallas kernels for 18%

profile of v15, /device:TPU:10, one launch (start us, length us, event | category | flops | bytes accessed | tf_op | source)
XLA Modules:
  0.0 216.5 jit_solution(10636073077301536463)
XLA Ops:
  0.6 3.2 %gather_lines.1 = f32[4,4,4,8,1536]{4,3,2,1,0:T(8,128)} custom-call(f32[4,6,1,4,8,1536]{5,4,3,2,1,0:T(8,128)} %bitcast.27), custom_call_target="tpu_custom_call" | custom-call | bytes 6291456 | tf_op jit(solution)/shard_map/gather_lines/pallas_call | solution.py:260
  3.8 5.3 %all-to-all-start = ((f32[4,4,4,8,1536]{4,3,2,1,0:T(8,128)}), f32[4,4,4,8,1536]{4,3,2,1,0:T(8,128)}, u32[]{:S(2)}, u32[]{:S(2)}) async-start(f32[4,4,4,8,1536]{4,3,2,1,0:T(8,128)} %gather_lines.1), calls=%async_computation | async-start | bytes 6291456 | tf_op jit(solution)/shard_map/all_to_all | solution.py:552
  9.1 0.0 copy-start.9
  9.1 0.0 copy-start.3
  9.1 0.0 copy-start.2
  9.2 2.9 %fusion.6 = (f32[4,3,2,8,1536]{4,3,2,1,0:T(8,128)}, f32[4,3,2,8,1536]{4,3,2,1,0:T(8,128)S(1)}) fusion(f32[4,3,2,32,1536]{4,3,2,1,0:T(8,128)} %field_ref.1), kind=kLoop, calls=%fused_computation.16 | loop fusion | bytes 4718592 | tf_op jit(solution)/shard_map/slice | solution.py:569
  12.0 1.9 collective-permute-start.1
  14.0 2.4 %collective-permute-start = (f32[4,3,2,8,1536]{4,3,2,1,0:T(8,128)S(1)}, f32[4,3,2,8,1536]{4,3,2,1,0:T(8,128)S(1)}, u32[]{:S(2)}, u32[]{:S(2)}) collective-permute-start(f32[4,3,2,8,1536]{4,3,2,1,0:T(8,128)S(1)} %get-tuple-element.28), channel_id=1, source_target_pairs={{0,4},{4,8},{8,12},{12,16},{16,20},{20,24},{24,28},{1,5},{5,9},{9,... | collective-permute-start | bytes 3538952 | tf_op jit(solution)/shard_map/ppermute | solution.py:568
  16.4 0.0 copy-done.9
  16.4 2.3 %dynamic-slice_bitcast_fusion = (f32[2,4,8,1536]{3,2,1,0:T(8,128)}, f32[2,4,8,1536]{3,2,1,0:T(8,128)}, f32[2,4,8,1536]{3,2,1,0:T(8,128)}) fusion(f32[4,6,1,4,8,1536]{5,4,3,2,1,0:T(8,128)} %bitcast.28, s32[]{:T(128)S(6)} %select_n.72, s32[]{:T(128)S(6)} %select_n.71, s32[]{:T(128)S(6)} %select_n.70), kind=kLoop, calls=%fused_computation.1 | loop fusion | bytes 2359308 | tf_op jit(solution)/shard_map/reshape | solution.py:580
  18.7 18.9 %collective-permute-done.1.high_ref = f32[4,3,2,8,1536]{4,3,2,1,0:T(8,128)S(1)} collective-permute-done((f32[4,3,2,8,1536]{4,3,2,1,0:T(8,128)}, f32[4,3,2,8,1536]{4,3,2,1,0:T(8,128)S(1)}, u32[]{:S(2)}, u32[]{:S(2)}) %collective-permute-start.1) | collective-permute-done | bytes 1179680 | tf_op jit(solution)/shard_map/ppermute | solution.py:569
  37.6 0.0 collective-permute-done.low_ref
  37.6 0.0 copy-done.3
  37.6 0.1 broadcast_in_dim.46.flow_ref
  37.7 0.0 copy-done.2
  37.7 0.1 broadcast_in_dim.45.coef_ref
  37.8 0.0 copy-start
  37.8 2.3 %copy-done = f32[4,3,2,32,1536]{4,3,2,1,0:T(8,128)S(1)} copy-done((f32[4,3,2,32,1536]{4,3,2,1,0:T(8,128)S(1)}, f32[4,3,2,32,1536]{4,3,2,1,0:T(8,128)}, u32[]{:S(2)}) %copy-start) | copy-done | bytes 4718616
  40.1 0.0 copy-start.4
  40.2 15.0 %local_terms.1 = f32[4,3,2,32,1536]{4,3,2,1,0:T(8,128)} custom-call(f32[4]{0:T(128)S(1)} %convert_multiply_fusion.rate_ref, f32[15,32,128]{2,1,0:T(8,128)S(1)} %broadcast_in_dim.45.coef_ref, f32[2,32,128]{2,1,0:T(8,128)S(1)} %broadcast_in_dim.46.flow_ref, f32[4,3,2,32,1536]{4,3,2,1,0:T(8,128)S(1)} %copy-done, ...), custom_call_target="tpu_custom_call" | custom-call | flops 47185920 | bytes 11796480 | tf_op jit(solution)/shard_map/local_terms/pallas_call | solution.py:410
  55.1 0.0 collective-permute-start.2
  55.1 2.9 %collective-permute-start.3 = (f32[2,4,8,1536]{3,2,1,0:T(8,128)}, f32[2,4,8,1536]{3,2,1,0:T(8,128)S(1)}, u32[]{:S(2)}, u32[]{:S(2)}) collective-permute-start(f32[2,4,8,1536]{3,2,1,0:T(8,128)} %get-tuple-element.17), channel_id=1, source_target_pairs={{0,2},{1,3},{2,0},{3,1},{4,6},{5,7},{6,4},{7,5},{8,10},{9,11},{10,... | collective-permute-start | bytes 1179656 | tf_op jit(solution)/shard_map/ppermute | solution.py:555
  58.0 0.6 collective-permute-start.4
  58.6 0.0 copy-done.4
  58.6 0.1 rev.3
  58.7 36.2 %all-to-all-done.lines_hbm = f32[4,4,4,8,1536]{4,3,2,1,0:T(8,128)} async-done(((f32[4,4,4,8,1536]{4,3,2,1,0:T(8,128)}), f32[4,4,4,8,1536]{4,3,2,1,0:T(8,128)}, u32[]{:S(2)}, u32[]{:S(2)}) %all-to-all-start) | async-done | bytes 3145760 | tf_op jit(solution)/shard_map/all_to_all | solution.py:552
  94.9 5.3 %filter_first.1 = f32[4,4,2,8,1536]{4,3,2,1,0:T(8,128)} custom-call(bf16[24,2,256,256]{3,2,1,0:T(8,128)(2,1)} %constant.92.clone.table_hbm, f32[4,4,4,8,1536]{4,3,2,1,0:T(8,128)} %all-to-all-done.lines_hbm), custom_call_target="tpu_custom_call" | custom-call | flops 1000000 | tf_op jit(solution)/shard_map/filter_first/pallas_call | solution.py:358
  100.3 6.6 %all-to-all-start.1 = ((f32[4,4,2,8,1536]{4,3,2,1,0:T(8,128)}), f32[4,4,2,8,1536]{4,3,2,1,0:T(8,128)S(1)}, u32[]{:S(2)}, u32[]{:S(2)}) async-start(f32[4,4,2,8,1536]{4,3,2,1,0:T(8,128)} %filter_first.1), calls=%async_computation.1 | async-start | bytes 3145728 | tf_op jit(solution)/shard_map/all_to_all | solution.py:552
  106.8 0.0 collective-permute-done.2.refs_0_
  106.8 0.0 collective-permute-done.3.refs_1_
  106.8 0.0 copy-start.6
  106.9 14.8 %collective-permute-done.4.refs_2_ = f32[2,4,8,1536]{3,2,1,0:T(8,128)S(1)} collective-permute-done((f32[2,4,8,1536]{3,2,1,0:T(8,128)}, f32[2,4,8,1536]{3,2,1,0:T(8,128)S(1)}, u32[]{:S(2)}, u32[]{:S(2)}) %collective-permute-start.4) | collective-permute-done | bytes 393248 | tf_op jit(solution)/shard_map/ppermute | solution.py:555
  121.7 0.0 copy-done.5
  121.7 0.0 copy-done.6
  121.7 0.8 copy-done.7
  122.4 9.2 %filter_rest.1 = (f32[16,8,1536]{2,1,0:T(8,128)}, f32[16,8,1536]{2,1,0:T(8,128)}, f32[16,8,1536]{2,1,0:T(8,128)}, f32[16,8,1536]{2,1,0:T(8,128)}) custom-call(s32[1]{0:T(128)} %bitcast.me_ref, bf16[24,2,256,256]{3,2,1,0:T(8,128)(2,1)} %constant.92.clone.table_hbm, f32[4,4,4,8,1536]{4,3,2,1,0:T(8,128)} %all-to-all-done.lines_hbm, ...), custom_call_target="tpu_custom_call" | custom-call | flops 99999997952 | tf_op jit(solution)/shard_map/filter_rest/pallas_call | solution.py:370
  131.6 0.1 collective-permute-start.5
  131.7 1.1 collective-permute-start.6
  132.8 2.4 %collective-permute-start.7 = (f32[16,8,1536]{2,1,0:T(8,128)}, f32[16,8,1536]{2,1,0:T(8,128)S(1)}, u32[]{:S(2)}, u32[]{:S(2)}) collective-permute-start(f32[16,8,1536]{2,1,0:T(8,128)} %get-tuple-element.22), channel_id=1, source_target_pairs={{0,3},{1,2},{2,1},{3,0},{4,7},{5,6},{6,5},{7,4},{8,11},{9,10},{10,... | collective-permute-start | bytes 2359304 | tf_op jit(solution)/shard_map/ppermute | solution.py:555
  135.2 10.2 %all-to-all-done.1.term_hbm = f32[4,4,2,8,1536]{4,3,2,1,0:T(8,128)S(1)} async-done(((f32[4,4,2,8,1536]{4,3,2,1,0:T(8,128)}), f32[4,4,2,8,1536]{4,3,2,1,0:T(8,128)S(1)}, u32[]{:S(2)}, u32[]{:S(2)}) %all-to-all-start.1) | async-done | bytes 1572896 | tf_op jit(solution)/shard_map/all_to_all | solution.py:552
  145.4 0.1 broadcast_in_dim.50.weight_ref
  145.5 2.8 %add_first.1 = (f32[4,6,1,4,8,1536]{5,4,3,2,1,0:T(8,128)}, f32[4,4,1536]{2,1,0:T(4,128)S(1)}) custom-call(s32[1]{0:T(128)} %bitcast.me_ref, f32[4,6,1,4,8,1536]{5,4,3,2,1,0:T(8,128)} %bitcast.30, f32[4,2,8,128]{3,2,1,0:T(8,128)S(1)} %broadcast_in_dim.50.weight_ref, f32[4,4,2,8,1536]{4,3,2,1,0:T(8,128)S(1)} %all-to-all-done.1.term_hbm), custom_call_target="tpu_custom_call", output_to_operand_aliasing={{0}: (1, {})} | custom-call | flops 393216 | bytes 4718592 | tf_op jit(solution)/shard_map/add_first/pallas_call | solution.py:459
  148.3 0.0 copy-done.8
  148.3 0.3 fusion.1
  148.7 0.1 collective-permute-start.8
  148.7 1.2 collective-permute-done.8
  149.9 0.5 collective-permute-start.9
  150.4 3.2 %collective-permute-done.9 = f32[4,2,2,64]{3,2,0,1:T(2,128)S(1)} collective-permute-done((f32[4,2,2,64]{3,2,0,1:T(2,128)S(1)}, f32[4,2,2,64]{3,2,0,1:T(2,128)S(1)}, u32[]{:S(2)}, u32[]{:S(2)}) %collective-permute-start.9) | collective-permute-done | bytes 4128 | tf_op jit(solution)/shard_map/ppermute | solution.py:602
  153.6 1.5 collective-permute-start.10
  155.1 2.1 collective-permute-done.10
  157.2 1.2 collective-permute-start.13
  158.4 4.2 %collective-permute-start.12 = (f32[4,2,2,64]{3,2,0,1:T(2,128)S(1)}, f32[4,2,2,64]{3,2,0,1:T(2,128)S(1)}, u32[]{:S(2)}, u32[]{:S(2)}) collective-permute-start(f32[4,2,2,64]{3,2,0,1:T(2,128)S(1)} %add.60), channel_id=1, source_target_pairs={{0,2},{1,3},{2,0},{3,1},{4,6},{5,7},{6,4},{7,5},{8,10},{9,11},{10,... | collective-permute-start | bytes 12296 | tf_op jit(solution)/shard_map/ppermute | solution.py:555
  162.6 0.0 collective-permute-done.5.refs_1_
  162.6 0.0 collective-permute-start.11
  162.6 1.1 copy-done.1
  163.8 3.0 %add_rest.3.base_hbm = f32[4,6,1,4,8,1536]{5,4,3,2,1,0:T(8,128)} custom-call(s32[1]{0:T(128)} %bitcast.me_ref, f32[4,6,1,4,8,1536]{5,4,3,2,1,0:T(8,128)} %get-tuple-element.14.base_hbm, f32[16,8,1536]{2,1,0:T(8,128)S(1)} %copy-done.1, f32[16,8,1536]{2,1,0:T(8,128)} %collective-permute-done.5.refs_1_), custom_call_target="tpu_custom_call", output_to_operand_aliasing={{}: (1, {})} | custom-call | flops 393216 | bytes 4718592 | tf_op jit(solution)/shard_map/add_rest/pallas_call | solution.py:516
  166.7 29.7 %collective-permute-done.6.refs_0_ = f32[16,8,1536]{2,1,0:T(8,128)S(1)} collective-permute-done((f32[16,8,1536]{2,1,0:T(8,128)}, f32[16,8,1536]{2,1,0:T(8,128)S(1)}, u32[]{:S(2)}, u32[]{:S(2)}) %collective-permute-start.6) | collective-permute-done | bytes 786464 | tf_op jit(solution)/shard_map/ppermute | solution.py:555
  196.4 2.0 add_rest.4.base_hbm
  198.4 15.4 %collective-permute-done.7.refs_0_ = f32[16,8,1536]{2,1,0:T(8,128)S(1)} collective-permute-done((f32[16,8,1536]{2,1,0:T(8,128)}, f32[16,8,1536]{2,1,0:T(8,128)S(1)}, u32[]{:S(2)}, u32[]{:S(2)}) %collective-permute-start.7) | collective-permute-done | bytes 786464 | tf_op jit(solution)/shard_map/ppermute | solution.py:555
  213.8 2.0 add_rest.5
  215.8 0.0 collective-permute-done.13
  215.8 0.0 collective-permute-done.12
  215.9 0.0 collective-permute-done.11
  215.9 0.6 add_bitcast_fusion
  (15 shorter events, 0.1 us)
Async XLA Ops:
  3.8 91.1 %all-to-all-start = ((f32[4,4,4,8,1536]{4,3,2,1,0:T(8,128)}), f32[4,4,4,8,1536]{4,3,2,1,0:T(8,128)}, u32[]{:S(2)}, u32[]{:S(2)}) async-start(f32[4,4,4,8,1536]{4,3,2,1,0:T(8,128)} %gather_lines.1), calls=%async_computation | async-start | bytes 6291456 | tf_op jit(solution)/shard_map/all_to_all | solution.py:552
  9.1 7.3 %copy-start.9 = (s32[4]{0:T(128)S(1)}, s32[4]{0:T(128)}, u32[]{:S(2)}) copy-start(s32[4]{0:T(128)} %param.11) | copy-start | bytes 52
  9.1 28.5 %copy-start.3 = (f32[2,32]{1,0:T(2,128)S(1)}, f32[2,32]{1,0:T(2,128)}, u32[]{:S(2)}) copy-start(f32[2,32]{1,0:T(2,128)} %param.8) | copy-start | bytes 772
  9.1 28.5 %copy-start.2 = (f32[15,32]{1,0:T(8,128)S(1)}, f32[15,32]{1,0:T(8,128)}, u32[]{:S(2)}) copy-start(f32[15,32]{1,0:T(8,128)} %param.9) | copy-start | bytes 5764
  12.0 25.6 %collective-permute-start.1 = (f32[4,3,2,8,1536]{4,3,2,1,0:T(8,128)}, f32[4,3,2,8,1536]{4,3,2,1,0:T(8,128)S(1)}, u32[]{:S(2)}, u32[]{:S(2)}) collective-permute-start(f32[4,3,2,8,1536]{4,3,2,1,0:T(8,128)} %get-tuple-element.27), channel_id=1, source_target_pairs={{4,0},{8,4},{12,8},{16,12},{20,16},{24,20},{28,24},{5,1},{9,5},{13... | collective-permute-start | bytes 3538952 | tf_op jit(solution)/shard_map/ppermute | solution.py:569
  14.0 23.6 %collective-permute-start = (f32[4,3,2,8,1536]{4,3,2,1,0:T(8,128)S(1)}, f32[4,3,2,8,1536]{4,3,2,1,0:T(8,128)S(1)}, u32[]{:S(2)}, u32[]{:S(2)}) collective-permute-start(f32[4,3,2,8,1536]{4,3,2,1,0:T(8,128)S(1)} %get-tuple-element.28), channel_id=1, source_target_pairs={{0,4},{4,8},{8,12},{12,16},{16,20},{20,24},{24,28},{1,5},{5,9},{9,... | collective-permute-start | bytes 3538952 | tf_op jit(solution)/shard_map/ppermute | solution.py:568
  37.8 2.3 %copy-start = (f32[4,3,2,32,1536]{4,3,2,1,0:T(8,128)S(1)}, f32[4,3,2,32,1536]{4,3,2,1,0:T(8,128)}, u32[]{:S(2)}) copy-start(f32[4,3,2,32,1536]{4,3,2,1,0:T(8,128)} %field_ref.1) | copy-start | bytes 14155780
  40.1 18.5 %copy-start.4 = (f32[2,8]{1,0:T(2,128)S(1)}, f32[2,8]{1,0:T(2,128)}, u32[]{:S(2)}) copy-start(f32[2,8]{1,0:T(2,128)} %param.10) | copy-start | bytes 196
  55.1 51.7 %collective-permute-start.2 = (f32[2,4,8,1536]{3,2,1,0:T(8,128)}, f32[2,4,8,1536]{3,2,1,0:T(8,128)S(1)}, u32[]{:S(2)}, u32[]{:S(2)}) collective-permute-start(f32[2,4,8,1536]{3,2,1,0:T(8,128)} %get-tuple-element.15), channel_id=1, source_target_pairs={{0,1},{1,0},{2,3},{3,2},{4,5},{5,4},{6,7},{7,6},{8,9},{9,8},{10,11... | collective-permute-start | bytes 1179656 | tf_op jit(solution)/shard_map/ppermute | solution.py:555
  55.1 51.7 %collective-permute-start.3 = (f32[2,4,8,1536]{3,2,1,0:T(8,128)}, f32[2,4,8,1536]{3,2,1,0:T(8,128)S(1)}, u32[]{:S(2)}, u32[]{:S(2)}) collective-permute-start(f32[2,4,8,1536]{3,2,1,0:T(8,128)} %get-tuple-element.17), channel_id=1, source_target_pairs={{0,2},{1,3},{2,0},{3,1},{4,6},{5,7},{6,4},{7,5},{8,10},{9,11},{10,... | collective-permute-start | bytes 1179656 | tf_op jit(solution)/shard_map/ppermute | solution.py:555
  58.0 63.6 %collective-permute-start.4 = (f32[2,4,8,1536]{3,2,1,0:T(8,128)}, f32[2,4,8,1536]{3,2,1,0:T(8,128)S(1)}, u32[]{:S(2)}, u32[]{:S(2)}) collective-permute-start(f32[2,4,8,1536]{3,2,1,0:T(8,128)} %get-tuple-element.18), channel_id=1, source_target_pairs={{0,3},{1,2},{2,1},{3,0},{4,7},{5,6},{6,5},{7,4},{8,11},{9,10},{10,... | collective-permute-start | bytes 1179656 | tf_op jit(solution)/shard_map/ppermute | solution.py:555
  100.3 45.2 %all-to-all-start.1 = ((f32[4,4,2,8,1536]{4,3,2,1,0:T(8,128)}), f32[4,4,2,8,1536]{4,3,2,1,0:T(8,128)S(1)}, u32[]{:S(2)}, u32[]{:S(2)}) async-start(f32[4,4,2,8,1536]{4,3,2,1,0:T(8,128)} %filter_first.1), calls=%async_computation.1 | async-start | bytes 3145728 | tf_op jit(solution)/shard_map/all_to_all | solution.py:552
  106.8 14.8 %copy-start.5 = (f32[2,4,8,1536]{3,2,1,0:T(8,128)}, f32[2,4,8,1536]{3,2,1,0:T(8,128)S(1)}, u32[]{:S(2)}) copy-start(f32[2,4,8,1536]{3,2,1,0:T(8,128)S(1)} %collective-permute-done.2.refs_0_) | copy-start | bytes 1179652
  106.8 14.8 %copy-start.6 = (f32[2,4,8,1536]{3,2,1,0:T(8,128)}, f32[2,4,8,1536]{3,2,1,0:T(8,128)S(1)}, u32[]{:S(2)}) copy-start(f32[2,4,8,1536]{3,2,1,0:T(8,128)S(1)} %collective-permute-done.3.refs_1_) | copy-start | bytes 1179652
  121.7 0.8 copy-start.7
  131.6 31.0 %collective-permute-start.5 = (f32[16,8,1536]{2,1,0:T(8,128)}, f32[16,8,1536]{2,1,0:T(8,128)}, u32[]{:S(2)}, u32[]{:S(2)}) collective-permute-start(f32[16,8,1536]{2,1,0:T(8,128)} %get-tuple-element.20), channel_id=1, source_target_pairs={{0,1},{1,0},{2,3},{3,2},{4,5},{5,4},{6,7},{7,6},{8,9},{9,8},{10,11... | collective-permute-start | bytes 2359304 | tf_op jit(solution)/shard_map/ppermute | solution.py:555
  131.7 64.7 %collective-permute-start.6 = (f32[16,8,1536]{2,1,0:T(8,128)}, f32[16,8,1536]{2,1,0:T(8,128)S(1)}, u32[]{:S(2)}, u32[]{:S(2)}) collective-permute-start(f32[16,8,1536]{2,1,0:T(8,128)} %get-tuple-element.21), channel_id=1, source_target_pairs={{0,2},{1,3},{2,0},{3,1},{4,6},{5,7},{6,4},{7,5},{8,10},{9,11},{10,... | collective-permute-start | bytes 2359304 | tf_op jit(solution)/shard_map/ppermute | solution.py:555
  132.8 81.0 %collective-permute-start.7 = (f32[16,8,1536]{2,1,0:T(8,128)}, f32[16,8,1536]{2,1,0:T(8,128)S(1)}, u32[]{:S(2)}, u32[]{:S(2)}) collective-permute-start(f32[16,8,1536]{2,1,0:T(8,128)} %get-tuple-element.22), channel_id=1, source_target_pairs={{0,3},{1,2},{2,1},{3,0},{4,7},{5,6},{6,5},{7,4},{8,11},{9,10},{10,... | collective-permute-start | bytes 2359304 | tf_op jit(solution)/shard_map/ppermute | solution.py:555
  145.5 2.8 %copy-start.8 = (s32[1536]{0:T(1024)S(1)}, s32[1536]{0:T(1024)}, u32[]{:S(2)}) copy-start(s32[1536]{0:T(1024)} %param.12) | copy-start | bytes 18436
  148.7 1.2 collective-permute-start.8
  149.9 3.7 %collective-permute-start.9 = (f32[4,2,2,64]{3,2,0,1:T(2,128)S(1)}, f32[4,2,2,64]{3,2,0,1:T(2,128)S(1)}, u32[]{:S(2)}, u32[]{:S(2)}) collective-permute-start(f32[4,2,2,64]{3,2,0,1:T(2,128)S(1)} %copy_add_fusion), channel_id=1, source_target_pairs={{0,8},{4,12},{8,0},{12,4},{16,24},{20,28},{24,16},{28,20},{1,9},{5... | collective-permute-start | bytes 12296 | tf_op jit(solution)/shard_map/ppermute | solution.py:602
  153.6 3.7 %collective-permute-start.10 = (f32[4,2,2,64]{3,2,0,1:T(2,128)S(1)}, f32[4,2,2,64]{3,2,0,1:T(2,128)S(1)}, u32[]{:S(2)}, u32[]{:S(2)}) collective-permute-start(f32[4,2,2,64]{3,2,0,1:T(2,128)S(1)} %add.59), channel_id=1, source_target_pairs={{0,16},{4,20},{8,24},{12,28},{16,0},{20,4},{24,8},{28,12},{1,17},{... | collective-permute-start | bytes 12296 | tf_op jit(solution)/shard_map/ppermute | solution.py:602
  157.2 58.6 %collective-permute-start.13 = (f32[4,2,2,64]{3,2,0,1:T(2,128)S(1)}, f32[4,2,2,64]{3,2,0,1:T(2,128)S(1)}, u32[]{:S(2)}, u32[]{:S(2)}) collective-permute-start(f32[4,2,2,64]{3,2,0,1:T(2,128)S(1)} %add.60), channel_id=1, source_target_pairs={{0,3},{1,2},{2,1},{3,0},{4,7},{5,6},{6,5},{7,4},{8,11},{9,10},{10,... | collective-permute-start | bytes 12296 | tf_op jit(solution)/shard_map/ppermute | solution.py:555
  158.4 57.4 %collective-permute-start.12 = (f32[4,2,2,64]{3,2,0,1:T(2,128)S(1)}, f32[4,2,2,64]{3,2,0,1:T(2,128)S(1)}, u32[]{:S(2)}, u32[]{:S(2)}) collective-permute-start(f32[4,2,2,64]{3,2,0,1:T(2,128)S(1)} %add.60), channel_id=1, source_target_pairs={{0,2},{1,3},{2,0},{3,1},{4,6},{5,7},{6,4},{7,5},{8,10},{9,11},{10,... | collective-permute-start | bytes 12296 | tf_op jit(solution)/shard_map/ppermute | solution.py:555
  162.6 53.2 %collective-permute-start.11 = (f32[4,2,2,64]{3,2,0,1:T(2,128)S(1)}, f32[4,2,2,64]{3,2,0,1:T(2,128)S(1)}, u32[]{:S(2)}, u32[]{:S(2)}) collective-permute-start(f32[4,2,2,64]{3,2,0,1:T(2,128)S(1)} %add.60), channel_id=1, source_target_pairs={{0,1},{1,0},{2,3},{3,2},{4,5},{5,4},{6,7},{7,6},{8,9},{9,8},{10,11... | collective-permute-start | bytes 12296 | tf_op jit(solution)/shard_map/ppermute | solution.py:555
  162.6 1.1 copy-start.1

commit v16 on v13

--- a/solution.py
+++ b/solution.py
@@ -162,8 +162,12 @@
     return piece[1] * piece[3]
 
 
-def piece_at(ref, piece):
-    return ref.at[:, pl.ds(piece[0], piece[1]), pl.ds(piece[2], piece[3])]
+def bring_piece(piece, first_pair, me, field_hbm, received, line_ref, sems, start):
+    count, split = len(received) + 1, field_hbm.shape[2]
+    groups = pl.ds(piece[2], piece[3])
+    sources = [field_hbm.at[me // split, pl.ds(piece[0], piece[1]), me % split, groups]]
+    sources += [block.at[pl.ds(piece[0] - first_pair, piece[1]), groups] for block in received]
+    return [pltpu.make_async_copy(sources[x], line_ref.at[me ^ x], sems.at[start + x]) for x in range(count)]
 
 
 def start_all(copies):
@@ -238,11 +242,11 @@
     wait_all(away)
 
 
-def filter_first_kernel(pieces, table_hbm, lines_hbm, out_hbm, *scratch):
-    *scratch, out_sems = scratch
+def filter_first_kernel(pieces, count, me_ref, table_hbm, field_hbm, *refs):
+    received, out_hbm, scratch, out_sems = refs[: count - 1], refs[count - 1], refs[count:-1], refs[-1]
 
     def bring(i, line_ref, sems):
-        return [pltpu.make_async_copy(piece_at(lines_hbm, pieces[i]), line_ref, sems.at[i])]
+        return bring_piece(pieces[i], 0, me_ref[0], field_hbm, received, line_ref, sems, i * count)
 
     def send(i, line_ref):
         return [pltpu.make_async_copy(line_ref.at[:, :, 0], out_hbm.at[:, i], out_sems.at[i])]
@@ -250,18 +254,14 @@
     run_filter(pieces, table_hbm, bring, send, scratch)
 
 
-def filter_rest_kernel(pieces, me_ref, table_hbm, lines_hbm, field_hbm, *refs):
-    count, split, me = lines_hbm.shape[0], field_hbm.shape[2], me_ref[0]
-    received, sent, scratch, out_sems = refs[: count - 1], refs[count - 1 : 2 * count - 1], refs[2 * count - 1 : -1], refs[-1]
+def filter_rest_kernel(pieces, count, me_ref, table_hbm, field_hbm, *refs):
+    main, tail, sent = refs[: count - 1], refs[count - 1 : 2 * count - 2], refs[2 * count - 2 : 3 * count - 2]
+    scratch, out_sems, me = refs[3 * count - 2 : -1], refs[-1], me_ref[0]
     places = rest_places(pieces)
-    final = len(pieces) - 1
 
     def bring(i, line_ref, sems):
-        if i < final:
-            return [pltpu.make_async_copy(piece_at(lines_hbm, pieces[i]), line_ref, sems.at[i])]
-        own = field_hbm.at[me // split, pl.ds(pieces[i][0], pieces[i][1]), me % split]
-        sources = (own,) + received
-        return [pltpu.make_async_copy(sources[x], line_ref.at[me ^ x], sems.at[i + x]) for x in range(count)]
+        received, first_pair = (main, 0) if i < len(pieces) - 1 else (tail, pieces[i][0])
+        return bring_piece(pieces[i], first_pair, me, field_hbm, received, line_ref, sems, i * count)
 
     def send(i, line_ref):
         copies = []
@@ -291,48 +291,44 @@
 WHOLE = pl.BlockSpec(memory_space=pltpu.VMEM)
 
 
-def filter_call(kernel, name, pieces, lines, tables, in_specs, out_specs, out_shape, sems, flops):
-    count, _, _, _, width = lines.shape
+def filter_call(kernel, name, pieces, field, received, spots, tables, out_shape, out_sems, flops):
+    count, width = field.shape[0] * field.shape[2], field.shape[5]
     rows = sum(map(group_count, pieces)) * PAD
     return pl.pallas_call(
-        functools.partial(kernel, pieces),
+        functools.partial(kernel, pieces, count),
         out_shape=out_shape,
-        in_specs=in_specs,
-        out_specs=out_specs,
+        in_specs=[SCALARS] + [HBM] * (2 + len(received)),
+        out_specs=[HBM] * len(out_shape),
         scratch_shapes=[pltpu.VMEM((count, piece[1], piece[3], PAD, width), jnp.float32) for piece in pieces]
         + [
             pltpu.VMEM((TILES, rows, 2 * LANES), jnp.float32),
             pltpu.VMEM(tables.shape, tables.dtype),
             pltpu.SemaphoreType.DMA((TABLE_COPIES,)),
-            pltpu.SemaphoreType.DMA((sems[0],)),
-            pltpu.SemaphoreType.DMA((sems[1],)),
+            pltpu.SemaphoreType.DMA((len(pieces) * count,)),
+            pltpu.SemaphoreType.DMA((out_sems,)),
         ],
         compiler_params=pltpu.CompilerParams(vmem_limit_bytes=FILTER_VMEM),
         cost_estimate=pl.CostEstimate(flops=flops, bytes_accessed=0, transcendentals=0),
         name=name,
+    )(spots, tables, field, *received)
+
+
+def filter_first(field, main, spots, tables, pieces):
+    out_shape = [jax.ShapeDtypeStruct((len(main) + 1, len(pieces), 2, PAD, field.shape[5]), jnp.float32)]
+    return filter_call(
+        filter_first_kernel, "filter_first", pieces, field, main, spots, tables, out_shape, len(pieces), 10**6
+    )[0]
+
+
+def filter_rest(field, main, tail, spots, tables, pieces):
+    count = len(main) + 1
+    shape = (sum(map(group_count, pieces)), PAD, field.shape[5])
+    out_shape = [jax.ShapeDtypeStruct(shape, jnp.float32)] * count
+    sems = count * sum(piece[1] for piece in pieces)
+    received = list(main) + list(tail)
+    return filter_call(
+        filter_rest_kernel, "filter_rest", pieces, field, received, spots, tables, out_shape, sems, 10**11
     )
-
-
-def filter_first(lines, tables, pieces):
-    count, _, _, _, width = lines.shape
-    out_shape = jax.ShapeDtypeStruct((count, len(pieces), 2, PAD, width), jnp.float32)
-    sems = (len(pieces), len(pieces))
-    call = filter_call(
-        filter_first_kernel, "filter_first", pieces, lines, tables, [HBM, HBM], HBM, out_shape, sems, 10**6
-    )
-    return call(tables, lines)
-
-
-def filter_rest(lines, field, received, spots, tables, pieces):
-    count, _, _, _, width = lines.shape
-    shape = (sum(map(group_count, pieces)), PAD, width)
-    out_shape = [jax.ShapeDtypeStruct(shape, jnp.float32)] * count
-    sems = (len(pieces) - 1 + count, count * sum(piece[1] for piece in pieces))
-    ins = [SCALARS] + [HBM] * (count + 2)
-    call = filter_call(
-        filter_rest_kernel, "filter_rest", pieces, lines, tables, ins, [HBM] * count, out_shape, sems, 10**11
-    )
-    return call(spots, tables, lines, field, *received)
 
 
 def local_kernel(rate_ref, coef_ref, flow_ref, field_ref, low_ref, high_ref, out_ref, pad_ref):
@@ -387,7 +383,7 @@
         out_specs=pl.BlockSpec(block, by_mode),
         scratch_shapes=[pltpu.VMEM((comp_count, part_count, row_count + 2 * PAD, width), jnp.float32)],
         compiler_params=pltpu.CompilerParams(vmem_limit_bytes=24 << 20),
-        cost_estimate=pl.CostEstimate(flops=40 * field.size, bytes_accessed=10 * field.size, transcendentals=0),
+        cost_estimate=pl.CostEstimate(flops=10**6, bytes_accessed=0, transcendentals=0),
         name="local_terms",
     )(rate, coef, flow, field, low, high)
 
@@ -523,7 +519,14 @@
     shares = (mode_split, pairs_count, row_split, groups, PAD, width)
     shared = field.reshape(shares)
     last = pairs_count - part_count
-    lines = exchange(shared[:, :last].transpose(0, 2, 1, 3, 4, 5).reshape(span, last, groups, PAD, width))
+
+    def block_of(x, first_pair, pairs_here):
+        other = me ^ x
+        start = (other // row_split, first_pair, other % row_split, 0, 0, 0)
+        block = lax.dynamic_slice(shared, start, (1, pairs_here, 1, groups, PAD, width))
+        return block.reshape(pairs_here, groups, PAD, width)
+
+    main = swap([None] + [block_of(x, 0, last) for x in range(1, span)])
 
     first_pieces = tuple((0, 2, group, 1) for group in range(groups))
     rest_pieces = tuple((2 * comp, 2, 0, groups) for comp in range(1, comp_count))
@@ -538,19 +541,13 @@
     flow = jnp.broadcast_to(mean_flow[:, :, None], (2, row_count, LANES))
     base = local_terms(field, low, high, rate, coef, flow)
 
-    def last_block(x):
-        other = me ^ x
-        start = (other // row_split, last, other % row_split, 0, 0, 0)
-        block = lax.dynamic_slice(shared, start, (1, part_count, 1, groups, PAD, width))
-        return block.reshape(part_count, groups, PAD, width)
-
-    blocks = tuple(last_block(x) for x in range(1, span))
-    received = swap((None,) + lax.optimization_barrier((blocks, base))[0])
-    lines = after(lines, base)
-    filtered = filter_first(lines, tables, first_pieces)
+    blocks = tuple(block_of(x, last, part_count) for x in range(1, span))
+    tail = swap((None,) + lax.optimization_barrier((blocks, base))[0])
+    main[0] = after(main[0], base)
+    filtered = filter_first(shared, main, spots, tables, first_pieces)
     back = exchange(filtered)
-    received[0] = after(received[0], filtered)
-    sent = filter_rest(lines, shared, received, spots, tables, rest_pieces)
+    tail[0] = after(tail[0], filtered)
+    sent = filter_rest(shared, main, tail, spots, tables, rest_pieces)
     returned = [sent[0]] + swap(sent)
 
     lower = jnp.where(wall_index == 0, wall_coef[0], 0.0)

time: 218 us -> 223 us (1.023)
  starting transfers between devices: 30.7 us -> 35.3 us
  local copies, waits for them, and re-layouts: 13.7 us -> 9.4 us
    ppermute x9 -> x12, waiting for transfers between devices: 59.9 us -> 104 us  [swap(): lax.ppermute(blocks[x], 'span', pairs[x])]
    all_to_all x2 -> x1, waiting for transfers between devices: 46.4 us -> 11.6 us  [exchange(): return lax.all_to_all(lines, 'span', split_axis=0, concat_axis=0)]
    ppermute x1, waiting for transfers between devices: 18.9 us -> 12.1 us  [on_device(): high = lax.ppermute(field[:, :, :, :PAD], 'wall', backward)]
    ppermute x3, starting transfers between devices: 2.05 us -> 8.04 us  [on_device(): lax.ppermute(grad, 'wall', [(i, i ^ distance) for i in range(wall_count)])]
    all_to_all x2 -> x1, starting transfers between devices: 11.9 us -> 6.12 us  [exchange(): return lax.all_to_all(lines, 'span', split_axis=0, concat_axis=0)]
    ppermute x9 -> x12, starting transfers between devices: 12.5 us -> 16.6 us  [swap(): lax.ppermute(blocks[x], 'span', pairs[x])]
    another operation x1 -> x0, local copies, waits for them, and re-layouts: 3.85 us -> none  [on_device(): shared[:, :last].transpose(0, 2, 1, 3, 4, 5)]
    unnamed x20, local copies, waits for them, and re-layouts: 4.27 us -> 1.98 us
  transfers between devices with their start and end apart: 16 -> 18, of which waited for: 9 -> 10; matrix products, arithmetic and copies ran while one was open for 3% -> 2% of each run, Pallas kernels for 18% -> 18%
where the time goes in v16:
time: 223 us; the launch traced here: 220 us
  waiting for transfers between devices  133 us (60%)
  Pallas kernels  40.5 us (18%)
  starting transfers between devices  35.3 us (16%)
  local copies, waits for them, and re-layouts  9.4 us (4%)
    ppermute x12, waiting for transfers between devices, swap(): lax.ppermute(blocks[x], 'span', pairs[x])  104 us
    ppermute x12, starting transfers between devices, swap(): lax.ppermute(blocks[x], 'span', pairs[x])  16.6 us
    pallas_call x2, Pallas kernels, filter_call(): pl.pallas_call(functools.partial(kernel, pieces, count), out_shape=out_sh...  15.7 us
    pallas_call x1, Pallas kernels, local_terms(): pl.pallas_call(local_kernel, grid=(mode_count,), out_shape=jax.ShapeDtype...  15.1 us
    ppermute x1, waiting for transfers between devices, on_device(): high = lax.ppermute(field[:, :, :, :PAD], 'wall', backward)  12.1 us
    all_to_all x1, waiting for transfers between devices, exchange(): return lax.all_to_all(lines, 'span', split_axis=0, concat_axis=0)  11.6 us
    ppermute x3, starting transfers between devices, on_device(): lax.ppermute(grad, 'wall', [(i, i ^ distance) for i in range(wall_count)])  8.04 us
    pallas_call x3, Pallas kernels, add_rest(): pl.pallas_call(functools.partial(add_rest_kernel, pieces, partners), out_...  6.97 us
  transfers between devices with their start and end apart: 18, of which 10 were waited for; matrix products, arithmetic and copies ran while one was open for 2% of the time, Pallas kernels for 18%

profile of v16, /device:TPU:10, one launch (start us, length us, event | category | flops | bytes accessed | tf_op | source)
XLA Modules:
  0.0 220.4 jit_solution(16272626904626565922)
XLA Ops:
  0.6 0.0 copy-start.9
  0.6 2.9 %fusion.6 = (f32[4,3,2,8,1536]{4,3,2,1,0:T(8,128)}, f32[4,3,2,8,1536]{4,3,2,1,0:T(8,128)S(1)}) fusion(f32[4,3,2,32,1536]{4,3,2,1,0:T(8,128)} %field_ref.1), kind=kLoop, calls=%fused_computation.19 | loop fusion | bytes 4718592 | tf_op jit(solution)/shard_map/slice | solution.py:537
  3.5 2.0 collective-permute-start.1
  5.5 2.4 %collective-permute-start = (f32[4,3,2,8,1536]{4,3,2,1,0:T(8,128)S(1)}, f32[4,3,2,8,1536]{4,3,2,1,0:T(8,128)S(1)}, u32[]{:S(2)}, u32[]{:S(2)}) collective-permute-start(f32[4,3,2,8,1536]{4,3,2,1,0:T(8,128)S(1)} %get-tuple-element.31), channel_id=1, source_target_pairs={{0,4},{4,8},{8,12},{12,16},{16,20},{20,24},{24,28},{1,5},{5,9},{9,... | collective-permute-start | bytes 3538952 | tf_op jit(solution)/shard_map/ppermute | solution.py:536
  8.0 0.0 copy-start
  8.0 3.1 %dynamic-slice_bitcast_fusion = (f32[4,4,8,1536]{3,2,1,0:T(8,128)}, f32[4,4,8,1536]{3,2,1,0:T(8,128)}, f32[4,4,8,1536]{3,2,1,0:T(8,128)S(1)}) fusion(f32[4,6,1,4,8,1536]{5,4,3,2,1,0:T(8,128)} %bitcast.33, s32[]{:T(128)S(6)} %select_n.87, s32[]{:T(128)S(6)} %select_n.86, s32[]{:T(128)S(6)} %select_n.85), kind=kLoop, calls=%fused_computation | loop fusion | bytes 4718604 | tf_op jit(solution)/shard_map/reshape | solution.py:527
  11.1 0.4 collective-permute-start.2
  11.6 2.7 %collective-permute-start.4 = (f32[4,4,8,1536]{3,2,1,0:T(8,128)}, f32[4,4,8,1536]{3,2,1,0:T(8,128)}, u32[]{:S(2)}, u32[]{:S(2)}) collective-permute-start(f32[4,4,8,1536]{3,2,1,0:T(8,128)} %get-tuple-element.27), channel_id=1, source_target_pairs={{0,3},{1,2},{2,1},{3,0},{4,7},{5,6},{6,5},{7,4},{8,11},{9,10},{10,... | collective-permute-start | bytes 2359304 | tf_op jit(solution)/shard_map/ppermute | solution.py:516
  14.3 1.2 collective-permute-start.3
  15.5 0.0 copy-done.9
  15.5 0.0 copy-done
  15.5 1.1 dynamic-slice_bitcast_fusion.3
  16.6 12.1 %collective-permute-done.1.high_ref = f32[4,3,2,8,1536]{4,3,2,1,0:T(8,128)S(1)} collective-permute-done((f32[4,3,2,8,1536]{4,3,2,1,0:T(8,128)}, f32[4,3,2,8,1536]{4,3,2,1,0:T(8,128)S(1)}, u32[]{:S(2)}, u32[]{:S(2)}) %collective-permute-start.1) | collective-permute-done | bytes 1179680 | tf_op jit(solution)/shard_map/ppermute | solution.py:537
  28.7 0.0 collective-permute-done.low_ref
  28.7 0.0 copy-done.3
  28.7 0.1 broadcast_in_dim.46.flow_ref
  28.7 0.0 copy-done.2
  28.7 0.1 broadcast_in_dim.45.coef_ref
  28.9 0.0 copy-start.4
  28.9 15.1 %local_terms.1 = f32[4,3,2,32,1536]{4,3,2,1,0:T(8,128)} custom-call(f32[4]{0:T(128)S(1)} %convert_multiply_fusion.rate_ref, f32[15,32,128]{2,1,0:T(8,128)S(1)} %broadcast_in_dim.45.coef_ref, f32[2,32,128]{2,1,0:T(8,128)S(1)} %broadcast_in_dim.46.flow_ref, f32[4,3,2,32,1536]{4,3,2,1,0:T(8,128)S(1)} %copy-done, ...), custom_call_target="tpu_custom_call" | custom-call | flops 1000000 | tf_op jit(solution)/shard_map/local_terms/pallas_call | solution.py:371
  43.9 0.4 collective-permute-start.5
  44.4 2.6 %collective-permute-start.6 = (f32[2,4,8,1536]{3,2,1,0:T(8,128)}, f32[2,4,8,1536]{3,2,1,0:T(8,128)S(1)}, u32[]{:S(2)}, u32[]{:S(2)}) collective-permute-start(f32[2,4,8,1536]{3,2,1,0:T(8,128)} %get-tuple-element.17), channel_id=1, source_target_pairs={{0,2},{1,3},{2,0},{3,1},{4,6},{5,7},{6,4},{7,5},{8,10},{9,11},{10,... | collective-permute-start | bytes 1179656 | tf_op jit(solution)/shard_map/ppermute | solution.py:516
  47.0 0.0 collective-permute-done.2.refs_0_
  47.0 0.5 collective-permute-start.7
  47.4 0.0 copy-done.4
  47.4 0.1 rev.3
  47.5 17.7 %collective-permute-done.4.refs_2_ = f32[4,4,8,1536]{3,2,1,0:T(8,128)} collective-permute-done((f32[4,4,8,1536]{3,2,1,0:T(8,128)}, f32[4,4,8,1536]{3,2,1,0:T(8,128)}, u32[]{:S(2)}, u32[]{:S(2)}) %collective-permute-start.4) | collective-permute-done | bytes 786464 | tf_op jit(solution)/shard_map/ppermute | solution.py:516
  65.2 34.0 %collective-permute-done.3.refs_1_ = f32[4,4,8,1536]{3,2,1,0:T(8,128)} collective-permute-done((f32[4,4,8,1536]{3,2,1,0:T(8,128)}, f32[4,4,8,1536]{3,2,1,0:T(8,128)}, u32[]{:S(2)}, u32[]{:S(2)}) %collective-permute-start.3) | collective-permute-done | bytes 786464 | tf_op jit(solution)/shard_map/ppermute | solution.py:516
  99.3 6.5 %filter_first.1 = f32[4,4,2,8,1536]{4,3,2,1,0:T(8,128)} custom-call(s32[1]{0:T(128)} %bitcast.me_ref, bf16[24,2,256,256]{3,2,1,0:T(8,128)(2,1)} %constant.107.clone.table_hbm, f32[4,6,1,4,8,1536]{5,4,3,2,1,0:T(8,128)} %bitcast.34, f32[4,4,8,1536]{3,2,1,0:T(8,128)} %collective-permute-done.2.refs_0_, f32[4,4,8,1536]{3,2,1,0:T(8,128)} %collective-permute-done.3.refs_1_, ...), custom_call_target="tpu_custom_call" | custom-call | flops 1000000 | tf_op jit(solution)/shard_map/filter_first/pallas_call | solution.py:297
  105.8 6.1 %all-to-all-start = ((f32[4,4,2,8,1536]{4,3,2,1,0:T(8,128)}), f32[4,4,2,8,1536]{4,3,2,1,0:T(8,128)S(1)}, u32[]{:S(2)}, u32[]{:S(2)}) async-start(f32[4,4,2,8,1536]{4,3,2,1,0:T(8,128)} %filter_first.1), calls=%async_computation | async-start | bytes 3145728 | tf_op jit(solution)/shard_map/all_to_all | solution.py:513
  111.9 0.0 collective-permute-done.5.refs_3_
  111.9 0.0 collective-permute-done.6.refs_4_
  111.9 0.0 copy-start.6
  111.9 12.7 %collective-permute-done.7.refs_5_ = f32[2,4,8,1536]{3,2,1,0:T(8,128)S(1)} collective-permute-done((f32[2,4,8,1536]{3,2,1,0:T(8,128)}, f32[2,4,8,1536]{3,2,1,0:T(8,128)S(1)}, u32[]{:S(2)}, u32[]{:S(2)}) %collective-permute-start.7) | collective-permute-done | bytes 393248 | tf_op jit(solution)/shard_map/ppermute | solution.py:516
  124.6 0.8 copy-done.7
  125.4 9.2 %filter_rest.1 = (f32[16,8,1536]{2,1,0:T(8,128)}, f32[16,8,1536]{2,1,0:T(8,128)}, f32[16,8,1536]{2,1,0:T(8,128)}, f32[16,8,1536]{2,1,0:T(8,128)}) custom-call(s32[1]{0:T(128)} %bitcast.me_ref, bf16[24,2,256,256]{3,2,1,0:T(8,128)(2,1)} %constant.107.clone.table_hbm, f32[4,6,1,4,8,1536]{5,4,3,2,1,0:T(8,128)} %bitcast.35, ...), custom_call_target="tpu_custom_call" | custom-call | flops 99999997952 | tf_op jit(solution)/shard_map/filter_rest/pallas_call | solution.py:297
  134.6 0.0 copy-start.8
  134.7 0.1 collective-permute-start.8
  134.7 0.1 collective-permute-start.9
  134.8 3.4 %collective-permute-start.10 = (f32[16,8,1536]{2,1,0:T(8,128)}, f32[16,8,1536]{2,1,0:T(8,128)S(1)}, u32[]{:S(2)}, u32[]{:S(2)}) collective-permute-start(f32[16,8,1536]{2,1,0:T(8,128)} %get-tuple-element.22), channel_id=1, source_target_pairs={{0,3},{1,2},{2,1},{3,0},{4,7},{5,6},{6,5},{7,4},{8,11},{9,10},{10,... | collective-permute-start | bytes 2359304 | tf_op jit(solution)/shard_map/ppermute | solution.py:516
  138.2 11.6 %all-to-all-done.term_hbm = f32[4,4,2,8,1536]{4,3,2,1,0:T(8,128)S(1)} async-done(((f32[4,4,2,8,1536]{4,3,2,1,0:T(8,128)}), f32[4,4,2,8,1536]{4,3,2,1,0:T(8,128)S(1)}, u32[]{:S(2)}, u32[]{:S(2)}) %all-to-all-start) | async-done | bytes 1572896 | tf_op jit(solution)/shard_map/all_to_all | solution.py:513
  149.9 0.1 broadcast_in_dim.50.weight_ref
  149.9 2.8 %add_first.1 = (f32[4,6,1,4,8,1536]{5,4,3,2,1,0:T(8,128)}, f32[4,4,1536]{2,1,0:T(4,128)S(1)}) custom-call(s32[1]{0:T(128)} %bitcast.me_ref, f32[4,6,1,4,8,1536]{5,4,3,2,1,0:T(8,128)} %bitcast.37, f32[4,2,8,128]{3,2,1,0:T(8,128)S(1)} %broadcast_in_dim.50.weight_ref, f32[4,4,2,8,1536]{4,3,2,1,0:T(8,128)S(1)} %all-to-all-done.term_hbm), custom_call_target="tpu_custom_call", output_to_operand_aliasing={{0}: (1, {})} | custom-call | flops 393216 | bytes 4718592 | tf_op jit(solution)/shard_map/add_first/pallas_call | solution.py:420
  152.7 0.3 fusion.1
  153.1 1.5 collective-permute-start.11
  154.6 0.8 collective-permute-done.11
  155.4 0.2 collective-permute-start.12
  155.6 3.5 %collective-permute-done.12 = f32[4,2,2,64]{3,2,0,1:T(2,128)S(1)} collective-permute-done((f32[4,2,2,64]{3,2,0,1:T(2,128)S(1)}, f32[4,2,2,64]{3,2,0,1:T(2,128)S(1)}, u32[]{:S(2)}, u32[]{:S(2)}) %collective-permute-start.12) | collective-permute-done | bytes 4128 | tf_op jit(solution)/shard_map/ppermute | solution.py:564
  159.1 6.3 %collective-permute-start.13 = (f32[4,2,2,64]{3,2,0,1:T(2,128)S(1)}, f32[4,2,2,64]{3,2,0,1:T(2,128)S(1)}, u32[]{:S(2)}, u32[]{:S(2)}) collective-permute-start(f32[4,2,2,64]{3,2,0,1:T(2,128)S(1)} %add.68), channel_id=1, source_target_pairs={{0,16},{4,20},{8,24},{12,28},{16,0},{20,4},{24,8},{28,12},{1,17},{... | collective-permute-start | bytes 12296 | tf_op jit(solution)/shard_map/ppermute | solution.py:564
  165.5 1.6 collective-permute-done.13
  167.1 0.0 collective-permute-start.16
  167.1 3.8 %collective-permute-start.15 = (f32[4,2,2,64]{3,2,0,1:T(2,128)S(1)}, f32[4,2,2,64]{3,2,0,1:T(2,128)S(1)}, u32[]{:S(2)}, u32[]{:S(2)}) collective-permute-start(f32[4,2,2,64]{3,2,0,1:T(2,128)S(1)} %add.69), channel_id=1, source_target_pairs={{0,2},{1,3},{2,0},{3,1},{4,6},{5,7},{6,4},{7,5},{8,10},{9,11},{10,... | collective-permute-start | bytes 12296 | tf_op jit(solution)/shard_map/ppermute | solution.py:516
  170.9 0.0 collective-permute-done.8.refs_1_
  170.9 1.4 collective-permute-start.14
  172.3 1.1 copy-done.1
  173.5 3.0 %add_rest.3.base_hbm = f32[4,6,1,4,8,1536]{5,4,3,2,1,0:T(8,128)} custom-call(s32[1]{0:T(128)} %bitcast.me_ref, f32[4,6,1,4,8,1536]{5,4,3,2,1,0:T(8,128)} %get-tuple-element.14.base_hbm, f32[16,8,1536]{2,1,0:T(8,128)S(1)} %copy-done.1, f32[16,8,1536]{2,1,0:T(8,128)} %collective-permute-done.8.refs_1_), custom_call_target="tpu_custom_call", output_to_operand_aliasing={{}: (1, {})} | custom-call | flops 393216 | bytes 4718592 | tf_op jit(solution)/shard_map/add_rest/pallas_call | solution.py:477
  176.4 24.4 %collective-permute-done.9.refs_0_ = f32[16,8,1536]{2,1,0:T(8,128)S(1)} collective-permute-done((f32[16,8,1536]{2,1,0:T(8,128)}, f32[16,8,1536]{2,1,0:T(8,128)S(1)}, u32[]{:S(2)}, u32[]{:S(2)}) %collective-permute-start.9) | collective-permute-done | bytes 786464 | tf_op jit(solution)/shard_map/ppermute | solution.py:516
  200.8 2.0 add_rest.4.base_hbm
  202.8 14.9 %collective-permute-done.10.refs_0_ = f32[16,8,1536]{2,1,0:T(8,128)S(1)} collective-permute-done((f32[16,8,1536]{2,1,0:T(8,128)}, f32[16,8,1536]{2,1,0:T(8,128)S(1)}, u32[]{:S(2)}, u32[]{:S(2)}) %collective-permute-start.10) | collective-permute-done | bytes 786464 | tf_op jit(solution)/shard_map/ppermute | solution.py:516
  217.7 2.0 add_rest.5
  219.7 0.0 collective-permute-done.16
  219.7 0.0 collective-permute-done.15
  219.7 0.0 collective-permute-done.14
  219.8 0.6 add_bitcast_fusion
  (19 shorter events, 0.1 us)
Async XLA Ops:
  0.6 14.9 %copy-start.9 = (s32[4]{0:T(128)S(1)}, s32[4]{0:T(128)}, u32[]{:S(2)}) copy-start(s32[4]{0:T(128)} %param.11) | copy-start | bytes 52
  3.5 25.2 %copy-start.3 = (f32[2,32]{1,0:T(2,128)S(1)}, f32[2,32]{1,0:T(2,128)}, u32[]{:S(2)}) copy-start(f32[2,32]{1,0:T(2,128)} %param.8) | copy-start | bytes 772
  3.5 25.2 %copy-start.2 = (f32[15,32]{1,0:T(8,128)S(1)}, f32[15,32]{1,0:T(8,128)}, u32[]{:S(2)}) copy-start(f32[15,32]{1,0:T(8,128)} %param.9) | copy-start | bytes 5764
  3.5 25.2 %collective-permute-start.1 = (f32[4,3,2,8,1536]{4,3,2,1,0:T(8,128)}, f32[4,3,2,8,1536]{4,3,2,1,0:T(8,128)S(1)}, u32[]{:S(2)}, u32[]{:S(2)}) collective-permute-start(f32[4,3,2,8,1536]{4,3,2,1,0:T(8,128)} %get-tuple-element.30), channel_id=1, source_target_pairs={{4,0},{8,4},{12,8},{16,12},{20,16},{24,20},{28,24},{5,1},{9,5},{13... | collective-permute-start | bytes 3538952 | tf_op jit(solution)/shard_map/ppermute | solution.py:537
  5.5 23.1 %collective-permute-start = (f32[4,3,2,8,1536]{4,3,2,1,0:T(8,128)S(1)}, f32[4,3,2,8,1536]{4,3,2,1,0:T(8,128)S(1)}, u32[]{:S(2)}, u32[]{:S(2)}) collective-permute-start(f32[4,3,2,8,1536]{4,3,2,1,0:T(8,128)S(1)} %get-tuple-element.31), channel_id=1, source_target_pairs={{0,4},{4,8},{8,12},{12,16},{16,20},{20,24},{24,28},{1,5},{5,9},{9,... | collective-permute-start | bytes 3538952 | tf_op jit(solution)/shard_map/ppermute | solution.py:536
  8.0 7.5 %copy-start = (f32[4,3,2,32,1536]{4,3,2,1,0:T(8,128)S(1)}, f32[4,3,2,32,1536]{4,3,2,1,0:T(8,128)}, u32[]{:S(2)}) copy-start(f32[4,3,2,32,1536]{4,3,2,1,0:T(8,128)} %field_ref.1) | copy-start | bytes 14155780
  11.1 35.8 %collective-permute-start.2 = (f32[4,4,8,1536]{3,2,1,0:T(8,128)S(1)}, f32[4,4,8,1536]{3,2,1,0:T(8,128)}, u32[]{:S(2)}, u32[]{:S(2)}) collective-permute-start(f32[4,4,8,1536]{3,2,1,0:T(8,128)S(1)} %get-tuple-element.29), channel_id=1, source_target_pairs={{0,1},{1,0},{2,3},{3,2},{4,5},{5,4},{6,7},{7,6},{8,9},{9,8},{10,11... | collective-permute-start | bytes 2359304 | tf_op jit(solution)/shard_map/ppermute | solution.py:516
  11.6 53.7 %collective-permute-start.4 = (f32[4,4,8,1536]{3,2,1,0:T(8,128)}, f32[4,4,8,1536]{3,2,1,0:T(8,128)}, u32[]{:S(2)}, u32[]{:S(2)}) collective-permute-start(f32[4,4,8,1536]{3,2,1,0:T(8,128)} %get-tuple-element.27), channel_id=1, source_target_pairs={{0,3},{1,2},{2,1},{3,0},{4,7},{5,6},{6,5},{7,4},{8,11},{9,10},{10,... | collective-permute-start | bytes 2359304 | tf_op jit(solution)/shard_map/ppermute | solution.py:516
  14.3 85.0 %collective-permute-start.3 = (f32[4,4,8,1536]{3,2,1,0:T(8,128)}, f32[4,4,8,1536]{3,2,1,0:T(8,128)}, u32[]{:S(2)}, u32[]{:S(2)}) collective-permute-start(f32[4,4,8,1536]{3,2,1,0:T(8,128)} %get-tuple-element.28), channel_id=1, source_target_pairs={{0,2},{1,3},{2,0},{3,1},{4,6},{5,7},{6,4},{7,5},{8,10},{9,11},{10,... | collective-permute-start | bytes 2359304 | tf_op jit(solution)/shard_map/ppermute | solution.py:516
  28.9 18.6 %copy-start.4 = (f32[2,8]{1,0:T(2,128)S(1)}, f32[2,8]{1,0:T(2,128)}, u32[]{:S(2)}) copy-start(f32[2,8]{1,0:T(2,128)} %param.10) | copy-start | bytes 196
  43.9 67.9 %collective-permute-start.5 = (f32[2,4,8,1536]{3,2,1,0:T(8,128)}, f32[2,4,8,1536]{3,2,1,0:T(8,128)S(1)}, u32[]{:S(2)}, u32[]{:S(2)}) collective-permute-start(f32[2,4,8,1536]{3,2,1,0:T(8,128)} %get-tuple-element.15), channel_id=1, source_target_pairs={{0,1},{1,0},{2,3},{3,2},{4,5},{5,4},{6,7},{7,6},{8,9},{9,8},{10,11... | collective-permute-start | bytes 1179656 | tf_op jit(solution)/shard_map/ppermute | solution.py:516
  44.4 67.5 %collective-permute-start.6 = (f32[2,4,8,1536]{3,2,1,0:T(8,128)}, f32[2,4,8,1536]{3,2,1,0:T(8,128)S(1)}, u32[]{:S(2)}, u32[]{:S(2)}) collective-permute-start(f32[2,4,8,1536]{3,2,1,0:T(8,128)} %get-tuple-element.17), channel_id=1, source_target_pairs={{0,2},{1,3},{2,0},{3,1},{4,6},{5,7},{6,4},{7,5},{8,10},{9,11},{10,... | collective-permute-start | bytes 1179656 | tf_op jit(solution)/shard_map/ppermute | solution.py:516
  47.0 77.6 %collective-permute-start.7 = (f32[2,4,8,1536]{3,2,1,0:T(8,128)}, f32[2,4,8,1536]{3,2,1,0:T(8,128)S(1)}, u32[]{:S(2)}, u32[]{:S(2)}) collective-permute-start(f32[2,4,8,1536]{3,2,1,0:T(8,128)} %get-tuple-element.18), channel_id=1, source_target_pairs={{0,3},{1,2},{2,1},{3,0},{4,7},{5,6},{6,5},{7,4},{8,11},{9,10},{10,... | collective-permute-start | bytes 1179656 | tf_op jit(solution)/shard_map/ppermute | solution.py:516
  105.8 44.1 %all-to-all-start = ((f32[4,4,2,8,1536]{4,3,2,1,0:T(8,128)}), f32[4,4,2,8,1536]{4,3,2,1,0:T(8,128)S(1)}, u32[]{:S(2)}, u32[]{:S(2)}) async-start(f32[4,4,2,8,1536]{4,3,2,1,0:T(8,128)} %filter_first.1), calls=%async_computation | async-start | bytes 3145728 | tf_op jit(solution)/shard_map/all_to_all | solution.py:513
  111.9 12.7 %copy-start.5 = (f32[2,4,8,1536]{3,2,1,0:T(8,128)}, f32[2,4,8,1536]{3,2,1,0:T(8,128)S(1)}, u32[]{:S(2)}) copy-start(f32[2,4,8,1536]{3,2,1,0:T(8,128)S(1)} %collective-permute-done.5.refs_3_) | copy-start | bytes 1179652
  111.9 12.7 %copy-start.6 = (f32[2,4,8,1536]{3,2,1,0:T(8,128)}, f32[2,4,8,1536]{3,2,1,0:T(8,128)S(1)}, u32[]{:S(2)}) copy-start(f32[2,4,8,1536]{3,2,1,0:T(8,128)S(1)} %collective-permute-done.6.refs_4_) | copy-start | bytes 1179652
  124.6 0.8 copy-start.7
  134.6 18.1 %copy-start.8 = (s32[1536]{0:T(1024)S(1)}, s32[1536]{0:T(1024)}, u32[]{:S(2)}) copy-start(s32[1536]{0:T(1024)} %param.12) | copy-start | bytes 18436
  134.7 36.3 %collective-permute-start.8 = (f32[16,8,1536]{2,1,0:T(8,128)}, f32[16,8,1536]{2,1,0:T(8,128)}, u32[]{:S(2)}, u32[]{:S(2)}) collective-permute-start(f32[16,8,1536]{2,1,0:T(8,128)} %get-tuple-element.20), channel_id=1, source_target_pairs={{0,1},{1,0},{2,3},{3,2},{4,5},{5,4},{6,7},{7,6},{8,9},{9,8},{10,11... | collective-permute-start | bytes 2359304 | tf_op jit(solution)/shard_map/ppermute | solution.py:516
  134.7 66.1 %collective-permute-start.9 = (f32[16,8,1536]{2,1,0:T(8,128)}, f32[16,8,1536]{2,1,0:T(8,128)S(1)}, u32[]{:S(2)}, u32[]{:S(2)}) collective-permute-start(f32[16,8,1536]{2,1,0:T(8,128)} %get-tuple-element.21), channel_id=1, source_target_pairs={{0,2},{1,3},{2,0},{3,1},{4,6},{5,7},{6,4},{7,5},{8,10},{9,11},{10,... | collective-permute-start | bytes 2359304 | tf_op jit(solution)/shard_map/ppermute | solution.py:516
  134.8 82.9 %collective-permute-start.10 = (f32[16,8,1536]{2,1,0:T(8,128)}, f32[16,8,1536]{2,1,0:T(8,128)S(1)}, u32[]{:S(2)}, u32[]{:S(2)}) collective-permute-start(f32[16,8,1536]{2,1,0:T(8,128)} %get-tuple-element.22), channel_id=1, source_target_pairs={{0,3},{1,2},{2,1},{3,0},{4,7},{5,6},{6,5},{7,4},{8,11},{9,10},{10,... | collective-permute-start | bytes 2359304 | tf_op jit(solution)/shard_map/ppermute | solution.py:516
  153.1 2.4 %collective-permute-start.11 = (f32[4,2,2,64]{3,2,0,1:T(2,128)S(1)}, f32[4,2,2,64]{3,2,0,1:T(2,128)S(1)}, u32[]{:S(2)}, u32[]{:S(2)}) collective-permute-start(f32[4,2,2,64]{3,2,0,1:T(2,128)S(1)} %copy.14), channel_id=1, source_target_pairs={{0,4},{4,0},{8,12},{12,8},{16,20},{20,16},{24,28},{28,24},{1,5},{5... | collective-permute-start | bytes 12296 | tf_op jit(solution)/shard_map/ppermute | solution.py:564
  155.4 3.7 %collective-permute-start.12 = (f32[4,2,2,64]{3,2,0,1:T(2,128)S(1)}, f32[4,2,2,64]{3,2,0,1:T(2,128)S(1)}, u32[]{:S(2)}, u32[]{:S(2)}) collective-permute-start(f32[4,2,2,64]{3,2,0,1:T(2,128)S(1)} %copy_add_fusion), channel_id=1, source_target_pairs={{0,8},{4,12},{8,0},{12,4},{16,24},{20,28},{24,16},{28,20},{1,9},{5... | collective-permute-start | bytes 12296 | tf_op jit(solution)/shard_map/ppermute | solution.py:564
  159.1 8.0 %collective-permute-start.13 = (f32[4,2,2,64]{3,2,0,1:T(2,128)S(1)}, f32[4,2,2,64]{3,2,0,1:T(2,128)S(1)}, u32[]{:S(2)}, u32[]{:S(2)}) collective-permute-start(f32[4,2,2,64]{3,2,0,1:T(2,128)S(1)} %add.68), channel_id=1, source_target_pairs={{0,16},{4,20},{8,24},{12,28},{16,0},{20,4},{24,8},{28,12},{1,17},{... | collective-permute-start | bytes 12296 | tf_op jit(solution)/shard_map/ppermute | solution.py:564
  167.1 52.6 %collective-permute-start.16 = (f32[4,2,2,64]{3,2,0,1:T(2,128)S(1)}, f32[4,2,2,64]{3,2,0,1:T(2,128)S(1)}, u32[]{:S(2)}, u32[]{:S(2)}) collective-permute-start(f32[4,2,2,64]{3,2,0,1:T(2,128)S(1)} %add.69), channel_id=1, source_target_pairs={{0,3},{1,2},{2,1},{3,0},{4,7},{5,6},{6,5},{7,4},{8,11},{9,10},{10,... | collective-permute-start | bytes 12296 | tf_op jit(solution)/shard_map/ppermute | solution.py:516
  167.1 52.6 %collective-permute-start.15 = (f32[4,2,2,64]{3,2,0,1:T(2,128)S(1)}, f32[4,2,2,64]{3,2,0,1:T(2,128)S(1)}, u32[]{:S(2)}, u32[]{:S(2)}) collective-permute-start(f32[4,2,2,64]{3,2,0,1:T(2,128)S(1)} %add.69), channel_id=1, source_target_pairs={{0,2},{1,3},{2,0},{3,1},{4,6},{5,7},{6,4},{7,5},{8,10},{9,11},{10,... | collective-permute-start | bytes 12296 | tf_op jit(solution)/shard_map/ppermute | solution.py:516
  170.9 48.8 %collective-permute-start.14 = (f32[4,2,2,64]{3,2,0,1:T(2,128)S(1)}, f32[4,2,2,64]{3,2,0,1:T(2,128)S(1)}, u32[]{:S(2)}, u32[]{:S(2)}) collective-permute-start(f32[4,2,2,64]{3,2,0,1:T(2,128)S(1)} %add.69), channel_id=1, source_target_pairs={{0,1},{1,0},{2,3},{3,2},{4,5},{5,4},{6,7},{7,6},{8,9},{9,8},{10,11... | collective-permute-start | bytes 12296 | tf_op jit(solution)/shard_map/ppermute | solution.py:516
  172.3 1.1 copy-start.1

commit v17 on v15

--- a/solution.py
+++ b/solution.py
@@ -498,12 +498,16 @@
 
     loads = [pltpu.make_async_copy(far(base_hbm, at), near(at), base_sems.at[n]) for n, at in enumerate(spots)]
     stores = [pltpu.make_async_copy(near(at), far(out_hbm, at), base_sems.at[n]) for n, at in enumerate(spots)]
-    copies = [pltpu.make_async_copy(terms[n], term_ref.at[n], term_sems.at[n]) for n in range(count)]
-    start_all(copies)
-    start_all(loads)
-    wait_all(copies)
-    for load, store, at in zip(loads, stores, spots):
+    copies = [
+        pltpu.make_async_copy(terms[at[0]].at[at[4]], term_ref.at[at[0], at[4]], term_sems.at[n])
+        for n, at in enumerate(spots)
+    ]
+    for load, copy in zip(loads, copies):
+        load.start()
+        copy.start()
+    for load, copy, store, at in zip(loads, copies, stores, spots):
         load.wait()
+        copy.wait()
         base_ref[at[0], at[4]] = base_ref[at[0], at[4]] + term_ref[at[0], at[4]]
         store.start()
     wait_all(stores)
@@ -522,7 +526,7 @@
             buffer,
             buffer,
             pltpu.SemaphoreType.DMA((copies,)),
-            pltpu.SemaphoreType.DMA((len(terms),)),
+            pltpu.SemaphoreType.DMA((copies,)),
         ],
         input_output_aliases={1: 0},
         compiler_params=pltpu.CompilerParams(vmem_limit_bytes=24 << 20),

time: 218 us -> 218 us (level)
  transfers between devices with their start and end apart: 16 -> 16, of which waited for: 9 -> 9; matrix products, arithmetic and copies ran while one was open for 3% -> 3% of each run, Pallas kernels for 18% -> 19%
where the time goes in v17:
time: 218 us; the launch traced here: 217 us
  waiting for transfers between devices  131 us (60%)
  Pallas kernels  43.9 us (20%)
  starting transfers between devices  30.8 us (14%)
  local copies, waits for them, and re-layouts  9.8 us (4%)
    ppermute x9, waiting for transfers between devices, swap(): lax.ppermute(blocks[x], 'span', pairs[x])  58.9 us
    all_to_all x2, waiting for transfers between devices, exchange(): return lax.all_to_all(lines, 'span', split_axis=0, concat_axis=0)  46.4 us
    ppermute x1, waiting for transfers between devices, on_device(): high = lax.ppermute(field[:, :, :, :PAD], 'wall', backward)  18.9 us
    pallas_call x1, Pallas kernels, local_terms(): pl.pallas_call(local_kernel, grid=(mode_count,), out_shape=jax.ShapeDtype...  15 us
    ppermute x9, starting transfers between devices, swap(): lax.ppermute(blocks[x], 'span', pairs[x])  12.5 us
    all_to_all x2, starting transfers between devices, exchange(): return lax.all_to_all(lines, 'span', split_axis=0, concat_axis=0)  11.9 us
    pallas_call x1, Pallas kernels, filter_rest(): return call(spots, tables, lines, field, *received)  9.16 us
    pallas_call x3, Pallas kernels, add_rest(): pl.pallas_call(functools.partial(add_rest_kernel, pieces, partners), out_...  8.45 us
  transfers between devices with their start and end apart: 16, of which 9 were waited for; matrix products, arithmetic and copies ran while one was open for 3% of the time, Pallas kernels for 19%

profile of v17, /device:TPU:10, one launch (start us, length us, event | category | flops | bytes accessed | tf_op | source)
XLA Modules:
  0.0 217.0 jit_solution(12029469465365415606)
XLA Ops:
  0.6 3.2 %gather_lines.1 = f32[4,4,4,8,1536]{4,3,2,1,0:T(8,128)} custom-call(f32[4,6,1,4,8,1536]{5,4,3,2,1,0:T(8,128)} %bitcast.27), custom_call_target="tpu_custom_call" | custom-call | bytes 6291456 | tf_op jit(solution)/shard_map/gather_lines/pallas_call | solution.py:260
  3.8 5.3 %all-to-all-start = ((f32[4,4,4,8,1536]{4,3,2,1,0:T(8,128)}), f32[4,4,4,8,1536]{4,3,2,1,0:T(8,128)}, u32[]{:S(2)}, u32[]{:S(2)}) async-start(f32[4,4,4,8,1536]{4,3,2,1,0:T(8,128)} %gather_lines.1), calls=%async_computation | async-start | bytes 6291456 | tf_op jit(solution)/shard_map/all_to_all | solution.py:556
  9.1 0.0 copy-start.9
  9.1 0.0 copy-start.3
  9.1 0.0 copy-start.2
  9.2 2.9 %fusion.6 = (f32[4,3,2,8,1536]{4,3,2,1,0:T(8,128)}, f32[4,3,2,8,1536]{4,3,2,1,0:T(8,128)S(1)}) fusion(f32[4,3,2,32,1536]{4,3,2,1,0:T(8,128)} %field_ref.1), kind=kLoop, calls=%fused_computation.16 | loop fusion | bytes 4718592 | tf_op jit(solution)/shard_map/slice | solution.py:573
  12.0 1.9 collective-permute-start.1
  14.0 2.4 %collective-permute-start = (f32[4,3,2,8,1536]{4,3,2,1,0:T(8,128)S(1)}, f32[4,3,2,8,1536]{4,3,2,1,0:T(8,128)S(1)}, u32[]{:S(2)}, u32[]{:S(2)}) collective-permute-start(f32[4,3,2,8,1536]{4,3,2,1,0:T(8,128)S(1)} %get-tuple-element.28), channel_id=1, source_target_pairs={{0,4},{4,8},{8,12},{12,16},{16,20},{20,24},{24,28},{1,5},{5,9},{9,... | collective-permute-start | bytes 3538952 | tf_op jit(solution)/shard_map/ppermute | solution.py:572
  16.4 0.0 copy-done.9
  16.4 2.3 %dynamic-slice_bitcast_fusion = (f32[2,4,8,1536]{3,2,1,0:T(8,128)}, f32[2,4,8,1536]{3,2,1,0:T(8,128)}, f32[2,4,8,1536]{3,2,1,0:T(8,128)}) fusion(f32[4,6,1,4,8,1536]{5,4,3,2,1,0:T(8,128)} %bitcast.28, s32[]{:T(128)S(6)} %select_n.72, s32[]{:T(128)S(6)} %select_n.71, s32[]{:T(128)S(6)} %select_n.70), kind=kLoop, calls=%fused_computation.1 | loop fusion | bytes 2359308 | tf_op jit(solution)/shard_map/reshape | solution.py:584
  18.7 18.9 %collective-permute-done.1.high_ref = f32[4,3,2,8,1536]{4,3,2,1,0:T(8,128)S(1)} collective-permute-done((f32[4,3,2,8,1536]{4,3,2,1,0:T(8,128)}, f32[4,3,2,8,1536]{4,3,2,1,0:T(8,128)S(1)}, u32[]{:S(2)}, u32[]{:S(2)}) %collective-permute-start.1) | collective-permute-done | bytes 1179680 | tf_op jit(solution)/shard_map/ppermute | solution.py:573
  37.6 0.0 collective-permute-done.low_ref
  37.6 0.0 copy-done.3
  37.6 0.1 broadcast_in_dim.46.flow_ref
  37.7 0.0 copy-done.2
  37.7 0.1 broadcast_in_dim.45.coef_ref
  37.8 0.0 copy-start
  37.8 2.3 %copy-done = f32[4,3,2,32,1536]{4,3,2,1,0:T(8,128)S(1)} copy-done((f32[4,3,2,32,1536]{4,3,2,1,0:T(8,128)S(1)}, f32[4,3,2,32,1536]{4,3,2,1,0:T(8,128)}, u32[]{:S(2)}) %copy-start) | copy-done | bytes 4718616
  40.1 0.0 copy-start.4
  40.2 15.0 %local_terms.1 = f32[4,3,2,32,1536]{4,3,2,1,0:T(8,128)} custom-call(f32[4]{0:T(128)S(1)} %convert_multiply_fusion.rate_ref, f32[15,32,128]{2,1,0:T(8,128)S(1)} %broadcast_in_dim.45.coef_ref, f32[2,32,128]{2,1,0:T(8,128)S(1)} %broadcast_in_dim.46.flow_ref, f32[4,3,2,32,1536]{4,3,2,1,0:T(8,128)S(1)} %copy-done, ...), custom_call_target="tpu_custom_call" | custom-call | flops 47185920 | bytes 11796480 | tf_op jit(solution)/shard_map/local_terms/pallas_call | solution.py:410
  55.1 0.0 collective-permute-start.2
  55.1 2.9 %collective-permute-start.3 = (f32[2,4,8,1536]{3,2,1,0:T(8,128)}, f32[2,4,8,1536]{3,2,1,0:T(8,128)S(1)}, u32[]{:S(2)}, u32[]{:S(2)}) collective-permute-start(f32[2,4,8,1536]{3,2,1,0:T(8,128)} %get-tuple-element.17), channel_id=1, source_target_pairs={{0,2},{1,3},{2,0},{3,1},{4,6},{5,7},{6,4},{7,5},{8,10},{9,11},{10,... | collective-permute-start | bytes 1179656 | tf_op jit(solution)/shard_map/ppermute | solution.py:559
  58.0 0.6 collective-permute-start.4
  58.6 0.0 copy-done.4
  58.6 0.1 rev.3
  58.7 36.2 %all-to-all-done.lines_hbm = f32[4,4,4,8,1536]{4,3,2,1,0:T(8,128)} async-done(((f32[4,4,4,8,1536]{4,3,2,1,0:T(8,128)}), f32[4,4,4,8,1536]{4,3,2,1,0:T(8,128)}, u32[]{:S(2)}, u32[]{:S(2)}) %all-to-all-start) | async-done | bytes 3145760 | tf_op jit(solution)/shard_map/all_to_all | solution.py:556
  94.9 5.3 %filter_first.1 = f32[4,4,2,8,1536]{4,3,2,1,0:T(8,128)} custom-call(bf16[24,2,256,256]{3,2,1,0:T(8,128)(2,1)} %constant.92.clone.table_hbm, f32[4,4,4,8,1536]{4,3,2,1,0:T(8,128)} %all-to-all-done.lines_hbm), custom_call_target="tpu_custom_call" | custom-call | flops 1000000 | tf_op jit(solution)/shard_map/filter_first/pallas_call | solution.py:358
  100.3 6.6 %all-to-all-start.1 = ((f32[4,4,2,8,1536]{4,3,2,1,0:T(8,128)}), f32[4,4,2,8,1536]{4,3,2,1,0:T(8,128)S(1)}, u32[]{:S(2)}, u32[]{:S(2)}) async-start(f32[4,4,2,8,1536]{4,3,2,1,0:T(8,128)} %filter_first.1), calls=%async_computation.1 | async-start | bytes 3145728 | tf_op jit(solution)/shard_map/all_to_all | solution.py:556
  106.8 0.0 collective-permute-done.2.refs_0_
  106.8 0.0 collective-permute-done.3.refs_1_
  106.8 0.0 copy-start.6
  106.9 14.8 %collective-permute-done.4.refs_2_ = f32[2,4,8,1536]{3,2,1,0:T(8,128)S(1)} collective-permute-done((f32[2,4,8,1536]{3,2,1,0:T(8,128)}, f32[2,4,8,1536]{3,2,1,0:T(8,128)S(1)}, u32[]{:S(2)}, u32[]{:S(2)}) %collective-permute-start.4) | collective-permute-done | bytes 393248 | tf_op jit(solution)/shard_map/ppermute | solution.py:559
  121.7 0.0 copy-done.5
  121.7 0.0 copy-done.6
  121.7 0.8 copy-done.7
  122.4 9.2 %filter_rest.1 = (f32[16,8,1536]{2,1,0:T(8,128)}, f32[16,8,1536]{2,1,0:T(8,128)}, f32[16,8,1536]{2,1,0:T(8,128)}, f32[16,8,1536]{2,1,0:T(8,128)}) custom-call(s32[1]{0:T(128)} %bitcast.me_ref, bf16[24,2,256,256]{3,2,1,0:T(8,128)(2,1)} %constant.92.clone.table_hbm, f32[4,4,4,8,1536]{4,3,2,1,0:T(8,128)} %all-to-all-done.lines_hbm, ...), custom_call_target="tpu_custom_call" | custom-call | flops 99999997952 | tf_op jit(solution)/shard_map/filter_rest/pallas_call | solution.py:370
  131.6 0.1 collective-permute-start.5
  131.7 1.1 collective-permute-start.6
  132.8 2.4 %collective-permute-start.7 = (f32[16,8,1536]{2,1,0:T(8,128)}, f32[16,8,1536]{2,1,0:T(8,128)S(1)}, u32[]{:S(2)}, u32[]{:S(2)}) collective-permute-start(f32[16,8,1536]{2,1,0:T(8,128)} %get-tuple-element.22), channel_id=1, source_target_pairs={{0,3},{1,2},{2,1},{3,0},{4,7},{5,6},{6,5},{7,4},{8,11},{9,10},{10,... | collective-permute-start | bytes 2359304 | tf_op jit(solution)/shard_map/ppermute | solution.py:559
  135.2 10.2 %all-to-all-done.1.term_hbm = f32[4,4,2,8,1536]{4,3,2,1,0:T(8,128)S(1)} async-done(((f32[4,4,2,8,1536]{4,3,2,1,0:T(8,128)}), f32[4,4,2,8,1536]{4,3,2,1,0:T(8,128)S(1)}, u32[]{:S(2)}, u32[]{:S(2)}) %all-to-all-start.1) | async-done | bytes 1572896 | tf_op jit(solution)/shard_map/all_to_all | solution.py:556
  145.4 0.1 broadcast_in_dim.50.weight_ref
  145.5 2.8 %add_first.1 = (f32[4,6,1,4,8,1536]{5,4,3,2,1,0:T(8,128)}, f32[4,4,1536]{2,1,0:T(4,128)S(1)}) custom-call(s32[1]{0:T(128)} %bitcast.me_ref, f32[4,6,1,4,8,1536]{5,4,3,2,1,0:T(8,128)} %bitcast.30, f32[4,2,8,128]{3,2,1,0:T(8,128)S(1)} %broadcast_in_dim.50.weight_ref, f32[4,4,2,8,1536]{4,3,2,1,0:T(8,128)S(1)} %all-to-all-done.1.term_hbm), custom_call_target="tpu_custom_call", output_to_operand_aliasing={{0}: (1, {})} | custom-call | flops 393216 | bytes 4718592 | tf_op jit(solution)/shard_map/add_first/pallas_call | solution.py:459
  148.3 0.0 copy-done.8
  148.3 0.3 fusion.1
  148.7 0.1 collective-permute-start.8
  148.7 1.2 collective-permute-done.8
  149.9 0.5 collective-permute-start.9
  150.4 3.2 %collective-permute-done.9 = f32[4,2,2,64]{3,2,0,1:T(2,128)S(1)} collective-permute-done((f32[4,2,2,64]{3,2,0,1:T(2,128)S(1)}, f32[4,2,2,64]{3,2,0,1:T(2,128)S(1)}, u32[]{:S(2)}, u32[]{:S(2)}) %collective-permute-start.9) | collective-permute-done | bytes 4128 | tf_op jit(solution)/shard_map/ppermute | solution.py:606
  153.6 1.5 collective-permute-start.10
  155.1 2.1 collective-permute-done.10
  157.2 1.2 collective-permute-start.13
  158.4 4.2 %collective-permute-start.12 = (f32[4,2,2,64]{3,2,0,1:T(2,128)S(1)}, f32[4,2,2,64]{3,2,0,1:T(2,128)S(1)}, u32[]{:S(2)}, u32[]{:S(2)}) collective-permute-start(f32[4,2,2,64]{3,2,0,1:T(2,128)S(1)} %add.60), channel_id=1, source_target_pairs={{0,2},{1,3},{2,0},{3,1},{4,6},{5,7},{6,4},{7,5},{8,10},{9,11},{10,... | collective-permute-start | bytes 12296 | tf_op jit(solution)/shard_map/ppermute | solution.py:559
  162.6 0.0 collective-permute-done.5.refs_1_
  162.6 0.0 collective-permute-start.11
  162.6 1.1 copy-done.1
  163.8 3.5 %add_rest.3.base_hbm = f32[4,6,1,4,8,1536]{5,4,3,2,1,0:T(8,128)} custom-call(s32[1]{0:T(128)} %bitcast.me_ref, f32[4,6,1,4,8,1536]{5,4,3,2,1,0:T(8,128)} %get-tuple-element.14.base_hbm, f32[16,8,1536]{2,1,0:T(8,128)S(1)} %copy-done.1, f32[16,8,1536]{2,1,0:T(8,128)} %collective-permute-done.5.refs_1_), custom_call_target="tpu_custom_call", output_to_operand_aliasing={{}: (1, {})} | custom-call | flops 393216 | bytes 4718592 | tf_op jit(solution)/shard_map/add_rest/pallas_call | solution.py:520
  167.2 29.2 %collective-permute-done.6.refs_0_ = f32[16,8,1536]{2,1,0:T(8,128)S(1)} collective-permute-done((f32[16,8,1536]{2,1,0:T(8,128)}, f32[16,8,1536]{2,1,0:T(8,128)S(1)}, u32[]{:S(2)}, u32[]{:S(2)}) %collective-permute-start.6) | collective-permute-done | bytes 786464 | tf_op jit(solution)/shard_map/ppermute | solution.py:559
  196.4 2.5 %add_rest.4.base_hbm = f32[4,6,1,4,8,1536]{5,4,3,2,1,0:T(8,128)} custom-call(s32[1]{0:T(128)} %bitcast.me_ref, f32[4,6,1,4,8,1536]{5,4,3,2,1,0:T(8,128)} %add_rest.3.base_hbm, f32[16,8,1536]{2,1,0:T(8,128)S(1)} %collective-permute-done.6.refs_0_), custom_call_target="tpu_custom_call", output_to_operand_aliasing={{}: (1, {})} | custom-call | flops 196608 | bytes 2359296 | tf_op jit(solution)/shard_map/add_rest/pallas_call | solution.py:520
  198.9 14.9 %collective-permute-done.7.refs_0_ = f32[16,8,1536]{2,1,0:T(8,128)S(1)} collective-permute-done((f32[16,8,1536]{2,1,0:T(8,128)}, f32[16,8,1536]{2,1,0:T(8,128)S(1)}, u32[]{:S(2)}, u32[]{:S(2)}) %collective-permute-start.7) | collective-permute-done | bytes 786464 | tf_op jit(solution)/shard_map/ppermute | solution.py:559
  213.8 2.5 %add_rest.5 = f32[4,6,1,4,8,1536]{5,4,3,2,1,0:T(8,128)} custom-call(s32[1]{0:T(128)} %bitcast.me_ref, f32[4,6,1,4,8,1536]{5,4,3,2,1,0:T(8,128)} %add_rest.4.base_hbm, f32[16,8,1536]{2,1,0:T(8,128)S(1)} %collective-permute-done.7.refs_0_), custom_call_target="tpu_custom_call", output_to_operand_aliasing={{}: (1, {})} | custom-call | flops 196608 | bytes 2359296 | tf_op jit(solution)/shard_map/add_rest/pallas_call | solution.py:520
  216.3 0.0 collective-permute-done.13
  216.3 0.0 collective-permute-done.12
  216.3 0.0 collective-permute-done.11
  216.4 0.6 add_bitcast_fusion
  (15 shorter events, 0.1 us)
Async XLA Ops:
  3.8 91.1 %all-to-all-start = ((f32[4,4,4,8,1536]{4,3,2,1,0:T(8,128)}), f32[4,4,4,8,1536]{4,3,2,1,0:T(8,128)}, u32[]{:S(2)}, u32[]{:S(2)}) async-start(f32[4,4,4,8,1536]{4,3,2,1,0:T(8,128)} %gather_lines.1), calls=%async_computation | async-start | bytes 6291456 | tf_op jit(solution)/shard_map/all_to_all | solution.py:556
  9.1 7.3 %copy-start.9 = (s32[4]{0:T(128)S(1)}, s32[4]{0:T(128)}, u32[]{:S(2)}) copy-start(s32[4]{0:T(128)} %param.11) | copy-start | bytes 52
  9.1 28.5 %copy-start.3 = (f32[2,32]{1,0:T(2,128)S(1)}, f32[2,32]{1,0:T(2,128)}, u32[]{:S(2)}) copy-start(f32[2,32]{1,0:T(2,128)} %param.8) | copy-start | bytes 772
  9.1 28.5 %copy-start.2 = (f32[15,32]{1,0:T(8,128)S(1)}, f32[15,32]{1,0:T(8,128)}, u32[]{:S(2)}) copy-start(f32[15,32]{1,0:T(8,128)} %param.9) | copy-start | bytes 5764
  12.0 25.6 %collective-permute-start.1 = (f32[4,3,2,8,1536]{4,3,2,1,0:T(8,128)}, f32[4,3,2,8,1536]{4,3,2,1,0:T(8,128)S(1)}, u32[]{:S(2)}, u32[]{:S(2)}) collective-permute-start(f32[4,3,2,8,1536]{4,3,2,1,0:T(8,128)} %get-tuple-element.27), channel_id=1, source_target_pairs={{4,0},{8,4},{12,8},{16,12},{20,16},{24,20},{28,24},{5,1},{9,5},{13... | collective-permute-start | bytes 3538952 | tf_op jit(solution)/shard_map/ppermute | solution.py:573
  14.0 23.6 %collective-permute-start = (f32[4,3,2,8,1536]{4,3,2,1,0:T(8,128)S(1)}, f32[4,3,2,8,1536]{4,3,2,1,0:T(8,128)S(1)}, u32[]{:S(2)}, u32[]{:S(2)}) collective-permute-start(f32[4,3,2,8,1536]{4,3,2,1,0:T(8,128)S(1)} %get-tuple-element.28), channel_id=1, source_target_pairs={{0,4},{4,8},{8,12},{12,16},{16,20},{20,24},{24,28},{1,5},{5,9},{9,... | collective-permute-start | bytes 3538952 | tf_op jit(solution)/shard_map/ppermute | solution.py:572
  37.8 2.3 %copy-start = (f32[4,3,2,32,1536]{4,3,2,1,0:T(8,128)S(1)}, f32[4,3,2,32,1536]{4,3,2,1,0:T(8,128)}, u32[]{:S(2)}) copy-start(f32[4,3,2,32,1536]{4,3,2,1,0:T(8,128)} %field_ref.1) | copy-start | bytes 14155780
  40.1 18.5 %copy-start.4 = (f32[2,8]{1,0:T(2,128)S(1)}, f32[2,8]{1,0:T(2,128)}, u32[]{:S(2)}) copy-start(f32[2,8]{1,0:T(2,128)} %param.10) | copy-start | bytes 196
  55.1 51.7 %collective-permute-start.2 = (f32[2,4,8,1536]{3,2,1,0:T(8,128)}, f32[2,4,8,1536]{3,2,1,0:T(8,128)S(1)}, u32[]{:S(2)}, u32[]{:S(2)}) collective-permute-start(f32[2,4,8,1536]{3,2,1,0:T(8,128)} %get-tuple-element.15), channel_id=1, source_target_pairs={{0,1},{1,0},{2,3},{3,2},{4,5},{5,4},{6,7},{7,6},{8,9},{9,8},{10,11... | collective-permute-start | bytes 1179656 | tf_op jit(solution)/shard_map/ppermute | solution.py:559
  55.1 51.7 %collective-permute-start.3 = (f32[2,4,8,1536]{3,2,1,0:T(8,128)}, f32[2,4,8,1536]{3,2,1,0:T(8,128)S(1)}, u32[]{:S(2)}, u32[]{:S(2)}) collective-permute-start(f32[2,4,8,1536]{3,2,1,0:T(8,128)} %get-tuple-element.17), channel_id=1, source_target_pairs={{0,2},{1,3},{2,0},{3,1},{4,6},{5,7},{6,4},{7,5},{8,10},{9,11},{10,... | collective-permute-start | bytes 1179656 | tf_op jit(solution)/shard_map/ppermute | solution.py:559
  58.0 63.6 %collective-permute-start.4 = (f32[2,4,8,1536]{3,2,1,0:T(8,128)}, f32[2,4,8,1536]{3,2,1,0:T(8,128)S(1)}, u32[]{:S(2)}, u32[]{:S(2)}) collective-permute-start(f32[2,4,8,1536]{3,2,1,0:T(8,128)} %get-tuple-element.18), channel_id=1, source_target_pairs={{0,3},{1,2},{2,1},{3,0},{4,7},{5,6},{6,5},{7,4},{8,11},{9,10},{10,... | collective-permute-start | bytes 1179656 | tf_op jit(solution)/shard_map/ppermute | solution.py:559
  100.3 45.2 %all-to-all-start.1 = ((f32[4,4,2,8,1536]{4,3,2,1,0:T(8,128)}), f32[4,4,2,8,1536]{4,3,2,1,0:T(8,128)S(1)}, u32[]{:S(2)}, u32[]{:S(2)}) async-start(f32[4,4,2,8,1536]{4,3,2,1,0:T(8,128)} %filter_first.1), calls=%async_computation.1 | async-start | bytes 3145728 | tf_op jit(solution)/shard_map/all_to_all | solution.py:556
  106.8 14.8 %copy-start.5 = (f32[2,4,8,1536]{3,2,1,0:T(8,128)}, f32[2,4,8,1536]{3,2,1,0:T(8,128)S(1)}, u32[]{:S(2)}) copy-start(f32[2,4,8,1536]{3,2,1,0:T(8,128)S(1)} %collective-permute-done.2.refs_0_) | copy-start | bytes 1179652
  106.8 14.8 %copy-start.6 = (f32[2,4,8,1536]{3,2,1,0:T(8,128)}, f32[2,4,8,1536]{3,2,1,0:T(8,128)S(1)}, u32[]{:S(2)}) copy-start(f32[2,4,8,1536]{3,2,1,0:T(8,128)S(1)} %collective-permute-done.3.refs_1_) | copy-start | bytes 1179652
  121.7 0.8 copy-start.7
  131.6 31.0 %collective-permute-start.5 = (f32[16,8,1536]{2,1,0:T(8,128)}, f32[16,8,1536]{2,1,0:T(8,128)}, u32[]{:S(2)}, u32[]{:S(2)}) collective-permute-start(f32[16,8,1536]{2,1,0:T(8,128)} %get-tuple-element.20), channel_id=1, source_target_pairs={{0,1},{1,0},{2,3},{3,2},{4,5},{5,4},{6,7},{7,6},{8,9},{9,8},{10,11... | collective-permute-start | bytes 2359304 | tf_op jit(solution)/shard_map/ppermute | solution.py:559
  131.7 64.7 %collective-permute-start.6 = (f32[16,8,1536]{2,1,0:T(8,128)}, f32[16,8,1536]{2,1,0:T(8,128)S(1)}, u32[]{:S(2)}, u32[]{:S(2)}) collective-permute-start(f32[16,8,1536]{2,1,0:T(8,128)} %get-tuple-element.21), channel_id=1, source_target_pairs={{0,2},{1,3},{2,0},{3,1},{4,6},{5,7},{6,4},{7,5},{8,10},{9,11},{10,... | collective-permute-start | bytes 2359304 | tf_op jit(solution)/shard_map/ppermute | solution.py:559
  132.8 81.0 %collective-permute-start.7 = (f32[16,8,1536]{2,1,0:T(8,128)}, f32[16,8,1536]{2,1,0:T(8,128)S(1)}, u32[]{:S(2)}, u32[]{:S(2)}) collective-permute-start(f32[16,8,1536]{2,1,0:T(8,128)} %get-tuple-element.22), channel_id=1, source_target_pairs={{0,3},{1,2},{2,1},{3,0},{4,7},{5,6},{6,5},{7,4},{8,11},{9,10},{10,... | collective-permute-start | bytes 2359304 | tf_op jit(solution)/shard_map/ppermute | solution.py:559
  145.5 2.8 %copy-start.8 = (s32[1536]{0:T(1024)S(1)}, s32[1536]{0:T(1024)}, u32[]{:S(2)}) copy-start(s32[1536]{0:T(1024)} %param.12) | copy-start | bytes 18436
  148.7 1.2 collective-permute-start.8
  149.9 3.7 %collective-permute-start.9 = (f32[4,2,2,64]{3,2,0,1:T(2,128)S(1)}, f32[4,2,2,64]{3,2,0,1:T(2,128)S(1)}, u32[]{:S(2)}, u32[]{:S(2)}) collective-permute-start(f32[4,2,2,64]{3,2,0,1:T(2,128)S(1)} %copy_add_fusion), channel_id=1, source_target_pairs={{0,8},{4,12},{8,0},{12,4},{16,24},{20,28},{24,16},{28,20},{1,9},{5... | collective-permute-start | bytes 12296 | tf_op jit(solution)/shard_map/ppermute | solution.py:606
  153.6 3.7 %collective-permute-start.10 = (f32[4,2,2,64]{3,2,0,1:T(2,128)S(1)}, f32[4,2,2,64]{3,2,0,1:T(2,128)S(1)}, u32[]{:S(2)}, u32[]{:S(2)}) collective-permute-start(f32[4,2,2,64]{3,2,0,1:T(2,128)S(1)} %add.59), channel_id=1, source_target_pairs={{0,16},{4,20},{8,24},{12,28},{16,0},{20,4},{24,8},{28,12},{1,17},{... | collective-permute-start | bytes 12296 | tf_op jit(solution)/shard_map/ppermute | solution.py:606
  157.2 59.1 %collective-permute-start.13 = (f32[4,2,2,64]{3,2,0,1:T(2,128)S(1)}, f32[4,2,2,64]{3,2,0,1:T(2,128)S(1)}, u32[]{:S(2)}, u32[]{:S(2)}) collective-permute-start(f32[4,2,2,64]{3,2,0,1:T(2,128)S(1)} %add.60), channel_id=1, source_target_pairs={{0,3},{1,2},{2,1},{3,0},{4,7},{5,6},{6,5},{7,4},{8,11},{9,10},{10,... | collective-permute-start | bytes 12296 | tf_op jit(solution)/shard_map/ppermute | solution.py:559
  158.4 57.9 %collective-permute-start.12 = (f32[4,2,2,64]{3,2,0,1:T(2,128)S(1)}, f32[4,2,2,64]{3,2,0,1:T(2,128)S(1)}, u32[]{:S(2)}, u32[]{:S(2)}) collective-permute-start(f32[4,2,2,64]{3,2,0,1:T(2,128)S(1)} %add.60), channel_id=1, source_target_pairs={{0,2},{1,3},{2,0},{3,1},{4,6},{5,7},{6,4},{7,5},{8,10},{9,11},{10,... | collective-permute-start | bytes 12296 | tf_op jit(solution)/shard_map/ppermute | solution.py:559
  162.6 53.7 %collective-permute-start.11 = (f32[4,2,2,64]{3,2,0,1:T(2,128)S(1)}, f32[4,2,2,64]{3,2,0,1:T(2,128)S(1)}, u32[]{:S(2)}, u32[]{:S(2)}) collective-permute-start(f32[4,2,2,64]{3,2,0,1:T(2,128)S(1)} %add.60), channel_id=1, source_target_pairs={{0,1},{1,0},{2,3},{3,2},{4,5},{5,4},{6,7},{7,6},{8,9},{9,8},{10,11... | collective-permute-start | bytes 12296 | tf_op jit(solution)/shard_map/ppermute | solution.py:559
  162.6 1.1 copy-start.1
